TPU v7x, 32 devices: a whole 2x2x4 slice. The times are simulated.
32 devices in a mesh: dp: 32 (over z, y, x, core).
Axes of the slice: x: 2, y: 2, z: 4, core: 2. Of those that a mesh axis runs over, the one named last changes fastest.
Arguments:
- embeds: bfloat16 [8192, 8, 512], P('dp'), may hold values from -6 to 6
- piece_counts: int32 [8192], P('dp'), may hold values from 1 to 8
- group_ids: int32 [8192], P('dp'), may hold values from 0 to 7
- group_table: bfloat16 [8, 512], P(None, 'dp'), may hold values from -3 to 3
- gain_attn: bfloat16 [512], P('dp'), may hold values from 0.5 to 1.5
- shift_attn: bfloat16 [512], P('dp'), may hold values from -2 to 2
- w_qkv: bfloat16 [512, 1536], P('dp'), may hold values from -0.25 to 0.25
- w_out: bfloat16 [512, 512], P('dp'), may hold values from -0.375 to 0.375
- gain_ffn: bfloat16 [512], P('dp'), may hold values from 0.5 to 1.5
- shift_ffn: bfloat16 [512], P('dp'), may hold values from -2 to 2
- w_up: bfloat16 [512, 2048], P('dp'), may hold values from -0.25 to 0.25
- bias_up: bfloat16 [2048], P('dp'), may hold values from -2 to 2
- w_down: bfloat16 [2048, 512], P('dp'), may hold values from -0.1875 to 0.1875
- bias_down: bfloat16 [512], P('dp'), may hold values from -2 to 2
- w_proj: bfloat16 [512, 2048], P('dp'), may hold values from -0.25 to 0.25
- cotangent: bfloat16 [8192, 2048], P('dp'), may hold values from -6 to 6
Outputs:
- output: bfloat16 [8192, 2048], P('dp')
- grad_embeds: bfloat16 [8192, 8, 512], P('dp')
- grad_table: float32 [8, 512], P(None, 'dp')
- grad_gain_attn: float32 [512], P('dp')
- grad_shift_attn: float32 [512], P('dp')
- grad_qkv: float32 [512, 1536], P('dp')
- grad_out: float32 [512, 512], P('dp')
- grad_gain_ffn: float32 [512], P('dp')
- grad_shift_ffn: float32 [512], P('dp')
- grad_up: float32 [512, 2048], P('dp')
- grad_bias_up: float32 [2048], P('dp')
- grad_down: float32 [2048, 512], P('dp')
- grad_bias_down: float32 [512], P('dp')
- grad_proj: float32 [512, 2048], P('dp')
Inputs may be any that keep to these rules, and one draw needn't show every extreme that they name: An entry's slots from piece_counts on are padding.
All inputs are finite; a program needn't handle non-finite values.
Results may differ from a plain program's by a relative error of at most 0.013.
Values may be sent and summed in bfloat16 or wider, within the bound.
No kernel may reach another device: no remote copies, remote signals or barrier semaphores. Data moves between devices by JAX's collectives and lax.ppermute only.
A program may use at most 128 MiB of HBM per device.

v0:
```python
import jax
import jax.numpy as jnp
from jax import lax
from jax.sharding import PartitionSpec as P

HEADS = 8


def layer_norm(values, gain, shift):
    center = values - jnp.mean(values, axis=-1, keepdims=True)
    spread = jnp.mean(center * center, axis=-1, keepdims=True)
    return center * lax.rsqrt(spread + 1e-05) * gain + shift


def gelu_exact(values):
    return jax.nn.gelu(values, approximate=False)


def softmax_last(values):
    return jax.nn.softmax(values, axis=-1)


def on_device(
    embeds,
    piece_counts,
    group_ids,
    group_table,
    gain_attn,
    shift_attn,
    w_qkv,
    w_out,
    gain_ffn,
    shift_ffn,
    w_up,
    bias_up,
    w_down,
    bias_down,
    w_proj,
    cotangent,
):
    (
        table_all,
        gain_one,
        shift_one,
        qkv_all,
        out_all,
        gain_two,
        shift_two,
        up_all,
        upbias_all,
        down_all,
        downbias_all,
        proj_all,
    ) = (
        lax.all_gather(group_table, "dp", axis=1, tiled=True),
        lax.all_gather(gain_attn, "dp", axis=0, tiled=True),
        lax.all_gather(shift_attn, "dp", axis=0, tiled=True),
        lax.all_gather(w_qkv, "dp", axis=0, tiled=True),
        lax.all_gather(w_out, "dp", axis=0, tiled=True),
        lax.all_gather(gain_ffn, "dp", axis=0, tiled=True),
        lax.all_gather(shift_ffn, "dp", axis=0, tiled=True),
        lax.all_gather(w_up, "dp", axis=0, tiled=True),
        lax.all_gather(bias_up, "dp", axis=0, tiled=True),
        lax.all_gather(w_down, "dp", axis=0, tiled=True),
        lax.all_gather(bias_down, "dp", axis=0, tiled=True),
        lax.all_gather(w_proj, "dp", axis=0, tiled=True),
    )
    entries, slots, width = embeds.shape
    head_dim = width // HEADS
    scale = head_dim ** (-0.5)
    onehot = (
        group_ids[:, None] == jnp.arange(table_all.shape[0], dtype=jnp.int32)[None, :]
    ).astype(jnp.bfloat16)
    group_rows = jnp.dot(onehot, table_all, preferred_element_type=jnp.float32)
    base = embeds.astype(jnp.float32) + group_rows[:, None, :]
    normed, norm_back = jax.vjp(
        layer_norm, base, gain_one.astype(jnp.float32), shift_one.astype(jnp.float32)
    )
    normed_low = normed.astype(jnp.bfloat16)
    normed_flat = normed_low.reshape(entries * slots, width)
    query = (
        jnp.dot(normed_low[:, 0, :], qkv_all[:, :width], preferred_element_type=jnp.float32)
        .astype(jnp.bfloat16)
        .reshape(entries, HEADS, head_dim)
    )
    keyval = (
        jnp.dot(normed_flat, qkv_all[:, width:], preferred_element_type=jnp.float32)
        .astype(jnp.bfloat16)
        .reshape(entries, slots, 2, HEADS, head_dim)
    )
    keys = keyval[:, :, 0]
    values = keyval[:, :, 1]
    scores = jnp.einsum("ehd,eshd->ehs", query, keys, preferred_element_type=jnp.float32) * scale
    live = (jnp.arange(slots, dtype=jnp.int32)[None, :] < piece_counts[:, None])[:, None, :]
    probs, soft_back = jax.vjp(softmax_last, jnp.where(live, scores, -1000000000.0))
    probs_low = probs.astype(jnp.bfloat16)
    mixed = (
        jnp.einsum("ehs,eshd->ehd", probs_low, values, preferred_element_type=jnp.float32)
        .reshape(entries, width)
        .astype(jnp.bfloat16)
    )
    first = base[:, 0, :] + jnp.dot(mixed, out_all, preferred_element_type=jnp.float32)
    normed_ffn, ffn_back = jax.vjp(
        layer_norm, first, gain_two.astype(jnp.float32), shift_two.astype(jnp.float32)
    )
    ffn_low = normed_ffn.astype(jnp.bfloat16)
    hidden, gelu_back = jax.vjp(
        gelu_exact,
        jnp.dot(ffn_low, up_all, preferred_element_type=jnp.float32)
        + upbias_all.astype(jnp.float32),
    )
    hidden_low = hidden.astype(jnp.bfloat16)
    second = (
        first
        + jnp.dot(hidden_low, down_all, preferred_element_type=jnp.float32)
        + downbias_all.astype(jnp.float32)
    )
    pooled_low = second.astype(jnp.bfloat16)
    output = jnp.dot(pooled_low, proj_all, preferred_element_type=jnp.float32).astype(jnp.bfloat16)
    grad_proj = jnp.einsum("ed,eo->do", pooled_low, cotangent, preferred_element_type=jnp.float32)
    grad_pool = jnp.einsum("eo,do->ed", cotangent, proj_all, preferred_element_type=jnp.float32)
    grad_downbias = jnp.sum(grad_pool, axis=0)
    pool_low = grad_pool.astype(jnp.bfloat16)
    grad_down = jnp.einsum("ef,ed->fd", hidden_low, pool_low, preferred_element_type=jnp.float32)
    grad_hidden = jnp.einsum("ed,fd->ef", pool_low, down_all, preferred_element_type=jnp.float32)
    grad_pre = gelu_back(grad_hidden)[0]
    grad_upbias = jnp.sum(grad_pre, axis=0)
    pre_low = grad_pre.astype(jnp.bfloat16)
    grad_up = jnp.einsum("ed,ef->df", ffn_low, pre_low, preferred_element_type=jnp.float32)
    grad_normffn = jnp.einsum("ef,df->ed", pre_low, up_all, preferred_element_type=jnp.float32)
    grad_first, grad_gaintwo, grad_shifttwo = ffn_back(grad_normffn)
    grad_first = grad_first + grad_pool
    branch_low = grad_first.astype(jnp.bfloat16)
    grad_out = jnp.einsum("ed,ef->df", mixed, branch_low, preferred_element_type=jnp.float32)
    grad_mixed = (
        jnp.einsum("ef,df->ed", branch_low, out_all, preferred_element_type=jnp.float32)
        .astype(jnp.bfloat16)
        .reshape(entries, HEADS, head_dim)
    )
    grad_probs = jnp.einsum("ehd,eshd->ehs", grad_mixed, values, preferred_element_type=jnp.float32)
    grad_values = jnp.einsum(
        "ehs,ehd->eshd", probs_low, grad_mixed, preferred_element_type=jnp.float32
    )
    scores_low = jnp.where(live, soft_back(grad_probs)[0], 0.0).astype(jnp.bfloat16)
    grad_query = (
        (jnp.einsum("ehs,eshd->ehd", scores_low, keys, preferred_element_type=jnp.float32) * scale)
        .astype(jnp.bfloat16)
        .reshape(entries, width)
    )
    grad_keys = (
        jnp.einsum("ehs,ehd->eshd", scores_low, query, preferred_element_type=jnp.float32) * scale
    )
    grad_keyval = (
        jnp.stack([grad_keys, grad_values], axis=2)
        .astype(jnp.bfloat16)
        .reshape(entries * slots, 2 * width)
    )
    grad_qkv = jnp.concatenate(
        [
            jnp.einsum(
                "ed,ef->df", normed_low[:, 0, :], grad_query, preferred_element_type=jnp.float32
            ),
            jnp.einsum("nd,nf->df", normed_flat, grad_keyval, preferred_element_type=jnp.float32),
        ],
        axis=1,
    )
    grad_normed = jnp.einsum(
        "nf,df->nd", grad_keyval, qkv_all[:, width:], preferred_element_type=jnp.float32
    ).reshape(entries, slots, width)
    grad_normed = grad_normed.at[:, 0, :].add(
        jnp.einsum("ef,df->ed", grad_query, qkv_all[:, :width], preferred_element_type=jnp.float32)
    )
    grad_base, grad_gainone, grad_shiftone = norm_back(grad_normed)
    grad_base = grad_base.at[:, 0, :].add(grad_first)
    grad_groups = jnp.dot(
        onehot.astype(jnp.float32).T, jnp.sum(grad_base, axis=1), precision=lax.Precision.HIGHEST
    )
    (
        sum_groups,
        sum_gainone,
        sum_shiftone,
        sum_qkv,
        sum_out,
        sum_gaintwo,
        sum_shifttwo,
        sum_up,
        sum_upbias,
        sum_down,
        sum_downbias,
        sum_proj,
    ) = (
        lax.psum_scatter(grad_groups, "dp", scatter_dimension=1, tiled=True),
        lax.psum_scatter(grad_gainone, "dp", scatter_dimension=0, tiled=True),
        lax.psum_scatter(grad_shiftone, "dp", scatter_dimension=0, tiled=True),
        lax.psum_scatter(grad_qkv, "dp", scatter_dimension=0, tiled=True),
        lax.psum_scatter(grad_out, "dp", scatter_dimension=0, tiled=True),
        lax.psum_scatter(grad_gaintwo, "dp", scatter_dimension=0, tiled=True),
        lax.psum_scatter(grad_shifttwo, "dp", scatter_dimension=0, tiled=True),
        lax.psum_scatter(grad_up, "dp", scatter_dimension=0, tiled=True),
        lax.psum_scatter(grad_upbias, "dp", scatter_dimension=0, tiled=True),
        lax.psum_scatter(grad_down, "dp", scatter_dimension=0, tiled=True),
        lax.psum_scatter(grad_downbias, "dp", scatter_dimension=0, tiled=True),
        lax.psum_scatter(grad_proj, "dp", scatter_dimension=0, tiled=True),
    )
    return (
        output,
        grad_base.astype(jnp.bfloat16),
        sum_groups,
        sum_gainone,
        sum_shiftone,
        sum_qkv,
        sum_out,
        sum_gaintwo,
        sum_shifttwo,
        sum_up,
        sum_upbias,
        sum_down,
        sum_downbias,
        sum_proj,
    )


def solution(mesh):
    placed = (
        P("dp", None, None),
        P("dp"),
        P("dp"),
        P(None, "dp"),
        P("dp"),
        P("dp"),
        P("dp", None),
        P("dp", None),
        P("dp"),
        P("dp"),
        P("dp", None),
        P("dp"),
        P("dp", None),
        P("dp"),
        P("dp", None),
        P("dp", None),
    )
    return jax.shard_map(
        on_device,
        mesh=mesh,
        in_specs=placed,
        out_specs=(
            P("dp", None),
            P("dp", None, None),
            P(None, "dp"),
            P("dp"),
            P("dp"),
            P("dp", None),
            P("dp", None),
            P("dp"),
            P("dp"),
            P("dp", None),
            P("dp"),
            P("dp", None),
            P("dp"),
            P("dp", None),
        ),
        check_vma=False,
    )
```

profile of v0, /device:TPU:0, one launch (start us, length us, event | category | flops | bytes accessed | tf_op | source)
XLA Modules:
  0.0 1096.4 jit_solution(17195277781464469324)
XLA Ops:
  10.1 43.7 %all-gather = bf16[32,16,8]{1,2,0:T(8,128)(2,1)S(1)} all-gather(bf16[1,16,8]{1,2,0:T(8,128)(2,1)} %bitcast.95), channel_id=1, replica_groups=mesh['dp'=32] {'dp'}, dimensions={0}, use_global_device_ids=true | all-gather | bytes 8448 | tf_op jit(solution)/shard_map/all_gather | solution.py:55
  59.0 37.2 %all-reduce.13 = (bf16[512]{0:T(512)(128)(2,1)S(1)}, bf16[512]{0:T(512)(128)(2,1)S(1)}, bf16[2048]{0:T(1024)(128)(2,1)S(1)}, bf16[512]{0:T(512)(128)(2,1)S(1)}, ...) all-reduce(bf16[512]{0:T(512)(128)(2,1)S(1)} %dynamic-update-slice.7, ...), channel_id=1, replica_groups=mesh['dp'=32] {'dp'}, use_global_device_ids=true, to_apply=%add.1 | all-reduce | flops 4608 | bytes 18432
  96.2 0.9 fusion.38
  97.2 3.1 fusion
  100.3 1.4 multiply_reduce_fusion.6
  102.3 45.4 %all_gather.40 = bf16[512,512]{1,0:T(8,128)(2,1)} all-gather(bf16[16,512]{1,0:T(8,128)(2,1)S(1)} %copy-done.39), channel_id=1, replica_groups=mesh['dp'=32] {'dp'}, dimensions={0}, use_global_device_ids=true | all-gather | bytes 540672 | tf_op jit(solution)/shard_map/all_gather | solution.py:59
  149.4 3.3 convert_add_fusion
  152.7 2.1 convolution_convert_fusion.3
  154.9 1.1 copy.44
  156.0 1.2 copy.81
  157.2 6.5 convolution_convert_fusion
  163.7 11.6 %reshape.219 = bf16[256,8,2,8,64]{4,3,2,1,0:T(8,128)(2,1)} reshape(bf16[2048,1024]{1,0:T(8,128)(2,1)} %convolution_convert_fusion) | data formatting | bytes 8388608 | tf_op jit(solution)/shard_map/reshape | solution.py:89
  175.3 5.9 multiply_reduce_fusion.3
  182.0 1.5 copy.57
  184.9 1.3 copy.82
  186.2 5.7 multiply_reduce_fusion.2
  191.9 1.3 copy.63
  193.2 1.6 fusion.52
  197.1 3.2 fusion.54
  200.3 8.6 multiply_convert_fusion
  208.9 34.9 %all-gather.10.cloned.1.call-done = bf16[2048,512]{1,0:T(8,128)(2,1)} async-done(((bf16[64,512]{1,0:T(8,128)(2,1)}), bf16[2048,512]{1,0:T(8,128)(2,1)}) %all-gather.10.cloned.1.call-update) | async-done | bytes 2097168 | tf_op jit(solution)/shard_map/all_gather | solution.py:64
  243.8 5.0 fusion.53
  248.9 1.5 multiply_reduce_fusion.7
  252.2 1.1 convolution_convert_fusion.2
  253.2 1.8 copy.46
  255.0 1.8 convert.20
  256.8 2.2 copy.83
  259.0 5.8 multiply_reduce_fusion.1
  264.8 2.2 copy.70
  267.8 1.5 fusion.43
  269.4 2.2 copy.84
  271.5 6.0 multiply_reduce_fusion
  277.5 2.4 copy.77
  279.9 1.1 multiply_convert_fusion.1
  281.0 2.4 multiply_bitcast_fusion
  283.9 1.1 copy-done.21
  285.0 2.4 fusion.17
  288.5 1.5 fusion.47
  290.0 2.3 multiply_reduce_fusion.4
  292.3 1.7 broadcast_add_fusion
  294.2 1.9 fusion.50
  296.1 1.3 convolution_bitcast_fusion.1
  297.5 1.3 fusion.29
  298.9 13.2 %copy.48 = bf16[256,8,2,8,64]{4,3,2,1,0:T(8,128)(2,1)} copy(bf16[256,8,2,8,64]{0,4,3,2,1:T(8,128)(2,1)} %copy-done.4) | data formatting | bytes 8388608 | tf_op jit(solution)/shard_map/convert_element_type | solution.py:155
  312.1 12.0 %convert_element_type.117 = bf16[2048,1024]{1,0:T(8,128)(2,1)} reshape(bf16[256,8,2,8,64]{4,3,2,1,0:T(8,128)(2,1)} %copy.48) | data formatting | bytes 8388608 | tf_op jit(solution)/shard_map/convert_element_type | solution.py:155
  324.1 1.3 fusion.28
  325.4 5.3 fusion.2
  330.7 1.9 pad_maximum_fusion
  334.0 2.8 fusion.22
  336.9 1.1 copy-done.13
  338.2 2.7 fusion.32
  341.6 2.3 fusion.15
  343.9 2.7 fusion.55
  346.6 1.6 copy-done.11
  348.2 2.5 copy.50
  350.7 38.9 %all-reduce.12 = (f32[512]{0:T(512)S(1)}, f32[512]{0:T(512)S(1)}, f32[512]{0:T(512)S(1)}, f32[512]{0:T(512)S(1)}, f32[2048]{0:T(1024)S(1)}, /*index=5*/f32[512]{0:T(512)S(1)}) all-reduce(f32[512]{0:T(512)S(1)} %get-tuple-element.80, f32[512]{0:T(512)S(1)} %get-tuple-element.82, ...), channel_id=3, replica_groups=mesh['dp'=32] {'dp'}, use_global_device_ids=true, to_apply=%region_14.15.clone | all-reduce | flops 4608 | bytes 36864
  393.1 3.3 convolution_convert_fusion.1
  396.3 34.0 %reduce-scatter.19.cloned.1.call-done = f32[16,8]{1,0:T(8,128)} async-done(((f32[512,8]{1,0:T(8,128)}), f32[16,8]{1,0:T(8,128)}) %reduce-scatter.19.cloned.1.call-update) | async-done | bytes 528
  430.3 1.4 copy.80
  431.7 132.1 %reduce-scatter.11.cloned.1.call-done = f32[16,512]{1,0:T(8,128)} async-done(((f32[512,512]{1,0:T(8,128)}), f32[16,512]{1,0:T(8,128)}) %reduce-scatter.11.cloned.1.call-update) | async-done | bytes 32784 | tf_op jit(solution)/shard_map/reduce_scatter | solution.py:196
  563.8 103.5 %reduce-scatter.9.cloned.1.call-done = f32[16,1536]{1,0:T(8,128)} async-done(((f32[512,1536]{1,0:T(8,128)}), f32[16,1536]{1,0:T(8,128)}) %reduce-scatter.9.cloned.1.call-update) | async-done | bytes 98320 | tf_op jit(solution)/shard_map/reduce_scatter | solution.py:195
  667.3 142.8 %reduce-scatter.13.cloned.1.call-done = f32[16,2048]{1,0:T(8,128)} async-done(((f32[512,2048]{1,0:T(8,128)}), f32[16,2048]{1,0:T(8,128)}) %reduce-scatter.13.cloned.1.call-update) | async-done | bytes 131088 | tf_op jit(solution)/shard_map/reduce_scatter | solution.py:199
  810.1 139.7 %reduce-scatter.15.cloned.1.call-done = f32[64,512]{1,0:T(8,128)} async-done(((f32[2048,512]{1,0:T(8,128)}), f32[64,512]{1,0:T(8,128)}) %reduce-scatter.15.cloned.1.call-update) | async-done | bytes 131088 | tf_op jit(solution)/shard_map/reduce_scatter | solution.py:201
  949.8 139.5 %reduce-scatter.17.cloned.1.call-done = f32[16,2048]{1,0:T(8,128)} async-done(((f32[512,2048]{1,0:T(8,128)}), f32[16,2048]{1,0:T(8,128)}) %reduce-scatter.17.cloned.1.call-update) | async-done | bytes 131088 | tf_op jit(solution)/shard_map/reduce_scatter | solution.py:203
  (168 shorter events, 24.9 us)
Async XLA Ops:
  7.2 189.9 %copy-start = (bf16[256,2048]{1,0:T(8,128)(2,1)S(1)}, bf16[256,2048]{1,0:T(8,128)(2,1)}, u32[]{:S(2)}) copy-start(bf16[256,2048]{1,0:T(8,128)(2,1)} %param.35) | copy-start | bytes 3145732
  7.2 93.1 %copy-start.1 = (bf16[256,8,512]{2,1,0:T(8,128)(2,1)S(1)}, bf16[256,8,512]{2,1,0:T(8,128)(2,1)}, u32[]{:S(2)}) copy-start(bf16[256,8,512]{2,1,0:T(8,128)(2,1)} %param.20) | copy-start | bytes 6291460
  7.2 145.5 %all-gather.6.cloned.1.call-start = ((), (), s32[]{:S(2)}) async-start(), calls=%async_computation.6 | async-start | bytes 1622016 | tf_op jit(solution)/shard_map/all_gather | solution.py:58
  7.9 189.2 %all-gather.12.cloned.1.call-start = ((), (), s32[]{:S(2)}) async-start(), calls=%async_computation.9 | async-start | bytes 2162688 | tf_op jit(solution)/shard_map/all_gather | solution.py:66
  8.7 191.6 %all-gather.8.cloned.1.call-start = ((), (), s32[]{:S(2)}) async-start(), calls=%async_computation.7 | async-start | bytes 2162688 | tf_op jit(solution)/shard_map/all_gather | solution.py:62
  9.4 234.4 %all-gather.10.cloned.1.call-start = ((), (), s32[]{:S(2)}) async-start(), calls=%async_computation.8 | async-start | bytes 2162688 | tf_op jit(solution)/shard_map/all_gather | solution.py:64
  10.0 420.3 %reduce-scatter.19.cloned.1.call-start = ((), (), s32[]{:S(2)}) async-start(), calls=%async_computation.15 | async-start | bytes 270336
  96.2 53.3 %copy-start.32 = (f32[512]{0:T(512)}, f32[512]{0:T(512)S(1)}, u32[]{:S(2)}) copy-start(f32[512]{0:T(512)S(1)} %convert_element_type.92) | copy-start | bytes 6148
  97.1 52.3 %copy-start.2 = (f32[256,512]{1,0:T(8,128)}, f32[256,512]{1,0:T(8,128)S(1)}, u32[]{:S(2)}) copy-start(f32[256,512]{1,0:T(8,128)S(1)} %fusion.38) | copy-start | bytes 1572868
  97.1 5.1 copy-start.47
  97.2 5.1 copy-start.39
  101.7 0.6 copy-start.29
  102.3 47.2 %copy-start.24 = (f32[256,8]{0,1:T(8,128)}, f32[256,8]{0,1:T(8,128)S(1)}, u32[]{:S(2)}) copy-start(f32[256,8]{0,1:T(8,128)S(1)} %fusion.44) | copy-start | bytes 24580
  102.3 81.2 %copy-start.28 = (pred[256,8]{0,1:T(8,128)(4,1)}, pred[256,8]{0,1:T(8,128)(4,1)S(1)}, u32[]{:S(2)}) copy-start(pred[256,8]{0,1:T(8,128)(4,1)S(1)} %iota_compare_fusion.3) | copy-start | bytes 6148
  183.5 0.6 copy-start.22
  193.2 3.3 copy-start.23
  194.8 0.9 copy-start.5
  194.8 1.0 copy-start.34
  195.9 0.6 copy-start.40
  243.8 5.0 copy-start.6
  243.8 5.0 copy-start.26
  243.8 5.0 copy-start.35
  243.8 5.0 copy-start.37
  243.8 5.0 copy-start.49
  248.8 1.6 copy-start.18
  248.9 1.6 copy-start.41
  248.9 1.9 copy-start.16
  250.4 1.7 copy-start.12
  251.3 0.8 copy-start.8
  277.5 3.5 copy-start.20
  281.0 6.4 copy-start.14
  283.5 1.6 copy-start.21
  283.9 3.6 copy-start.4
  285.0 2.8 copy-start.33
  287.4 1.0 copy-start.3
  288.5 1.5 copy-start.30
  288.5 1.5 copy-start.25
  292.3 1.7 copy-start.9
  294.2 1.9 copy-start.44
  294.2 3.3 copy-start.10
  297.5 266.3 %reduce-scatter.11.cloned.1.call-start = ((), (), s32[]{:S(2)}) async-start(), calls=%async_computation.11 | async-start | bytes 1081344 | tf_op jit(solution)/shard_map/reduce_scatter | solution.py:196
  298.9 368.4 %reduce-scatter.9.cloned.1.call-start = ((), (), s32[]{:S(2)}) async-start(), calls=%async_computation.10 | async-start | bytes 3244032 | tf_op jit(solution)/shard_map/reduce_scatter | solution.py:195
  312.1 12.0 %copy-start.15 = (bf16[256,8,64]{0,2,1:T(8,128)(2,1)S(1)}, bf16[256,8,64]{0,2,1:T(8,128)(2,1)}, u32[]{:S(2)}) copy-start(bf16[256,8,64]{0,2,1:T(8,128)(2,1)} %copy-done.14) | copy-start | bytes 786436
  332.6 1.0 copy-start.7
  332.6 1.4 copy-start.19
  332.6 1.4 copy-start.27
  332.6 1.4 copy-start.31
  332.6 1.4 copy-start.36
  332.7 1.4 copy-start.38
  332.7 477.4 %reduce-scatter.13.cloned.1.call-start = ((), (), s32[]{:S(2)}) async-start(), calls=%async_computation.12 | async-start | bytes 4325376 | tf_op jit(solution)/shard_map/reduce_scatter | solution.py:199
  336.9 1.2 copy-start.13
  336.9 1.4 copy-start.17
  336.9 612.9 %reduce-scatter.15.cloned.1.call-start = ((), (), s32[]{:S(2)}) async-start(), calls=%async_computation.13 | async-start | bytes 4325376 | tf_op jit(solution)/shard_map/reduce_scatter | solution.py:201
  340.9 0.7 copy-start.48
  341.0 748.3 %reduce-scatter.17.cloned.1.call-start = ((), (), s32[]{:S(2)}) async-start(), calls=%async_computation.14 | async-start | bytes 4325376 | tf_op jit(solution)/shard_map/reduce_scatter | solution.py:203
  346.6 1.6 copy-start.11
  348.2 2.5 copy-start.42
  348.2 2.5 copy-start.43
  348.2 2.5 copy-start.45
  348.2 2.5 copy-start.46
Sparse Core Ops, SparseCore 0:
  10.9 58.0 all-gather.5
  71.9 56.2 all-gather.11
  131.0 54.7 all-gather.7
  188.6 55.2 all-gather.9
  297.6 132.6 reduce-scatter.18
  433.1 130.6 reduce-scatter.10
  569.8 97.4 reduce-scatter.8
  670.1 139.9 reduce-scatter.12
  813.0 136.7 reduce-scatter.14
  952.5 136.7 reduce-scatter.16
where the time goes:
time: 1100 us
  waiting for transfers between devices  729 us (66%)
  blocking collectives  165 us (15%)
  local copies, waits for them, and re-layouts  76 us (7%)
  matrix products  56.4 us (5%)
  other arithmetic  54.3 us (5%)
  between operations  15 us (1%)
    reduce_scatter x1, waiting for transfers between devices, on_device(): lax.psum_scatter(grad_up, 'dp', scatter_dimension=0, tiled=True)  143 us
    reduce_scatter x1, waiting for transfers between devices, on_device(): lax.psum_scatter(grad_down, 'dp', scatter_dimension=0, tiled=True)  140 us
    reduce_scatter x1, waiting for transfers between devices, on_device(): lax.psum_scatter(grad_proj, 'dp', scatter_dimension=0, tiled=True)  140 us
    reduce_scatter x1, waiting for transfers between devices, on_device(): lax.psum_scatter(grad_out, 'dp', scatter_dimension=0, tiled=True)  132 us
    reduce_scatter x1, waiting for transfers between devices, on_device(): lax.psum_scatter(grad_qkv, 'dp', scatter_dimension=0, tiled=True)  103 us
    unnamed x2, blocking collectives  76 us
    all_gather x1, blocking collectives, on_device(): lax.all_gather(w_out, 'dp', axis=0, tiled=True)  45.4 us
    all_gather x1, blocking collectives, on_device(): lax.all_gather(group_table, 'dp', axis=1, tiled=True)  43.7 us
  transfers between devices with their start and end apart: 10, of which 7 were waited for; matrix products, arithmetic and copies ran while one was open for 12% of the time, Pallas kernels for 0%

commit v1 on v0

v1 whole, which is shorter than its diff:
```python
import jax
import jax.numpy as jnp
from jax import lax
from jax.experimental import pallas as pl
from jax.experimental.pallas import tpu as pltpu
from jax.sharding import PartitionSpec as P

HEADS = 8
HEAD_DIM = 64
SLOTS = 8
SHARDS = 32
EB = 32
RB = EB * SLOTS
CH = 64
SCALE = HEAD_DIM ** (-0.5)
F32 = jnp.float32
LOW = jnp.bfloat16
VMEM_LIMIT = 48 * 2**20


def pairs(partner):
    return [(i, partner(i)) for i in range(32)]


CORE = pairs(lambda i: i ^ 1)
NEAR = pairs(lambda i: i ^ (2 if i % 2 == 0 else 4))
FAR = pairs(lambda i: i ^ (4 if i % 2 == 0 else 2))
LAYER = {p: pairs(lambda i: i ^ (p << 3)) for p in (1, 2, 3)}


def send(value, to):
    return lax.ppermute(value, "dp", to)


def shard_order():
    me = lax.axis_index("dp").astype(jnp.int32)
    near = jnp.where(me % 2 == 0, 2, 4).astype(jnp.int32)
    far = 6 - near
    none = 0 * near
    quads = jnp.stack([none, near, far, none + 6, none + 1, far + 1, near + 1, none + 7])
    layers = jnp.arange(4, dtype=jnp.int32) * 8
    return me ^ (quads[:, None] ^ layers[None, :]).reshape(32)


def gather(shard):
    own = jnp.stack([shard] + [send(shard, LAYER[p]) for p in (1, 2, 3)])
    near = send(own, NEAR)
    far = send(own, FAR)
    both = send(near, FAR)
    mine = [own, near, far, both]
    return mine + [send(part, CORE) for part in mine]


def scatter(own, other):
    core = send(other, CORE)
    first = send((own[8:] + core[8:].astype(F32)).astype(LOW), FAR)
    total = own[:8] + core[:8].astype(F32) + first.astype(F32)
    second = send(total[4:].astype(LOW), NEAR)
    total = total[:4] + second.astype(F32)
    last = [send(total[p].astype(LOW), LAYER[p]) for p in (1, 2, 3)]
    return total[0] + last[0].astype(F32) + last[1].astype(F32) + last[2].astype(F32)


def dot(left, right):
    return jnp.dot(left, right, preferred_element_type=F32)


def dot_nt(left, right):
    return lax.dot_general(left, right, (((1,), (1,)), ((), ())), preferred_element_type=F32)


def dot_tn(left, right):
    return lax.dot_general(left, right, (((0,), (0,)), ((), ())), preferred_element_type=F32)


def iota(shape, axis):
    return lax.broadcasted_iota(jnp.int32, shape, axis)


def norm_parts(values):
    center = values - jnp.mean(values, axis=-1, keepdims=True)
    rate = lax.rsqrt(jnp.mean(center * center, axis=-1, keepdims=True) + 1e-05)
    return center * rate, rate


def norm_back(grad, unit, rate, gain):
    scaled = grad * gain
    return rate * (
        scaled
        - jnp.mean(scaled, axis=-1, keepdims=True)
        - unit * jnp.mean(scaled * unit, axis=-1, keepdims=True)
    )


def fold(values):
    rows, width = values.shape
    return jnp.sum(values.reshape(rows // 8, 8, width), axis=0)


def spread_heads(rows):
    tiled = jnp.concatenate([rows] * HEADS, axis=0)
    shape = (HEADS * EB, HEADS * HEAD_DIM)
    return jnp.where(iota(shape, 0) // EB == iota(shape, 1) // HEAD_DIM, tiled, jnp.zeros_like(tiled))


def pick_heads(full):
    parts = []
    for k in range(HEADS // 2):
        lanes = slice(128 * k, 128 * k + 128)
        even = full[2 * k * EB : (2 * k + 1) * EB, lanes]
        odd = full[(2 * k + 1) * EB : (2 * k + 2) * EB, lanes]
        parts.append(jnp.where(iota(even.shape, 1) < HEAD_DIM, even, odd))
    return jnp.concatenate(parts, axis=1)


def slots_first(ref, out, at):
    for k in range(4):
        out[at, 128 * k : 128 * k + 128] = ref[pl.ds(k * RB, EB, stride=SLOTS), :]


def put_first(ref, values):
    for k in range(4):
        ref[pl.ds(k * RB, EB, stride=SLOTS), :] = values[:, 128 * k : 128 * k + 128]


def put_tall(ref, start, values):
    for k in range(4):
        ref[pl.ds(k * RB + start, values.shape[0]), :] = values[:, 128 * k : 128 * k + 128]


def get_tall(ref, start, rows):
    return jnp.concatenate([ref[pl.ds(k * RB + start, rows), :] for k in range(4)], axis=1)


def block(i, rows):
    return pl.ds(pl.multiple_of(i * rows, rows), rows)


def attend_kernel(order, p0, p1, p2, p3, p4, p5, p6, p7, embeds, marks,
                  w_qkv, w_out, vec, bias_up, normed, normed0, query, keyval, probs, mixed, first, norm_ffn,
                  small, table, rows, tall, rows0, base0, norm0):
    for i, piece in enumerate((p0, p1, p2, p3, p4, p5, p6, p7)):
        for p in range(4):
            r = order[4 * i + p]
            at = block(r, 16)
            w_qkv[at, :] = piece[p, :, :1536]
            w_out[at, :] = piece[p, :, 1536:2048]
            small[r] = piece[p, :, 2048:2176].astype(F32)
    lane = iota((16, 128), 1)
    for k in range(4):
        tile = jnp.zeros((16, 128), F32)
        for t in range(8):
            tile = jnp.where(lane // 16 == t, small[8 * k + t], tile)
        vec[:, 128 * k : 128 * k + 128] = tile
    lane = iota((1, 128), 1)
    for k in range(16):
        tile = jnp.where(lane < 64, small[2 * k, 13:14, :], small[2 * k + 1, 13:14, :])
        bias_up[:, 128 * k : 128 * k + 128] = jnp.broadcast_to(tile, (8, 128))
    table[...] = jnp.zeros_like(table)
    table[0:8, :] = vec[0:8, :]

    gain, shift = vec[8:9, :], vec[9:10, :]
    blocks = embeds.shape[0] // RB

    def norm_block(b, _):
        rows[...] = dot(marks[block(b, RB), :], table[...].astype(LOW))
        for c in range(RB // CH):
            at = pl.ds(c * CH, CH)
            here = pl.ds(pl.multiple_of(b * RB + c * CH, CH), CH)
            base = embeds[here, :].astype(F32) + rows[at, :]
            put_tall(tall, c * CH, base)
            unit, _rate = norm_parts(base)
            value = unit * gain + shift
            put_tall(rows0, c * CH, value)
            normed[here, :] = value.astype(LOW)
        out = block(b, EB)
        slots_first(tall, base0, out)
        slots_first(rows0, norm0, out)
        keyval[block(b, RB), :] = dot(normed[block(b, RB), :], w_qkv[:, 512:]).astype(LOW)
        return 0

    lax.fori_loop(0, blocks, norm_block, 0)
    normed0[...] = norm0[...].astype(LOW)
    query[...] = dot(normed0[...], w_qkv[:, :512]).astype(LOW)

    shape = (RB, HEADS * EB)
    match = iota(shape, 0) // SLOTS == iota(shape, 1) % EB
    liver = jnp.where(iota((128, HEADS * EB), 0) == 8, 1.0, 0.0).astype(LOW)

    def attend_block(b, _):
        at, out = block(b, RB), block(b, EB)
        scores = dot_nt(keyval[at, :512], spread_heads(query[out, :])) * SCALE
        live = dot(marks[at, :], liver) > 0.5
        scores = jnp.where(live, scores, -1000000000.0).reshape(EB, SLOTS, HEADS * EB)
        top = jnp.max(scores, axis=1, keepdims=True)
        power = jnp.exp(scores - top)
        part = (power / jnp.sum(power, axis=1, keepdims=True)).reshape(shape)
        low = jnp.where(match, part, 0.0).astype(LOW)
        probs[at, :] = low
        mixed[out, :] = pick_heads(dot_tn(low, keyval[at, 512:])).astype(LOW)
        return 0

    lax.fori_loop(0, blocks, attend_block, 0)

    def ffn_block(b, _):
        at = block(b, CH)
        value = base0[at, :] + dot(mixed[at, :], w_out[...])
        first[at, :] = value
        unit, _rate = norm_parts(value)
        norm_ffn[at, :] = (unit * vec[10:11, :] + vec[11:12, :]).astype(LOW)
        return 0

    lax.fori_loop(0, first.shape[0] // CH, ffn_block, 0)


def hidden_kernel(order, p0, p1, p2, p3, p4, p5, p6, p7, norm_ffn, bias_up, cotangent,
                  w_proj, w_up, dpool, hidden, slope, own, other, sum_pool, total):
    for i, piece in enumerate((p0, p1, p2, p3, p4, p5, p6, p7)):
        for p in range(4):
            at = block(order[4 * i + p], 16)
            w_proj[at, :] = piece[p, :16, :]
            w_up[at, :] = piece[p, 16:, :]
    grad = dot_nt(cotangent[...], w_proj[...])
    dpool[...] = grad
    sum_pool[...] = fold(grad)
    low = grad.astype(LOW)
    for k in range(8):
        lanes = slice(256 * k, 256 * k + 256)
        pre = dot(norm_ffn[...], w_up[:, lanes])
        rows = pre.shape[0] // 4
        for c in range(4):
            at = slice(rows * c, rows * c + rows)
            value = pre[at] + bias_up[0:1, lanes]
            below = 0.5 * (1.0 + lax.erf(value * (0.5**0.5)))
            hidden[at, lanes] = (value * below).astype(LOW)
            slope[at, lanes] = below + value * (jnp.exp(-0.5 * value * value) * 0.3989422804014327)
        total[256 * k : 256 * k + 256, :] = dot_tn(hidden[:, lanes], low)
    for i in range(16):
        own[i] = total[block(order[i], 64), :]
        other[i] = total[block(order[16 + i], 64), :].astype(LOW)


def ffn_back_kernel(order, p0, p1, p2, p3, p4, p5, p6, p7, dpool, hidden, slope, w_up, w_out, w_proj, vec, first,
                    norm_ffn, mixed, cotangent,
                    output, dfirst, dmixed, grad_out, own, other, sum_up, sum_gain, sum_shift,
                    w_down, pre_low, grad_proj, grad_up):
    for i, piece in enumerate((p0, p1, p2, p3, p4, p5, p6, p7)):
        for p in range(4):
            w_down[block(order[4 * i + p], 64), :] = piece[p]
    low = dpool[...].astype(LOW)
    for k in range(8):
        lanes = slice(256 * k, 256 * k + 256)
        dpre = slope[:, lanes] * dot_nt(low, w_down[lanes, :])
        sum_up[:, lanes] = fold(dpre)
        pre_low[:, lanes] = dpre.astype(LOW)
    dfirst[...] = dot_nt(pre_low[...], w_up[...])
    gains = jnp.zeros((8, 512), F32)
    shifts = jnp.zeros((8, 512), F32)
    for c in range(first.shape[0] // CH):
        at = slice(CH * c, CH * c + CH)
        grad = dfirst[at, :]
        unit, rate = norm_parts(first[at, :])
        gains += fold(grad * unit)
        shifts += fold(grad)
        dfirst[at, :] = norm_back(grad, unit, rate, vec[10:11, :]) + dpool[at, :]
    sum_gain[...] = gains
    sum_shift[...] = shifts
    first_low = dfirst[...].astype(LOW)
    dmixed[...] = dot_nt(first_low, w_out[...]).astype(LOW)
    grad_out[...] = dot_tn(mixed[...], first_low)
    pooled = (first[...] + dot(hidden[...], w_down[...]) + vec[12:13, :]).astype(LOW)
    for k in range(8):
        lanes = slice(256 * k, 256 * k + 256)
        output[:, lanes] = dot(pooled, w_proj[:, lanes]).astype(LOW)
        grad_proj[:, lanes] = dot_tn(pooled, cotangent[:, lanes])
        grad_up[:, lanes] = dot_tn(norm_ffn[...], pre_low[:, lanes])
    for i in range(16):
        at, there = block(order[i], 16), block(order[16 + i], 16)
        own[i, :16, :] = grad_proj[at, :]
        own[i, 16:, :] = grad_up[at, :]
        other[i, :16, :] = grad_proj[there, :].astype(LOW)
        other[i, 16:, :] = grad_up[there, :].astype(LOW)


def attend_back_kernel(order, embeds, marks, w_qkv, vec, normed, normed0, query, keyval, probs, dmixed, dfirst,
                       grad_out, sum_gain_ffn, sum_shift_ffn, sum_pool, sum_up,
                       grad_embeds, own, other,
                       table, rows, work, spread_query, spread_first, dquery, dkeyval, query_part, grad_qkv, small, sums):
    blocks = embeds.shape[0] // RB
    table[...] = jnp.zeros_like(table)
    table[0:8, :] = vec[0:8, :].astype(LOW)

    def attend_block(b, _):
        at, out = block(b, RB), block(b, EB)
        low = probs[at, :]
        part = low.astype(F32)
        dmix = spread_heads(dmixed[out, :])
        grad = dot_nt(keyval[at, 512:], dmix)
        shape = (EB, SLOTS, HEADS * EB)
        whole = jnp.sum((part * grad).reshape(shape), axis=1, keepdims=True)
        dscores = (part.reshape(shape) * (grad.reshape(shape) - whole)).reshape(RB, HEADS * EB).astype(LOW)
        dkeyval[at, 512:] = dot(low, dmix).astype(LOW)
        dkeyval[at, :512] = (dot(dscores, spread_heads(query[out, :])) * SCALE).astype(LOW)
        dquery[out, :] = (pick_heads(dot_tn(dscores, keyval[at, :512])) * SCALE).astype(LOW)
        return 0

    lax.fori_loop(0, blocks, attend_block, 0)
    grad_qkv[:, :512] = dot_tn(normed0[...], dquery[...])
    for k in range(4):
        lanes = slice(256 * k, 256 * k + 256)
        grad_qkv[:, 512 + 256 * k : 768 + 256 * k] = dot_tn(normed[...], dkeyval[:, lanes])
    query_part[...] = dot_nt(dquery[...], w_qkv[:, :512])
    sums[...] = jnp.zeros_like(sums)
    spread_query[...] = jnp.zeros_like(spread_query)
    spread_first[...] = jnp.zeros_like(spread_first)
    gain = vec[8:9, :]

    def norm_block(b, _):
        at, out = block(b, RB), block(b, EB)
        put_first(spread_query, query_part[out, :])
        put_first(spread_first, dfirst[out, :])
        rows[...] = dot(marks[at, :], table[...])
        work[...] = dot_nt(dkeyval[at, :], w_qkv[:, 512:])
        for c in range(RB // CH):
            local = pl.ds(c * CH, CH)
            here = pl.ds(pl.multiple_of(b * RB + c * CH, CH), CH)
            grad = work[local, :] + get_tall(spread_query, c * CH, CH)
            unit, rate = norm_parts(embeds[here, :].astype(F32) + rows[local, :])
            sums[0:8, :] += fold(grad * unit)
            sums[8:16, :] += fold(grad)
            work[local, :] = norm_back(grad, unit, rate, gain) + get_tall(spread_first, c * CH, CH)
        value = work[...]
        high = value.astype(LOW)
        rest = (value - high.astype(F32)).astype(LOW)
        grad_embeds[at, :] = high
        sums[16:144, :] += dot_tn(marks[at, :], high) + dot_tn(marks[at, :], rest)
        return 0

    lax.fori_loop(0, blocks, norm_block, 0)
    small[...] = jnp.zeros_like(small)
    small[0:8, :] = sums[16:24, :]
    for i, value in enumerate((sums[0:8, :], sums[8:16, :], sum_gain_ffn[...], sum_shift_ffn[...], sum_pool[...])):
        small[8 + i : 9 + i, :] = jnp.sum(value, axis=0, keepdims=True)
    up = jnp.sum(sum_up[...], axis=0, keepdims=True)
    row = iota((16, 128), 0)
    for r in range(SHARDS):
        tile = small[:, 128 * (r // 8) : 128 * (r // 8) + 128]
        tile = jnp.where(row == 13, up[:, 128 * (r // 2) : 128 * (r // 2) + 128], tile)
        rows[8 * r : 8 * r + 8, 0:128] = tile[0:8]
        rows[8 * r : 8 * r + 8, 128:256] = tile[8:16]
    for i in range(16):
        for k, half in ((i, own), (16 + i, other)):
            r = order[k]
            at = block(r, 16)
            near = block(r, 8)
            half[i, :, :1536] = grad_qkv[at, :].astype(half.dtype)
            half[i, :, 1536:2048] = grad_out[at, :].astype(half.dtype)
            half[i, :, 2048:2176] = jnp.concatenate([rows[near, 0:128], rows[near, 128:256]]).astype(half.dtype)


def call(kernel, args, outs, scratch=(), flops=10**9):
    vmem = pl.BlockSpec(memory_space=pltpu.VMEM)
    size = sum(a.size * a.dtype.itemsize for a in args) + sum(
        jnp.dtype(t).itemsize * jnp.prod(jnp.array(s)).item() if False else 0 for s, t in outs
    )
    return pl.pallas_call(
        kernel,
        out_shape=[jax.ShapeDtypeStruct(s, t) for s, t in outs],
        in_specs=[pl.BlockSpec(memory_space=pltpu.SMEM)] + [vmem] * (len(args) - 1),
        out_specs=[vmem] * len(outs),
        scratch_shapes=[pltpu.VMEM(s, t) for s, t in scratch],
        compiler_params=pltpu.CompilerParams(vmem_limit_bytes=VMEM_LIMIT),
        cost_estimate=pl.CostEstimate(flops=flops, bytes_accessed=size, transcendentals=0),
    )(*args)


def on_device(
    embeds,
    piece_counts,
    group_ids,
    group_table,
    gain_attn,
    shift_attn,
    w_qkv,
    w_out,
    gain_ffn,
    shift_ffn,
    w_up,
    bias_up,
    w_down,
    bias_down,
    w_proj,
    cotangent,
):
    tuned = lax.axis_size("dp") == 32
    entries = embeds.shape[0]
    rows = entries * SLOTS
    flat = embeds.reshape(rows, 512)
    lane = jnp.arange(128, dtype=jnp.int32)
    slot = jnp.arange(SLOTS, dtype=jnp.int32)
    marks = jnp.where(
        lane[None, None, :] < 8,
        group_ids[:, None, None] == lane[None, None, :],
        slot[None, :, None] < piece_counts[:, None, None],
    )
    marks = marks.astype(LOW).reshape(rows, 128)
    vectors = jnp.concatenate([group_table, jnp.stack([gain_attn, shift_attn, gain_ffn, shift_ffn, bias_down])])
    if tuned:
        order = shard_order()
        small = jnp.concatenate(
            [jnp.tile(vectors, (1, 8)), jnp.tile(bias_up[None, :], (1, 2)), jnp.zeros((2, 128), LOW)]
        )
        pieces = [
            gather(jnp.concatenate([w_qkv, w_out, small], axis=1)),
            gather(jnp.concatenate([w_proj, w_up])),
            gather(w_down),
        ]
    else:
        order = jnp.arange(32, dtype=jnp.int32)

        def whole(shard, axis=0):
            return lax.all_gather(shard, "dp", axis=axis, tiled=True)

        def cut(full):
            return [full[4 * i : 4 * i + 4] for i in range(8)]

        spread = jnp.transpose(whole(vectors, 1).reshape(13, SHARDS, 16), (1, 0, 2))
        small = jnp.concatenate(
            [
                jnp.tile(spread, (1, 1, 8)),
                jnp.tile(whole(bias_up).reshape(SHARDS, 1, 64), (1, 1, 2)),
                jnp.zeros((SHARDS, 2, 128), LOW),
            ],
            axis=1,
        )
        pieces = [
            cut(
                jnp.concatenate(
                    [whole(w_qkv).reshape(SHARDS, 16, 1536), whole(w_out).reshape(SHARDS, 16, 512), small], axis=2
                )
            ),
            cut(
                jnp.concatenate(
                    [whole(w_proj).reshape(SHARDS, 16, 2048), whole(w_up).reshape(SHARDS, 16, 2048)], axis=1
                )
            ),
            cut(whole(w_down).reshape(SHARDS, 64, 512)),
        ]
    (qkv_all, out_all, vec, upbias, normed, normed0, query, keyval, probs, mixed, first, norm_ffn) = call(
        attend_kernel,
        [order, *pieces[0], flat, marks],
        [
            ((512, 1536), LOW), ((512, 512), LOW), ((16, 512), F32), ((8, 2048), F32), ((rows, 512), LOW),
            ((entries, 512), LOW), ((entries, 512), LOW), ((rows, 1024), LOW), ((rows, HEADS * EB), LOW),
            ((entries, 512), LOW), ((entries, 512), F32), ((entries, 512), LOW),
        ],
        [
            ((32, 16, 128), F32), ((128, 512), F32), ((RB, 512), F32), ((4 * RB, 128), F32), ((4 * RB, 128), F32), ((entries, 512), F32),
            ((entries, 512), F32),
        ],
        flops=4 * 10**9,
    )
    (proj_all, up_all, dpool, hidden, slope, own_down, other_down, sum_pool) = call(
        hidden_kernel,
        [order, *pieces[1], norm_ffn, upbias, cotangent],
        [
            ((512, 2048), LOW), ((512, 2048), LOW), ((entries, 512), F32), ((entries, 2048), LOW),
            ((entries, 2048), F32), ((16, 64, 512), F32), ((16, 64, 512), LOW), ((8, 512), F32),
        ],
        [((2048, 512), F32)],
        flops=2 * 10**9,
    )
    (output, dfirst, dmixed, grad_out, own_pair, other_pair, sum_up, sum_gain, sum_shift) = call(
        ffn_back_kernel,
        [order, *pieces[2], dpool, hidden, slope, up_all, out_all, proj_all, vec, first, norm_ffn, mixed, cotangent],
        [
            ((entries, 2048), LOW), ((entries, 512), F32), ((entries, 512), LOW), ((512, 512), F32),
            ((16, 32, 2048), F32), ((16, 32, 2048), LOW), ((8, 2048), F32), ((8, 512), F32), ((8, 512), F32),
        ],
        [((2048, 512), LOW), ((entries, 2048), LOW), ((512, 2048), F32), ((512, 2048), F32)],
        flops=4 * 10**9,
    )
    (grad_embeds, own_last, other_last) = call(
        attend_back_kernel,
        [order, flat, marks, qkv_all, vec, normed, normed0, query, keyval, probs, dmixed, dfirst, grad_out, sum_gain,
         sum_shift, sum_pool, sum_up],
        [((rows, 512), LOW), ((16, 16, 2176), F32), ((16, 16, 2176), LOW)],
        [
            ((128, 512), LOW), ((RB, 512), F32), ((RB, 512), F32), ((4 * RB, 128), F32), ((4 * RB, 128), F32), ((entries, 512), LOW), ((rows, 1024), LOW),
            ((entries, 512), F32), ((512, 1536), F32), ((16, 512), F32), ((144, 512), F32),
        ],
        flops=8 * 10**9,
    )
    if tuned:
        sum_down = scatter(own_down, other_down)
        pair = scatter(own_pair, other_pair)
        last = scatter(own_last, other_last)
        sum_proj, sum_up = pair[:16], pair[16:]
        sum_qkv, sum_out = last[:, :1536], last[:, 1536:2048]
        me = lax.axis_index("dp")
        sums = lax.dynamic_slice(last, (0, 2048 + 16 * (me % 8)), (13, 16))
        sum_upbias = lax.dynamic_slice(last, (13, 2048 + 64 * (me % 2)), (1, 64))[0]
    else:

        def share(own, other, axis=0):
            full = jnp.concatenate([own, other.astype(F32)])
            return lax.psum_scatter(full.reshape(-1, full.shape[-1]), "dp", scatter_dimension=0, tiled=True)

        sum_down = share(own_down, other_down)
        sum_proj = share(own_pair[:, :16], other_pair[:, :16])
        sum_up = share(own_pair[:, 16:], other_pair[:, 16:])
        sum_qkv = share(own_last[:, :, :1536], other_last[:, :, :1536])
        sum_out = share(own_last[:, :, 1536:2048], other_last[:, :, 1536:2048])
        small = jnp.concatenate([own_last[:, :, 2048:], other_last[:, :, 2048:].astype(F32)])
        vectors = jnp.concatenate([small[8 * k, :13] for k in range(4)], axis=1)
        sums = lax.psum_scatter(vectors, "dp", scatter_dimension=1, tiled=True)
        upbias = jnp.concatenate([small[2 * k, 13] for k in range(16)])
        sum_upbias = lax.psum_scatter(upbias, "dp", scatter_dimension=0, tiled=True)
    return (
        output,
        grad_embeds.reshape(entries, SLOTS, 512),
        sums[:8],
        sums[8],
        sums[9],
        sum_qkv,
        sum_out,
        sums[10],
        sums[11],
        sum_up,
        sum_upbias,
        sum_down,
        sums[12],
        sum_proj,
    )


def solution(mesh):
    placed = (
        P("dp", None, None),
        P("dp"),
        P("dp"),
        P(None, "dp"),
        P("dp"),
        P("dp"),
        P("dp", None),
        P("dp", None),
        P("dp"),
        P("dp"),
        P("dp", None),
        P("dp"),
        P("dp", None),
        P("dp"),
        P("dp", None),
        P("dp", None),
    )
    return jax.shard_map(
        on_device,
        mesh=mesh,
        in_specs=placed,
        out_specs=(
            P("dp", None),
            P("dp", None, None),
            P(None, "dp"),
            P("dp"),
            P("dp"),
            P("dp", None),
            P("dp", None),
            P("dp"),
            P("dp"),
            P("dp", None),
            P("dp"),
            P("dp", None),
            P("dp"),
            P("dp", None),
        ),
        check_vma=False,
    )
```

time: 1100 us -> 203 us (0.18)
  waiting for transfers between devices: 729 us -> 57.5 us
  blocking collectives: 165 us -> 0 us
  local copies, waits for them, and re-layouts: 76 us -> 14.6 us
  Pallas kernels: 0 us -> 60.5 us
  starting transfers between devices: 0.4 us -> 57.3 us
  matrix products: 56.4 us -> 0 us
  other arithmetic: 54.3 us -> 11.1 us
  between operations: 15 us -> 0.98 us
    reduce_scatter x5 -> x0, waiting for transfers between devices: 658 us -> none  [the longest x1 143 us: on_device(): lax.psum_scatter(grad_up, 'dp', scatter_dimension=0, tiled=True)]
    all_gather x2 -> x0, blocking collectives: 89.1 us -> none  [the longest x1 45.4 us: on_device(): lax.all_gather(w_out, 'dp', axis=0, tiled=True)]
    unnamed x2 -> x0, blocking collectives: 76 us -> none
    pallas_call x0 -> x4, Pallas kernels: none -> 60.5 us  [call(): pl.pallas_call(kernel, out_shape=[jax.ShapeDtypeStruct(s, t) for s, t in...]
    ppermute x0 -> x48, waiting for transfers between devices: none -> 57.5 us  [send(): return lax.ppermute(value, 'dp', to)]
    ppermute x0 -> x48, starting transfers between devices: none -> 57.3 us  [send(): return lax.ppermute(value, 'dp', to)]
    dot_general x19 -> x0, matrix products: 55 us -> none  [the longest x1 8.6 us: on_device(): jnp.dot(ffn_low, up_all, preferred_element_type=jnp.float32)]
    unnamed x11 -> x0, waiting for transfers between devices: 36.7 us -> none
  transfers between devices with their start and end apart: 10 -> 48, of which waited for: 7 -> 15; matrix products, arithmetic and copies ran while one was open for 12% -> 8% of each run, Pallas kernels for 0% -> 30%
where the time goes in v1:
time: 203 us; the launch traced here: 202 us
  Pallas kernels  60.5 us (30%)
  waiting for transfers between devices  57.5 us (28%)
  starting transfers between devices  57.3 us (28%)
  local copies, waits for them, and re-layouts  14.6 us (7%)
  other arithmetic  11.1 us (5%)
    pallas_call x4, Pallas kernels, call(): pl.pallas_call(kernel, out_shape=[jax.ShapeDtypeStruct(s, t) for s, t in...  60.5 us
    ppermute x48, waiting for transfers between devices, send(): return lax.ppermute(value, 'dp', to)  57.5 us
    ppermute x48, starting transfers between devices, send(): return lax.ppermute(value, 'dp', to)  57.3 us
    unnamed x35, local copies, waits for them, and re-layouts  7.13 us
  transfers between devices with their start and end apart: 48, of which 15 were waited for; matrix products, arithmetic and copies ran while one was open for 8% of the time, Pallas kernels for 30%

profile of v1, /device:TPU:0, one launch (start us, length us, event | category | flops | bytes accessed | tf_op | source)
XLA Modules:
  0.0 202.0 jit_solution(4034868932485222845)
XLA Ops:
  0.7 1.4 concatenate.13
  2.2 0.7 tile.19
  3.0 0.8 maximum_maximum_fusion
  3.8 3.1 %collective-permute-start.20 = (bf16[16,2176]{1,0:T(8,128)(2,1)S(1)}, bf16[16,2176]{1,0:T(8,128)(2,1)S(1)}, u32[]{:S(2)}, u32[]{:S(2)}) collective-permute-start(bf16[16,2176]{1,0:T(8,128)(2,1)S(1)} %maximum_maximum_fusion), channel_id=1, source_target_pairs={{0,8},{1,9},{2,10},{3,11},{4,12},{5,13},{6,14},{7,15},{8,0},{9,1},... | collective-permute-start | bytes 208904 | tf_op jit(solution)/shard_map/ppermute | solution.py:32
  6.9 2.6 %collective-permute-start.21 = (bf16[16,2176]{1,0:T(8,128)(2,1)S(1)}, bf16[16,2176]{1,0:T(8,128)(2,1)S(1)}, u32[]{:S(2)}, u32[]{:S(2)}) collective-permute-start(bf16[16,2176]{1,0:T(8,128)(2,1)S(1)} %maximum_maximum_fusion), channel_id=1, source_target_pairs={{0,16},{1,17},{2,18},{3,19},{4,20},{5,21},{6,22},{7,23},{8,24},{9,... | collective-permute-start | bytes 208904 | tf_op jit(solution)/shard_map/ppermute | solution.py:32
  9.9 3.9 %collective-permute-start.2 = (bf16[64,512]{1,0:T(8,128)(2,1)}, bf16[64,512]{1,0:T(8,128)(2,1)S(1)}, u32[]{:S(2)}, u32[]{:S(2)}) collective-permute-start(bf16[64,512]{1,0:T(8,128)(2,1)} %param.28), channel_id=1, source_target_pairs={{0,24},{1,25},{2,26},{3,27},{4,28},{5,29},{6,30},{7,31},{8,16},{9,... | collective-permute-start | bytes 196616 | tf_op jit(solution)/shard_map/ppermute | solution.py:32
  13.9 0.8 fusion.14
  14.7 0.8 constant_dynamic-update-slice_fusion.1
  15.5 0.8 constant_dynamic-update-slice_fusion
  16.4 2.0 %collective-permute-done.1 = bf16[64,512]{1,0:T(8,128)(2,1)S(1)} collective-permute-done((bf16[64,512]{1,0:T(8,128)(2,1)}, bf16[64,512]{1,0:T(8,128)(2,1)S(1)}, u32[]{:S(2)}, u32[]{:S(2)}) %collective-permute-start.1) | collective-permute-done | bytes 65568 | tf_op jit(solution)/shard_map/ppermute | solution.py:32
  18.4 7.9 %collective-permute-start.12 = (bf16[32,2048]{1,0:T(8,128)(2,1)S(1)}, bf16[32,2048]{1,0:T(8,128)(2,1)S(1)}, u32[]{:S(2)}, u32[]{:S(2)}) collective-permute-start(bf16[32,2048]{1,0:T(8,128)(2,1)S(1)} %constant_dynamic-update-slice_fusion), channel_id=1, source_target_pairs={{0,24},{1,25},{2,26},{3,27},{4,28},{5,29},{6,30},{7,31},{8,16},{9,... | collective-permute-start | bytes 393224 | tf_op jit(solution)/shard_map/ppermute | solution.py:32
  26.3 0.9 pad_maximum_fusion.2.p0
  27.2 1.1 collective-permute-start.10
  28.3 1.5 collective-permute-start.3
  29.8 1.5 collective-permute-start.4
  32.2 1.5 collective-permute-start.24
  33.8 3.8 %collective-permute-done.3.p1 = bf16[4,64,512]{2,1,0:T(8,128)(2,1)S(1)} collective-permute-done((bf16[4,64,512]{2,1,0:T(8,128)(2,1)S(1)}, bf16[4,64,512]{2,1,0:T(8,128)(2,1)S(1)}, u32[]{:S(2)}, u32[]{:S(2)}) %collective-permute-start.3) | collective-permute-done | bytes 262176 | tf_op jit(solution)/shard_map/ppermute | solution.py:32
  37.6 1.5 collective-permute-start.13
  39.1 1.5 collective-permute-start.14
  40.7 2.8 %collective-permute-done.23.p1 = bf16[4,16,2176]{2,1,0:T(8,128)(2,1)S(1)} collective-permute-done((bf16[4,16,2176]{2,1,0:T(8,128)(2,1)S(1)}, bf16[4,16,2176]{2,1,0:T(8,128)(2,1)S(1)}, u32[]{:S(2)}, u32[]{:S(2)}) %collective-permute-start.23) | collective-permute-done | bytes 278560 | tf_op jit(solution)/shard_map/ppermute | solution.py:32
  43.5 1.5 collective-permute-start.5
  45.6 0.7 copy-done
  46.5 7.9 %collective-permute-done.5.p3 = bf16[4,64,512]{2,1,0:T(8,128)(2,1)} collective-permute-done((bf16[4,64,512]{2,1,0:T(8,128)(2,1)S(1)}, bf16[4,64,512]{2,1,0:T(8,128)(2,1)}, u32[]{:S(2)}, u32[]{:S(2)}) %collective-permute-start.5) | collective-permute-done | bytes 262176 | tf_op jit(solution)/shard_map/ppermute | solution.py:32
  54.4 1.4 collective-permute-start.16
  55.8 1.6 collective-permute-done.25.p3
  57.4 1.1 collective-permute-start.28
  59.1 0.7 copy-done.2
  59.8 0.6 collective-permute-start.17
  60.8 0.7 copy-done.4
  62.1 5.7 %collective-permute-done.15.p3 = bf16[4,32,2048]{2,1,0:T(8,128)(2,1)} collective-permute-done((bf16[4,32,2048]{2,1,0:T(8,128)(2,1)S(1)}, bf16[4,32,2048]{2,1,0:T(8,128)(2,1)}, u32[]{:S(2)}, u32[]{:S(2)}) %collective-permute-start.15) | collective-permute-done | bytes 524320 | tf_op jit(solution)/shard_map/ppermute | solution.py:32
  69.1 1.0 copy-done.1
  70.1 1.0 copy-done.3
  71.0 1.0 copy-done.5
  72.0 19.6 %shard_map.263 = (bf16[512,1536]{1,0:T(8,128)(2,1)}, bf16[512,512]{1,0:T(8,128)(2,1)S(1)}, f32[16,512]{1,0:T(8,128)S(1)}, f32[8,2048]{1,0:T(8,128)S(1)}, bf16[20...) custom-call(s32[32]{0:T(128)S(1)} %xor.28.order, ...), custom_call_target="tpu_custom_call" | custom-call | flops 4000000000 | bytes 4849792 | tf_op jit(solution)/shard_map/pallas_call | solution.py:366
  91.6 7.8 %shard_map.264 = (bf16[512,2048]{1,0:T(8,128)(2,1)}, bf16[512,2048]{1,0:T(8,128)(2,1)}, f32[256,512]{1,0:T(8,128)S(1)}, bf16[256,2048]{1,0:T(8,128)(2,1)S(1)}, f...) custom-call(s32[32]{0:T(128)S(1)} %xor.28.order, ...), custom_call_target="tpu_custom_call" | custom-call | flops 2000000000 | bytes 5570688 | tf_op jit(solution)/shard_map/pallas_call | solution.py:366
  99.4 1.0 copy-done.8
  100.8 11.2 %shard_map.265 = (bf16[256,2048]{1,0:T(8,128)(2,1)}, f32[256,512]{1,0:T(8,128)S(1)}, bf16[256,512]{1,0:T(8,128)(2,1)S(1)}, f32[512,512]{1,0:T(8,128)S(1)}, f32[1...) custom-call(s32[32]{0:T(128)S(1)} %xor.28.order, ...), custom_call_target="tpu_custom_call" | custom-call | flops 4000000000 | bytes 12615808 | tf_op jit(solution)/shard_map/pallas_call | solution.py:366
  112.1 21.9 %shard_map.266 = (bf16[2048,512]{1,0:T(8,128)(2,1)}, f32[16,16,2176]{2,1,0:T(8,128)}, bf16[16,16,2176]{2,1,0:T(8,128)(2,1)S(1)}) custom-call(s32[32]{0:T(128)S(1)} %xor.28.order, bf16[2048,512]{1,0:T(8,128)(2,1)} %bitcast.99, bf16[2048,128]{1,0:T(8,128)(2,1)S(1)} %fusion.marks, bf16[512,1536]{1,0:T(8,128)(2,1)} %get-tuple-element.58.w_qkv, ...), custom_call_target="tpu_custom_call" | custom-call | flops 8000000000 | bytes 14041216 | tf_op jit(solution)/shard_map/pallas_call | solution.py:366
  134.9 1.1 collective-permute-start.36
  136.0 7.5 %collective-permute-done.43 = bf16[8,64,512]{2,1,0:T(8,128)(2,1)S(1)} collective-permute-done((bf16[8,64,512]{2,1,0:T(8,128)(2,1)S(1)}, bf16[8,64,512]{2,1,0:T(8,128)(2,1)S(1)}, u32[]{:S(2)}, u32[]{:S(2)}) %collective-permute-start.43) | collective-permute-done | bytes 524320 | tf_op jit(solution)/shard_map/ppermute | solution.py:32
  143.8 1.5 collective-permute-start.44
  145.3 0.9 add_convert_fusion.1
  147.1 5.7 %collective-permute-done.44 = bf16[4,64,512]{2,1,0:T(8,128)(2,1)} collective-permute-done((bf16[4,64,512]{2,1,0:T(8,128)(2,1)S(1)}, bf16[4,64,512]{2,1,0:T(8,128)(2,1)}, u32[]{:S(2)}, u32[]{:S(2)}) %collective-permute-start.44) | collective-permute-done | bytes 262176 | tf_op jit(solution)/shard_map/ppermute | solution.py:32
  152.8 1.0 fusion.10
  154.0 1.1 collective-permute-start.46
  155.1 3.3 %collective-permute-start.47 = (bf16[64,512]{1,0:T(8,128)(2,1)S(1)}, bf16[64,512]{1,0:T(8,128)(2,1)S(1)}, u32[]{:S(2)}, u32[]{:S(2)}) collective-permute-start(bf16[64,512]{1,0:T(8,128)(2,1)S(1)} %get-tuple-element.93), channel_id=1, source_target_pairs={{0,24},{1,25},{2,26},{3,27},{4,28},{5,29},{6,30},{7,31},{8,16},{9,... | collective-permute-start | bytes 196616 | tf_op jit(solution)/shard_map/ppermute | solution.py:32
  158.4 1.2 convert_add_fusion.1
  159.6 1.5 collective-permute-start.32
  161.3 0.7 fusion.9
  162.0 1.6 add_convert_fusion
  163.6 1.6 collective-permute-start.37
  165.1 4.1 %collective-permute-done.32 = bf16[4,16,2176]{2,1,0:T(8,128)(2,1)S(1)} collective-permute-done((bf16[4,16,2176]{2,1,0:T(8,128)(2,1)S(1)}, bf16[4,16,2176]{2,1,0:T(8,128)(2,1)S(1)}, u32[]{:S(2)}, u32[]{:S(2)}) %collective-permute-start.32) | collective-permute-done | bytes 278560 | tf_op jit(solution)/shard_map/ppermute | solution.py:32
  169.4 1.0 collective-permute-start.34
  170.4 3.4 %collective-permute-start.35 = (bf16[16,2176]{1,0:T(8,128)(2,1)S(1)}, bf16[16,2176]{1,0:T(8,128)(2,1)S(1)}, u32[]{:S(2)}, u32[]{:S(2)}) collective-permute-start(bf16[16,2176]{1,0:T(8,128)(2,1)S(1)} %get-tuple-element.88), channel_id=1, source_target_pairs={{0,24},{1,25},{2,26},{3,27},{4,28},{5,29},{6,30},{7,31},{8,16},{9,... | collective-permute-start | bytes 208904 | tf_op jit(solution)/shard_map/ppermute | solution.py:32
  173.8 4.7 %collective-permute-done.37 = bf16[8,32,2048]{2,1,0:T(8,128)(2,1)S(1)} collective-permute-done((bf16[8,32,2048]{2,1,0:T(8,128)(2,1)S(1)}, bf16[8,32,2048]{2,1,0:T(8,128)(2,1)S(1)}, u32[]{:S(2)}, u32[]{:S(2)}) %collective-permute-start.37) | collective-permute-done | bytes 1048608 | tf_op jit(solution)/shard_map/ppermute | solution.py:32
  178.4 1.7 convert_add_fusion
  180.2 2.0 collective-permute-start.38
  182.9 6.6 %collective-permute-done.38 = bf16[4,32,2048]{2,1,0:T(8,128)(2,1)S(1)} collective-permute-done((bf16[4,32,2048]{2,1,0:T(8,128)(2,1)S(1)}, bf16[4,32,2048]{2,1,0:T(8,128)(2,1)S(1)}, u32[]{:S(2)}, u32[]{:S(2)}) %collective-permute-start.38) | collective-permute-done | bytes 524320 | tf_op jit(solution)/shard_map/ppermute | solution.py:32
  189.8 3.7 %collective-permute-start.40 = (bf16[32,2048]{1,0:T(8,128)(2,1)S(1)}, bf16[32,2048]{1,0:T(8,128)(2,1)S(1)}, u32[]{:S(2)}, u32[]{:S(2)}) collective-permute-start(bf16[32,2048]{1,0:T(8,128)(2,1)S(1)} %get-tuple-element.86), channel_id=1, source_target_pairs={{0,16},{1,17},{2,18},{3,19},{4,20},{5,21},{6,22},{7,23},{8,24},{9,... | collective-permute-start | bytes 393224 | tf_op jit(solution)/shard_map/ppermute | solution.py:32
  193.4 0.7 collective-permute-start.41
  194.7 0.6 slice.180
  196.0 0.7 constant_dynamic-slice_fusion
  196.9 4.3 %collective-permute-done.40 = bf16[32,2048]{1,0:T(8,128)(2,1)S(1)} collective-permute-done((bf16[32,2048]{1,0:T(8,128)(2,1)S(1)}, bf16[32,2048]{1,0:T(8,128)(2,1)S(1)}, u32[]{:S(2)}, u32[]{:S(2)}) %collective-permute-start.40) | collective-permute-done | bytes 131104 | tf_op jit(solution)/shard_map/ppermute | solution.py:32
  201.3 0.7 fusion.13
  (116 shorter events, 10.7 us)
Async XLA Ops:
  0.6 39.9 %copy-start.15 = (s32[256]{0:T(256)S(1)}, s32[256]{0:T(256)}, u32[]{:S(2)}) copy-start(s32[256]{0:T(256)} %param.17) | copy-start | bytes 3076
  0.7 45.8 %copy-start.16 = (s32[256]{0:T(256)S(1)}, s32[256]{0:T(256)}, u32[]{:S(2)}) copy-start(s32[256]{0:T(256)} %param.18) | copy-start | bytes 3076
  3.8 23.4 %collective-permute-start.20 = (bf16[16,2176]{1,0:T(8,128)(2,1)S(1)}, bf16[16,2176]{1,0:T(8,128)(2,1)S(1)}, u32[]{:S(2)}, u32[]{:S(2)}) collective-permute-start(bf16[16,2176]{1,0:T(8,128)(2,1)S(1)} %maximum_maximum_fusion), channel_id=1, source_target_pairs={{0,8},{1,9},{2,10},{3,11},{4,12},{5,13},{6,14},{7,15},{8,0},{9,1},... | collective-permute-start | bytes 208904 | tf_op jit(solution)/shard_map/ppermute | solution.py:32
  6.9 21.5 %collective-permute-start.21 = (bf16[16,2176]{1,0:T(8,128)(2,1)S(1)}, bf16[16,2176]{1,0:T(8,128)(2,1)S(1)}, u32[]{:S(2)}, u32[]{:S(2)}) collective-permute-start(bf16[16,2176]{1,0:T(8,128)(2,1)S(1)} %maximum_maximum_fusion), channel_id=1, source_target_pairs={{0,16},{1,17},{2,18},{3,19},{4,20},{5,21},{6,22},{7,23},{8,24},{9,... | collective-permute-start | bytes 208904 | tf_op jit(solution)/shard_map/ppermute | solution.py:32
  9.5 6.9 %collective-permute-start = (bf16[64,512]{1,0:T(8,128)(2,1)}, bf16[64,512]{1,0:T(8,128)(2,1)S(1)}, u32[]{:S(2)}, u32[]{:S(2)}) collective-permute-start(bf16[64,512]{1,0:T(8,128)(2,1)} %param.28), channel_id=1, source_target_pairs={{0,8},{1,9},{2,10},{3,11},{4,12},{5,13},{6,14},{7,15},{8,0},{9,1},... | collective-permute-start | bytes 196616 | tf_op jit(solution)/shard_map/ppermute | solution.py:32
  9.9 8.5 %collective-permute-start.1 = (bf16[64,512]{1,0:T(8,128)(2,1)}, bf16[64,512]{1,0:T(8,128)(2,1)S(1)}, u32[]{:S(2)}, u32[]{:S(2)}) collective-permute-start(bf16[64,512]{1,0:T(8,128)(2,1)} %param.28), channel_id=1, source_target_pairs={{0,16},{1,17},{2,18},{3,19},{4,20},{5,21},{6,22},{7,23},{8,24},{9,... | collective-permute-start | bytes 196616 | tf_op jit(solution)/shard_map/ppermute | solution.py:32
  9.9 8.5 %collective-permute-start.2 = (bf16[64,512]{1,0:T(8,128)(2,1)}, bf16[64,512]{1,0:T(8,128)(2,1)S(1)}, u32[]{:S(2)}, u32[]{:S(2)}) collective-permute-start(bf16[64,512]{1,0:T(8,128)(2,1)} %param.28), channel_id=1, source_target_pairs={{0,24},{1,25},{2,26},{3,27},{4,28},{5,29},{6,30},{7,31},{8,16},{9,... | collective-permute-start | bytes 196616 | tf_op jit(solution)/shard_map/ppermute | solution.py:32
  16.4 13.5 %collective-permute-start.22 = (bf16[16,2176]{1,0:T(8,128)(2,1)S(1)}, bf16[16,2176]{1,0:T(8,128)(2,1)S(1)}, u32[]{:S(2)}, u32[]{:S(2)}) collective-permute-start(bf16[16,2176]{1,0:T(8,128)(2,1)S(1)} %maximum_maximum_fusion), channel_id=1, source_target_pairs={{0,24},{1,25},{2,26},{3,27},{4,28},{5,29},{6,30},{7,31},{8,16},{9,... | collective-permute-start | bytes 208904 | tf_op jit(solution)/shard_map/ppermute | solution.py:32
  18.4 13.0 %collective-permute-start.11 = (bf16[32,2048]{1,0:T(8,128)(2,1)S(1)}, bf16[32,2048]{1,0:T(8,128)(2,1)S(1)}, u32[]{:S(2)}, u32[]{:S(2)}) collective-permute-start(bf16[32,2048]{1,0:T(8,128)(2,1)S(1)} %constant_dynamic-update-slice_fusion), channel_id=1, source_target_pairs={{0,16},{1,17},{2,18},{3,19},{4,20},{5,21},{6,22},{7,23},{8,24},{9,... | collective-permute-start | bytes 393224 | tf_op jit(solution)/shard_map/ppermute | solution.py:32
  18.4 13.7 %collective-permute-start.12 = (bf16[32,2048]{1,0:T(8,128)(2,1)S(1)}, bf16[32,2048]{1,0:T(8,128)(2,1)S(1)}, u32[]{:S(2)}, u32[]{:S(2)}) collective-permute-start(bf16[32,2048]{1,0:T(8,128)(2,1)S(1)} %constant_dynamic-update-slice_fusion), channel_id=1, source_target_pairs={{0,24},{1,25},{2,26},{3,27},{4,28},{5,29},{6,30},{7,31},{8,16},{9,... | collective-permute-start | bytes 393224 | tf_op jit(solution)/shard_map/ppermute | solution.py:32
  27.2 6.5 %collective-permute-start.10 = (bf16[32,2048]{1,0:T(8,128)(2,1)S(1)}, bf16[32,2048]{1,0:T(8,128)(2,1)S(1)}, u32[]{:S(2)}, u32[]{:S(2)}) collective-permute-start(bf16[32,2048]{1,0:T(8,128)(2,1)S(1)} %constant_dynamic-update-slice_fusion), channel_id=1, source_target_pairs={{0,8},{1,9},{2,10},{3,11},{4,12},{5,13},{6,14},{7,15},{8,0},{9,1},... | collective-permute-start | bytes 393224 | tf_op jit(solution)/shard_map/ppermute | solution.py:32
  28.3 9.2 %collective-permute-start.3 = (bf16[4,64,512]{2,1,0:T(8,128)(2,1)S(1)}, bf16[4,64,512]{2,1,0:T(8,128)(2,1)S(1)}, u32[]{:S(2)}, u32[]{:S(2)}) collective-permute-start(bf16[4,64,512]{2,1,0:T(8,128)(2,1)S(1)} %pad_maximum_fusion.2.p0), channel_id=1, source_target_pairs={{0,2},{1,5},{2,0},{3,7},{4,6},{5,1},{6,4},{7,3},{8,10},{9,13},{10,... | collective-permute-start | bytes 786440 | tf_op jit(solution)/shard_map/ppermute | solution.py:32
  29.8 9.2 %collective-permute-start.4 = (bf16[4,64,512]{2,1,0:T(8,128)(2,1)S(1)}, bf16[4,64,512]{2,1,0:T(8,128)(2,1)}, u32[]{:S(2)}, u32[]{:S(2)}) collective-permute-start(bf16[4,64,512]{2,1,0:T(8,128)(2,1)S(1)} %pad_maximum_fusion.2.p0), channel_id=1, source_target_pairs={{0,4},{1,3},{2,6},{3,1},{4,0},{5,7},{6,2},{7,5},{8,12},{9,11},{10,... | collective-permute-start | bytes 786440 | tf_op jit(solution)/shard_map/ppermute | solution.py:32
  31.4 12.1 %collective-permute-start.23 = (bf16[4,16,2176]{2,1,0:T(8,128)(2,1)S(1)}, bf16[4,16,2176]{2,1,0:T(8,128)(2,1)S(1)}, u32[]{:S(2)}, u32[]{:S(2)}) collective-permute-start(bf16[4,16,2176]{2,1,0:T(8,128)(2,1)S(1)} %pad_maximum_fusion.1.p0), channel_id=1, source_target_pairs={{0,2},{1,5},{2,0},{3,7},{4,6},{5,1},{6,4},{7,3},{8,10},{9,13},{10,... | collective-permute-start | bytes 835592 | tf_op jit(solution)/shard_map/ppermute | solution.py:32
  32.2 12.9 %collective-permute-start.24 = (bf16[4,16,2176]{2,1,0:T(8,128)(2,1)S(1)}, bf16[4,16,2176]{2,1,0:T(8,128)(2,1)}, u32[]{:S(2)}, u32[]{:S(2)}) collective-permute-start(bf16[4,16,2176]{2,1,0:T(8,128)(2,1)S(1)} %pad_maximum_fusion.1.p0), channel_id=1, source_target_pairs={{0,4},{1,3},{2,6},{3,1},{4,0},{5,7},{6,2},{7,5},{8,12},{9,11},{10,... | collective-permute-start | bytes 835592 | tf_op jit(solution)/shard_map/ppermute | solution.py:32
  33.7 11.9 %collective-permute-start.26 = (bf16[4,16,2176]{2,1,0:T(8,128)(2,1)S(1)}, bf16[4,16,2176]{2,1,0:T(8,128)(2,1)S(1)}, u32[]{:S(2)}, u32[]{:S(2)}) collective-permute-start(bf16[4,16,2176]{2,1,0:T(8,128)(2,1)S(1)} %pad_maximum_fusion.1.p0), channel_id=1, source_target_pairs={{0,1},{1,0},{2,3},{3,2},{4,5},{5,4},{6,7},{7,6},{8,9},{9,8},{10,11... | collective-permute-start | bytes 835592 | tf_op jit(solution)/shard_map/ppermute | solution.py:32
  37.6 9.0 %copy-start.6 = (bf16[4,64,512]{2,1,0:T(8,128)(2,1)}, bf16[4,64,512]{2,1,0:T(8,128)(2,1)S(1)}, u32[]{:S(2)}) copy-start(bf16[4,64,512]{2,1,0:T(8,128)(2,1)S(1)} %collective-permute-done.3.p1) | copy-start | bytes 786436
  37.6 20.9 %collective-permute-start.13 = (bf16[4,32,2048]{2,1,0:T(8,128)(2,1)S(1)}, bf16[4,32,2048]{2,1,0:T(8,128)(2,1)S(1)}, u32[]{:S(2)}, u32[]{:S(2)}) collective-permute-start(bf16[4,32,2048]{2,1,0:T(8,128)(2,1)S(1)} %pad_maximum_fusion.p0), channel_id=1, source_target_pairs={{0,2},{1,5},{2,0},{3,7},{4,6},{5,1},{6,4},{7,3},{8,10},{9,13},{10,... | collective-permute-start | bytes 1572872 | tf_op jit(solution)/shard_map/ppermute | solution.py:32
  39.1 21.4 %collective-permute-start.14 = (bf16[4,32,2048]{2,1,0:T(8,128)(2,1)S(1)}, bf16[4,32,2048]{2,1,0:T(8,128)(2,1)S(1)}, u32[]{:S(2)}, u32[]{:S(2)}) collective-permute-start(bf16[4,32,2048]{2,1,0:T(8,128)(2,1)S(1)} %pad_maximum_fusion.p0), channel_id=1, source_target_pairs={{0,4},{1,3},{2,6},{3,1},{4,0},{5,7},{6,2},{7,5},{8,12},{9,11},{10,... | collective-permute-start | bytes 1572872 | tf_op jit(solution)/shard_map/ppermute | solution.py:32
  43.5 10.9 %collective-permute-start.5 = (bf16[4,64,512]{2,1,0:T(8,128)(2,1)S(1)}, bf16[4,64,512]{2,1,0:T(8,128)(2,1)}, u32[]{:S(2)}, u32[]{:S(2)}) collective-permute-start(bf16[4,64,512]{2,1,0:T(8,128)(2,1)S(1)} %collective-permute-done.3.p1), channel_id=1, source_target_pairs={{0,4},{1,3},{2,6},{3,1},{4,0},{5,7},{6,2},{7,5},{8,12},{9,11},{10,... | collective-permute-start | bytes 786440 | tf_op jit(solution)/shard_map/ppermute | solution.py:32
  45.1 12.4 %collective-permute-start.25 = (bf16[4,16,2176]{2,1,0:T(8,128)(2,1)S(1)}, bf16[4,16,2176]{2,1,0:T(8,128)(2,1)}, u32[]{:S(2)}, u32[]{:S(2)}) collective-permute-start(bf16[4,16,2176]{2,1,0:T(8,128)(2,1)S(1)} %collective-permute-done.23.p1), channel_id=1, source_target_pairs={{0,4},{1,3},{2,6},{3,1},{4,0},{5,7},{6,2},{7,5},{8,12},{9,11},{10,... | collective-permute-start | bytes 835592 | tf_op jit(solution)/shard_map/ppermute | solution.py:32
  45.6 0.7 copy-start
  46.3 12.8 %collective-permute-start.27 = (bf16[4,16,2176]{2,1,0:T(8,128)(2,1)S(1)}, bf16[4,16,2176]{2,1,0:T(8,128)(2,1)S(1)}, u32[]{:S(2)}, u32[]{:S(2)}) collective-permute-start(bf16[4,16,2176]{2,1,0:T(8,128)(2,1)S(1)} %collective-permute-done.23.p1), channel_id=1, source_target_pairs={{0,1},{1,0},{2,3},{3,2},{4,5},{5,4},{6,7},{7,6},{8,9},{9,8},{10,11... | collective-permute-start | bytes 835592 | tf_op jit(solution)/shard_map/ppermute | solution.py:32
  54.4 13.5 %collective-permute-start.16 = (bf16[4,32,2048]{2,1,0:T(8,128)(2,1)S(1)}, bf16[4,32,2048]{2,1,0:T(8,128)(2,1)S(1)}, u32[]{:S(2)}, u32[]{:S(2)}) collective-permute-start(bf16[4,32,2048]{2,1,0:T(8,128)(2,1)S(1)} %pad_maximum_fusion.p0), channel_id=1, source_target_pairs={{0,1},{1,0},{2,3},{3,2},{4,5},{5,4},{6,7},{7,6},{8,9},{9,8},{10,11... | collective-permute-start | bytes 1572872 | tf_op jit(solution)/shard_map/ppermute | solution.py:32
  57.4 3.3 %collective-permute-start.28 = (bf16[4,16,2176]{2,1,0:T(8,128)(2,1)}, bf16[4,16,2176]{2,1,0:T(8,128)(2,1)S(1)}, u32[]{:S(2)}, u32[]{:S(2)}) collective-permute-start(bf16[4,16,2176]{2,1,0:T(8,128)(2,1)} %collective-permute-done.24.p2), channel_id=1, source_target_pairs={{0,1},{1,0},{2,3},{3,2},{4,5},{5,4},{6,7},{7,6},{8,9},{9,8},{10,11... | collective-permute-start | bytes 835592 | tf_op jit(solution)/shard_map/ppermute | solution.py:32
  58.5 9.3 %collective-permute-start.15 = (bf16[4,32,2048]{2,1,0:T(8,128)(2,1)S(1)}, bf16[4,32,2048]{2,1,0:T(8,128)(2,1)}, u32[]{:S(2)}, u32[]{:S(2)}) collective-permute-start(bf16[4,32,2048]{2,1,0:T(8,128)(2,1)S(1)} %collective-permute-done.13.p1), channel_id=1, source_target_pairs={{0,4},{1,3},{2,6},{3,1},{4,0},{5,7},{6,2},{7,5},{8,12},{9,11},{10,... | collective-permute-start | bytes 1572872 | tf_op jit(solution)/shard_map/ppermute | solution.py:32
  59.8 8.8 %collective-permute-start.17 = (bf16[4,32,2048]{2,1,0:T(8,128)(2,1)S(1)}, bf16[4,32,2048]{2,1,0:T(8,128)(2,1)}, u32[]{:S(2)}, u32[]{:S(2)}) collective-permute-start(bf16[4,32,2048]{2,1,0:T(8,128)(2,1)S(1)} %collective-permute-done.13.p1), channel_id=1, source_target_pairs={{0,1},{1,0},{2,3},{3,2},{4,5},{5,4},{6,7},{7,6},{8,9},{9,8},{10,11... | collective-permute-start | bytes 1572872 | tf_op jit(solution)/shard_map/ppermute | solution.py:32
  60.4 8.6 %collective-permute-start.18 = (bf16[4,32,2048]{2,1,0:T(8,128)(2,1)S(1)}, bf16[4,32,2048]{2,1,0:T(8,128)(2,1)}, u32[]{:S(2)}, u32[]{:S(2)}) collective-permute-start(bf16[4,32,2048]{2,1,0:T(8,128)(2,1)S(1)} %collective-permute-done.14.p2), channel_id=1, source_target_pairs={{0,1},{1,0},{2,3},{3,2},{4,5},{5,4},{6,7},{7,6},{8,9},{9,8},{10,11... | collective-permute-start | bytes 1572872 | tf_op jit(solution)/shard_map/ppermute | solution.py:32
  60.8 0.7 copy-start.4
  61.5 7.0 %collective-permute-start.29 = (bf16[4,16,2176]{2,1,0:T(8,128)(2,1)}, bf16[4,16,2176]{2,1,0:T(8,128)(2,1)}, u32[]{:S(2)}, u32[]{:S(2)}) collective-permute-start(bf16[4,16,2176]{2,1,0:T(8,128)(2,1)} %collective-permute-done.25.p3), channel_id=1, source_target_pairs={{0,1},{1,0},{2,3},{3,2},{4,5},{5,4},{6,7},{7,6},{8,9},{9,8},{10,11... | collective-permute-start | bytes 835592 | tf_op jit(solution)/shard_map/ppermute | solution.py:32
  67.8 23.8 %collective-permute-start.19 = (bf16[4,32,2048]{2,1,0:T(8,128)(2,1)}, bf16[4,32,2048]{2,1,0:T(8,128)(2,1)}, u32[]{:S(2)}, u32[]{:S(2)}) collective-permute-start(bf16[4,32,2048]{2,1,0:T(8,128)(2,1)} %collective-permute-done.15.p3), channel_id=1, source_target_pairs={{0,1},{1,0},{2,3},{3,2},{4,5},{5,4},{6,7},{7,6},{8,9},{9,8},{10,11... | collective-permute-start | bytes 1572872 | tf_op jit(solution)/shard_map/ppermute | solution.py:32
  67.9 32.9 %collective-permute-start.6 = (bf16[4,64,512]{2,1,0:T(8,128)(2,1)S(1)}, bf16[4,64,512]{2,1,0:T(8,128)(2,1)S(1)}, u32[]{:S(2)}, u32[]{:S(2)}) collective-permute-start(bf16[4,64,512]{2,1,0:T(8,128)(2,1)S(1)} %pad_maximum_fusion.2.p0), channel_id=1, source_target_pairs={{0,1},{1,0},{2,3},{3,2},{4,5},{5,4},{6,7},{7,6},{8,9},{9,8},{10,11... | collective-permute-start | bytes 786440 | tf_op jit(solution)/shard_map/ppermute | solution.py:32
  68.5 32.3 %collective-permute-start.7 = (bf16[4,64,512]{2,1,0:T(8,128)(2,1)}, bf16[4,64,512]{2,1,0:T(8,128)(2,1)S(1)}, u32[]{:S(2)}, u32[]{:S(2)}) collective-permute-start(bf16[4,64,512]{2,1,0:T(8,128)(2,1)} %copy-done.6), channel_id=1, source_target_pairs={{0,1},{1,0},{2,3},{3,2},{4,5},{5,4},{6,7},{7,6},{8,9},{9,8},{10,11... | collective-permute-start | bytes 786440 | tf_op jit(solution)/shard_map/ppermute | solution.py:32
  68.6 32.2 %collective-permute-start.8 = (bf16[4,64,512]{2,1,0:T(8,128)(2,1)}, bf16[4,64,512]{2,1,0:T(8,128)(2,1)S(1)}, u32[]{:S(2)}, u32[]{:S(2)}) collective-permute-start(bf16[4,64,512]{2,1,0:T(8,128)(2,1)} %collective-permute-done.4.p2), channel_id=1, source_target_pairs={{0,1},{1,0},{2,3},{3,2},{4,5},{5,4},{6,7},{7,6},{8,9},{9,8},{10,11... | collective-permute-start | bytes 786440 | tf_op jit(solution)/shard_map/ppermute | solution.py:32
  69.0 31.8 %collective-permute-start.9 = (bf16[4,64,512]{2,1,0:T(8,128)(2,1)}, bf16[4,64,512]{2,1,0:T(8,128)(2,1)S(1)}, u32[]{:S(2)}, u32[]{:S(2)}) collective-permute-start(bf16[4,64,512]{2,1,0:T(8,128)(2,1)} %collective-permute-done.5.p3), channel_id=1, source_target_pairs={{0,1},{1,0},{2,3},{3,2},{4,5},{5,4},{6,7},{7,6},{8,9},{9,8},{10,11... | collective-permute-start | bytes 786440 | tf_op jit(solution)/shard_map/ppermute | solution.py:32
  69.1 1.0 copy-start.1
  70.1 1.0 copy-start.3
  71.0 1.0 copy-start.5
  91.6 9.3 %copy-start.7 = (bf16[4,64,512]{2,1,0:T(8,128)(2,1)S(1)}, bf16[4,64,512]{2,1,0:T(8,128)(2,1)}, u32[]{:S(2)}) copy-start(bf16[4,64,512]{2,1,0:T(8,128)(2,1)} %copy-done.6) | copy-start | bytes 786436
  99.4 1.0 copy-start.8
  100.4 33.7 %collective-permute-start.42 = (bf16[16,64,512]{2,1,0:T(8,128)(2,1)}, bf16[16,64,512]{2,1,0:T(8,128)(2,1)S(1)}, u32[]{:S(2)}, u32[]{:S(2)}) collective-permute-start(bf16[16,64,512]{2,1,0:T(8,128)(2,1)} %get-tuple-element.77), channel_id=1, source_target_pairs={{0,1},{1,0},{2,3},{3,2},{4,5},{5,4},{6,7},{7,6},{8,9},{9,8},{10,11... | collective-permute-start | bytes 3145736 | tf_op jit(solution)/shard_map/ppermute | solution.py:32
  112.0 22.0 %copy-start.12 = (f32[16,64,512]{2,1,0:T(8,128)S(1)}, f32[16,64,512]{2,1,0:T(8,128)}, u32[]{:S(2)}) copy-start(f32[16,64,512]{2,1,0:T(8,128)} %get-tuple-element.76) | copy-start | bytes 6291460
  134.0 11.3 %collective-permute-start.30 = (bf16[16,16,2176]{2,1,0:T(8,128)(2,1)S(1)}, bf16[16,16,2176]{2,1,0:T(8,128)(2,1)S(1)}, u32[]{:S(2)}, u32[]{:S(2)}) collective-permute-start(bf16[16,16,2176]{2,1,0:T(8,128)(2,1)S(1)} %get-tuple-element.73), channel_id=1, source_target_pairs={{0,1},{1,0},{2,3},{3,2},{4,5},{5,4},{6,7},{7,6},{8,9},{9,8},{10,11... | collective-permute-start | bytes 3342344 | tf_op jit(solution)/shard_map/ppermute | solution.py:32
  134.2 11.1 %copy-start.10 = (f32[16,16,2176]{2,1,0:T(8,128)S(1)}, f32[16,16,2176]{2,1,0:T(8,128)}, u32[]{:S(2)}) copy-start(f32[16,16,2176]{2,1,0:T(8,128)} %get-tuple-element.72) | copy-start | bytes 6684676
  134.3 9.2 %collective-permute-start.43 = (bf16[8,64,512]{2,1,0:T(8,128)(2,1)S(1)}, bf16[8,64,512]{2,1,0:T(8,128)(2,1)S(1)}, u32[]{:S(2)}, u32[]{:S(2)}) collective-permute-start(bf16[8,64,512]{2,1,0:T(8,128)(2,1)S(1)} %add_convert_fusion.2), channel_id=1, source_target_pairs={{0,4},{1,3},{2,6},{3,1},{4,0},{5,7},{6,2},{7,5},{8,12},{9,11},{10,... | collective-permute-start | bytes 1572872 | tf_op jit(solution)/shard_map/ppermute | solution.py:32
  134.9 27.1 %collective-permute-start.36 = (bf16[16,32,2048]{2,1,0:T(8,128)(2,1)}, bf16[16,32,2048]{2,1,0:T(8,128)(2,1)}, u32[]{:S(2)}, u32[]{:S(2)}) collective-permute-start(bf16[16,32,2048]{2,1,0:T(8,128)(2,1)} %get-tuple-element.75), channel_id=1, source_target_pairs={{0,1},{1,0},{2,3},{3,2},{4,5},{5,4},{6,7},{7,6},{8,9},{9,8},{10,11... | collective-permute-start | bytes 6291464 | tf_op jit(solution)/shard_map/ppermute | solution.py:32
  143.8 9.1 %collective-permute-start.44 = (bf16[4,64,512]{2,1,0:T(8,128)(2,1)S(1)}, bf16[4,64,512]{2,1,0:T(8,128)(2,1)}, u32[]{:S(2)}, u32[]{:S(2)}) collective-permute-start(bf16[4,64,512]{2,1,0:T(8,128)(2,1)S(1)} %slice.250), channel_id=1, source_target_pairs={{0,2},{1,5},{2,0},{3,7},{4,6},{5,1},{6,4},{7,3},{8,10},{9,13},{10,... | collective-permute-start | bytes 786440 | tf_op jit(solution)/shard_map/ppermute | solution.py:32
  145.3 1.2 copy-start.13
  145.3 13.0 %copy-start.11 = (f32[16,16,2176]{2,1,0:T(8,128)S(1)}, f32[16,16,2176]{2,1,0:T(8,128)}, u32[]{:S(2)}) copy-start(f32[16,16,2176]{2,1,0:T(8,128)} %get-tuple-element.72) | copy-start | bytes 6684676
  146.5 11.8 %collective-permute-start.31 = (bf16[8,16,2176]{2,1,0:T(8,128)(2,1)}, bf16[8,16,2176]{2,1,0:T(8,128)(2,1)}, u32[]{:S(2)}, u32[]{:S(2)}) collective-permute-start(bf16[8,16,2176]{2,1,0:T(8,128)(2,1)} %add_convert_fusion.1), channel_id=1, source_target_pairs={{0,4},{1,3},{2,6},{3,1},{4,0},{5,7},{6,2},{7,5},{8,12},{9,11},{10,... | collective-permute-start | bytes 1671176 | tf_op jit(solution)/shard_map/ppermute | solution.py:32
  147.1 11.3 %copy-start.14 = (bf16[16,16,2176]{2,1,0:T(8,128)(2,1)S(1)}, bf16[16,16,2176]{2,1,0:T(8,128)(2,1)}, u32[]{:S(2)}) copy-start(bf16[16,16,2176]{2,1,0:T(8,128)(2,1)} %copy-done.13) | copy-start | bytes 3342340
  153.9 7.3 %collective-permute-start.45 = (bf16[64,512]{1,0:T(8,128)(2,1)S(1)}, bf16[64,512]{1,0:T(8,128)(2,1)S(1)}, u32[]{:S(2)}, u32[]{:S(2)}) collective-permute-start(bf16[64,512]{1,0:T(8,128)(2,1)S(1)} %get-tuple-element.92), channel_id=1, source_target_pairs={{0,8},{1,9},{2,10},{3,11},{4,12},{5,13},{6,14},{7,15},{8,0},{9,1},... | collective-permute-start | bytes 196616 | tf_op jit(solution)/shard_map/ppermute | solution.py:32
  154.0 7.2 %collective-permute-start.46 = (bf16[64,512]{1,0:T(8,128)(2,1)S(1)}, bf16[64,512]{1,0:T(8,128)(2,1)S(1)}, u32[]{:S(2)}, u32[]{:S(2)}) collective-permute-start(bf16[64,512]{1,0:T(8,128)(2,1)S(1)} %get-tuple-element.94), channel_id=1, source_target_pairs={{0,16},{1,17},{2,18},{3,19},{4,20},{5,21},{6,22},{7,23},{8,24},{9,... | collective-permute-start | bytes 196616 | tf_op jit(solution)/shard_map/ppermute | solution.py:32
  155.1 7.0 %copy-start.9 = (f32[16,32,2048]{2,1,0:T(8,128)S(1)}, f32[16,32,2048]{2,1,0:T(8,128)}, u32[]{:S(2)}) copy-start(f32[16,32,2048]{2,1,0:T(8,128)} %get-tuple-element.74) | copy-start | bytes 12582916
  155.1 6.3 %collective-permute-start.47 = (bf16[64,512]{1,0:T(8,128)(2,1)S(1)}, bf16[64,512]{1,0:T(8,128)(2,1)S(1)}, u32[]{:S(2)}, u32[]{:S(2)}) collective-permute-start(bf16[64,512]{1,0:T(8,128)(2,1)S(1)} %get-tuple-element.93), channel_id=1, source_target_pairs={{0,24},{1,25},{2,26},{3,27},{4,28},{5,29},{6,30},{7,31},{8,16},{9,... | collective-permute-start | bytes 196616 | tf_op jit(solution)/shard_map/ppermute | solution.py:32
  159.6 9.6 %collective-permute-start.32 = (bf16[4,16,2176]{2,1,0:T(8,128)(2,1)S(1)}, bf16[4,16,2176]{2,1,0:T(8,128)(2,1)S(1)}, u32[]{:S(2)}, u32[]{:S(2)}) collective-permute-start(bf16[4,16,2176]{2,1,0:T(8,128)(2,1)S(1)} %slice.249), channel_id=1, source_target_pairs={{0,2},{1,5},{2,0},{3,7},{4,6},{5,1},{6,4},{7,3},{8,10},{9,13},{10,... | collective-permute-start | bytes 835592 | tf_op jit(solution)/shard_map/ppermute | solution.py:32
  163.6 14.9 %collective-permute-start.37 = (bf16[8,32,2048]{2,1,0:T(8,128)(2,1)S(1)}, bf16[8,32,2048]{2,1,0:T(8,128)(2,1)S(1)}, u32[]{:S(2)}, u32[]{:S(2)}) collective-permute-start(bf16[8,32,2048]{2,1,0:T(8,128)(2,1)S(1)} %add_convert_fusion), channel_id=1, source_target_pairs={{0,4},{1,3},{2,6},{3,1},{4,0},{5,7},{6,2},{7,5},{8,12},{9,11},{10,... | collective-permute-start | bytes 3145736 | tf_op jit(solution)/shard_map/ppermute | solution.py:32
  169.3 12.9 %collective-permute-start.33 = (bf16[16,2176]{1,0:T(8,128)(2,1)S(1)}, bf16[16,2176]{1,0:T(8,128)(2,1)S(1)}, u32[]{:S(2)}, u32[]{:S(2)}) collective-permute-start(bf16[16,2176]{1,0:T(8,128)(2,1)S(1)} %get-tuple-element.87), channel_id=1, source_target_pairs={{0,8},{1,9},{2,10},{3,11},{4,12},{5,13},{6,14},{7,15},{8,0},{9,1},... | collective-permute-start | bytes 208904 | tf_op jit(solution)/shard_map/ppermute | solution.py:32
  169.4 12.8 %collective-permute-start.34 = (bf16[16,2176]{1,0:T(8,128)(2,1)S(1)}, bf16[16,2176]{1,0:T(8,128)(2,1)S(1)}, u32[]{:S(2)}, u32[]{:S(2)}) collective-permute-start(bf16[16,2176]{1,0:T(8,128)(2,1)S(1)} %get-tuple-element.89), channel_id=1, source_target_pairs={{0,16},{1,17},{2,18},{3,19},{4,20},{5,21},{6,22},{7,23},{8,24},{9,... | collective-permute-start | bytes 208904 | tf_op jit(solution)/shard_map/ppermute | solution.py:32
  170.4 11.8 %collective-permute-start.35 = (bf16[16,2176]{1,0:T(8,128)(2,1)S(1)}, bf16[16,2176]{1,0:T(8,128)(2,1)S(1)}, u32[]{:S(2)}, u32[]{:S(2)}) collective-permute-start(bf16[16,2176]{1,0:T(8,128)(2,1)S(1)} %get-tuple-element.88), channel_id=1, source_target_pairs={{0,24},{1,25},{2,26},{3,27},{4,28},{5,29},{6,30},{7,31},{8,16},{9,... | collective-permute-start | bytes 208904 | tf_op jit(solution)/shard_map/ppermute | solution.py:32
  180.2 9.2 %collective-permute-start.38 = (bf16[4,32,2048]{2,1,0:T(8,128)(2,1)S(1)}, bf16[4,32,2048]{2,1,0:T(8,128)(2,1)S(1)}, u32[]{:S(2)}, u32[]{:S(2)}) collective-permute-start(bf16[4,32,2048]{2,1,0:T(8,128)(2,1)S(1)} %slice.248), channel_id=1, source_target_pairs={{0,2},{1,5},{2,0},{3,7},{4,6},{5,1},{6,4},{7,3},{8,10},{9,13},{10,... | collective-permute-start | bytes 1572872 | tf_op jit(solution)/shard_map/ppermute | solution.py:32
  189.7 7.3 %collective-permute-start.39 = (bf16[32,2048]{1,0:T(8,128)(2,1)S(1)}, bf16[32,2048]{1,0:T(8,128)(2,1)S(1)}, u32[]{:S(2)}, u32[]{:S(2)}) collective-permute-start(bf16[32,2048]{1,0:T(8,128)(2,1)S(1)} %get-tuple-element.84), channel_id=1, source_target_pairs={{0,8},{1,9},{2,10},{3,11},{4,12},{5,13},{6,14},{7,15},{8,0},{9,1},... | collective-permute-start | bytes 393224 | tf_op jit(solution)/shard_map/ppermute | solution.py:32
  189.8 11.5 %collective-permute-start.40 = (bf16[32,2048]{1,0:T(8,128)(2,1)S(1)}, bf16[32,2048]{1,0:T(8,128)(2,1)S(1)}, u32[]{:S(2)}, u32[]{:S(2)}) collective-permute-start(bf16[32,2048]{1,0:T(8,128)(2,1)S(1)} %get-tuple-element.86), channel_id=1, source_target_pairs={{0,16},{1,17},{2,18},{3,19},{4,20},{5,21},{6,22},{7,23},{8,24},{9,... | collective-permute-start | bytes 393224 | tf_op jit(solution)/shard_map/ppermute | solution.py:32
  193.4 7.8 %collective-permute-start.41 = (bf16[32,2048]{1,0:T(8,128)(2,1)S(1)}, bf16[32,2048]{1,0:T(8,128)(2,1)S(1)}, u32[]{:S(2)}, u32[]{:S(2)}) collective-permute-start(bf16[32,2048]{1,0:T(8,128)(2,1)S(1)} %get-tuple-element.85), channel_id=1, source_target_pairs={{0,24},{1,25},{2,26},{3,27},{4,28},{5,29},{6,30},{7,31},{8,16},{9,... | collective-permute-start | bytes 393224 | tf_op jit(solution)/shard_map/ppermute | solution.py:32
  (1 other events, 0.7 us)

commit v2 on v1

v2 whole, which is shorter than its diff:
```python
import jax
import jax.numpy as jnp
from jax import lax
from jax.experimental import pallas as pl
from jax.experimental.pallas import tpu as pltpu
from jax.sharding import PartitionSpec as P

HEADS = 8
HEAD_DIM = 64
SLOTS = 8
SHARDS = 32
EB = 32
RB = EB * SLOTS
CH = 64
VMEM_LIMIT = 58 * 2**20
SCALE = HEAD_DIM ** (-0.5)
F32 = jnp.float32
LOW = jnp.bfloat16


def pairs(partner):
    return [(i, partner(i)) for i in range(32)]


CORE = pairs(lambda i: i ^ 1)
NEAR = pairs(lambda i: i ^ (2 if i % 2 == 0 else 4))
FAR = pairs(lambda i: i ^ (4 if i % 2 == 0 else 2))
ACROSS = pairs(lambda i: i ^ 6)
LAYER = {p: pairs(lambda i: i ^ (p << 3)) for p in (1, 2, 3)}


def send(value, to):
    return lax.ppermute(value, "dp", to)


def spread(value, *ways):
    return [send(value, way) for way in ways]


def tie(value, *after, every=False):
    tied = lax.optimization_barrier((value, *after))
    return tied if every else tied[0]


def side_by_side(parts, shape):
    total = None
    for row, column, part in parts:
        edges = [(row, shape[0] - row - part.shape[0], 0), (column, shape[1] - column - part.shape[1], 0)]
        padded = lax.pad(part, jnp.zeros((), part.dtype), edges)
        total = padded if total is None else total + padded
    return total


def side_by_side_lanes(parts):
    return jnp.concatenate(parts, axis=-1)


def widen(*values):
    total = values[0].astype(F32)
    for value in values[1:]:
        total = total + value.astype(F32)
    return total


class Sum:
    def __init__(self, own, other):
        self.own = own
        self.core = send(other, CORE)

    def first(self):
        part = widen(self.own[8:], self.core[8:]).astype(LOW)
        self.far = send(part, FAR)
        return part

    def second(self):
        part = widen(self.own[4:8], self.core[4:8], self.far[4:]).astype(LOW)
        self.near = send(part, NEAR)
        return part

    def total(self, at):
        return widen(self.own[at], self.core[at], self.far[at], self.near[at])

    def third(self):
        part = self.total(slice(1, 4, 2)).astype(LOW)
        self.beside = send(part, LAYER[1])
        return part

    def fourth(self):
        part = widen(self.total(2), self.beside[1]).astype(LOW)
        self.beyond = send(part, LAYER[2])
        return part

    def done(self):
        return widen(self.total(0), self.beside[0], self.beyond)


def shard_at(me, k, turned=False):
    if me is None:
        return k
    near = 2 + 2 * (me & 1)
    quads = [0, near, 6 - near, 6, 1, 7 - near, near + 1, 7]
    core, row, column = k // 16, k // 4 % 4, k % 4
    quad, layer = (4 * core + column, row) if turned else (4 * core + row, column)
    return me ^ quads[quad] ^ (layer << 3)


def dot(left, right):
    return jnp.dot(left, right, preferred_element_type=F32)


def dot_nt(left, right):
    return lax.dot_general(left, right, (((1,), (1,)), ((), ())), preferred_element_type=F32)


def dot_tn(left, right):
    return lax.dot_general(left, right, (((0,), (0,)), ((), ())), preferred_element_type=F32)


def iota(shape, axis):
    return lax.broadcasted_iota(jnp.int32, shape, axis)


def norm_parts(values):
    center = values - jnp.mean(values, axis=-1, keepdims=True)
    rate = lax.rsqrt(jnp.mean(center * center, axis=-1, keepdims=True) + 1e-05)
    return center * rate, rate


def norm_back(grad, unit, rate, gain):
    scaled = grad * gain
    return rate * (
        scaled
        - jnp.mean(scaled, axis=-1, keepdims=True)
        - unit * jnp.mean(scaled * unit, axis=-1, keepdims=True)
    )


def fold(values):
    rows, width = values.shape
    return jnp.sum(values.reshape(rows // 8, 8, width), axis=0)


def spread_heads(rows):
    tiled = jnp.concatenate([rows] * HEADS, axis=0)
    shape = (HEADS * EB, HEADS * HEAD_DIM)
    return jnp.where(iota(shape, 0) // EB == iota(shape, 1) // HEAD_DIM, tiled, jnp.zeros_like(tiled))


def pick_heads(full):
    parts = []
    for k in range(HEADS // 2):
        lanes = slice(128 * k, 128 * k + 128)
        even = full[2 * k * EB : (2 * k + 1) * EB, lanes]
        odd = full[(2 * k + 1) * EB : (2 * k + 2) * EB, lanes]
        parts.append(jnp.where(iota(even.shape, 1) < HEAD_DIM, even, odd))
    return jnp.concatenate(parts, axis=1)


def slots_first(ref, out, at):
    for k in range(4):
        out[at, 128 * k : 128 * k + 128] = ref[pl.ds(k * RB, EB, stride=SLOTS), :]


def put_first(ref, values):
    for k in range(4):
        ref[pl.ds(k * RB, EB, stride=SLOTS), :] = values[:, 128 * k : 128 * k + 128]


def put_tall(ref, start, values):
    for k in range(4):
        ref[pl.ds(k * RB + start, values.shape[0]), :] = values[:, 128 * k : 128 * k + 128]


def get_tall(ref, start, rows):
    return jnp.concatenate([ref[pl.ds(k * RB + start, rows), :] for k in range(4)], axis=1)


def block(i, rows):
    return pl.ds(pl.multiple_of(i * rows, rows), rows)


class Load:
    def __init__(self, source, buffer, sems, first, parts, box):
        self.buffer, self.parts, self.box = buffer, parts, box
        self.source, self.sems, self.first = source, sems, first
        for i in range(parts):
            self.copy(i).start()

    def copy(self, i):
        rows = self.buffer.shape[0] // self.parts
        at = block(i, rows) if self.parts > 1 else pl.ds(0, rows)
        if self.box is None:
            source = self.source.at[at]
        else:
            row, _rows, column, columns = self.box
            start = row + i * rows
            if not isinstance(start, int):
                start = pl.multiple_of(start, rows)
            source = self.source.at[pl.ds(start, rows), pl.ds(column, columns)]
        return pltpu.make_async_copy(source, self.buffer.at[at], self.sems.at[self.first + i])

    def part(self, i):
        self.copy(i).wait()

    def whole(self):
        for i in range(self.parts):
            self.copy(i).wait()
        return self.buffer


class Store:
    def __init__(self, target, buffer, sems, first, parts, row=0):
        self.buffer, self.parts, self.row = buffer, parts, row
        self.target, self.sems, self.first = target, sems, first

    def copy(self, i):
        rows = self.buffer.shape[0] // self.parts
        at = block(i, rows) if self.parts > 1 else pl.ds(0, rows)
        if self.row == 0:
            target = self.target.at[at]
        else:
            start = self.row + i * rows
            target = self.target.at[pl.ds(start if isinstance(start, int) else pl.multiple_of(start, rows), rows)]
        return pltpu.make_async_copy(self.buffer.at[at], target, self.sems.at[self.first + i])

    def part(self, i):
        self.copy(i).start()

    def send(self):
        for i in range(self.parts):
            self.copy(i).start()


def call(body, micros, me, near, loads, stores, scratch=(), after=(), into=None):
    far = pl.BlockSpec(memory_space=pltpu.HBM)
    given = [] if into is None or isinstance(into[0], tuple) else [into[0]]
    counts = [len(near), len(loads), len(after) + len(given), len(stores), len(loads), len(stores), len(scratch)]
    shapes = [shape for shape, _type, _parts in stores]
    if into is not None:
        shapes[0] = into[0] if not given else into[0].shape

    def kernel(me_ref, *refs):
        groups, at = [], 0
        for count in counts:
            groups.append(refs[at : at + count])
            at += count
        near_refs, sources, _unused, targets, in_buffers, out_buffers, rest = groups
        in_sems, out_sems, near_sem = refs[at:]
        first, reads = 0, []
        for (_array, parts, box), source, buffer in zip(loads, sources, in_buffers):
            reads.append(Load(source, buffer, in_sems, first, parts, box))
            first += parts
        first, writes = 0, []
        for (_shape, _type, parts), target, buffer in zip(stores, targets, out_buffers):
            row = target.shape[0] - buffer.shape[0] if given and not writes else 0
            writes.append(Store(target, buffer, out_sems, first, parts, row))
            first += parts
        body(None if me is None else me_ref[0], (near_refs, near_sem), reads, writes, rest)
        for write in writes:
            for i in range(write.parts):
                write.copy(i).wait()

    buffers = [(a.shape if box is None else (box[1], box[3]), a.dtype) for a, _parts, box in loads]
    buffers += [(s, t) for s, t, _parts in stores]
    return pl.pallas_call(
        kernel,
        out_shape=[jax.ShapeDtypeStruct(s, t) for s, (_shape, t, _parts) in zip(shapes, stores)],
        in_specs=[pl.BlockSpec(memory_space=pltpu.SMEM)]
        + [far] * (len(near) + len(loads))
        + [pl.BlockSpec(memory_space=pl.ANY)] * len(after)
        + [far] * len(given),
        out_specs=[far] * len(stores),
        scratch_shapes=[pltpu.VMEM(s, t) for s, t in buffers + list(scratch)]
        + [
            pltpu.SemaphoreType.DMA((max(1, sum(parts for _array, parts, _box in loads)),)),
            pltpu.SemaphoreType.DMA((max(1, sum(parts for _shape, _type, parts in stores)),)),
            pltpu.SemaphoreType.DMA((4,)),
        ],
        input_output_aliases={1 + len(near) + len(loads) + len(after): 0} if given else {},
        compiler_params=pltpu.CompilerParams(vmem_limit_bytes=VMEM_LIMIT),
        cost_estimate=pl.CostEstimate(flops=int(micros * 1.1e9), bytes_accessed=1000, transcendentals=0),
    )(jnp.zeros((1,), jnp.int32) if me is None else me, *near, *[a for a, _parts, _box in loads], *after, *given)


class Place:
    def __init__(self, me, pieces, target, sem, cut, turned=False):
        self.copies = []
        rows = target.shape[0] // SHARDS
        for i, piece in enumerate(pieces):
            for p in range(4):
                at = block(shard_at(me, 4 * i + p, turned), rows)
                copy = pltpu.make_async_copy(cut(piece.at[p]), target.at[at], sem)
                copy.start()
                self.copies.append(copy)

    def wait(self):
        for copy in self.copies:
            copy.wait()


def attend_kernel(me, near, reads, writes, scratch):
    marks, embeds = reads
    weights, vec, bias_up, base0, normed, normed0, query, keyval, probs, mixed = writes
    small, table, rows, tall, rows0, norm0 = scratch
    pieces, sem = near
    Place(me, pieces, weights.buffer, sem.at[0], lambda piece: piece).wait()
    small[...] = weights.buffer[:, 1536:].astype(F32).reshape(SHARDS, 16, 128)
    lane = iota((16, 128), 1)
    for k in range(4):
        tile = small[8 * k]
        for t in range(1, 8):
            tile = jnp.where(lane // 16 == t, pltpu.roll(small[8 * k + t], 16 * t, 1), tile)
        vec.buffer[:, 128 * k : 128 * k + 128] = tile
    lane = iota((16, 128), 1)
    for k in range(16):
        tile = jnp.where(lane < 64, small[2 * k], pltpu.roll(small[2 * k + 1], 64, 1))
        bias_up.buffer[:, 128 * k : 128 * k + 128] = jnp.broadcast_to(tile[13:14], (8, 128))
    for write in (weights, vec, bias_up):
        write.send()
    table[...] = jnp.zeros_like(table)
    table[0:8, :] = vec.buffer[0:8, :]
    gain, shift = vec.buffer[8:9, :], vec.buffer[9:10, :]
    marks.whole()
    blocks = embeds.buffer.shape[0] // RB

    def norm_pair(pair, _):
        embeds.part(pair)
        for half in range(2):
            b = 2 * pair + half
            rows[half] = dot(marks.buffer[block(b, RB), :], table[...].astype(LOW))
            for c in range(RB // CH):
                at = pl.ds(c * CH, CH)
                here = pl.ds(pl.multiple_of(b * RB + c * CH, CH), CH)
                base = embeds.buffer[here, :].astype(F32) + rows[half, at, :]
                put_tall(tall.at[half], c * CH, base)
                unit, _rate = norm_parts(base)
                value = unit * gain + shift
                put_tall(rows0.at[half], c * CH, value)
                normed.buffer[here, :] = value.astype(LOW)
            out = block(b, EB)
            slots_first(tall.at[half], base0.buffer, out)
            slots_first(rows0.at[half], norm0, out)
            keyval.buffer[block(b, RB), :] = dot(normed.buffer[block(b, RB), :], weights.buffer[:, 512:1536]).astype(LOW)
        normed.part(pair)
        keyval.part(pair)
        return 0

    lax.fori_loop(0, blocks // 2, norm_pair, 0)
    normed0.buffer[...] = norm0[...].astype(LOW)
    query.buffer[...] = dot(normed0.buffer[...], weights.buffer[:, :512]).astype(LOW)
    normed0.send()
    query.send()
    base0.send()
    shape = (RB, HEADS * EB)
    match = iota(shape, 0) // SLOTS == iota(shape, 1) % EB
    liver = jnp.where(iota((128, HEADS * EB), 0) == 8, 1.0, 0.0).astype(LOW)

    def attend_pair(pair, _):
        for half in range(2):
            b = 2 * pair + half
            at, out = block(b, RB), block(b, EB)
            scores = dot_nt(keyval.buffer[at, :512], spread_heads(query.buffer[out, :])) * SCALE
            live = dot(marks.buffer[at, :], liver) > 0.5
            scores = jnp.where(live, scores, -1000000000.0).reshape(EB, SLOTS, HEADS * EB)
            top = jnp.max(scores, axis=1, keepdims=True)
            power = jnp.exp(scores - top)
            part = (power / jnp.sum(power, axis=1, keepdims=True)).reshape(shape)
            low = jnp.where(match, part, 0.0).astype(LOW)
            probs.buffer[at, :] = low
            mixed.buffer[out, :] = pick_heads(dot_tn(low, keyval.buffer[at, 512:])).astype(LOW)
        probs.part(pair)
        return 0

    lax.fori_loop(0, blocks // 2, attend_pair, 0)
    mixed.send()


def ffn_kernel(me, near, reads, writes, scratch):
    cotangent, base0, mixed, vec, bias_up = reads
    output, dfirst, dmixed, sum_up, sum_gain, sum_shift, sum_pool, own_down, other_down, own, other = writes
    w_proj, w_up, w_down, w_out, first, norm_ffn, dpool, hidden, slope, pre_low, total = scratch
    pieces, sem = near
    out = Place(me, pieces[8:], w_out, sem.at[3], lambda piece: piece.at[pl.ds(64, 16)], turned=True)
    proj = Place(me, pieces[:8], w_proj, sem.at[0], lambda piece: piece.at[pl.ds(0, 16)])
    up = Place(me, pieces[:8], w_up, sem.at[1], lambda piece: piece.at[pl.ds(16, 16)])
    down = Place(me, pieces[8:], w_down, sem.at[2], lambda piece: piece.at[pl.ds(0, 64)], turned=True)

    def share(mine, theirs, row, rows, lanes, base=0):
        for k in range(SHARDS):
            half = mine if k < 16 else theirs
            half.buffer[k % 16, row : row + rows, lanes] = total[block(base + shard_at(me, k), rows), :].astype(LOW)

    for read in (base0, mixed, vec):
        read.whole()
    out.wait()
    first[...] = base0.buffer[...] + dot(mixed.buffer[...], w_out[...])
    for c in range(first.shape[0] // CH):
        at = pl.ds(c * CH, CH)
        unit, _rate = norm_parts(first[at, :])
        norm_ffn[at, :] = (unit * vec.buffer[10:11, :] + vec.buffer[11:12, :]).astype(LOW)
    cotangent.whole()
    proj.wait()
    grad = dot_nt(cotangent.buffer[...], w_proj[...])
    dpool[...] = grad
    sum_pool.buffer[...] = fold(grad)
    low = grad.astype(LOW)
    bias_up.whole()
    up.wait()
    for k in range(8):
        lanes = slice(256 * k, 256 * k + 256)
        pre = dot(norm_ffn[...], w_up[:, lanes])
        rows = pre.shape[0] // 4
        for c in range(4):
            at = slice(rows * c, rows * c + rows)
            value = pre[at] + bias_up.buffer[0:1, lanes]
            below = 0.5 * (1.0 + lax.erf(value * (0.5**0.5)))
            hidden[at, lanes] = (value * below).astype(LOW)
            slope[at, lanes] = below + value * (jnp.exp(-0.5 * value * value) * 0.3989422804014327)
        total[256 * k : 256 * k + 256, :] = dot_tn(hidden[:, lanes], low)
    share(own_down, other_down, 0, 64, slice(0, 512))
    other_down.send()
    own_down.send()
    down.wait()
    for k in range(8):
        lanes = slice(256 * k, 256 * k + 256)
        dpre = slope[:, lanes] * dot_nt(low, w_down[lanes, :])
        sum_up.buffer[:, lanes] = fold(dpre)
        pre_low[:, lanes] = dpre.astype(LOW)
    dfirst.buffer[...] = dot_nt(pre_low[...], w_up[...])
    gains = jnp.zeros((8, 512), F32)
    shifts = jnp.zeros((8, 512), F32)
    for c in range(first.shape[0] // CH):
        at = slice(CH * c, CH * c + CH)
        grad = dfirst.buffer[at, :]
        unit, rate = norm_parts(first[at, :])
        gains += fold(grad * unit)
        shifts += fold(grad)
        dfirst.buffer[at, :] = norm_back(grad, unit, rate, vec.buffer[10:11, :]) + dpool[at, :]
    sum_gain.buffer[...] = gains
    sum_shift.buffer[...] = shifts
    dmixed.buffer[...] = dot_nt(dfirst.buffer[...].astype(LOW), w_out[...]).astype(LOW)
    for write in (dfirst, dmixed, sum_up, sum_gain, sum_shift, sum_pool):
        write.send()
    pooled = (first[...] + dot(hidden[...], w_down[...]) + vec.buffer[12:13, :]).astype(LOW)
    for k in range(4):
        lanes = slice(512 * k, 512 * k + 512)
        total[:512, :] = dot_tn(pooled, cotangent.buffer[:, lanes])
        share(own, other, 0, 16, lanes)
        total[512:1024, :] = dot_tn(norm_ffn[...], pre_low[:, lanes])
        share(own, other, 16, 16, lanes, SHARDS)
        output.buffer[:, lanes] = dot(pooled, w_proj[:, lanes]).astype(LOW)
    other.send()
    own.send()
    output.send()


def attend_back_kernel(me, _near, reads, writes, scratch):
    dmixed, query, probs, keyval, weights = reads
    dkeyval, dquery, query_part = writes
    dmixed.whole()
    query.whole()

    def attend_pair(pair, _):
        probs.part(pair)
        keyval.part(pair)
        for half in range(2):
            b = 2 * pair + half
            at, out = block(b, RB), block(b, EB)
            low = probs.buffer[at, :]
            part = low.astype(F32)
            dmix = spread_heads(dmixed.buffer[out, :])
            grad = dot_nt(keyval.buffer[at, 512:], dmix)
            shape = (EB, SLOTS, HEADS * EB)
            whole = jnp.sum((part * grad).reshape(shape), axis=1, keepdims=True)
            dscores = (part.reshape(shape) * (grad.reshape(shape) - whole)).reshape(RB, HEADS * EB).astype(LOW)
            dkeyval.buffer[at, 512:] = dot(low, dmix).astype(LOW)
            dkeyval.buffer[at, :512] = (dot(dscores, spread_heads(query.buffer[out, :])) * SCALE).astype(LOW)
            dquery.buffer[out, :] = (pick_heads(dot_tn(dscores, keyval.buffer[at, :512])) * SCALE).astype(LOW)
        dkeyval.part(pair)
        return 0

    lax.fori_loop(0, keyval.buffer.shape[0] // RB // 2, attend_pair, 0)
    dquery.send()
    query_part.buffer[...] = dot_nt(dquery.buffer[...], weights.whole()[...])
    query_part.send()


def grad_qkv_kernel(me, _near, reads, writes, scratch):
    mixed, dfirst, normed0, dquery, normed, dkeyval = reads
    own, other = writes
    grad_qkv, grad_out = scratch
    grad_out[...] = dot_tn(mixed.whole()[...], dfirst.whole()[...].astype(LOW))
    grad_qkv[:, :512] = dot_tn(normed0.whole()[...], dquery.whole()[...])
    normed.whole()
    dkeyval.whole()
    for k in range(4):
        lanes = slice(256 * k, 256 * k + 256)
        grad_qkv[:, 512 + 256 * k : 768 + 256 * k] = dot_tn(normed.buffer[...], dkeyval.buffer[:, lanes])
    for i in range(16):
        for k, half in ((i, own.buffer), (16 + i, other.buffer)):
            at = block(shard_at(me, k), 16)
            half[i, :, :1536] = grad_qkv[at, :].astype(half.dtype)
            half[i, :, 1536:2048] = grad_out[at, :].astype(half.dtype)
    other.send()
    own.send()


def norm_back_kernel(me, _near, reads, writes, scratch):
    vec, query_part, dfirst, marks, weights, dkeyval, embeds, *more = reads
    grad_embeds, *results = writes
    table, rows, work, lower, spread_query, spread_first, small, sums = scratch
    for read in (weights, query_part, dfirst, vec, marks):
        read.whole()
    table[...] = jnp.zeros_like(table)
    table[0:8, :] = vec.buffer[0:8, :].astype(LOW)
    sums[...] = jnp.zeros_like(sums)
    spread_query[...] = jnp.zeros_like(spread_query)
    spread_first[...] = jnp.zeros_like(spread_first)
    gain = vec.buffer[8:9, :]

    def norm_pair(pair, _):
        dkeyval.part(pair)
        embeds.part(pair)
        for half in range(2):
            b = 2 * pair + half
            at, out = block(b, RB), block(b, EB)
            put_first(spread_query.at[half], query_part.buffer[out, :])
            put_first(spread_first.at[half], dfirst.buffer[out, :])
            rows[half] = dot(marks.buffer[at, :], table[...])
            work[half] = dot_nt(dkeyval.buffer[at, :], weights.buffer[...])
            gains, shifts = jnp.zeros((8, 512), F32), jnp.zeros((8, 512), F32)
            for c in range(RB // CH):
                local = pl.ds(c * CH, CH)
                here = pl.ds(pl.multiple_of(b * RB + c * CH, CH), CH)
                grad = work[half, local, :] + get_tall(spread_query.at[half], c * CH, CH)
                unit, rate = norm_parts(embeds.buffer[here, :].astype(F32) + rows[half, local, :])
                gains += fold(grad * unit)
                shifts += fold(grad)
                value = norm_back(grad, unit, rate, gain) + get_tall(spread_first.at[half], c * CH, CH)
                high = value.astype(LOW)
                grad_embeds.buffer[here, :] = high
                lower[half, local, :] = (value - high.astype(F32)).astype(LOW)
            sums[half, 0:8, :] += gains
            sums[half, 8:16, :] += shifts
            mark = marks.buffer[at, :]
            sums[half, 16:144, :] += dot_tn(mark, grad_embeds.buffer[at, :]) + dot_tn(mark, lower[half])
        grad_embeds.part(pair)
        return 0

    lax.fori_loop(0, embeds.buffer.shape[0] // RB // 2, norm_pair, 0)
    if not more:
        results[0].buffer[...] = sums[0] + sums[1]
        results[0].send()
        return
    before, gain_ffn, shift_ffn, pool, up = more
    own, other = results
    sums[0] = sums[0] + sums[1] + before.whole()[...]
    small[...] = jnp.zeros_like(small)
    small[0:8, :] = sums[0, 16:24, :]
    folded = (sums[0, 0:8, :], sums[0, 8:16, :], gain_ffn.whole()[...], shift_ffn.whole()[...], pool.whole()[...])
    for i, value in enumerate(folded):
        small[8 + i : 9 + i, :] = jnp.sum(value, axis=0, keepdims=True)
    up_row = jnp.sum(up.whole()[...], axis=0, keepdims=True)
    row = iota((16, 128), 0)
    for r in range(SHARDS):
        tile = small[:, 128 * (r // 8) : 128 * (r // 8) + 128]
        tile = jnp.where(row == 13, up_row[:, 128 * (r // 2) : 128 * (r // 2) + 128], tile)
        rows[0, 8 * r : 8 * r + 8, 0:128] = tile[0:8]
        rows[0, 8 * r : 8 * r + 8, 128:256] = tile[8:16]
    for i in range(16):
        for k, half in ((i, own.buffer), (16 + i, other.buffer)):
            at = block(shard_at(me, k), 8)
            half[i] = jnp.concatenate([rows[0, at, 0:128], rows[0, at, 128:256]]).astype(half.dtype)
    other.send()
    own.send()


def on_device(
    embeds,
    piece_counts,
    group_ids,
    group_table,
    gain_attn,
    shift_attn,
    w_qkv,
    w_out,
    gain_ffn,
    shift_ffn,
    w_up,
    bias_up,
    w_down,
    bias_down,
    w_proj,
    cotangent,
):
    tuned = lax.axis_size("dp") == 32
    entries = embeds.shape[0]
    rows = entries * SLOTS
    flat = embeds.reshape(rows, 512)
    lane = jnp.arange(128, dtype=jnp.int32)
    slot = jnp.arange(SLOTS, dtype=jnp.int32)
    vectors = [gain_attn, shift_attn, gain_ffn, shift_ffn, bias_down]
    later = [embeds]
    if tuned:
        me = lax.axis_index("dp").astype(jnp.int32).reshape(1)
        parts = [(0, 0, w_qkv), (0, 1536, group_table), (13, 1536, bias_up[None, :])]
        parts += [(8 + i, 1536, vector[None, :]) for i, vector in enumerate(vectors)]
        shard = side_by_side(parts, (16, 1664))
        own = jnp.stack([shard, *spread(shard, LAYER[1], LAYER[2], LAYER[3])])
        third = side_by_side([(0, 0, w_down), (64, 0, w_out)], (80, 512))
        quad = [third, *spread(third, NEAR, FAR, ACROSS)]
        mine = [own, *spread(own, NEAR, FAR, ACROSS)]
        pieces = [mine + [send(part, CORE) for part in mine]]
        shard = side_by_side([(0, 0, w_proj), (16, 0, w_up)], (32, 2048))
        upper, lower = spread(shard, LAYER[2], LAYER[1])
        quad = jnp.stack([tie(third, own), *quad[1:]])
        own2 = jnp.stack([tie(shard, quad), lower, upper, send(tie(upper, own), LAYER[1])])
        pieces.append([own2, *spread(own2, NEAR, FAR, ACROSS)])
        pieces.append([quad, *spread(quad, LAYER[1], LAYER[2], LAYER[3])])
        later = [tie(own2, quad)]
        group_ids, piece_counts = tie(group_ids, piece_counts, own, every=True)[:2]
    else:
        me = None

        def whole(shard, axis=0):
            return lax.all_gather(shard, "dp", axis=axis, tiled=True)

        def cut(full):
            return [full[4 * i : 4 * i + 4] for i in range(8)]

        gathered = whole(jnp.concatenate([group_table, jnp.stack(vectors)]), 1)
        gathered = jnp.transpose(gathered.reshape(13, SHARDS, 16), (1, 0, 2))
        small = jnp.concatenate(
            [
                jnp.pad(gathered, ((0, 0), (0, 0), (0, 112))),
                jnp.pad(whole(bias_up).reshape(SHARDS, 1, 64), ((0, 0), (0, 2), (0, 64))),
            ],
            axis=1,
        )
        pieces = [
            cut(
                jnp.concatenate(
                    [whole(w_qkv).reshape(SHARDS, 16, 1536), small], axis=2
                )
            ),
            cut(
                jnp.concatenate(
                    [whole(w_proj).reshape(SHARDS, 16, 2048), whole(w_up).reshape(SHARDS, 16, 2048)], axis=1
                )
            ),
            cut(
                jnp.concatenate([whole(w_down).reshape(SHARDS, 64, 512), whole(w_out).reshape(SHARDS, 16, 512)], axis=1)
            ),
        ]
    marks = jnp.where(
        lane[None, None, :] < 8,
        group_ids[:, None, None] == lane[None, None, :],
        slot[None, :, None] < piece_counts[:, None, None],
    )
    marks = marks.astype(LOW).reshape(rows, 128)
    steps = rows // RB // 2
    low, wide = LOW, F32
    (qkv_all, vec, upbias, base0, normed, normed0, query, keyval, probs, mixed) = call(
        attend_kernel, 15,
        me,
        pieces[0],
        [(marks, 1, None), (flat, steps, None)],
        [
            ((512, 1664), low, 1), ((16, 512), wide, 1), ((8, 2048), wide, 1), ((entries, 512), wide, 1),
            ((rows, 512), low, steps), ((entries, 512), low, 1), ((entries, 512), low, 1), ((rows, 1024), low, steps),
            ((rows, HEADS * EB), low, steps), ((entries, 512), low, 1),
        ],
        scratch=[
            ((32, 16, 128), wide), ((128, 512), wide), ((2, RB, 512), wide), ((2, 4 * RB, 128), wide),
            ((2, 4 * RB, 128), wide), ((entries, 512), wide),
        ],
        after=later,
    )
    if tuned:
        mixed, *came = tie(mixed, *pieces[1], *pieces[2], every=True)
        came += [send(part, CORE) for part in came]
        pieces[1:] = [came[0:4] + came[8:12], came[4:8] + came[12:16]]
    (
        output, dfirst, dmixed, sum_up, sum_gain, sum_shift, sum_pool, own_down, other_down, own_pair, other_pair
    ) = call(
        ffn_kernel, 14,
        me,
        [*pieces[1], *pieces[2]],
        [
            (cotangent, 1, None), (base0, 1, None), (mixed, 1, None), (vec, 1, None), (upbias, 1, None),
        ],
        [
            ((entries, 2048), low, 1), ((entries, 512), wide, 1), ((entries, 512), low, 1), ((8, 2048), wide, 1),
            ((8, 512), wide, 1), ((8, 512), wide, 1), ((8, 512), wide, 1), ((16, 64, 512), low, 1),
            ((16, 64, 512), low, 1), ((16, 32, 2048), low, 1), ((16, 32, 2048), low, 1),
        ],
        [
            ((512, 2048), low), ((512, 2048), low), ((2048, 512), low), ((512, 512), low), ((entries, 512), wide),
            ((entries, 512), low), ((entries, 512), wide), ((entries, 2048), low),
            ((entries, 2048), wide), ((entries, 2048), low), ((2048, 512), wide),
        ],
    )
    if tuned:
        down = Sum(own_down, other_down)
        pair = Sum(own_pair, other_pair)
    (dkeyval, dquery, query_part) = call(
        attend_back_kernel, 8,
        me,
        [],
        [
            (dmixed, 1, None), (query, 1, None), (probs, steps, None), (keyval, steps, None),
            (qkv_all, 1, (0, 512, 0, 512)),
        ],
        [((rows, 1024), low, steps), ((entries, 512), low, 1), ((entries, 512), wide, 1)],
    )
    part = own_pair
    if tuned:
        query_part, down.core, pair.core = tie(query_part, down.core, pair.core, every=True)
        part = down.first()
        pair.core = tie(pair.core, part)
        part = pair.first()
    (own_last, other_last) = call(
        grad_qkv_kernel, 7,
        me,
        [],
        [
            (mixed, 1, None), (dfirst, 1, None), (normed0, 1, None), (dquery, 1, None), (normed, 1, None),
            (dkeyval, steps, None),
        ],
        [((16, 16, 2048), low, 1), ((16, 16, 2048), low, 1)],
        [((512, 1536), wide), ((512, 512), wide)],
        after=[part],
    )
    if tuned:
        last = Sum(own_last, other_last)

    def norm_back(start, count, more, stores, after, into):
        return call(
            norm_back_kernel, 6.6,
            me,
            [],
            [
                (vec, 1, None), (query_part, 1, (start // 8, count // 8, 0, 512)),
                (dfirst, 1, (start // 8, count // 8, 0, 512)), (marks, 1, (start, count, 0, 128)),
                (qkv_all, 1, (0, 512, 512, 1024)), (dkeyval, steps // 2, (start, count, 0, 1024)),
                (flat, steps // 2, (start, count, 0, 512)), *[(array, 1, None) for array in more],
            ],
            [((count, 512), low, steps // 2), *stores],
            [
                ((128, 512), low), ((2, RB, 512), wide), ((2, RB, 512), wide), ((2, RB, 512), low),
                ((2, 4 * RB, 128), wide), ((2, 4 * RB, 128), wide), ((16, 512), wide), ((2, 144, 512), wide),
            ],
            after=after,
            into=into,
        )

    half = rows // 2
    (grad_embeds, half_sums) = norm_back(0, half, [], [((144, 512), wide, 1)], [other_last], ((rows, 512), half))
    part = half_sums
    if tuned:
        half_sums, down.far, last.core = tie(half_sums, down.far, last.core, every=True)
        part = last.first()
        down.far = tie(down.far, part)
        part = down.second()
    (grad_embeds, own_small, other_small) = norm_back(
        half,
        half,
        [half_sums, sum_gain, sum_shift, sum_pool, sum_up],
        [((16, 16, 128), low, 1), ((16, 16, 128), low, 1)],
        [part],
        (grad_embeds, half),
    )
    if tuned:
        other_small, pair.far, down.near = tie(other_small, pair.far, down.near, every=True)
        little = Sum(own_small, other_small)
        part = pair.second()
        down.near = tie(down.near, part)
        part = down.third()
        little.core = tie(little.core, part)
        part = little.first()
        last.far, little.far = tie(last.far, little.far, part, every=True)[:2]
        near = [widen(sums.own[4:8], sums.core[4:8], sums.far[4:]).astype(LOW) for sums in (last, little)]
        near = side_by_side_lanes(near)
        came = send(near, NEAR)
        pair.near = tie(pair.near, near)
        part = pair.third()
        down.beside = tie(down.beside, part)
        part = down.fourth()
        came = tie(came, part)
        last.near, little.near = came[:, :, :2048], came[:, :, 2048:]
        near = side_by_side_lanes([sums.total(slice(1, 4, 2)).astype(LOW) for sums in (last, little)])
        came = send(near, LAYER[1])
        pair.beside = tie(pair.beside, near)
        part = pair.fourth()
        came = tie(came, part)
        last.beside, little.beside = came[:, :, :2048], came[:, :, 2048:]
        near = side_by_side_lanes([widen(sums.total(2), sums.beside[1]).astype(LOW) for sums in (last, little)])
        came = send(near, LAYER[2])
        down.beyond, pair.beyond = tie(down.beyond, pair.beyond, near, every=True)[:2]
        sum_down, pair = down.done(), pair.done()
        came = tie(came, sum_down, pair)
        last.beyond, little.beyond = came[:, :2048], came[:, 2048:]
        last_small = little.done()
        sum_proj, sum_up = pair[:16], pair[16:]
        sum_qkv, sum_out = [
            widen(last.total(0)[:, at], last.beside[0][:, at], last.beyond[:, at])
            for at in (slice(0, 1536), slice(1536, 2048))
        ]
        me = lax.axis_index("dp")
        sums = lax.dynamic_slice(last_small, (0, 16 * (me % 8)), (13, 16))
        sum_upbias = lax.dynamic_slice(last_small, (13, 64 * (me % 2)), (1, 64))[0]
    else:

        def share(own, other, axis=0):
            full = jnp.concatenate([own, other.astype(F32)])
            return lax.psum_scatter(full.reshape(-1, full.shape[-1]), "dp", scatter_dimension=0, tiled=True)

        sum_down = share(own_down, other_down)
        sum_proj = share(own_pair[:, :16], other_pair[:, :16])
        sum_up = share(own_pair[:, 16:], other_pair[:, 16:])
        sum_qkv = share(own_last[:, :, :1536], other_last[:, :, :1536])
        sum_out = share(own_last[:, :, 1536:], other_last[:, :, 1536:])
        small = jnp.concatenate([own_small, other_small.astype(F32)])
        vectors = jnp.concatenate([small[8 * k, :13] for k in range(4)], axis=1)
        sums = lax.psum_scatter(vectors, "dp", scatter_dimension=1, tiled=True)
        upbias = jnp.concatenate([small[2 * k, 13] for k in range(16)])
        sum_upbias = lax.psum_scatter(upbias, "dp", scatter_dimension=0, tiled=True)
    return (
        output,
        grad_embeds.reshape(entries, SLOTS, 512),
        sums[:8],
        sums[8],
        sums[9],
        sum_qkv,
        sum_out,
        sums[10],
        sums[11],
        sum_up,
        sum_upbias,
        sum_down,
        sums[12],
        sum_proj,
    )


def solution(mesh):
    placed = (
        P("dp", None, None),
        P("dp"),
        P("dp"),
        P(None, "dp"),
        P("dp"),
        P("dp"),
        P("dp", None),
        P("dp", None),
        P("dp"),
        P("dp"),
        P("dp", None),
        P("dp"),
        P("dp", None),
        P("dp"),
        P("dp", None),
        P("dp", None),
    )
    return jax.shard_map(
        on_device,
        mesh=mesh,
        in_specs=placed,
        out_specs=(
            P("dp", None),
            P("dp", None, None),
            P(None, "dp"),
            P("dp"),
            P("dp"),
            P("dp", None),
            P("dp", None),
            P("dp"),
            P("dp"),
            P("dp", None),
            P("dp"),
            P("dp", None),
            P("dp"),
            P("dp", None),
        ),
        check_vma=False,
    )
```

time: 203 us -> 176 us (0.87)
  waiting for transfers between devices: 57.5 us -> 33 us
  other arithmetic: 11.1 us -> 29.9 us
  local copies, waits for them, and re-layouts: 14.6 us -> 4.3 us
  starting transfers between devices: 57.3 us -> 49.8 us
  Pallas kernels: 60.5 us -> 56.9 us
    ppermute x48 -> x47, waiting for transfers between devices: 57.5 us -> 33 us  [send(): return lax.ppermute(value, 'dp', to)]
    convert_element_type x3 -> x15, other arithmetic: 2.63 us -> 17.8 us  [the longest x4 5.69 us: first(): part = widen(self.own[8:], self.core[8:]).astype(LOW)]
    ppermute x48 -> x47, starting transfers between devices: 57.3 us -> 49.8 us  [send(): return lax.ppermute(value, 'dp', to)]
    unnamed x35 -> x66, local copies, waits for them, and re-layouts: 7.13 us -> 1.59 us
    add x6 -> x9, other arithmetic: 3.95 us -> 8.35 us  [the longest x6 5.67 us: widen(): total = total + value.astype(F32)]
    pallas_call x4 -> x6, Pallas kernels: 60.5 us -> 56.9 us  [call(): pl.pallas_call(kernel, out_shape=[jax.ShapeDtypeStruct(s, t) for s, (_sha...]
    concatenate x2 -> x0, local copies, waits for them, and re-layouts: 2.29 us -> none  [the longest x1 1.44 us: on_device(): jnp.concatenate([group_table, jnp.stack([gain_attn, shift_attn, gain_ffn,...]
  transfers between devices with their start and end apart: 48 -> 47, of which waited for: 15 -> 16; matrix products, arithmetic and copies ran while one was open for 8% -> 14% of each run, Pallas kernels for 30% -> 20%
where the time goes in v2:
time: 176 us; the launch traced here: 175 us
  Pallas kernels  56.9 us (32%)
  starting transfers between devices  49.8 us (28%)
  waiting for transfers between devices  33 us (19%)
  other arithmetic  29.9 us (17%)
  local copies, waits for them, and re-layouts  4.3 us (2%)
    pallas_call x6, Pallas kernels, call(): pl.pallas_call(kernel, out_shape=[jax.ShapeDtypeStruct(s, t) for s, (_sha...  56.9 us
    ppermute x47, starting transfers between devices, send(): return lax.ppermute(value, 'dp', to)  49.8 us
    ppermute x47, waiting for transfers between devices, send(): return lax.ppermute(value, 'dp', to)  33 us
    convert_element_type x4, other arithmetic, first(): part = widen(self.own[8:], self.core[8:]).astype(LOW)  5.69 us
    add x6, other arithmetic, widen(): total = total + value.astype(F32)  5.67 us
  transfers between devices with their start and end apart: 47, of which 16 were waited for; matrix products, arithmetic and copies ran while one was open for 14% of the time, Pallas kernels for 20%

profile of v2, /device:TPU:0, one launch (start us, length us, event | category | flops | bytes accessed | tf_op | source)
XLA Modules:
  0.0 175.1 jit_solution(15928711778802942819)
XLA Ops:
  0.6 0.9 pad_add_fusion.2
  1.6 5.1 %collective-permute-start.2 = (bf16[16,1664]{1,0:T(8,128)(2,1)S(1)}, bf16[16,1664]{1,0:T(8,128)(2,1)S(1)}, u32[]{:S(2)}, u32[]{:S(2)}) collective-permute-start(bf16[16,1664]{1,0:T(8,128)(2,1)S(1)} %pad_add_fusion.2), channel_id=1, source_target_pairs={{0,24},{1,25},{2,26},{3,27},{4,28},{5,29},{6,30},{7,31},{8,16},{9,... | collective-permute-start | bytes 159752 | tf_op jit(solution)/shard_map/ppermute | solution.py:33
  7.3 0.9 pad_add_fusion.1
  8.2 1.6 collective-permute-start.10
  9.8 1.5 collective-permute-start.11
  11.4 0.9 fusion.8
  12.3 0.9 pad_add_fusion
  13.6 2.3 %collective-permute-start.14 = (bf16[32,2048]{1,0:T(8,128)(2,1)S(1)}, bf16[32,2048]{1,0:T(8,128)(2,1)S(1)}, u32[]{:S(2)}, u32[]{:S(2)}) collective-permute-start(bf16[32,2048]{1,0:T(8,128)(2,1)S(1)} %pad_add_fusion), channel_id=1, source_target_pairs={{0,16},{1,17},{2,18},{3,19},{4,20},{5,21},{6,22},{7,23},{8,24},{9,... | collective-permute-start | bytes 393224 | tf_op jit(solution)/shard_map/ppermute | solution.py:33
  15.9 2.0 %collective-permute-start.13 = (bf16[32,2048]{1,0:T(8,128)(2,1)S(1)}, bf16[32,2048]{1,0:T(8,128)(2,1)S(1)}, u32[]{:S(2)}, u32[]{:S(2)}) collective-permute-start(bf16[32,2048]{1,0:T(8,128)(2,1)S(1)} %pad_add_fusion), channel_id=1, source_target_pairs={{0,8},{1,9},{2,10},{3,11},{4,12},{5,13},{6,14},{7,15},{8,0},{9,1},... | collective-permute-start | bytes 393224 | tf_op jit(solution)/shard_map/ppermute | solution.py:33
  18.0 0.8 iota_compare_fusion
  18.8 0.8 iota_compare_fusion.1
  19.7 1.6 collective-permute-start.3
  21.2 1.5 collective-permute-start.4
  23.4 2.0 %collective-permute-start.15 = (bf16[32,2048]{1,0:T(8,128)(2,1)S(1)}, bf16[32,2048]{1,0:T(8,128)(2,1)S(1)}, u32[]{:S(2)}, u32[]{:S(2)}) collective-permute-start(bf16[32,2048]{1,0:T(8,128)(2,1)S(1)} %collective-permute-done.14), channel_id=1, source_target_pairs={{0,8},{1,9},{2,10},{3,11},{4,12},{5,13},{6,14},{7,15},{8,0},{9,1},... | collective-permute-start | bytes 393224 | tf_op jit(solution)/shard_map/ppermute | solution.py:33
  25.4 1.1 fusion.refs_8_.refs_3_
  26.5 6.0 %collective-permute-done.15 = bf16[32,2048]{1,0:T(8,128)(2,1)S(1)} collective-permute-done((bf16[32,2048]{1,0:T(8,128)(2,1)S(1)}, bf16[32,2048]{1,0:T(8,128)(2,1)S(1)}, u32[]{:S(2)}, u32[]{:S(2)}) %collective-permute-start.15) | collective-permute-done | bytes 131104 | tf_op jit(solution)/shard_map/ppermute | solution.py:33
  34.6 2.1 %collective-permute-start.21 = (bf16[4,80,512]{2,1,0:T(8,128)(2,1)S(1)}, bf16[4,80,512]{2,1,0:T(8,128)(2,1)S(1)}, u32[]{:S(2)}, u32[]{:S(2)}) collective-permute-start(bf16[4,80,512]{2,1,0:T(8,128)(2,1)S(1)} %pad_maximum_fusion.1.refs_8_), channel_id=1, source_target_pairs={{0,24},{1,25},{2,26},{3,27},{4,28},{5,29},{6,30},{7,31},{8,16},{9,... | collective-permute-start | bytes 983048 | tf_op jit(solution)/shard_map/ppermute | solution.py:33
  36.7 1.5 collective-permute-start.16
  38.2 1.5 collective-permute-start.17
  40.4 14.8 %shard_map.263 = (bf16[512,1664]{1,0:T(8,128)(2,1)}, f32[16,512]{1,0:T(8,128)}, f32[8,2048]{1,0:T(8,128)}, f32[256,512]{1,0:T(8,128)}, bf16[2048,512]{1,0:T(8,12...) custom-call(s32[1]{0:T(128)} %bitcast.me_ref, ...), custom_call_target="tpu_custom_call" | custom-call | flops 16499999744 | bytes 1000 | tf_op jit(solution)/shard_map/pallas_call | solution.py:265
  55.2 3.3 %collective-permute-done.20.refs_10_ = bf16[4,80,512]{2,1,0:T(8,128)(2,1)S(1)} collective-permute-done((bf16[4,80,512]{2,1,0:T(8,128)(2,1)S(1)}, bf16[4,80,512]{2,1,0:T(8,128)(2,1)S(1)}, u32[]{:S(2)}, u32[]{:S(2)}) %collective-permute-start.20) | collective-permute-done | bytes 327712 | tf_op jit(solution)/shard_map/ppermute | solution.py:33
  58.6 4.0 %collective-permute-done.18.refs_3_ = bf16[4,32,2048]{2,1,0:T(8,128)(2,1)S(1)} collective-permute-done((bf16[4,32,2048]{2,1,0:T(8,128)(2,1)S(1)}, bf16[4,32,2048]{2,1,0:T(8,128)(2,1)S(1)}, u32[]{:S(2)}, u32[]{:S(2)}) %collective-permute-start.18) | collective-permute-done | bytes 524320 | tf_op jit(solution)/shard_map/ppermute | solution.py:33
  64.8 0.8 collective-permute-done.28.refs_14_
  65.7 2.9 %collective-permute-done.29.refs_15_ = bf16[4,80,512]{2,1,0:T(8,128)(2,1)S(1)} collective-permute-done((bf16[4,80,512]{2,1,0:T(8,128)(2,1)S(1)}, bf16[4,80,512]{2,1,0:T(8,128)(2,1)S(1)}, u32[]{:S(2)}, u32[]{:S(2)}) %collective-permute-start.29) | collective-permute-done | bytes 327712 | tf_op jit(solution)/shard_map/ppermute | solution.py:33
  70.0 13.8 %shard_map.264 = (bf16[256,2048]{1,0:T(8,128)(2,1)}, f32[256,512]{1,0:T(8,128)}, bf16[256,512]{1,0:T(8,128)(2,1)}, f32[8,2048]{1,0:T(8,128)}, f32[8,512]{1,0:T(8...) custom-call(s32[1]{0:T(128)} %bitcast.me_ref, ...), custom_call_target="tpu_custom_call" | custom-call | flops 15399999488 | bytes 1000 | tf_op jit(solution)/shard_map/pallas_call | solution.py:265
  84.4 7.8 %shard_map.265 = (bf16[2048,1024]{1,0:T(8,128)(2,1)}, bf16[256,512]{1,0:T(8,128)(2,1)}, f32[256,512]{1,0:T(8,128)}) custom-call(s32[1]{0:T(128)} %bitcast.me_ref, bf16[256,512]{1,0:T(8,128)(2,1)} %get-tuple-element.103.refs_0_, bf16[256,512]{1,0:T(8,128)(2,1)} %get-tuple-element.104.refs_1_, bf16[2048,256]{1,0:T(8,128)(2,1)} %get-tuple-element.105.refs_2_, ...), custom_call_target="tpu_custom_call" | custom-call | flops 8800000000 | bytes 1000 | tf_op jit(solution)/shard_map/pallas_call | solution.py:265
  92.3 1.6 add_convert_fusion.3
  93.8 1.4 add_convert_fusion.refs_6_
  95.2 7.2 %shard_map.266 = (bf16[16,16,2048]{2,1,0:T(8,128)(2,1)}, bf16[16,16,2048]{2,1,0:T(8,128)(2,1)}) custom-call(s32[1]{0:T(128)} %bitcast.me_ref, bf16[256,512]{1,0:T(8,128)(2,1)} %get-tuple-element.99.refs_18_.refs_0_, f32[256,512]{1,0:T(8,128)} %get-tuple-element.112.refs_1_.refs_2_, bf16[256,512]{1,0:T(8,128)(2,1)} %get-tuple-element.114.refs_2_, ...), custom_call_target="tpu_custom_call" | custom-call | flops 7699999744 | bytes 1000 | tf_op jit(solution)/shard_map/pallas_call | solution.py:265
  102.7 1.5 collective-permute-start.32
  104.7 6.6 %shard_map.267 = (bf16[2048,512]{1,0:T(8,128)(2,1)}, f32[144,512]{1,0:T(8,128)}) custom-call(s32[1]{0:T(128)} %bitcast.me_ref, f32[16,512]{1,0:T(8,128)} %get-tuple-element.100.refs_19_.refs_0_, f32[256,512]{1,0:T(8,128)} %get-tuple-element.111.refs_1_, f32[256,512]{1,0:T(8,128)} %get-tuple-element.112.refs_1_.refs_2_, ...), custom_call_target="tpu_custom_call" | custom-call | flops 7260000256 | bytes 1000 | tf_op jit(solution)/shard_map/pallas_call | solution.py:265
  112.0 2.1 %add_convert_fusion.2 = bf16[8,16,2048]{2,1,0:T(8,128)(2,1)} fusion(bf16[16,16,2048]{2,1,0:T(8,128)(2,1)} %collective-permute-done.33, bf16[16,16,2048]{2,1,0:T(8,128)(2,1)} %get-tuple-element.130), kind=kLoop, calls=%fused_computation.2 | loop fusion | flops 1048576 | bytes 1572864 | tf_op jit(solution)/shard_map/convert_element_type | solution.py:71
  114.1 1.5 collective-permute-start.37
  115.6 1.2 add_convert_fusion.6.refs_12_
  116.8 1.6 collective-permute-start.35
  118.4 6.7 %shard_map.268 = (bf16[2048,512]{1,0:T(8,128)(2,1)}, bf16[16,16,128]{2,1,0:T(8,128)(2,1)}, bf16[16,16,128]{2,1,0:T(8,128)(2,1)}) custom-call(s32[1]{0:T(128)} %bitcast.me_ref, f32[16,512]{1,0:T(8,128)} %get-tuple-element.100.refs_19_.refs_0_, f32[256,512]{1,0:T(8,128)} %get-tuple-element.111.refs_1_, ...), custom_call_target="tpu_custom_call", output_to_operand_aliasing={{0}: (14, {})} | custom-call | flops 7260000256 | bytes 1000 | tf_op jit(solution)/shard_map/pallas_call | solution.py:265
  125.1 0.9 collective-permute-done.34
  126.1 2.2 %add_convert_fusion.1 = bf16[4,32,2048]{2,1,0:T(8,128)(2,1)} fusion(bf16[8,32,2048]{2,1,0:T(8,128)(2,1)} %collective-permute-done.34, bf16[16,32,2048]{2,1,0:T(8,128)(2,1)S(1)} %collective-permute-done.31, bf16[16,32,2048]{2,1,0:T(8,128)(2,1)S(1)} %copy-done), kind=kLoop, calls=%fused_computation.1 | loop fusion | flops 1572864 | bytes 2097152 | tf_op jit(solution)/shard_map/convert_element_type | solution.py:76
  128.3 1.1 add_convert_fusion.9
  130.2 1.4 collective-permute-start.38
  131.6 1.5 collective-permute-start.41
  133.1 3.6 %collective-permute-start.40 = (bf16[2,64,512]{2,1,0:T(8,128)(2,1)S(1)}, bf16[2,64,512]{2,1,0:T(8,128)(2,1)S(1)}, u32[]{:S(2)}, u32[]{:S(2)}) collective-permute-start(bf16[2,64,512]{2,1,0:T(8,128)(2,1)S(1)} %add_convert_fusion.9), channel_id=1, source_target_pairs={{0,8},{1,9},{2,10},{3,11},{4,12},{5,13},{6,14},{7,15},{8,0},{9,1},... | collective-permute-start | bytes 393224 | tf_op jit(solution)/shard_map/ppermute | solution.py:33
  136.8 1.1 add_convert_fusion.5
  137.9 0.8 add_convert_fusion.13
  139.3 1.7 collective-permute-done.41
  141.0 1.2 add_convert_fusion.4
  142.2 3.7 %collective-permute-start.43 = (bf16[2,32,2048]{2,1,0:T(8,128)(2,1)S(1)}, bf16[2,32,2048]{2,1,0:T(8,128)(2,1)S(1)}, u32[]{:S(2)}, u32[]{:S(2)}) collective-permute-start(bf16[2,32,2048]{2,1,0:T(8,128)(2,1)S(1)} %add_convert_fusion.4), channel_id=1, source_target_pairs={{0,8},{1,9},{2,10},{3,11},{4,12},{5,13},{6,14},{7,15},{8,0},{9,1},... | collective-permute-start | bytes 786440 | tf_op jit(solution)/shard_map/ppermute | solution.py:33
  145.9 0.9 fusion.3
  147.0 1.0 add_convert_fusion.8
  148.1 0.7 add_convert_fusion.14
  148.8 2.1 %collective-permute-start.42 = (bf16[2,16,2176]{2,1,0:T(8,128)(2,1)S(1)}, bf16[2,16,2176]{2,1,0:T(8,128)(2,1)S(1)}, u32[]{:S(2)}, u32[]{:S(2)}) collective-permute-start(bf16[2,16,2176]{2,1,0:T(8,128)(2,1)S(1)} %pad_maximum_fusion.4), channel_id=1, source_target_pairs={{0,8},{1,9},{2,10},{3,11},{4,12},{5,13},{6,14},{7,15},{8,0},{9,1},... | collective-permute-start | bytes 417800 | tf_op jit(solution)/shard_map/ppermute | solution.py:33
  150.9 3.6 %collective-permute-done.43 = bf16[2,32,2048]{2,1,0:T(8,128)(2,1)S(1)} collective-permute-done((bf16[2,32,2048]{2,1,0:T(8,128)(2,1)S(1)}, bf16[2,32,2048]{2,1,0:T(8,128)(2,1)S(1)}, u32[]{:S(2)}, u32[]{:S(2)}) %collective-permute-start.43) | collective-permute-done | bytes 262176 | tf_op jit(solution)/shard_map/ppermute | solution.py:33
  154.5 1.1 fusion.1
  156.1 1.0 add_bitcast_fusion
  157.1 0.7 fusion.6
  157.8 1.8 %collective-permute-start.46 = (bf16[32,2048]{1,0:T(8,128)(2,1)S(1)}, bf16[32,2048]{1,0:T(8,128)(2,1)S(1)}, u32[]{:S(2)}, u32[]{:S(2)}) collective-permute-start(bf16[32,2048]{1,0:T(8,128)(2,1)S(1)} %fusion.1), channel_id=1, source_target_pairs={{0,16},{1,17},{2,18},{3,19},{4,20},{5,21},{6,22},{7,23},{8,24},{9,... | collective-permute-start | bytes 393224 | tf_op jit(solution)/shard_map/ppermute | solution.py:33
  159.6 1.2 collective-permute-start.44
  160.8 7.1 %collective-permute-done.46 = bf16[32,2048]{1,0:T(8,128)(2,1)S(1)} collective-permute-done((bf16[32,2048]{1,0:T(8,128)(2,1)S(1)}, bf16[32,2048]{1,0:T(8,128)(2,1)S(1)}, u32[]{:S(2)}, u32[]{:S(2)}) %collective-permute-start.46) | collective-permute-done | bytes 131104 | tf_op jit(solution)/shard_map/ppermute | solution.py:33
  167.9 1.1 bitcast_add_fusion
  169.0 0.7 fusion.7
  169.7 1.6 bitcast_add_fusion.1
  171.3 0.7 bitcast_add_fusion.2
  172.6 0.7 fusion.2
  173.9 0.7 constant_dynamic-slice_fusion
  (145 shorter events, 14.3 us)
Async XLA Ops:
  1.6 11.6 %collective-permute-start.2 = (bf16[16,1664]{1,0:T(8,128)(2,1)S(1)}, bf16[16,1664]{1,0:T(8,128)(2,1)S(1)}, u32[]{:S(2)}, u32[]{:S(2)}) collective-permute-start(bf16[16,1664]{1,0:T(8,128)(2,1)S(1)} %pad_add_fusion.2), channel_id=1, source_target_pairs={{0,24},{1,25},{2,26},{3,27},{4,28},{5,29},{6,30},{7,31},{8,16},{9,... | collective-permute-start | bytes 159752 | tf_op jit(solution)/shard_map/ppermute | solution.py:33
  6.7 6.9 %collective-permute-start = (bf16[16,1664]{1,0:T(8,128)(2,1)S(1)}, bf16[16,1664]{1,0:T(8,128)(2,1)S(1)}, u32[]{:S(2)}, u32[]{:S(2)}) collective-permute-start(bf16[16,1664]{1,0:T(8,128)(2,1)S(1)} %pad_add_fusion.2), channel_id=1, source_target_pairs={{0,8},{1,9},{2,10},{3,11},{4,12},{5,13},{6,14},{7,15},{8,0},{9,1},... | collective-permute-start | bytes 159752 | tf_op jit(solution)/shard_map/ppermute | solution.py:33
  6.7 9.2 %collective-permute-start.1 = (bf16[16,1664]{1,0:T(8,128)(2,1)S(1)}, bf16[16,1664]{1,0:T(8,128)(2,1)S(1)}, u32[]{:S(2)}, u32[]{:S(2)}) collective-permute-start(bf16[16,1664]{1,0:T(8,128)(2,1)S(1)} %pad_add_fusion.2), channel_id=1, source_target_pairs={{0,16},{1,17},{2,18},{3,19},{4,20},{5,21},{6,22},{7,23},{8,24},{9,... | collective-permute-start | bytes 159752 | tf_op jit(solution)/shard_map/ppermute | solution.py:33
  8.2 11.5 %collective-permute-start.10 = (bf16[80,512]{1,0:T(8,128)(2,1)S(1)}, bf16[80,512]{1,0:T(8,128)(2,1)S(1)}, u32[]{:S(2)}, u32[]{:S(2)}) collective-permute-start(bf16[80,512]{1,0:T(8,128)(2,1)S(1)} %pad_add_fusion.1), channel_id=1, source_target_pairs={{0,2},{1,5},{2,0},{3,7},{4,6},{5,1},{6,4},{7,3},{8,10},{9,13},{10,... | collective-permute-start | bytes 245768 | tf_op jit(solution)/shard_map/ppermute | solution.py:33
  9.8 11.4 %collective-permute-start.11 = (bf16[80,512]{1,0:T(8,128)(2,1)S(1)}, bf16[80,512]{1,0:T(8,128)(2,1)S(1)}, u32[]{:S(2)}, u32[]{:S(2)}) collective-permute-start(bf16[80,512]{1,0:T(8,128)(2,1)S(1)} %pad_add_fusion.1), channel_id=1, source_target_pairs={{0,4},{1,3},{2,6},{3,1},{4,0},{5,7},{6,2},{7,5},{8,12},{9,11},{10,... | collective-permute-start | bytes 245768 | tf_op jit(solution)/shard_map/ppermute | solution.py:33
  13.2 9.6 %collective-permute-start.12 = (bf16[80,512]{1,0:T(8,128)(2,1)S(1)}, bf16[80,512]{1,0:T(8,128)(2,1)S(1)}, u32[]{:S(2)}, u32[]{:S(2)}) collective-permute-start(bf16[80,512]{1,0:T(8,128)(2,1)S(1)} %pad_add_fusion.1), channel_id=1, source_target_pairs={{0,6},{1,7},{2,4},{3,5},{4,2},{5,3},{6,0},{7,1},{8,14},{9,15},{10,... | collective-permute-start | bytes 245768 | tf_op jit(solution)/shard_map/ppermute | solution.py:33
  13.6 9.7 %collective-permute-start.14 = (bf16[32,2048]{1,0:T(8,128)(2,1)S(1)}, bf16[32,2048]{1,0:T(8,128)(2,1)S(1)}, u32[]{:S(2)}, u32[]{:S(2)}) collective-permute-start(bf16[32,2048]{1,0:T(8,128)(2,1)S(1)} %pad_add_fusion), channel_id=1, source_target_pairs={{0,16},{1,17},{2,18},{3,19},{4,20},{5,21},{6,22},{7,23},{8,24},{9,... | collective-permute-start | bytes 393224 | tf_op jit(solution)/shard_map/ppermute | solution.py:33
  15.9 7.5 %collective-permute-start.13 = (bf16[32,2048]{1,0:T(8,128)(2,1)S(1)}, bf16[32,2048]{1,0:T(8,128)(2,1)S(1)}, u32[]{:S(2)}, u32[]{:S(2)}) collective-permute-start(bf16[32,2048]{1,0:T(8,128)(2,1)S(1)} %pad_add_fusion), channel_id=1, source_target_pairs={{0,8},{1,9},{2,10},{3,11},{4,12},{5,13},{6,14},{7,15},{8,0},{9,1},... | collective-permute-start | bytes 393224 | tf_op jit(solution)/shard_map/ppermute | solution.py:33
  17.9 22.2 %copy-start.8 = (bf16[4,16,1664]{2,1,0:T(8,128)(2,1)}, bf16[4,16,1664]{2,1,0:T(8,128)(2,1)S(1)}, u32[]{:S(2)}) copy-start(bf16[4,16,1664]{2,1,0:T(8,128)(2,1)S(1)} %pad_maximum_fusion.3.refs_0_) | copy-start | bytes 638980
  19.7 12.9 %collective-permute-start.3 = (bf16[4,16,1664]{2,1,0:T(8,128)(2,1)S(1)}, bf16[4,16,1664]{2,1,0:T(8,128)(2,1)S(1)}, u32[]{:S(2)}, u32[]{:S(2)}) collective-permute-start(bf16[4,16,1664]{2,1,0:T(8,128)(2,1)S(1)} %pad_maximum_fusion.3.refs_0_), channel_id=1, source_target_pairs={{0,2},{1,5},{2,0},{3,7},{4,6},{5,1},{6,4},{7,3},{8,10},{9,13},{10,... | collective-permute-start | bytes 638984 | tf_op jit(solution)/shard_map/ppermute | solution.py:33
  21.2 11.8 %collective-permute-start.4 = (bf16[4,16,1664]{2,1,0:T(8,128)(2,1)S(1)}, bf16[4,16,1664]{2,1,0:T(8,128)(2,1)S(1)}, u32[]{:S(2)}, u32[]{:S(2)}) collective-permute-start(bf16[4,16,1664]{2,1,0:T(8,128)(2,1)S(1)} %pad_maximum_fusion.3.refs_0_), channel_id=1, source_target_pairs={{0,4},{1,3},{2,6},{3,1},{4,0},{5,7},{6,2},{7,5},{8,12},{9,11},{10,... | collective-permute-start | bytes 638984 | tf_op jit(solution)/shard_map/ppermute | solution.py:33
  22.8 10.4 %collective-permute-start.5 = (bf16[4,16,1664]{2,1,0:T(8,128)(2,1)S(1)}, bf16[4,16,1664]{2,1,0:T(8,128)(2,1)S(1)}, u32[]{:S(2)}, u32[]{:S(2)}) collective-permute-start(bf16[4,16,1664]{2,1,0:T(8,128)(2,1)S(1)} %pad_maximum_fusion.3.refs_0_), channel_id=1, source_target_pairs={{0,6},{1,7},{2,4},{3,5},{4,2},{5,3},{6,0},{7,1},{8,14},{9,15},{10,... | collective-permute-start | bytes 638984 | tf_op jit(solution)/shard_map/ppermute | solution.py:33
  23.3 39.2 %copy-start.6 = (bf16[4,80,512]{2,1,0:T(8,128)(2,1)}, bf16[4,80,512]{2,1,0:T(8,128)(2,1)S(1)}, u32[]{:S(2)}) copy-start(bf16[4,80,512]{2,1,0:T(8,128)(2,1)S(1)} %pad_maximum_fusion.1.refs_8_) | copy-start | bytes 983044
  23.3 11.3 %collective-permute-start.19 = (bf16[4,80,512]{2,1,0:T(8,128)(2,1)S(1)}, bf16[4,80,512]{2,1,0:T(8,128)(2,1)S(1)}, u32[]{:S(2)}, u32[]{:S(2)}) collective-permute-start(bf16[4,80,512]{2,1,0:T(8,128)(2,1)S(1)} %pad_maximum_fusion.1.refs_8_), channel_id=1, source_target_pairs={{0,8},{1,9},{2,10},{3,11},{4,12},{5,13},{6,14},{7,15},{8,0},{9,1},... | collective-permute-start | bytes 983048 | tf_op jit(solution)/shard_map/ppermute | solution.py:33
  23.4 9.2 %collective-permute-start.15 = (bf16[32,2048]{1,0:T(8,128)(2,1)S(1)}, bf16[32,2048]{1,0:T(8,128)(2,1)S(1)}, u32[]{:S(2)}, u32[]{:S(2)}) collective-permute-start(bf16[32,2048]{1,0:T(8,128)(2,1)S(1)} %collective-permute-done.14), channel_id=1, source_target_pairs={{0,8},{1,9},{2,10},{3,11},{4,12},{5,13},{6,14},{7,15},{8,0},{9,1},... | collective-permute-start | bytes 393224 | tf_op jit(solution)/shard_map/ppermute | solution.py:33
  32.6 1.5 collective-permute-start.6
  32.6 7.6 %copy-start.25 = (bf16[4,16,1664]{2,1,0:T(8,128)(2,1)}, bf16[4,16,1664]{2,1,0:T(8,128)(2,1)S(1)}, u32[]{:S(2)}) copy-start(bf16[4,16,1664]{2,1,0:T(8,128)(2,1)S(1)} %collective-permute-done.3.refs_1_) | copy-start | bytes 638980
  32.6 4.1 %collective-permute-start.7 = (bf16[4,16,1664]{2,1,0:T(8,128)(2,1)S(1)}, bf16[4,16,1664]{2,1,0:T(8,128)(2,1)S(1)}, u32[]{:S(2)}, u32[]{:S(2)}) collective-permute-start(bf16[4,16,1664]{2,1,0:T(8,128)(2,1)S(1)} %collective-permute-done.3.refs_1_), channel_id=1, source_target_pairs={{0,1},{1,0},{2,3},{3,2},{4,5},{5,4},{6,7},{7,6},{8,9},{9,8},{10,11... | collective-permute-start | bytes 638984 | tf_op jit(solution)/shard_map/ppermute | solution.py:33
  33.1 7.1 %copy-start.26 = (bf16[4,16,1664]{2,1,0:T(8,128)(2,1)}, bf16[4,16,1664]{2,1,0:T(8,128)(2,1)S(1)}, u32[]{:S(2)}) copy-start(bf16[4,16,1664]{2,1,0:T(8,128)(2,1)S(1)} %collective-permute-done.4.refs_2_) | copy-start | bytes 638980
  33.1 5.1 %collective-permute-start.8 = (bf16[4,16,1664]{2,1,0:T(8,128)(2,1)S(1)}, bf16[4,16,1664]{2,1,0:T(8,128)(2,1)S(1)}, u32[]{:S(2)}, u32[]{:S(2)}) collective-permute-start(bf16[4,16,1664]{2,1,0:T(8,128)(2,1)S(1)} %collective-permute-done.4.refs_2_), channel_id=1, source_target_pairs={{0,1},{1,0},{2,3},{3,2},{4,5},{5,4},{6,7},{7,6},{8,9},{9,8},{10,11... | collective-permute-start | bytes 638984 | tf_op jit(solution)/shard_map/ppermute | solution.py:33
  33.2 7.0 %copy-start.27 = (bf16[4,16,1664]{2,1,0:T(8,128)(2,1)}, bf16[4,16,1664]{2,1,0:T(8,128)(2,1)S(1)}, u32[]{:S(2)}) copy-start(bf16[4,16,1664]{2,1,0:T(8,128)(2,1)S(1)} %collective-permute-done.5.refs_3_) | copy-start | bytes 638980
  33.2 6.5 %collective-permute-start.9 = (bf16[4,16,1664]{2,1,0:T(8,128)(2,1)S(1)}, bf16[4,16,1664]{2,1,0:T(8,128)(2,1)S(1)}, u32[]{:S(2)}, u32[]{:S(2)}) collective-permute-start(bf16[4,16,1664]{2,1,0:T(8,128)(2,1)S(1)} %collective-permute-done.5.refs_3_), channel_id=1, source_target_pairs={{0,1},{1,0},{2,3},{3,2},{4,5},{5,4},{6,7},{7,6},{8,9},{9,8},{10,11... | collective-permute-start | bytes 638984 | tf_op jit(solution)/shard_map/ppermute | solution.py:33
  33.7 6.5 %copy-start.5 = (bf16[4,32,2048]{2,1,0:T(8,128)(2,1)}, bf16[4,32,2048]{2,1,0:T(8,128)(2,1)S(1)}, u32[]{:S(2)}) copy-start(bf16[4,32,2048]{2,1,0:T(8,128)(2,1)S(1)} %pad_maximum_fusion.refs_10_.refs_0_) | copy-start | bytes 1572868
  34.0 6.2 %copy-start.28 = (bf16[4,16,1664]{2,1,0:T(8,128)(2,1)}, bf16[4,16,1664]{2,1,0:T(8,128)(2,1)S(1)}, u32[]{:S(2)}) copy-start(bf16[4,16,1664]{2,1,0:T(8,128)(2,1)S(1)} %collective-permute-done.6.refs_4_) | copy-start | bytes 638980
  34.0 24.5 %collective-permute-start.20 = (bf16[4,80,512]{2,1,0:T(8,128)(2,1)S(1)}, bf16[4,80,512]{2,1,0:T(8,128)(2,1)S(1)}, u32[]{:S(2)}, u32[]{:S(2)}) collective-permute-start(bf16[4,80,512]{2,1,0:T(8,128)(2,1)S(1)} %pad_maximum_fusion.1.refs_8_), channel_id=1, source_target_pairs={{0,16},{1,17},{2,18},{3,19},{4,20},{5,21},{6,22},{7,23},{8,24},{9,... | collective-permute-start | bytes 983048 | tf_op jit(solution)/shard_map/ppermute | solution.py:33
  34.6 27.9 %copy-start.18 = (bf16[4,80,512]{2,1,0:T(8,128)(2,1)}, bf16[4,80,512]{2,1,0:T(8,128)(2,1)S(1)}, u32[]{:S(2)}) copy-start(bf16[4,80,512]{2,1,0:T(8,128)(2,1)S(1)} %collective-permute-done.19.refs_9_) | copy-start | bytes 983044
  34.6 23.9 %collective-permute-start.21 = (bf16[4,80,512]{2,1,0:T(8,128)(2,1)S(1)}, bf16[4,80,512]{2,1,0:T(8,128)(2,1)S(1)}, u32[]{:S(2)}, u32[]{:S(2)}) collective-permute-start(bf16[4,80,512]{2,1,0:T(8,128)(2,1)S(1)} %pad_maximum_fusion.1.refs_8_), channel_id=1, source_target_pairs={{0,24},{1,25},{2,26},{3,27},{4,28},{5,29},{6,30},{7,31},{8,16},{9,... | collective-permute-start | bytes 983048 | tf_op jit(solution)/shard_map/ppermute | solution.py:33
  36.7 21.8 %collective-permute-start.16 = (bf16[4,32,2048]{2,1,0:T(8,128)(2,1)S(1)}, bf16[4,32,2048]{2,1,0:T(8,128)(2,1)S(1)}, u32[]{:S(2)}, u32[]{:S(2)}) collective-permute-start(bf16[4,32,2048]{2,1,0:T(8,128)(2,1)S(1)} %pad_maximum_fusion.refs_10_.refs_0_), channel_id=1, source_target_pairs={{0,2},{1,5},{2,0},{3,7},{4,6},{5,1},{6,4},{7,3},{8,10},{9,13},{10,... | collective-permute-start | bytes 1572872 | tf_op jit(solution)/shard_map/ppermute | solution.py:33
  38.2 20.4 %collective-permute-start.17 = (bf16[4,32,2048]{2,1,0:T(8,128)(2,1)S(1)}, bf16[4,32,2048]{2,1,0:T(8,128)(2,1)S(1)}, u32[]{:S(2)}, u32[]{:S(2)}) collective-permute-start(bf16[4,32,2048]{2,1,0:T(8,128)(2,1)S(1)} %pad_maximum_fusion.refs_10_.refs_0_), channel_id=1, source_target_pairs={{0,4},{1,3},{2,6},{3,1},{4,0},{5,7},{6,2},{7,5},{8,12},{9,11},{10,... | collective-permute-start | bytes 1572872 | tf_op jit(solution)/shard_map/ppermute | solution.py:33
  39.7 22.8 %collective-permute-start.18 = (bf16[4,32,2048]{2,1,0:T(8,128)(2,1)S(1)}, bf16[4,32,2048]{2,1,0:T(8,128)(2,1)S(1)}, u32[]{:S(2)}, u32[]{:S(2)}) collective-permute-start(bf16[4,32,2048]{2,1,0:T(8,128)(2,1)S(1)} %pad_maximum_fusion.refs_10_.refs_0_), channel_id=1, source_target_pairs={{0,6},{1,7},{2,4},{3,5},{4,2},{5,3},{6,0},{7,1},{8,14},{9,15},{10,... | collective-permute-start | bytes 1572872 | tf_op jit(solution)/shard_map/ppermute | solution.py:33
  58.5 10.1 %copy-start.19 = (bf16[4,80,512]{2,1,0:T(8,128)(2,1)}, bf16[4,80,512]{2,1,0:T(8,128)(2,1)S(1)}, u32[]{:S(2)}) copy-start(bf16[4,80,512]{2,1,0:T(8,128)(2,1)S(1)} %collective-permute-done.20.refs_10_) | copy-start | bytes 983044
  58.5 10.1 %copy-start.20 = (bf16[4,80,512]{2,1,0:T(8,128)(2,1)}, bf16[4,80,512]{2,1,0:T(8,128)(2,1)S(1)}, u32[]{:S(2)}) copy-start(bf16[4,80,512]{2,1,0:T(8,128)(2,1)S(1)} %collective-permute-done.21.refs_11_) | copy-start | bytes 983044
  58.5 10.1 %copy-start.11 = (bf16[4,32,2048]{2,1,0:T(8,128)(2,1)}, bf16[4,32,2048]{2,1,0:T(8,128)(2,1)S(1)}, u32[]{:S(2)}) copy-start(bf16[4,32,2048]{2,1,0:T(8,128)(2,1)S(1)} %collective-permute-done.16.refs_1_) | copy-start | bytes 1572868
  58.6 10.1 %copy-start.12 = (bf16[4,32,2048]{2,1,0:T(8,128)(2,1)}, bf16[4,32,2048]{2,1,0:T(8,128)(2,1)S(1)}, u32[]{:S(2)}) copy-start(bf16[4,32,2048]{2,1,0:T(8,128)(2,1)S(1)} %collective-permute-done.17.refs_2_) | copy-start | bytes 1572868
  62.5 1.6 collective-permute-start.26
  62.5 2.1 %collective-permute-start.27 = (bf16[4,80,512]{2,1,0:T(8,128)(2,1)S(1)}, bf16[4,80,512]{2,1,0:T(8,128)(2,1)S(1)}, u32[]{:S(2)}, u32[]{:S(2)}) collective-permute-start(bf16[4,80,512]{2,1,0:T(8,128)(2,1)S(1)} %collective-permute-done.19.refs_9_), channel_id=1, source_target_pairs={{0,1},{1,0},{2,3},{3,2},{4,5},{5,4},{6,7},{7,6},{8,9},{9,8},{10,11... | collective-permute-start | bytes 983048 | tf_op jit(solution)/shard_map/ppermute | solution.py:33
  63.0 2.5 %collective-permute-start.28 = (bf16[4,80,512]{2,1,0:T(8,128)(2,1)S(1)}, bf16[4,80,512]{2,1,0:T(8,128)(2,1)S(1)}, u32[]{:S(2)}, u32[]{:S(2)}) collective-permute-start(bf16[4,80,512]{2,1,0:T(8,128)(2,1)S(1)} %collective-permute-done.20.refs_10_), channel_id=1, source_target_pairs={{0,1},{1,0},{2,3},{3,2},{4,5},{5,4},{6,7},{7,6},{8,9},{9,8},{10,11... | collective-permute-start | bytes 983048 | tf_op jit(solution)/shard_map/ppermute | solution.py:33
  63.1 5.4 %collective-permute-start.22 = (bf16[4,32,2048]{2,1,0:T(8,128)(2,1)}, bf16[4,32,2048]{2,1,0:T(8,128)(2,1)S(1)}, u32[]{:S(2)}, u32[]{:S(2)}) collective-permute-start(bf16[4,32,2048]{2,1,0:T(8,128)(2,1)} %copy-done.5), channel_id=1, source_target_pairs={{0,1},{1,0},{2,3},{3,2},{4,5},{5,4},{6,7},{7,6},{8,9},{9,8},{10,11... | collective-permute-start | bytes 1572872 | tf_op jit(solution)/shard_map/ppermute | solution.py:33
  63.5 5.0 %collective-permute-start.23 = (bf16[4,32,2048]{2,1,0:T(8,128)(2,1)S(1)}, bf16[4,32,2048]{2,1,0:T(8,128)(2,1)S(1)}, u32[]{:S(2)}, u32[]{:S(2)}) collective-permute-start(bf16[4,32,2048]{2,1,0:T(8,128)(2,1)S(1)} %collective-permute-done.16.refs_1_), channel_id=1, source_target_pairs={{0,1},{1,0},{2,3},{3,2},{4,5},{5,4},{6,7},{7,6},{8,9},{9,8},{10,11... | collective-permute-start | bytes 1572872 | tf_op jit(solution)/shard_map/ppermute | solution.py:33
  64.2 4.4 %collective-permute-start.24 = (bf16[4,32,2048]{2,1,0:T(8,128)(2,1)S(1)}, bf16[4,32,2048]{2,1,0:T(8,128)(2,1)S(1)}, u32[]{:S(2)}, u32[]{:S(2)}) collective-permute-start(bf16[4,32,2048]{2,1,0:T(8,128)(2,1)S(1)} %collective-permute-done.17.refs_2_), channel_id=1, source_target_pairs={{0,1},{1,0},{2,3},{3,2},{4,5},{5,4},{6,7},{7,6},{8,9},{9,8},{10,11... | collective-permute-start | bytes 1572872 | tf_op jit(solution)/shard_map/ppermute | solution.py:33
  64.6 4.0 %collective-permute-start.25 = (bf16[4,32,2048]{2,1,0:T(8,128)(2,1)S(1)}, bf16[4,32,2048]{2,1,0:T(8,128)(2,1)S(1)}, u32[]{:S(2)}, u32[]{:S(2)}) collective-permute-start(bf16[4,32,2048]{2,1,0:T(8,128)(2,1)S(1)} %collective-permute-done.18.refs_3_), channel_id=1, source_target_pairs={{0,1},{1,0},{2,3},{3,2},{4,5},{5,4},{6,7},{7,6},{8,9},{9,8},{10,11... | collective-permute-start | bytes 1572872 | tf_op jit(solution)/shard_map/ppermute | solution.py:33
  65.6 3.0 %collective-permute-start.29 = (bf16[4,80,512]{2,1,0:T(8,128)(2,1)S(1)}, bf16[4,80,512]{2,1,0:T(8,128)(2,1)S(1)}, u32[]{:S(2)}, u32[]{:S(2)}) collective-permute-start(bf16[4,80,512]{2,1,0:T(8,128)(2,1)S(1)} %collective-permute-done.21.refs_11_), channel_id=1, source_target_pairs={{0,1},{1,0},{2,3},{3,2},{4,5},{5,4},{6,7},{7,6},{8,9},{9,8},{10,11... | collective-permute-start | bytes 983048 | tf_op jit(solution)/shard_map/ppermute | solution.py:33
  83.8 8.4 %collective-permute-start.31 = (bf16[16,32,2048]{2,1,0:T(8,128)(2,1)}, bf16[16,32,2048]{2,1,0:T(8,128)(2,1)S(1)}, u32[]{:S(2)}, u32[]{:S(2)}) collective-permute-start(bf16[16,32,2048]{2,1,0:T(8,128)(2,1)} %get-tuple-element.110), channel_id=1, source_target_pairs={{0,1},{1,0},{2,3},{3,2},{4,5},{5,4},{6,7},{7,6},{8,9},{9,8},{10,11... | collective-permute-start | bytes 6291464 | tf_op jit(solution)/shard_map/ppermute | solution.py:33
  84.0 8.2 %collective-permute-start.30 = (bf16[16,64,512]{2,1,0:T(8,128)(2,1)}, bf16[16,64,512]{2,1,0:T(8,128)(2,1)}, u32[]{:S(2)}, u32[]{:S(2)}) collective-permute-start(bf16[16,64,512]{2,1,0:T(8,128)(2,1)} %get-tuple-element.109), channel_id=1, source_target_pairs={{0,1},{1,0},{2,3},{3,2},{4,5},{5,4},{6,7},{7,6},{8,9},{9,8},{10,11... | collective-permute-start | bytes 3145736 | tf_op jit(solution)/shard_map/ppermute | solution.py:33
  84.4 7.9 %copy-start.3 = (bf16[16,64,512]{2,1,0:T(8,128)(2,1)S(1)}, bf16[16,64,512]{2,1,0:T(8,128)(2,1)}, u32[]{:S(2)}) copy-start(bf16[16,64,512]{2,1,0:T(8,128)(2,1)} %get-tuple-element.119) | copy-start | bytes 3145732
  84.4 9.5 %copy-start = (bf16[16,32,2048]{2,1,0:T(8,128)(2,1)S(1)}, bf16[16,32,2048]{2,1,0:T(8,128)(2,1)}, u32[]{:S(2)}) copy-start(bf16[16,32,2048]{2,1,0:T(8,128)(2,1)} %get-tuple-element.117) | copy-start | bytes 6291460
  92.3 33.9 %copy-start.1 = (bf16[16,32,2048]{2,1,0:T(8,128)(2,1)}, bf16[16,32,2048]{2,1,0:T(8,128)(2,1)S(1)}, u32[]{:S(2)}) copy-start(bf16[16,32,2048]{2,1,0:T(8,128)(2,1)S(1)} %collective-permute-done.31) | copy-start | bytes 6291460
  95.2 9.0 %copy-start.2 = (bf16[8,32,2048]{2,1,0:T(8,128)(2,1)S(1)}, bf16[8,32,2048]{2,1,0:T(8,128)(2,1)}, u32[]{:S(2)}) copy-start(bf16[8,32,2048]{2,1,0:T(8,128)(2,1)} %add_convert_fusion.refs_6_) | copy-start | bytes 3145732
  102.5 9.5 %collective-permute-start.33 = (bf16[16,16,2048]{2,1,0:T(8,128)(2,1)}, bf16[16,16,2048]{2,1,0:T(8,128)(2,1)}, u32[]{:S(2)}, u32[]{:S(2)}) collective-permute-start(bf16[16,16,2048]{2,1,0:T(8,128)(2,1)} %get-tuple-element.122.refs_7_), channel_id=1, source_target_pairs={{0,1},{1,0},{2,3},{3,2},{4,5},{5,4},{6,7},{7,6},{8,9},{9,8},{10,11... | collective-permute-start | bytes 3145736 | tf_op jit(solution)/shard_map/ppermute | solution.py:33
  102.7 9.3 %collective-permute-start.32 = (bf16[8,64,512]{2,1,0:T(8,128)(2,1)S(1)}, bf16[8,64,512]{2,1,0:T(8,128)(2,1)}, u32[]{:S(2)}, u32[]{:S(2)}) collective-permute-start(bf16[8,64,512]{2,1,0:T(8,128)(2,1)S(1)} %add_convert_fusion.3), channel_id=1, source_target_pairs={{0,4},{1,3},{2,6},{3,1},{4,0},{5,7},{6,2},{7,5},{8,12},{9,11},{10,... | collective-permute-start | bytes 1572872 | tf_op jit(solution)/shard_map/ppermute | solution.py:33
  104.2 21.8 %collective-permute-start.34 = (bf16[8,32,2048]{2,1,0:T(8,128)(2,1)S(1)}, bf16[8,32,2048]{2,1,0:T(8,128)(2,1)}, u32[]{:S(2)}, u32[]{:S(2)}) collective-permute-start(bf16[8,32,2048]{2,1,0:T(8,128)(2,1)S(1)} %copy-done.2), channel_id=1, source_target_pairs={{0,4},{1,3},{2,6},{3,1},{4,0},{5,7},{6,2},{7,5},{8,12},{9,11},{10,... | collective-permute-start | bytes 3145736 | tf_op jit(solution)/shard_map/ppermute | solution.py:33
  114.1 22.6 %collective-permute-start.37 = (bf16[8,16,2048]{2,1,0:T(8,128)(2,1)}, bf16[8,16,2048]{2,1,0:T(8,128)(2,1)}, u32[]{:S(2)}, u32[]{:S(2)}) collective-permute-start(bf16[8,16,2048]{2,1,0:T(8,128)(2,1)} %add_convert_fusion.2), channel_id=1, source_target_pairs={{0,4},{1,3},{2,6},{3,1},{4,0},{5,7},{6,2},{7,5},{8,12},{9,11},{10,... | collective-permute-start | bytes 1572872 | tf_op jit(solution)/shard_map/ppermute | solution.py:33
  116.8 9.3 %collective-permute-start.35 = (bf16[4,64,512]{2,1,0:T(8,128)(2,1)S(1)}, bf16[4,64,512]{2,1,0:T(8,128)(2,1)S(1)}, u32[]{:S(2)}, u32[]{:S(2)}) collective-permute-start(bf16[4,64,512]{2,1,0:T(8,128)(2,1)S(1)} %add_convert_fusion.6.refs_12_), channel_id=1, source_target_pairs={{0,2},{1,5},{2,0},{3,7},{4,6},{5,1},{6,4},{7,3},{8,10},{9,13},{10,... | collective-permute-start | bytes 786440 | tf_op jit(solution)/shard_map/ppermute | solution.py:33
  126.0 10.7 %copy-start.4 = (bf16[16,16,2048]{2,1,0:T(8,128)(2,1)S(1)}, bf16[16,16,2048]{2,1,0:T(8,128)(2,1)}, u32[]{:S(2)}) copy-start(bf16[16,16,2048]{2,1,0:T(8,128)(2,1)} %get-tuple-element.130) | copy-start | bytes 3145732
  128.3 1.3 collective-permute-start.36
  130.2 6.5 %collective-permute-start.38 = (bf16[8,16,128]{2,1,0:T(8,128)(2,1)}, bf16[8,16,128]{2,1,0:T(8,128)(2,1)}, u32[]{:S(2)}, u32[]{:S(2)}) collective-permute-start(bf16[8,16,128]{2,1,0:T(8,128)(2,1)} %add_convert_fusion.12), channel_id=1, source_target_pairs={{0,4},{1,3},{2,6},{3,1},{4,0},{5,7},{6,2},{7,5},{8,12},{9,11},{10,... | collective-permute-start | bytes 98312 | tf_op jit(solution)/shard_map/ppermute | solution.py:33
  131.6 9.4 %collective-permute-start.41 = (bf16[4,32,2048]{2,1,0:T(8,128)(2,1)}, bf16[4,32,2048]{2,1,0:T(8,128)(2,1)S(1)}, u32[]{:S(2)}, u32[]{:S(2)}) collective-permute-start(bf16[4,32,2048]{2,1,0:T(8,128)(2,1)} %add_convert_fusion.1), channel_id=1, source_target_pairs={{0,2},{1,5},{2,0},{3,7},{4,6},{5,1},{6,4},{7,3},{8,10},{9,13},{10,... | collective-permute-start | bytes 1572872 | tf_op jit(solution)/shard_map/ppermute | solution.py:33
  133.1 12.8 %collective-permute-start.40 = (bf16[2,64,512]{2,1,0:T(8,128)(2,1)S(1)}, bf16[2,64,512]{2,1,0:T(8,128)(2,1)S(1)}, u32[]{:S(2)}, u32[]{:S(2)}) collective-permute-start(bf16[2,64,512]{2,1,0:T(8,128)(2,1)S(1)} %add_convert_fusion.9), channel_id=1, source_target_pairs={{0,8},{1,9},{2,10},{3,11},{4,12},{5,13},{6,14},{7,15},{8,0},{9,1},... | collective-permute-start | bytes 393224 | tf_op jit(solution)/shard_map/ppermute | solution.py:33
  138.7 8.3 %collective-permute-start.39 = (bf16[4,16,2176]{2,1,0:T(8,128)(2,1)S(1)}, bf16[4,16,2176]{2,1,0:T(8,128)(2,1)S(1)}, u32[]{:S(2)}, u32[]{:S(2)}) collective-permute-start(bf16[4,16,2176]{2,1,0:T(8,128)(2,1)S(1)} %pad_maximum_fusion.2), channel_id=1, source_target_pairs={{0,2},{1,5},{2,0},{3,7},{4,6},{5,1},{6,4},{7,3},{8,10},{9,13},{10,... | collective-permute-start | bytes 835592 | tf_op jit(solution)/shard_map/ppermute | solution.py:33
  142.2 12.3 %collective-permute-start.43 = (bf16[2,32,2048]{2,1,0:T(8,128)(2,1)S(1)}, bf16[2,32,2048]{2,1,0:T(8,128)(2,1)S(1)}, u32[]{:S(2)}, u32[]{:S(2)}) collective-permute-start(bf16[2,32,2048]{2,1,0:T(8,128)(2,1)S(1)} %add_convert_fusion.4), channel_id=1, source_target_pairs={{0,8},{1,9},{2,10},{3,11},{4,12},{5,13},{6,14},{7,15},{8,0},{9,1},... | collective-permute-start | bytes 786440 | tf_op jit(solution)/shard_map/ppermute | solution.py:33
  146.8 14.0 %collective-permute-start.45 = (bf16[64,512]{1,0:T(8,128)(2,1)S(1)}, bf16[64,512]{1,0:T(8,128)(2,1)S(1)}, u32[]{:S(2)}, u32[]{:S(2)}) collective-permute-start(bf16[64,512]{1,0:T(8,128)(2,1)S(1)} %fusion.3), channel_id=1, source_target_pairs={{0,16},{1,17},{2,18},{3,19},{4,20},{5,21},{6,22},{7,23},{8,24},{9,... | collective-permute-start | bytes 196616 | tf_op jit(solution)/shard_map/ppermute | solution.py:33
  148.8 7.2 %collective-permute-start.42 = (bf16[2,16,2176]{2,1,0:T(8,128)(2,1)S(1)}, bf16[2,16,2176]{2,1,0:T(8,128)(2,1)S(1)}, u32[]{:S(2)}, u32[]{:S(2)}) collective-permute-start(bf16[2,16,2176]{2,1,0:T(8,128)(2,1)S(1)} %pad_maximum_fusion.4), channel_id=1, source_target_pairs={{0,8},{1,9},{2,10},{3,11},{4,12},{5,13},{6,14},{7,15},{8,0},{9,1},... | collective-permute-start | bytes 417800 | tf_op jit(solution)/shard_map/ppermute | solution.py:33
  157.8 10.1 %collective-permute-start.46 = (bf16[32,2048]{1,0:T(8,128)(2,1)S(1)}, bf16[32,2048]{1,0:T(8,128)(2,1)S(1)}, u32[]{:S(2)}, u32[]{:S(2)}) collective-permute-start(bf16[32,2048]{1,0:T(8,128)(2,1)S(1)} %fusion.1), channel_id=1, source_target_pairs={{0,16},{1,17},{2,18},{3,19},{4,20},{5,21},{6,22},{7,23},{8,24},{9,... | collective-permute-start | bytes 393224 | tf_op jit(solution)/shard_map/ppermute | solution.py:33
  159.6 11.7 %collective-permute-start.44 = (bf16[16,2176]{1,0:T(8,128)(2,1)S(1)}, bf16[16,2176]{1,0:T(8,128)(2,1)S(1)}, u32[]{:S(2)}, u32[]{:S(2)}) collective-permute-start(bf16[16,2176]{1,0:T(8,128)(2,1)S(1)} %pad_maximum_fusion.5), channel_id=1, source_target_pairs={{0,16},{1,17},{2,18},{3,19},{4,20},{5,21},{6,22},{7,23},{8,24},{9,... | collective-permute-start | bytes 208904 | tf_op jit(solution)/shard_map/ppermute | solution.py:33
  (16 other events, 39.5 us)

commit v3 on v2

--- a/solution.py
+++ b/solution.py
@@ -63,22 +63,23 @@
 
 
 class Sum:
-    def __init__(self, own, other):
+    def __init__(self, own, low, high):
         self.own = own
-        self.core = send(other, CORE)
+        self.high = send(high, CORE)
+        self.low = send(low, CORE)
 
     def first(self):
-        part = widen(self.own[8:], self.core[8:]).astype(LOW)
+        part = widen(self.own[8:], self.high).astype(LOW)
         self.far = send(part, FAR)
         return part
 
     def second(self):
-        part = widen(self.own[4:8], self.core[4:8], self.far[4:]).astype(LOW)
+        part = widen(self.own[4:8], self.low[4:], self.far[4:]).astype(LOW)
         self.near = send(part, NEAR)
         return part
 
     def total(self, at):
-        return widen(self.own[at], self.core[at], self.far[at], self.near[at])
+        return widen(self.own[at], self.low[at], self.far[at], self.near[at])
 
     def third(self):
         part = self.total(slice(1, 4, 2)).astype(LOW)
@@ -88,10 +89,11 @@
     def fourth(self):
         part = widen(self.total(2), self.beside[1]).astype(LOW)
         self.beyond = send(part, LAYER[2])
+        self.rest = tie(widen(self.total(0), self.beside[0]), part)
         return part
 
     def done(self):
-        return widen(self.total(0), self.beside[0], self.beyond)
+        return widen(self.rest, self.beyond)
 
 
 def shard_at(me, k, turned=False):
@@ -209,19 +211,14 @@
 
 
 class Store:
-    def __init__(self, target, buffer, sems, first, parts, row=0):
-        self.buffer, self.parts, self.row = buffer, parts, row
+    def __init__(self, target, buffer, sems, first, parts):
+        self.buffer, self.parts = buffer, parts
         self.target, self.sems, self.first = target, sems, first
 
     def copy(self, i):
         rows = self.buffer.shape[0] // self.parts
         at = block(i, rows) if self.parts > 1 else pl.ds(0, rows)
-        if self.row == 0:
-            target = self.target.at[at]
-        else:
-            start = self.row + i * rows
-            target = self.target.at[pl.ds(start if isinstance(start, int) else pl.multiple_of(start, rows), rows)]
-        return pltpu.make_async_copy(self.buffer.at[at], target, self.sems.at[self.first + i])
+        return pltpu.make_async_copy(self.buffer.at[at], self.target.at[at], self.sems.at[self.first + i])
 
     def part(self, i):
         self.copy(i).start()
@@ -231,13 +228,9 @@
             self.copy(i).start()
 
 
-def call(body, micros, me, near, loads, stores, scratch=(), after=(), into=None):
+def call(body, micros, me, near, loads, stores, scratch=(), after=()):
     far = pl.BlockSpec(memory_space=pltpu.HBM)
-    given = [] if into is None or isinstance(into[0], tuple) else [into[0]]
-    counts = [len(near), len(loads), len(after) + len(given), len(stores), len(loads), len(stores), len(scratch)]
-    shapes = [shape for shape, _type, _parts in stores]
-    if into is not None:
-        shapes[0] = into[0] if not given else into[0].shape
+    counts = [len(near), len(loads), len(after), len(stores), len(loads), len(stores), len(scratch)]
 
     def kernel(me_ref, *refs):
         groups, at = [], 0
@@ -252,8 +245,7 @@
             first += parts
         first, writes = 0, []
         for (_shape, _type, parts), target, buffer in zip(stores, targets, out_buffers):
-            row = target.shape[0] - buffer.shape[0] if given and not writes else 0
-            writes.append(Store(target, buffer, out_sems, first, parts, row))
+            writes.append(Store(target, buffer, out_sems, first, parts))
             first += parts
         body(None if me is None else me_ref[0], (near_refs, near_sem), reads, writes, rest)
         for write in writes:
@@ -264,11 +256,10 @@
     buffers += [(s, t) for s, t, _parts in stores]
     return pl.pallas_call(
         kernel,
-        out_shape=[jax.ShapeDtypeStruct(s, t) for s, (_shape, t, _parts) in zip(shapes, stores)],
+        out_shape=[jax.ShapeDtypeStruct(s, t) for s, t, _parts in stores],
         in_specs=[pl.BlockSpec(memory_space=pltpu.SMEM)]
         + [far] * (len(near) + len(loads))
-        + [pl.BlockSpec(memory_space=pl.ANY)] * len(after)
-        + [far] * len(given),
+        + [pl.BlockSpec(memory_space=pl.ANY)] * len(after),
         out_specs=[far] * len(stores),
         scratch_shapes=[pltpu.VMEM(s, t) for s, t in buffers + list(scratch)]
         + [
@@ -276,10 +267,9 @@
             pltpu.SemaphoreType.DMA((max(1, sum(parts for _shape, _type, parts in stores)),)),
             pltpu.SemaphoreType.DMA((4,)),
         ],
-        input_output_aliases={1 + len(near) + len(loads) + len(after): 0} if given else {},
         compiler_params=pltpu.CompilerParams(vmem_limit_bytes=VMEM_LIMIT),
         cost_estimate=pl.CostEstimate(flops=int(micros * 1.1e9), bytes_accessed=1000, transcendentals=0),
-    )(jnp.zeros((1,), jnp.int32) if me is None else me, *near, *[a for a, _parts, _box in loads], *after, *given)
+    )(jnp.zeros((1,), jnp.int32) if me is None else me, *near, *[a for a, _parts, _box in loads], *after)
 
 
 class Place:
@@ -377,18 +367,20 @@
 
 def ffn_kernel(me, near, reads, writes, scratch):
     cotangent, base0, mixed, vec, bias_up = reads
-    output, dfirst, dmixed, sum_up, sum_gain, sum_shift, sum_pool, own_down, other_down, own, other = writes
-    w_proj, w_up, w_down, w_out, first, norm_ffn, dpool, hidden, slope, pre_low, total = scratch
+    output, dfirst, dmixed, sum_up, sum_gain, sum_shift, sum_pool, own, *halves = writes
+    w_proj, w_up, w_down, w_out, first, norm_ffn, pre_low, dpool, hidden, slope, total = scratch
     pieces, sem = near
     out = Place(me, pieces[8:], w_out, sem.at[3], lambda piece: piece.at[pl.ds(64, 16)], turned=True)
     proj = Place(me, pieces[:8], w_proj, sem.at[0], lambda piece: piece.at[pl.ds(0, 16)])
     up = Place(me, pieces[:8], w_up, sem.at[1], lambda piece: piece.at[pl.ds(16, 16)])
     down = Place(me, pieces[8:], w_down, sem.at[2], lambda piece: piece.at[pl.ds(0, 64)], turned=True)
 
-    def share(mine, theirs, row, rows, lanes, base=0):
+    def share(row, steps, target, base=0):
         for k in range(SHARDS):
-            half = mine if k < 16 else theirs
-            half.buffer[k % 16, row : row + rows, lanes] = total[block(base + shard_at(me, k), rows), :].astype(LOW)
+            half, place = (own, k) if k < 16 else (halves[k // 8 - 2], k % 8)
+            for step in range(steps):
+                at = pl.ds(pl.multiple_of(base + (shard_at(me, k) * steps + step) * 16, 16), 16)
+                half.buffer[place, row : row + 16, target(step)] = total[at, :].astype(LOW)
 
     for read in (base0, mixed, vec):
         read.whole()
@@ -417,9 +409,7 @@
             hidden[at, lanes] = (value * below).astype(LOW)
             slope[at, lanes] = below + value * (jnp.exp(-0.5 * value * value) * 0.3989422804014327)
         total[256 * k : 256 * k + 256, :] = dot_tn(hidden[:, lanes], low)
-    share(own_down, other_down, 0, 64, slice(0, 512))
-    other_down.send()
-    own_down.send()
+    share(32, 4, lambda step: slice(512 * step, 512 * step + 512))
     down.wait()
     for k in range(8):
         lanes = slice(256 * k, 256 * k + 256)
@@ -445,11 +435,12 @@
     for k in range(4):
         lanes = slice(512 * k, 512 * k + 512)
         total[:512, :] = dot_tn(pooled, cotangent.buffer[:, lanes])
-        share(own, other, 0, 16, lanes)
+        share(0, 1, lambda _step: lanes)
         total[512:1024, :] = dot_tn(norm_ffn[...], pre_low[:, lanes])
-        share(own, other, 16, 16, lanes, SHARDS)
+        share(16, 1, lambda _step: lanes, 512)
         output.buffer[:, lanes] = dot(pooled, w_proj[:, lanes]).astype(LOW)
-    other.send()
+    for half in halves:
+        half.send()
     own.send()
     output.send()
 
@@ -485,30 +476,10 @@
     query_part.send()
 
 
-def grad_qkv_kernel(me, _near, reads, writes, scratch):
-    mixed, dfirst, normed0, dquery, normed, dkeyval = reads
-    own, other = writes
-    grad_qkv, grad_out = scratch
-    grad_out[...] = dot_tn(mixed.whole()[...], dfirst.whole()[...].astype(LOW))
-    grad_qkv[:, :512] = dot_tn(normed0.whole()[...], dquery.whole()[...])
-    normed.whole()
-    dkeyval.whole()
-    for k in range(4):
-        lanes = slice(256 * k, 256 * k + 256)
-        grad_qkv[:, 512 + 256 * k : 768 + 256 * k] = dot_tn(normed.buffer[...], dkeyval.buffer[:, lanes])
-    for i in range(16):
-        for k, half in ((i, own.buffer), (16 + i, other.buffer)):
-            at = block(shard_at(me, k), 16)
-            half[i, :, :1536] = grad_qkv[at, :].astype(half.dtype)
-            half[i, :, 1536:2048] = grad_out[at, :].astype(half.dtype)
-    other.send()
-    own.send()
-
-
-def norm_back_kernel(me, _near, reads, writes, scratch):
-    vec, query_part, dfirst, marks, weights, dkeyval, embeds, *more = reads
-    grad_embeds, *results = writes
-    table, rows, work, lower, spread_query, spread_first, small, sums = scratch
+def input_back_kernel(me, _near, reads, writes, scratch):
+    vec, query_part, dfirst, marks, weights, dkeyval, embeds, gain_ffn, shift_ffn, pool, up, mixed, normed0, dquery, normed = reads
+    grad_embeds, own, *halves = writes
+    grad_qkv, grad_out, table, rows, work, lower, spread_query, spread_first, small, sums = scratch
     for read in (weights, query_part, dfirst, vec, marks):
         read.whole()
     table[...] = jnp.zeros_like(table)
@@ -548,13 +519,13 @@
         return 0
 
     lax.fori_loop(0, embeds.buffer.shape[0] // RB // 2, norm_pair, 0)
-    if not more:
-        results[0].buffer[...] = sums[0] + sums[1]
-        results[0].send()
-        return
-    before, gain_ffn, shift_ffn, pool, up = more
-    own, other = results
-    sums[0] = sums[0] + sums[1] + before.whole()[...]
+    grad_out[...] = dot_tn(mixed.whole()[...], dfirst.buffer[...].astype(LOW))
+    grad_qkv[:, :512] = dot_tn(normed0.whole()[...], dquery.whole()[...])
+    normed.whole()
+    for k in range(4):
+        lanes = slice(256 * k, 256 * k + 256)
+        grad_qkv[:, 512 + 256 * k : 768 + 256 * k] = dot_tn(normed.buffer[...], dkeyval.buffer[:, lanes])
+    sums[0] = sums[0] + sums[1]
     small[...] = jnp.zeros_like(small)
     small[0:8, :] = sums[0, 16:24, :]
     folded = (sums[0, 0:8, :], sums[0, 8:16, :], gain_ffn.whole()[...], shift_ffn.whole()[...], pool.whole()[...])
@@ -567,11 +538,15 @@
         tile = jnp.where(row == 13, up_row[:, 128 * (r // 2) : 128 * (r // 2) + 128], tile)
         rows[0, 8 * r : 8 * r + 8, 0:128] = tile[0:8]
         rows[0, 8 * r : 8 * r + 8, 128:256] = tile[8:16]
-    for i in range(16):
-        for k, half in ((i, own.buffer), (16 + i, other.buffer)):
-            at = block(shard_at(me, k), 8)
-            half[i] = jnp.concatenate([rows[0, at, 0:128], rows[0, at, 128:256]]).astype(half.dtype)
-    other.send()
+    for k in range(SHARDS):
+        half, place = (own, k) if k < 16 else (halves[k // 8 - 2], k % 8)
+        at, near = block(shard_at(me, k), 16), block(shard_at(me, k), 8)
+        half.buffer[place, :, :1536] = grad_qkv[at, :].astype(LOW)
+        half.buffer[place, :, 1536:2048] = grad_out[at, :].astype(LOW)
+        value = jnp.concatenate([rows[0, near, 0:128], rows[0, near, 128:256]])
+        half.buffer[place, :, 2048:2176] = value.astype(LOW)
+    for half in halves:
+        half.send()
     own.send()
 
 
@@ -616,8 +591,10 @@
         quad = jnp.stack([tie(third, own), *quad[1:]])
         own2 = jnp.stack([tie(shard, quad), lower, upper, send(tie(upper, own), LAYER[1])])
         pieces.append([own2, *spread(own2, NEAR, FAR, ACROSS)])
-        pieces.append([quad, *spread(quad, LAYER[1], LAYER[2], LAYER[3])])
-        later = [tie(own2, quad)]
+        lower, upper = spread(quad, LAYER[1], LAYER[2])
+        upper = tie(upper, own2)
+        pieces.append([quad, lower, upper, send(upper, LAYER[1])])
+        later = [tie(own2, upper)]
         group_ids, piece_counts = tie(group_ids, piece_counts, own, every=True)[:2]
     else:
         me = None
@@ -681,9 +658,10 @@
         came += [send(part, CORE) for part in came]
         pieces[1:] = [came[0:4] + came[8:12], came[4:8] + came[12:16]]
     (
-        output, dfirst, dmixed, sum_up, sum_gain, sum_shift, sum_pool, own_down, other_down, own_pair, other_pair
+        output, dfirst, dmixed, sum_up, sum_gain, sum_shift, sum_pool, own_pair, *other_pair
     ) = call(
-        ffn_kernel, 14,
+        ffn_kernel,
+        12,
         me,
         [*pieces[1], *pieces[2]],
         [
@@ -691,18 +669,17 @@
         ],
         [
             ((entries, 2048), low, 1), ((entries, 512), wide, 1), ((entries, 512), low, 1), ((8, 2048), wide, 1),
-            ((8, 512), wide, 1), ((8, 512), wide, 1), ((8, 512), wide, 1), ((16, 64, 512), low, 1),
-            ((16, 64, 512), low, 1), ((16, 32, 2048), low, 1), ((16, 32, 2048), low, 1),
+            ((8, 512), wide, 1), ((8, 512), wide, 1), ((8, 512), wide, 1), ((16, 48, 2048), low, 1),
+            ((8, 48, 2048), low, 1), ((8, 48, 2048), low, 1),
         ],
         [
             ((512, 2048), low), ((512, 2048), low), ((2048, 512), low), ((512, 512), low), ((entries, 512), wide),
-            ((entries, 512), low), ((entries, 512), wide), ((entries, 2048), low),
-            ((entries, 2048), wide), ((entries, 2048), low), ((2048, 512), wide),
+            ((entries, 512), low), ((entries, 2048), low), ((entries, 512), wide), ((entries, 2048), low),
+            ((entries, 2048), wide), ((2048, 512), wide),
         ],
     )
     if tuned:
-        down = Sum(own_down, other_down)
-        pair = Sum(own_pair, other_pair)
+        pair = Sum(own_pair, *other_pair)
     (dkeyval, dquery, query_part) = call(
         attend_back_kernel, 8,
         me,
@@ -715,112 +692,66 @@
     )
     part = own_pair
     if tuned:
-        query_part, down.core, pair.core = tie(query_part, down.core, pair.core, every=True)
-        part = down.first()
-        pair.core = tie(pair.core, part)
+        query_part, pair.high = tie(query_part, pair.high, every=True)
         part = pair.first()
-    (own_last, other_last) = call(
-        grad_qkv_kernel, 7,
+    (grad_embeds, own_last, *other_last) = call(
+        input_back_kernel,
+        18,
         me,
         [],
         [
-            (mixed, 1, None), (dfirst, 1, None), (normed0, 1, None), (dquery, 1, None), (normed, 1, None),
-            (dkeyval, steps, None),
+            (vec, 1, None), (query_part, 1, None), (dfirst, 1, None), (marks, 1, None), (qkv_all, 1, (0, 512, 512, 1024)),
+            (dkeyval, steps, None), (flat, steps, None), (sum_gain, 1, None), (sum_shift, 1, None), (sum_pool, 1, None),
+            (sum_up, 1, None), (mixed, 1, None), (normed0, 1, None), (dquery, 1, None), (normed, 1, None),
         ],
-        [((16, 16, 2048), low, 1), ((16, 16, 2048), low, 1)],
-        [((512, 1536), wide), ((512, 512), wide)],
+        [((rows, 512), low, steps), ((16, 16, 2176), low, 1), ((8, 16, 2176), low, 1), ((8, 16, 2176), low, 1)],
+        [
+            ((512, 1536), wide), ((512, 512), wide), ((128, 512), low), ((2, RB, 512), wide), ((2, RB, 512), wide),
+            ((2, RB, 512), low), ((2, 4 * RB, 128), wide), ((2, 4 * RB, 128), wide), ((16, 512), wide),
+            ((2, 144, 512), wide),
+        ],
         after=[part],
     )
     if tuned:
-        last = Sum(own_last, other_last)
-
-    def norm_back(start, count, more, stores, after, into):
-        return call(
-            norm_back_kernel, 6.6,
-            me,
-            [],
-            [
-                (vec, 1, None), (query_part, 1, (start // 8, count // 8, 0, 512)),
-                (dfirst, 1, (start // 8, count // 8, 0, 512)), (marks, 1, (start, count, 0, 128)),
-                (qkv_all, 1, (0, 512, 512, 1024)), (dkeyval, steps // 2, (start, count, 0, 1024)),
-                (flat, steps // 2, (start, count, 0, 512)), *[(array, 1, None) for array in more],
-            ],
-            [((count, 512), low, steps // 2), *stores],
-            [
-                ((128, 512), low), ((2, RB, 512), wide), ((2, RB, 512), wide), ((2, RB, 512), low),
-                ((2, 4 * RB, 128), wide), ((2, 4 * RB, 128), wide), ((16, 512), wide), ((2, 144, 512), wide),
-            ],
-            after=after,
-            into=into,
-        )
-
-    half = rows // 2
-    (grad_embeds, half_sums) = norm_back(0, half, [], [((144, 512), wide, 1)], [other_last], ((rows, 512), half))
-    part = half_sums
-    if tuned:
-        half_sums, down.far, last.core = tie(half_sums, down.far, last.core, every=True)
+        last = Sum(own_last, *other_last)
         part = last.first()
-        down.far = tie(down.far, part)
-        part = down.second()
-    (grad_embeds, own_small, other_small) = norm_back(
-        half,
-        half,
-        [half_sums, sum_gain, sum_shift, sum_pool, sum_up],
-        [((16, 16, 128), low, 1), ((16, 16, 128), low, 1)],
-        [part],
-        (grad_embeds, half),
-    )
-    if tuned:
-        other_small, pair.far, down.near = tie(other_small, pair.far, down.near, every=True)
-        little = Sum(own_small, other_small)
+        pair.far = tie(pair.far, part)
         part = pair.second()
-        down.near = tie(down.near, part)
-        part = down.third()
-        little.core = tie(little.core, part)
-        part = little.first()
-        last.far, little.far = tie(last.far, little.far, part, every=True)[:2]
-        near = [widen(sums.own[4:8], sums.core[4:8], sums.far[4:]).astype(LOW) for sums in (last, little)]
-        near = side_by_side_lanes(near)
-        came = send(near, NEAR)
-        pair.near = tie(pair.near, near)
+        last.far = tie(last.far, part)
+        part = last.second()
+        pair.near = tie(pair.near, part)
         part = pair.third()
-        down.beside = tie(down.beside, part)
-        part = down.fourth()
-        came = tie(came, part)
-        last.near, little.near = came[:, :, :2048], came[:, :, 2048:]
-        near = side_by_side_lanes([sums.total(slice(1, 4, 2)).astype(LOW) for sums in (last, little)])
-        came = send(near, LAYER[1])
-        pair.beside = tie(pair.beside, near)
+        last.near = tie(last.near, part)
+        part = last.third()
+        pair.beside = tie(pair.beside, part)
         part = pair.fourth()
-        came = tie(came, part)
-        last.beside, little.beside = came[:, :, :2048], came[:, :, 2048:]
-        near = side_by_side_lanes([widen(sums.total(2), sums.beside[1]).astype(LOW) for sums in (last, little)])
-        came = send(near, LAYER[2])
-        down.beyond, pair.beyond = tie(down.beyond, pair.beyond, near, every=True)[:2]
-        sum_down, pair = down.done(), pair.done()
-        came = tie(came, sum_down, pair)
-        last.beyond, little.beyond = came[:, :2048], came[:, 2048:]
-        last_small = little.done()
-        sum_proj, sum_up = pair[:16], pair[16:]
-        sum_qkv, sum_out = [
-            widen(last.total(0)[:, at], last.beside[0][:, at], last.beyond[:, at])
-            for at in (slice(0, 1536), slice(1536, 2048))
+        last.beside = tie(last.beside, part)
+        part = last.fourth()
+        last.beyond = tie(last.beyond, part)
+        sum_qkv, sum_out, last_small = [
+            widen(last.rest[:, at], last.beyond[:, at])
+            for at in (slice(0, 1536), slice(1536, 2048), slice(2048, 2176))
         ]
+        pair.beyond = tie(pair.beyond, sum_qkv)
+        pair = pair.done()
+        sum_proj, sum_up = pair[:16], pair[16:32]
+        sum_down = jnp.concatenate([pair[32:, 512 * j : 512 * j + 512] for j in range(4)])
         me = lax.axis_index("dp")
         sums = lax.dynamic_slice(last_small, (0, 16 * (me % 8)), (13, 16))
         sum_upbias = lax.dynamic_slice(last_small, (13, 64 * (me % 2)), (1, 64))[0]
     else:
 
-        def share(own, other, axis=0):
-            full = jnp.concatenate([own, other.astype(F32)])
+        def share(full):
             return lax.psum_scatter(full.reshape(-1, full.shape[-1]), "dp", scatter_dimension=0, tiled=True)
 
-        sum_down = share(own_down, other_down)
-        sum_proj = share(own_pair[:, :16], other_pair[:, :16])
-        sum_up = share(own_pair[:, 16:], other_pair[:, 16:])
-        sum_qkv = share(own_last[:, :, :1536], other_last[:, :, :1536])
-        sum_out = share(own_last[:, :, 1536:], other_last[:, :, 1536:])
-        small = jnp.concatenate([own_small, other_small.astype(F32)])
+        pair_all = jnp.concatenate([own_pair, *other_pair]).astype(F32)
+        last_all = jnp.concatenate([own_last, *other_last]).astype(F32)
+        sum_proj = share(pair_all[:, :16])
+        sum_up = share(pair_all[:, 16:32])
+        sum_down = share(pair_all[:, 32:].reshape(SHARDS, 16, 4, 512).transpose(0, 2, 1, 3))
+        sum_qkv = share(last_all[:, :, :1536])
+        sum_out = share(last_all[:, :, 1536:2048])
+        small = last_all[:, :, 2048:]
         vectors = jnp.concatenate([small[8 * k, :13] for k in range(4)], axis=1)
         sums = lax.psum_scatter(vectors, "dp", scatter_dimension=1, tiled=True)
         upbias = jnp.concatenate([small[2 * k, 13] for k in range(16)])

time: 176 us -> 167 us (0.949)
  waiting for transfers between devices: 33 us -> 51.5 us
  other arithmetic: 29.9 us -> 17.2 us
  starting transfers between devices: 49.8 us -> 40.8 us
  Pallas kernels: 56.9 us -> 52 us
    ppermute x47 -> x42, waiting for transfers between devices: 33 us -> 51.5 us  [send(): return lax.ppermute(value, 'dp', to)]
    ppermute x47 -> x42, starting transfers between devices: 49.8 us -> 40.8 us  [send(): return lax.ppermute(value, 'dp', to)]
    convert_element_type x11 -> x4, other arithmetic: 13.5 us -> 6.05 us  [the longest x2 4.42 us: first(): part = widen(self.own[8:], self.high).astype(LOW)]
    pallas_call x6 -> x4, Pallas kernels: 56.9 us -> 52 us  [call(): pl.pallas_call(kernel, out_shape=[jax.ShapeDtypeStruct(s, t) for s, t, _p...]
    add x6 -> x5, other arithmetic: 5.67 us -> 2.64 us  [widen(): total = total + value.astype(F32)]
    convert_element_type x2 -> x1, other arithmetic: 2.01 us -> 0.09 us  [fourth(): part = widen(self.total(2), self.beside[1]).astype(LOW)]
  transfers between devices with their start and end apart: 47 -> 42, of which waited for: 16 -> 15; matrix products, arithmetic and copies ran while one was open for 14% -> 10% of each run, Pallas kernels for 20% -> 22%
where the time goes in v3:
time: 167 us
  Pallas kernels  52 us (31%)
  waiting for transfers between devices  51.5 us (31%)
  starting transfers between devices  40.8 us (24%)
  other arithmetic  17.2 us (10%)
  local copies, waits for them, and re-layouts  4.11 us (2%)
    pallas_call x4, Pallas kernels, call(): pl.pallas_call(kernel, out_shape=[jax.ShapeDtypeStruct(s, t) for s, t, _p...  52 us
    ppermute x42, waiting for transfers between devices, send(): return lax.ppermute(value, 'dp', to)  51.5 us
    ppermute x42, starting transfers between devices, send(): return lax.ppermute(value, 'dp', to)  40.8 us
    convert_element_type x2, other arithmetic, first(): part = widen(self.own[8:], self.high).astype(LOW)  4.42 us
  transfers between devices with their start and end apart: 42, of which 15 were waited for; matrix products, arithmetic and copies ran while one was open for 10% of the time, Pallas kernels for 22%

profile of v3, /device:TPU:0, one launch (start us, length us, event | category | flops | bytes accessed | tf_op | source)
XLA Modules:
  0.0 166.7 jit_solution(17504937563658271886)
XLA Ops:
  0.6 0.9 pad_add_fusion.2
  1.6 5.1 %collective-permute-start.2 = (bf16[16,1664]{1,0:T(8,128)(2,1)S(1)}, bf16[16,1664]{1,0:T(8,128)(2,1)S(1)}, u32[]{:S(2)}, u32[]{:S(2)}) collective-permute-start(bf16[16,1664]{1,0:T(8,128)(2,1)S(1)} %pad_add_fusion.2), channel_id=1, source_target_pairs={{0,24},{1,25},{2,26},{3,27},{4,28},{5,29},{6,30},{7,31},{8,16},{9,... | collective-permute-start | bytes 159752 | tf_op jit(solution)/shard_map/ppermute | solution.py:33
  6.7 0.6 collective-permute-start.1
  7.3 0.9 pad_add_fusion.1
  8.2 1.6 collective-permute-start.10
  9.8 1.5 collective-permute-start.11
  11.4 0.9 fusion.5
  12.3 0.9 pad_add_fusion
  13.6 2.3 %collective-permute-start.14 = (bf16[32,2048]{1,0:T(8,128)(2,1)S(1)}, bf16[32,2048]{1,0:T(8,128)(2,1)S(1)}, u32[]{:S(2)}, u32[]{:S(2)}) collective-permute-start(bf16[32,2048]{1,0:T(8,128)(2,1)S(1)} %pad_add_fusion), channel_id=1, source_target_pairs={{0,16},{1,17},{2,18},{3,19},{4,20},{5,21},{6,22},{7,23},{8,24},{9,... | collective-permute-start | bytes 393224 | tf_op jit(solution)/shard_map/ppermute | solution.py:33
  15.9 2.0 %collective-permute-start.13 = (bf16[32,2048]{1,0:T(8,128)(2,1)S(1)}, bf16[32,2048]{1,0:T(8,128)(2,1)S(1)}, u32[]{:S(2)}, u32[]{:S(2)}) collective-permute-start(bf16[32,2048]{1,0:T(8,128)(2,1)S(1)} %pad_add_fusion), channel_id=1, source_target_pairs={{0,8},{1,9},{2,10},{3,11},{4,12},{5,13},{6,14},{7,15},{8,0},{9,1},... | collective-permute-start | bytes 393224 | tf_op jit(solution)/shard_map/ppermute | solution.py:33
  18.0 0.8 iota_compare_fusion
  18.8 0.8 iota_compare_fusion.1
  19.7 1.6 collective-permute-start.3
  21.2 1.5 collective-permute-start.4
  22.8 0.5 collective-permute-start.5
  23.5 1.4 collective-permute-start.15
  24.9 1.1 fusion.refs_8_.refs_3_
  26.0 4.4 %collective-permute-done.15 = bf16[32,2048]{1,0:T(8,128)(2,1)S(1)} collective-permute-done((bf16[32,2048]{1,0:T(8,128)(2,1)S(1)}, bf16[32,2048]{1,0:T(8,128)(2,1)S(1)}, u32[]{:S(2)}, u32[]{:S(2)}) %collective-permute-start.15) | collective-permute-done | bytes 131104 | tf_op jit(solution)/shard_map/ppermute | solution.py:33
  30.5 0.5 collective-permute-start.7
  31.6 5.8 %collective-permute-done.16.refs_10_ = bf16[4,80,512]{2,1,0:T(8,128)(2,1)S(1)} collective-permute-done((bf16[4,80,512]{2,1,0:T(8,128)(2,1)S(1)}, bf16[4,80,512]{2,1,0:T(8,128)(2,1)S(1)}, u32[]{:S(2)}, u32[]{:S(2)}) %collective-permute-start.16) | collective-permute-done | bytes 327712 | tf_op jit(solution)/shard_map/ppermute | solution.py:33
  37.4 1.6 collective-permute-start.17
  39.0 1.5 collective-permute-start.18
  40.5 0.5 collective-permute-start.19
  41.0 1.9 %collective-permute-start.21 = (bf16[4,80,512]{2,1,0:T(8,128)(2,1)S(1)}, bf16[4,80,512]{2,1,0:T(8,128)(2,1)S(1)}, u32[]{:S(2)}, u32[]{:S(2)}) collective-permute-start(bf16[4,80,512]{2,1,0:T(8,128)(2,1)S(1)} %collective-permute-done.16.refs_10_), channel_id=1, source_target_pairs={{0,8},{1,9},{2,10},{3,11},{4,12},{5,13},{6,14},{7,15},{8,0},{9,1},... | collective-permute-start | bytes 983048 | tf_op jit(solution)/shard_map/ppermute | solution.py:33
  43.0 14.8 %shard_map.263 = (bf16[512,1664]{1,0:T(8,128)(2,1)}, f32[16,512]{1,0:T(8,128)}, f32[8,2048]{1,0:T(8,128)}, f32[256,512]{1,0:T(8,128)}, bf16[2048,512]{1,0:T(8,12...) custom-call(s32[1]{0:T(128)} %bitcast.me_ref, ...), custom_call_target="tpu_custom_call" | custom-call | flops 16499999744 | bytes 1000 | tf_op jit(solution)/shard_map/pallas_call | solution.py:257
  57.9 5.2 %collective-permute-done.19.refs_3_ = bf16[4,32,2048]{2,1,0:T(8,128)(2,1)S(1)} collective-permute-done((bf16[4,32,2048]{2,1,0:T(8,128)(2,1)S(1)}, bf16[4,32,2048]{2,1,0:T(8,128)(2,1)S(1)}, u32[]{:S(2)}, u32[]{:S(2)}) %collective-permute-start.19) | collective-permute-done | bytes 524320 | tf_op jit(solution)/shard_map/ppermute | solution.py:33
  63.0 0.5 collective-permute-start.27
  63.6 0.4 collective-permute-start.22
  64.1 0.5 collective-permute-done.26.refs_12_
  65.3 0.8 collective-permute-done.28.refs_14_
  66.2 2.9 %collective-permute-done.29.refs_15_ = bf16[4,80,512]{2,1,0:T(8,128)(2,1)S(1)} collective-permute-done((bf16[4,80,512]{2,1,0:T(8,128)(2,1)S(1)}, bf16[4,80,512]{2,1,0:T(8,128)(2,1)S(1)}, u32[]{:S(2)}, u32[]{:S(2)}) %collective-permute-start.29) | collective-permute-done | bytes 327712 | tf_op jit(solution)/shard_map/ppermute | solution.py:33
  69.2 0.6 copy-done.18
  70.5 14.5 %shard_map.264 = (bf16[256,2048]{1,0:T(8,128)(2,1)}, f32[256,512]{1,0:T(8,128)}, bf16[256,512]{1,0:T(8,128)(2,1)}, f32[8,2048]{1,0:T(8,128)}, f32[8,512]{1,0:T(8...) custom-call(s32[1]{0:T(128)} %bitcast.me_ref, ...), custom_call_target="tpu_custom_call" | custom-call | flops 13200000000 | bytes 1000 | tf_op jit(solution)/shard_map/pallas_call | solution.py:257
  85.6 7.7 %shard_map.265 = (bf16[2048,1024]{1,0:T(8,128)(2,1)}, bf16[256,512]{1,0:T(8,128)(2,1)}, f32[256,512]{1,0:T(8,128)}) custom-call(s32[1]{0:T(128)} %bitcast.me_ref, bf16[256,512]{1,0:T(8,128)(2,1)} %get-tuple-element.90.refs_0_, bf16[256,512]{1,0:T(8,128)(2,1)} %get-tuple-element.91.refs_1_, bf16[2048,256]{1,0:T(8,128)(2,1)} %get-tuple-element.92.refs_2_, ...), custom_call_target="tpu_custom_call" | custom-call | flops 8800000000 | bytes 1000 | tf_op jit(solution)/shard_map/pallas_call | solution.py:257
  93.4 3.2 %add_convert_fusion.refs_15_ = bf16[8,48,2048]{2,1,0:T(8,128)(2,1)} fusion(bf16[8,48,2048]{2,1,0:T(8,128)(2,1)} %collective-permute-done.30, bf16[16,48,2048]{2,1,0:T(8,128)(2,1)S(1)} %copy-done), kind=kLoop, calls=%fused_computation | loop fusion | flops 3145728 | bytes 4718592 | tf_op jit(solution)/shard_map/convert_element_type | solution.py:72
  96.6 1.5 collective-permute-start.35
  98.1 15.0 %shard_map.266 = (bf16[2048,512]{1,0:T(8,128)(2,1)}, bf16[16,16,2176]{2,1,0:T(8,128)(2,1)}, bf16[8,16,2176]{2,1,0:T(8,128)(2,1)}, bf16[8,16,2176]{2,1,0:T(8,128)(2,1)}) custom-call(s32[1]{0:T(128)} %bitcast.me_ref, f32[16,512]{1,0:T(8,128)} %get-tuple-element.87.refs_19_.refs_0_, f32[256,512]{1,0:T(8,128)} %get-tuple-element.97.refs_1_, ...), custom_call_target="tpu_custom_call" | custom-call | flops 19800000512 | bytes 1000 | tf_op jit(solution)/shard_map/pallas_call | solution.py:257
  113.2 0.5 collective-permute-start.31
  113.7 1.7 collective-permute-done.32
  115.4 1.2 add_convert_fusion.2
  116.6 1.0 collective-permute-start.33
  117.6 1.5 add_convert_fusion.1
  119.1 1.3 collective-permute-start.37
  120.4 9.6 %collective-permute-done.33 = bf16[8,16,2176]{2,1,0:T(8,128)(2,1)S(1)} collective-permute-done((bf16[8,16,2176]{2,1,0:T(8,128)(2,1)S(1)}, bf16[8,16,2176]{2,1,0:T(8,128)(2,1)S(1)}, u32[]{:S(2)}, u32[]{:S(2)}) %collective-permute-start.33) | collective-permute-done | bytes 557088 | tf_op jit(solution)/shard_map/ppermute | solution.py:33
  130.2 2.6 %collective-permute-start.36 = (bf16[4,16,2176]{2,1,0:T(8,128)(2,1)S(1)}, bf16[4,16,2176]{2,1,0:T(8,128)(2,1)S(1)}, u32[]{:S(2)}, u32[]{:S(2)}) collective-permute-start(bf16[4,16,2176]{2,1,0:T(8,128)(2,1)S(1)} %add_convert_fusion.4), channel_id=1, source_target_pairs={{0,2},{1,5},{2,0},{3,7},{4,6},{5,1},{6,4},{7,3},{8,10},{9,13},{10,... | collective-permute-start | bytes 835592 | tf_op jit(solution)/shard_map/ppermute | solution.py:33
  132.7 1.0 collective-permute-done.37
  133.8 1.2 add_convert_fusion.3
  135.0 1.7 %collective-permute-start.39 = (bf16[2,48,2048]{2,1,0:T(8,128)(2,1)S(1)}, bf16[2,48,2048]{2,1,0:T(8,128)(2,1)S(1)}, u32[]{:S(2)}, u32[]{:S(2)}) collective-permute-start(bf16[2,48,2048]{2,1,0:T(8,128)(2,1)S(1)} %add_convert_fusion.3), channel_id=1, source_target_pairs={{0,8},{1,9},{2,10},{3,11},{4,12},{5,13},{6,14},{7,15},{8,0},{9,1},... | collective-permute-start | bytes 1179656 | tf_op jit(solution)/shard_map/ppermute | solution.py:33
  136.7 0.5 collective-permute-done.36
  137.3 1.7 %collective-permute-start.38 = (bf16[2,16,2176]{2,1,0:T(8,128)(2,1)S(1)}, bf16[2,16,2176]{2,1,0:T(8,128)(2,1)S(1)}, u32[]{:S(2)}, u32[]{:S(2)}) collective-permute-start(bf16[2,16,2176]{2,1,0:T(8,128)(2,1)S(1)} %add_convert_fusion.6), channel_id=1, source_target_pairs={{0,8},{1,9},{2,10},{3,11},{4,12},{5,13},{6,14},{7,15},{8,0},{9,1},... | collective-permute-start | bytes 417800 | tf_op jit(solution)/shard_map/ppermute | solution.py:33
  139.1 8.0 %collective-permute-done.39 = bf16[2,48,2048]{2,1,0:T(8,128)(2,1)S(1)} collective-permute-done((bf16[2,48,2048]{2,1,0:T(8,128)(2,1)S(1)}, bf16[2,48,2048]{2,1,0:T(8,128)(2,1)S(1)}, u32[]{:S(2)}, u32[]{:S(2)}) %collective-permute-start.39) | collective-permute-done | bytes 393248 | tf_op jit(solution)/shard_map/ppermute | solution.py:33
  147.0 1.3 add_bitcast_fusion
  148.4 1.7 collective-permute-done.38
  150.1 2.1 %collective-permute-start.40 = (bf16[16,2176]{1,0:T(8,128)(2,1)S(1)}, bf16[16,2176]{1,0:T(8,128)(2,1)S(1)}, u32[]{:S(2)}, u32[]{:S(2)}) collective-permute-start(bf16[16,2176]{1,0:T(8,128)(2,1)S(1)} %get-tuple-element.126), channel_id=1, source_target_pairs={{0,16},{1,17},{2,18},{3,19},{4,20},{5,21},{6,22},{7,23},{8,24},{9,... | collective-permute-start | bytes 208904 | tf_op jit(solution)/shard_map/ppermute | solution.py:33
  152.2 0.9 collective-permute-start.41
  153.1 8.4 %collective-permute-done.40 = bf16[16,2176]{1,0:T(8,128)(2,1)S(1)} collective-permute-done((bf16[16,2176]{1,0:T(8,128)(2,1)S(1)}, bf16[16,2176]{1,0:T(8,128)(2,1)S(1)}, u32[]{:S(2)}, u32[]{:S(2)}) %collective-permute-start.40) | collective-permute-done | bytes 69664 | tf_op jit(solution)/shard_map/ppermute | solution.py:33
  161.5 0.7 convert_add_fusion.1
  162.2 0.6 dynamic-slice_bitcast_fusion.5
  162.7 0.7 constant_dynamic-slice_fusion
  163.4 0.6 dynamic-slice_bitcast_fusion
  164.0 0.6 convert_add_fusion.2
  164.6 0.7 collective-permute-done.41
  165.4 0.7 fusion.3
  166.1 0.7 pad_maximum_fusion.3
  (106 shorter events, 4.1 us)
Async XLA Ops:
  1.6 11.6 %collective-permute-start.2 = (bf16[16,1664]{1,0:T(8,128)(2,1)S(1)}, bf16[16,1664]{1,0:T(8,128)(2,1)S(1)}, u32[]{:S(2)}, u32[]{:S(2)}) collective-permute-start(bf16[16,1664]{1,0:T(8,128)(2,1)S(1)} %pad_add_fusion.2), channel_id=1, source_target_pairs={{0,24},{1,25},{2,26},{3,27},{4,28},{5,29},{6,30},{7,31},{8,16},{9,... | collective-permute-start | bytes 159752 | tf_op jit(solution)/shard_map/ppermute | solution.py:33
  6.7 6.9 %collective-permute-start = (bf16[16,1664]{1,0:T(8,128)(2,1)S(1)}, bf16[16,1664]{1,0:T(8,128)(2,1)S(1)}, u32[]{:S(2)}, u32[]{:S(2)}) collective-permute-start(bf16[16,1664]{1,0:T(8,128)(2,1)S(1)} %pad_add_fusion.2), channel_id=1, source_target_pairs={{0,8},{1,9},{2,10},{3,11},{4,12},{5,13},{6,14},{7,15},{8,0},{9,1},... | collective-permute-start | bytes 159752 | tf_op jit(solution)/shard_map/ppermute | solution.py:33
  6.7 9.2 %collective-permute-start.1 = (bf16[16,1664]{1,0:T(8,128)(2,1)S(1)}, bf16[16,1664]{1,0:T(8,128)(2,1)S(1)}, u32[]{:S(2)}, u32[]{:S(2)}) collective-permute-start(bf16[16,1664]{1,0:T(8,128)(2,1)S(1)} %pad_add_fusion.2), channel_id=1, source_target_pairs={{0,16},{1,17},{2,18},{3,19},{4,20},{5,21},{6,22},{7,23},{8,24},{9,... | collective-permute-start | bytes 159752 | tf_op jit(solution)/shard_map/ppermute | solution.py:33
  8.2 11.5 %collective-permute-start.10 = (bf16[80,512]{1,0:T(8,128)(2,1)S(1)}, bf16[80,512]{1,0:T(8,128)(2,1)S(1)}, u32[]{:S(2)}, u32[]{:S(2)}) collective-permute-start(bf16[80,512]{1,0:T(8,128)(2,1)S(1)} %pad_add_fusion.1), channel_id=1, source_target_pairs={{0,2},{1,5},{2,0},{3,7},{4,6},{5,1},{6,4},{7,3},{8,10},{9,13},{10,... | collective-permute-start | bytes 245768 | tf_op jit(solution)/shard_map/ppermute | solution.py:33
  9.8 11.4 %collective-permute-start.11 = (bf16[80,512]{1,0:T(8,128)(2,1)S(1)}, bf16[80,512]{1,0:T(8,128)(2,1)S(1)}, u32[]{:S(2)}, u32[]{:S(2)}) collective-permute-start(bf16[80,512]{1,0:T(8,128)(2,1)S(1)} %pad_add_fusion.1), channel_id=1, source_target_pairs={{0,4},{1,3},{2,6},{3,1},{4,0},{5,7},{6,2},{7,5},{8,12},{9,11},{10,... | collective-permute-start | bytes 245768 | tf_op jit(solution)/shard_map/ppermute | solution.py:33
  13.2 9.6 %collective-permute-start.12 = (bf16[80,512]{1,0:T(8,128)(2,1)S(1)}, bf16[80,512]{1,0:T(8,128)(2,1)S(1)}, u32[]{:S(2)}, u32[]{:S(2)}) collective-permute-start(bf16[80,512]{1,0:T(8,128)(2,1)S(1)} %pad_add_fusion.1), channel_id=1, source_target_pairs={{0,6},{1,7},{2,4},{3,5},{4,2},{5,3},{6,0},{7,1},{8,14},{9,15},{10,... | collective-permute-start | bytes 245768 | tf_op jit(solution)/shard_map/ppermute | solution.py:33
  13.6 9.7 %collective-permute-start.14 = (bf16[32,2048]{1,0:T(8,128)(2,1)S(1)}, bf16[32,2048]{1,0:T(8,128)(2,1)S(1)}, u32[]{:S(2)}, u32[]{:S(2)}) collective-permute-start(bf16[32,2048]{1,0:T(8,128)(2,1)S(1)} %pad_add_fusion), channel_id=1, source_target_pairs={{0,16},{1,17},{2,18},{3,19},{4,20},{5,21},{6,22},{7,23},{8,24},{9,... | collective-permute-start | bytes 393224 | tf_op jit(solution)/shard_map/ppermute | solution.py:33
  15.9 7.6 %collective-permute-start.13 = (bf16[32,2048]{1,0:T(8,128)(2,1)S(1)}, bf16[32,2048]{1,0:T(8,128)(2,1)S(1)}, u32[]{:S(2)}, u32[]{:S(2)}) collective-permute-start(bf16[32,2048]{1,0:T(8,128)(2,1)S(1)} %pad_add_fusion), channel_id=1, source_target_pairs={{0,8},{1,9},{2,10},{3,11},{4,12},{5,13},{6,14},{7,15},{8,0},{9,1},... | collective-permute-start | bytes 393224 | tf_op jit(solution)/shard_map/ppermute | solution.py:33
  17.9 25.0 %copy-start.4 = (bf16[4,16,1664]{2,1,0:T(8,128)(2,1)}, bf16[4,16,1664]{2,1,0:T(8,128)(2,1)S(1)}, u32[]{:S(2)}) copy-start(bf16[4,16,1664]{2,1,0:T(8,128)(2,1)S(1)} %pad_maximum_fusion.2.refs_0_) | copy-start | bytes 638980
  19.7 10.8 %collective-permute-start.3 = (bf16[4,16,1664]{2,1,0:T(8,128)(2,1)S(1)}, bf16[4,16,1664]{2,1,0:T(8,128)(2,1)S(1)}, u32[]{:S(2)}, u32[]{:S(2)}) collective-permute-start(bf16[4,16,1664]{2,1,0:T(8,128)(2,1)S(1)} %pad_maximum_fusion.2.refs_0_), channel_id=1, source_target_pairs={{0,2},{1,5},{2,0},{3,7},{4,6},{5,1},{6,4},{7,3},{8,10},{9,13},{10,... | collective-permute-start | bytes 638984 | tf_op jit(solution)/shard_map/ppermute | solution.py:33
  21.2 9.7 %collective-permute-start.4 = (bf16[4,16,1664]{2,1,0:T(8,128)(2,1)S(1)}, bf16[4,16,1664]{2,1,0:T(8,128)(2,1)S(1)}, u32[]{:S(2)}, u32[]{:S(2)}) collective-permute-start(bf16[4,16,1664]{2,1,0:T(8,128)(2,1)S(1)} %pad_maximum_fusion.2.refs_0_), channel_id=1, source_target_pairs={{0,4},{1,3},{2,6},{3,1},{4,0},{5,7},{6,2},{7,5},{8,12},{9,11},{10,... | collective-permute-start | bytes 638984 | tf_op jit(solution)/shard_map/ppermute | solution.py:33
  22.8 8.3 %collective-permute-start.5 = (bf16[4,16,1664]{2,1,0:T(8,128)(2,1)S(1)}, bf16[4,16,1664]{2,1,0:T(8,128)(2,1)S(1)}, u32[]{:S(2)}, u32[]{:S(2)}) collective-permute-start(bf16[4,16,1664]{2,1,0:T(8,128)(2,1)S(1)} %pad_maximum_fusion.2.refs_0_), channel_id=1, source_target_pairs={{0,6},{1,7},{2,4},{3,5},{4,2},{5,3},{6,0},{7,1},{8,14},{9,15},{10,... | collective-permute-start | bytes 638984 | tf_op jit(solution)/shard_map/ppermute | solution.py:33
  23.3 39.8 %copy-start.3 = (bf16[4,80,512]{2,1,0:T(8,128)(2,1)}, bf16[4,80,512]{2,1,0:T(8,128)(2,1)S(1)}, u32[]{:S(2)}) copy-start(bf16[4,80,512]{2,1,0:T(8,128)(2,1)S(1)} %pad_maximum_fusion.1.refs_8_) | copy-start | bytes 983044
  23.3 14.1 %collective-permute-start.16 = (bf16[4,80,512]{2,1,0:T(8,128)(2,1)S(1)}, bf16[4,80,512]{2,1,0:T(8,128)(2,1)S(1)}, u32[]{:S(2)}, u32[]{:S(2)}) collective-permute-start(bf16[4,80,512]{2,1,0:T(8,128)(2,1)S(1)} %pad_maximum_fusion.1.refs_8_), channel_id=1, source_target_pairs={{0,16},{1,17},{2,18},{3,19},{4,20},{5,21},{6,22},{7,23},{8,24},{9,... | collective-permute-start | bytes 983048 | tf_op jit(solution)/shard_map/ppermute | solution.py:33
  23.5 7.0 %collective-permute-start.15 = (bf16[32,2048]{1,0:T(8,128)(2,1)S(1)}, bf16[32,2048]{1,0:T(8,128)(2,1)S(1)}, u32[]{:S(2)}, u32[]{:S(2)}) collective-permute-start(bf16[32,2048]{1,0:T(8,128)(2,1)S(1)} %collective-permute-done.14), channel_id=1, source_target_pairs={{0,8},{1,9},{2,10},{3,11},{4,12},{5,13},{6,14},{7,15},{8,0},{9,1},... | collective-permute-start | bytes 393224 | tf_op jit(solution)/shard_map/ppermute | solution.py:33
  30.5 6.9 %collective-permute-start.6 = (bf16[4,16,1664]{2,1,0:T(8,128)(2,1)S(1)}, bf16[4,16,1664]{2,1,0:T(8,128)(2,1)S(1)}, u32[]{:S(2)}, u32[]{:S(2)}) collective-permute-start(bf16[4,16,1664]{2,1,0:T(8,128)(2,1)S(1)} %pad_maximum_fusion.2.refs_0_), channel_id=1, source_target_pairs={{0,1},{1,0},{2,3},{3,2},{4,5},{5,4},{6,7},{7,6},{8,9},{9,8},{10,11... | collective-permute-start | bytes 638984 | tf_op jit(solution)/shard_map/ppermute | solution.py:33
  30.5 12.5 %copy-start.19 = (bf16[4,16,1664]{2,1,0:T(8,128)(2,1)}, bf16[4,16,1664]{2,1,0:T(8,128)(2,1)S(1)}, u32[]{:S(2)}) copy-start(bf16[4,16,1664]{2,1,0:T(8,128)(2,1)S(1)} %collective-permute-done.3.refs_1_) | copy-start | bytes 638980
  30.5 8.5 %collective-permute-start.7 = (bf16[4,16,1664]{2,1,0:T(8,128)(2,1)S(1)}, bf16[4,16,1664]{2,1,0:T(8,128)(2,1)S(1)}, u32[]{:S(2)}, u32[]{:S(2)}) collective-permute-start(bf16[4,16,1664]{2,1,0:T(8,128)(2,1)S(1)} %collective-permute-done.3.refs_1_), channel_id=1, source_target_pairs={{0,1},{1,0},{2,3},{3,2},{4,5},{5,4},{6,7},{7,6},{8,9},{9,8},{10,11... | collective-permute-start | bytes 638984 | tf_op jit(solution)/shard_map/ppermute | solution.py:33
  31.0 11.9 %copy-start.20 = (bf16[4,16,1664]{2,1,0:T(8,128)(2,1)}, bf16[4,16,1664]{2,1,0:T(8,128)(2,1)S(1)}, u32[]{:S(2)}) copy-start(bf16[4,16,1664]{2,1,0:T(8,128)(2,1)S(1)} %collective-permute-done.4.refs_2_) | copy-start | bytes 638980
  31.0 9.5 %collective-permute-start.8 = (bf16[4,16,1664]{2,1,0:T(8,128)(2,1)S(1)}, bf16[4,16,1664]{2,1,0:T(8,128)(2,1)S(1)}, u32[]{:S(2)}, u32[]{:S(2)}) collective-permute-start(bf16[4,16,1664]{2,1,0:T(8,128)(2,1)S(1)} %collective-permute-done.4.refs_2_), channel_id=1, source_target_pairs={{0,1},{1,0},{2,3},{3,2},{4,5},{5,4},{6,7},{7,6},{8,9},{9,8},{10,11... | collective-permute-start | bytes 638984 | tf_op jit(solution)/shard_map/ppermute | solution.py:33
  31.1 11.9 %copy-start.21 = (bf16[4,16,1664]{2,1,0:T(8,128)(2,1)}, bf16[4,16,1664]{2,1,0:T(8,128)(2,1)S(1)}, u32[]{:S(2)}) copy-start(bf16[4,16,1664]{2,1,0:T(8,128)(2,1)S(1)} %collective-permute-done.5.refs_3_) | copy-start | bytes 638980
  31.1 9.9 %collective-permute-start.9 = (bf16[4,16,1664]{2,1,0:T(8,128)(2,1)S(1)}, bf16[4,16,1664]{2,1,0:T(8,128)(2,1)S(1)}, u32[]{:S(2)}, u32[]{:S(2)}) collective-permute-start(bf16[4,16,1664]{2,1,0:T(8,128)(2,1)S(1)} %collective-permute-done.5.refs_3_), channel_id=1, source_target_pairs={{0,1},{1,0},{2,3},{3,2},{4,5},{5,4},{6,7},{7,6},{8,9},{9,8},{10,11... | collective-permute-start | bytes 638984 | tf_op jit(solution)/shard_map/ppermute | solution.py:33
  31.6 11.4 %copy-start.2 = (bf16[4,32,2048]{2,1,0:T(8,128)(2,1)}, bf16[4,32,2048]{2,1,0:T(8,128)(2,1)S(1)}, u32[]{:S(2)}) copy-start(bf16[4,32,2048]{2,1,0:T(8,128)(2,1)S(1)} %pad_maximum_fusion.refs_10_.refs_0_) | copy-start | bytes 1572868
  37.4 26.2 %copy-start.12 = (bf16[4,80,512]{2,1,0:T(8,128)(2,1)}, bf16[4,80,512]{2,1,0:T(8,128)(2,1)S(1)}, u32[]{:S(2)}) copy-start(bf16[4,80,512]{2,1,0:T(8,128)(2,1)S(1)} %collective-permute-done.16.refs_10_) | copy-start | bytes 983044
  37.4 20.4 %collective-permute-start.20 = (bf16[4,80,512]{2,1,0:T(8,128)(2,1)S(1)}, bf16[4,80,512]{2,1,0:T(8,128)(2,1)S(1)}, u32[]{:S(2)}, u32[]{:S(2)}) collective-permute-start(bf16[4,80,512]{2,1,0:T(8,128)(2,1)S(1)} %pad_maximum_fusion.1.refs_8_), channel_id=1, source_target_pairs={{0,8},{1,9},{2,10},{3,11},{4,12},{5,13},{6,14},{7,15},{8,0},{9,1},... | collective-permute-start | bytes 983048 | tf_op jit(solution)/shard_map/ppermute | solution.py:33
  37.4 5.6 %copy-start.22 = (bf16[4,16,1664]{2,1,0:T(8,128)(2,1)}, bf16[4,16,1664]{2,1,0:T(8,128)(2,1)S(1)}, u32[]{:S(2)}) copy-start(bf16[4,16,1664]{2,1,0:T(8,128)(2,1)S(1)} %collective-permute-done.6.refs_4_) | copy-start | bytes 638980
  37.4 20.4 %collective-permute-start.17 = (bf16[4,32,2048]{2,1,0:T(8,128)(2,1)S(1)}, bf16[4,32,2048]{2,1,0:T(8,128)(2,1)S(1)}, u32[]{:S(2)}, u32[]{:S(2)}) collective-permute-start(bf16[4,32,2048]{2,1,0:T(8,128)(2,1)S(1)} %pad_maximum_fusion.refs_10_.refs_0_), channel_id=1, source_target_pairs={{0,2},{1,5},{2,0},{3,7},{4,6},{5,1},{6,4},{7,3},{8,10},{9,13},{10,... | collective-permute-start | bytes 1572872 | tf_op jit(solution)/shard_map/ppermute | solution.py:33
  39.0 4.0 %copy-start.23 = (bf16[4,16,1664]{2,1,0:T(8,128)(2,1)}, bf16[4,16,1664]{2,1,0:T(8,128)(2,1)S(1)}, u32[]{:S(2)}) copy-start(bf16[4,16,1664]{2,1,0:T(8,128)(2,1)S(1)} %collective-permute-done.7.refs_5_) | copy-start | bytes 638980
  39.0 18.9 %collective-permute-start.18 = (bf16[4,32,2048]{2,1,0:T(8,128)(2,1)S(1)}, bf16[4,32,2048]{2,1,0:T(8,128)(2,1)S(1)}, u32[]{:S(2)}, u32[]{:S(2)}) collective-permute-start(bf16[4,32,2048]{2,1,0:T(8,128)(2,1)S(1)} %pad_maximum_fusion.refs_10_.refs_0_), channel_id=1, source_target_pairs={{0,4},{1,3},{2,6},{3,1},{4,0},{5,7},{6,2},{7,5},{8,12},{9,11},{10,... | collective-permute-start | bytes 1572872 | tf_op jit(solution)/shard_map/ppermute | solution.py:33
  40.5 2.5 %copy-start.24 = (bf16[4,16,1664]{2,1,0:T(8,128)(2,1)}, bf16[4,16,1664]{2,1,0:T(8,128)(2,1)S(1)}, u32[]{:S(2)}) copy-start(bf16[4,16,1664]{2,1,0:T(8,128)(2,1)S(1)} %collective-permute-done.8.refs_6_) | copy-start | bytes 638980
  40.5 22.5 %collective-permute-start.19 = (bf16[4,32,2048]{2,1,0:T(8,128)(2,1)S(1)}, bf16[4,32,2048]{2,1,0:T(8,128)(2,1)S(1)}, u32[]{:S(2)}, u32[]{:S(2)}) collective-permute-start(bf16[4,32,2048]{2,1,0:T(8,128)(2,1)S(1)} %pad_maximum_fusion.refs_10_.refs_0_), channel_id=1, source_target_pairs={{0,6},{1,7},{2,4},{3,5},{4,2},{5,3},{6,0},{7,1},{8,14},{9,15},{10,... | collective-permute-start | bytes 1572872 | tf_op jit(solution)/shard_map/ppermute | solution.py:33
  41.0 2.0 %copy-start.25 = (bf16[4,16,1664]{2,1,0:T(8,128)(2,1)}, bf16[4,16,1664]{2,1,0:T(8,128)(2,1)S(1)}, u32[]{:S(2)}) copy-start(bf16[4,16,1664]{2,1,0:T(8,128)(2,1)S(1)} %collective-permute-done.9.refs_7_) | copy-start | bytes 638980
  41.0 16.8 %collective-permute-start.21 = (bf16[4,80,512]{2,1,0:T(8,128)(2,1)S(1)}, bf16[4,80,512]{2,1,0:T(8,128)(2,1)S(1)}, u32[]{:S(2)}, u32[]{:S(2)}) collective-permute-start(bf16[4,80,512]{2,1,0:T(8,128)(2,1)S(1)} %collective-permute-done.16.refs_10_), channel_id=1, source_target_pairs={{0,8},{1,9},{2,10},{3,11},{4,12},{5,13},{6,14},{7,15},{8,0},{9,1},... | collective-permute-start | bytes 983048 | tf_op jit(solution)/shard_map/ppermute | solution.py:33
  57.8 11.4 %copy-start.13 = (bf16[4,80,512]{2,1,0:T(8,128)(2,1)}, bf16[4,80,512]{2,1,0:T(8,128)(2,1)S(1)}, u32[]{:S(2)}) copy-start(bf16[4,80,512]{2,1,0:T(8,128)(2,1)S(1)} %collective-permute-done.20.refs_9_) | copy-start | bytes 983044
  57.8 11.4 %copy-start.14 = (bf16[4,80,512]{2,1,0:T(8,128)(2,1)}, bf16[4,80,512]{2,1,0:T(8,128)(2,1)S(1)}, u32[]{:S(2)}) copy-start(bf16[4,80,512]{2,1,0:T(8,128)(2,1)S(1)} %collective-permute-done.21.refs_11_) | copy-start | bytes 983044
  57.8 11.3 %copy-start.5 = (bf16[4,32,2048]{2,1,0:T(8,128)(2,1)}, bf16[4,32,2048]{2,1,0:T(8,128)(2,1)S(1)}, u32[]{:S(2)}) copy-start(bf16[4,32,2048]{2,1,0:T(8,128)(2,1)S(1)} %collective-permute-done.17.refs_1_) | copy-start | bytes 1572868
  57.8 11.3 %copy-start.6 = (bf16[4,32,2048]{2,1,0:T(8,128)(2,1)}, bf16[4,32,2048]{2,1,0:T(8,128)(2,1)S(1)}, u32[]{:S(2)}) copy-start(bf16[4,32,2048]{2,1,0:T(8,128)(2,1)S(1)} %collective-permute-done.18.refs_2_) | copy-start | bytes 1572868
  63.0 6.1 %copy-start.7 = (bf16[4,32,2048]{2,1,0:T(8,128)(2,1)}, bf16[4,32,2048]{2,1,0:T(8,128)(2,1)S(1)}, u32[]{:S(2)}) copy-start(bf16[4,32,2048]{2,1,0:T(8,128)(2,1)S(1)} %collective-permute-done.19.refs_3_) | copy-start | bytes 1572868
  63.0 1.6 collective-permute-start.26
  63.0 2.1 %collective-permute-start.27 = (bf16[4,80,512]{2,1,0:T(8,128)(2,1)S(1)}, bf16[4,80,512]{2,1,0:T(8,128)(2,1)S(1)}, u32[]{:S(2)}, u32[]{:S(2)}) collective-permute-start(bf16[4,80,512]{2,1,0:T(8,128)(2,1)S(1)} %collective-permute-done.20.refs_9_), channel_id=1, source_target_pairs={{0,1},{1,0},{2,3},{3,2},{4,5},{5,4},{6,7},{7,6},{8,9},{9,8},{10,11... | collective-permute-start | bytes 983048 | tf_op jit(solution)/shard_map/ppermute | solution.py:33
  63.6 2.5 %collective-permute-start.28 = (bf16[4,80,512]{2,1,0:T(8,128)(2,1)S(1)}, bf16[4,80,512]{2,1,0:T(8,128)(2,1)S(1)}, u32[]{:S(2)}, u32[]{:S(2)}) collective-permute-start(bf16[4,80,512]{2,1,0:T(8,128)(2,1)S(1)} %collective-permute-done.16.refs_10_), channel_id=1, source_target_pairs={{0,1},{1,0},{2,3},{3,2},{4,5},{5,4},{6,7},{7,6},{8,9},{9,8},{10,11... | collective-permute-start | bytes 983048 | tf_op jit(solution)/shard_map/ppermute | solution.py:33
  63.6 5.5 %collective-permute-start.22 = (bf16[4,32,2048]{2,1,0:T(8,128)(2,1)}, bf16[4,32,2048]{2,1,0:T(8,128)(2,1)S(1)}, u32[]{:S(2)}, u32[]{:S(2)}) collective-permute-start(bf16[4,32,2048]{2,1,0:T(8,128)(2,1)} %copy-done.2), channel_id=1, source_target_pairs={{0,1},{1,0},{2,3},{3,2},{4,5},{5,4},{6,7},{7,6},{8,9},{9,8},{10,11... | collective-permute-start | bytes 1572872 | tf_op jit(solution)/shard_map/ppermute | solution.py:33
  64.1 5.0 %collective-permute-start.23 = (bf16[4,32,2048]{2,1,0:T(8,128)(2,1)S(1)}, bf16[4,32,2048]{2,1,0:T(8,128)(2,1)S(1)}, u32[]{:S(2)}, u32[]{:S(2)}) collective-permute-start(bf16[4,32,2048]{2,1,0:T(8,128)(2,1)S(1)} %collective-permute-done.17.refs_1_), channel_id=1, source_target_pairs={{0,1},{1,0},{2,3},{3,2},{4,5},{5,4},{6,7},{7,6},{8,9},{9,8},{10,11... | collective-permute-start | bytes 1572872 | tf_op jit(solution)/shard_map/ppermute | solution.py:33
  64.7 4.5 %copy-start.15 = (bf16[4,80,512]{2,1,0:T(8,128)(2,1)}, bf16[4,80,512]{2,1,0:T(8,128)(2,1)S(1)}, u32[]{:S(2)}) copy-start(bf16[4,80,512]{2,1,0:T(8,128)(2,1)S(1)} %collective-permute-done.26.refs_12_) | copy-start | bytes 983044
  64.7 4.4 %collective-permute-start.24 = (bf16[4,32,2048]{2,1,0:T(8,128)(2,1)S(1)}, bf16[4,32,2048]{2,1,0:T(8,128)(2,1)S(1)}, u32[]{:S(2)}, u32[]{:S(2)}) collective-permute-start(bf16[4,32,2048]{2,1,0:T(8,128)(2,1)S(1)} %collective-permute-done.18.refs_2_), channel_id=1, source_target_pairs={{0,1},{1,0},{2,3},{3,2},{4,5},{5,4},{6,7},{7,6},{8,9},{9,8},{10,11... | collective-permute-start | bytes 1572872 | tf_op jit(solution)/shard_map/ppermute | solution.py:33
  65.1 4.1 %copy-start.16 = (bf16[4,80,512]{2,1,0:T(8,128)(2,1)}, bf16[4,80,512]{2,1,0:T(8,128)(2,1)S(1)}, u32[]{:S(2)}) copy-start(bf16[4,80,512]{2,1,0:T(8,128)(2,1)S(1)} %collective-permute-done.27.refs_13_) | copy-start | bytes 983044
  65.1 4.0 %collective-permute-start.25 = (bf16[4,32,2048]{2,1,0:T(8,128)(2,1)S(1)}, bf16[4,32,2048]{2,1,0:T(8,128)(2,1)S(1)}, u32[]{:S(2)}, u32[]{:S(2)}) collective-permute-start(bf16[4,32,2048]{2,1,0:T(8,128)(2,1)S(1)} %collective-permute-done.19.refs_3_), channel_id=1, source_target_pairs={{0,1},{1,0},{2,3},{3,2},{4,5},{5,4},{6,7},{7,6},{8,9},{9,8},{10,11... | collective-permute-start | bytes 1572872 | tf_op jit(solution)/shard_map/ppermute | solution.py:33
  66.1 3.1 %copy-start.17 = (bf16[4,80,512]{2,1,0:T(8,128)(2,1)}, bf16[4,80,512]{2,1,0:T(8,128)(2,1)S(1)}, u32[]{:S(2)}) copy-start(bf16[4,80,512]{2,1,0:T(8,128)(2,1)S(1)} %collective-permute-done.28.refs_14_) | copy-start | bytes 983044
  66.1 3.0 %collective-permute-start.29 = (bf16[4,80,512]{2,1,0:T(8,128)(2,1)S(1)}, bf16[4,80,512]{2,1,0:T(8,128)(2,1)S(1)}, u32[]{:S(2)}, u32[]{:S(2)}) collective-permute-start(bf16[4,80,512]{2,1,0:T(8,128)(2,1)S(1)} %collective-permute-done.21.refs_11_), channel_id=1, source_target_pairs={{0,1},{1,0},{2,3},{3,2},{4,5},{5,4},{6,7},{7,6},{8,9},{9,8},{10,11... | collective-permute-start | bytes 983048 | tf_op jit(solution)/shard_map/ppermute | solution.py:33
  69.1 1.4 copy-start.11
  85.0 8.3 %collective-permute-start.30 = (bf16[8,48,2048]{2,1,0:T(8,128)(2,1)}, bf16[8,48,2048]{2,1,0:T(8,128)(2,1)}, u32[]{:S(2)}, u32[]{:S(2)}) collective-permute-start(bf16[8,48,2048]{2,1,0:T(8,128)(2,1)} %get-tuple-element.96), channel_id=1, source_target_pairs={{0,1},{1,0},{2,3},{3,2},{4,5},{5,4},{6,7},{7,6},{8,9},{9,8},{10,11... | collective-permute-start | bytes 4718600 | tf_op jit(solution)/shard_map/ppermute | solution.py:33
  85.2 32.4 %collective-permute-start.34 = (bf16[8,48,2048]{2,1,0:T(8,128)(2,1)}, bf16[8,48,2048]{2,1,0:T(8,128)(2,1)S(1)}, u32[]{:S(2)}, u32[]{:S(2)}) collective-permute-start(bf16[8,48,2048]{2,1,0:T(8,128)(2,1)} %get-tuple-element.113), channel_id=1, source_target_pairs={{0,1},{1,0},{2,3},{3,2},{4,5},{5,4},{6,7},{7,6},{8,9},{9,8},{10,11... | collective-permute-start | bytes 4718600 | tf_op jit(solution)/shard_map/ppermute | solution.py:33
  85.6 7.7 %copy-start = (bf16[16,48,2048]{2,1,0:T(8,128)(2,1)S(1)}, bf16[16,48,2048]{2,1,0:T(8,128)(2,1)}, u32[]{:S(2)}) copy-start(bf16[16,48,2048]{2,1,0:T(8,128)(2,1)} %get-tuple-element.107) | copy-start | bytes 9437188
  96.6 21.0 %collective-permute-start.35 = (bf16[8,48,2048]{2,1,0:T(8,128)(2,1)}, bf16[8,48,2048]{2,1,0:T(8,128)(2,1)}, u32[]{:S(2)}, u32[]{:S(2)}) collective-permute-start(bf16[8,48,2048]{2,1,0:T(8,128)(2,1)} %add_convert_fusion.refs_15_), channel_id=1, source_target_pairs={{0,4},{1,3},{2,6},{3,1},{4,0},{5,7},{6,2},{7,5},{8,12},{9,11},{10,... | collective-permute-start | bytes 4718600 | tf_op jit(solution)/shard_map/ppermute | solution.py:33
  113.1 2.2 %collective-permute-start.32 = (bf16[8,16,2176]{2,1,0:T(8,128)(2,1)}, bf16[8,16,2176]{2,1,0:T(8,128)(2,1)S(1)}, u32[]{:S(2)}, u32[]{:S(2)}) collective-permute-start(bf16[8,16,2176]{2,1,0:T(8,128)(2,1)} %get-tuple-element.112), channel_id=1, source_target_pairs={{0,1},{1,0},{2,3},{3,2},{4,5},{5,4},{6,7},{7,6},{8,9},{9,8},{10,11... | collective-permute-start | bytes 1671176 | tf_op jit(solution)/shard_map/ppermute | solution.py:33
  113.2 16.9 %collective-permute-start.31 = (bf16[8,16,2176]{2,1,0:T(8,128)(2,1)}, bf16[8,16,2176]{2,1,0:T(8,128)(2,1)S(1)}, u32[]{:S(2)}, u32[]{:S(2)}) collective-permute-start(bf16[8,16,2176]{2,1,0:T(8,128)(2,1)} %get-tuple-element.111), channel_id=1, source_target_pairs={{0,1},{1,0},{2,3},{3,2},{4,5},{5,4},{6,7},{7,6},{8,9},{9,8},{10,11... | collective-permute-start | bytes 1671176 | tf_op jit(solution)/shard_map/ppermute | solution.py:33
  116.6 13.5 %copy-start.1 = (bf16[16,16,2176]{2,1,0:T(8,128)(2,1)S(1)}, bf16[16,16,2176]{2,1,0:T(8,128)(2,1)}, u32[]{:S(2)}) copy-start(bf16[16,16,2176]{2,1,0:T(8,128)(2,1)} %get-tuple-element.110) | copy-start | bytes 3342340
  116.6 13.5 %collective-permute-start.33 = (bf16[8,16,2176]{2,1,0:T(8,128)(2,1)S(1)}, bf16[8,16,2176]{2,1,0:T(8,128)(2,1)S(1)}, u32[]{:S(2)}, u32[]{:S(2)}) collective-permute-start(bf16[8,16,2176]{2,1,0:T(8,128)(2,1)S(1)} %add_convert_fusion.2), channel_id=1, source_target_pairs={{0,4},{1,3},{2,6},{3,1},{4,0},{5,7},{6,2},{7,5},{8,12},{9,11},{10,... | collective-permute-start | bytes 1671176 | tf_op jit(solution)/shard_map/ppermute | solution.py:33
  119.1 14.6 %collective-permute-start.37 = (bf16[4,48,2048]{2,1,0:T(8,128)(2,1)S(1)}, bf16[4,48,2048]{2,1,0:T(8,128)(2,1)S(1)}, u32[]{:S(2)}, u32[]{:S(2)}) collective-permute-start(bf16[4,48,2048]{2,1,0:T(8,128)(2,1)S(1)} %add_convert_fusion.1), channel_id=1, source_target_pairs={{0,2},{1,5},{2,0},{3,7},{4,6},{5,1},{6,4},{7,3},{8,10},{9,13},{10,... | collective-permute-start | bytes 2359304 | tf_op jit(solution)/shard_map/ppermute | solution.py:33
  130.2 7.1 %collective-permute-start.36 = (bf16[4,16,2176]{2,1,0:T(8,128)(2,1)S(1)}, bf16[4,16,2176]{2,1,0:T(8,128)(2,1)S(1)}, u32[]{:S(2)}, u32[]{:S(2)}) collective-permute-start(bf16[4,16,2176]{2,1,0:T(8,128)(2,1)S(1)} %add_convert_fusion.4), channel_id=1, source_target_pairs={{0,2},{1,5},{2,0},{3,7},{4,6},{5,1},{6,4},{7,3},{8,10},{9,13},{10,... | collective-permute-start | bytes 835592 | tf_op jit(solution)/shard_map/ppermute | solution.py:33
  135.0 12.1 %collective-permute-start.39 = (bf16[2,48,2048]{2,1,0:T(8,128)(2,1)S(1)}, bf16[2,48,2048]{2,1,0:T(8,128)(2,1)S(1)}, u32[]{:S(2)}, u32[]{:S(2)}) collective-permute-start(bf16[2,48,2048]{2,1,0:T(8,128)(2,1)S(1)} %add_convert_fusion.3), channel_id=1, source_target_pairs={{0,8},{1,9},{2,10},{3,11},{4,12},{5,13},{6,14},{7,15},{8,0},{9,1},... | collective-permute-start | bytes 1179656 | tf_op jit(solution)/shard_map/ppermute | solution.py:33
  137.3 12.7 %collective-permute-start.38 = (bf16[2,16,2176]{2,1,0:T(8,128)(2,1)S(1)}, bf16[2,16,2176]{2,1,0:T(8,128)(2,1)S(1)}, u32[]{:S(2)}, u32[]{:S(2)}) collective-permute-start(bf16[2,16,2176]{2,1,0:T(8,128)(2,1)S(1)} %add_convert_fusion.6), channel_id=1, source_target_pairs={{0,8},{1,9},{2,10},{3,11},{4,12},{5,13},{6,14},{7,15},{8,0},{9,1},... | collective-permute-start | bytes 417800 | tf_op jit(solution)/shard_map/ppermute | solution.py:33
  150.1 11.4 %collective-permute-start.40 = (bf16[16,2176]{1,0:T(8,128)(2,1)S(1)}, bf16[16,2176]{1,0:T(8,128)(2,1)S(1)}, u32[]{:S(2)}, u32[]{:S(2)}) collective-permute-start(bf16[16,2176]{1,0:T(8,128)(2,1)S(1)} %get-tuple-element.126), channel_id=1, source_target_pairs={{0,16},{1,17},{2,18},{3,19},{4,20},{5,21},{6,22},{7,23},{8,24},{9,... | collective-permute-start | bytes 208904 | tf_op jit(solution)/shard_map/ppermute | solution.py:33
  152.2 13.1 %collective-permute-start.41 = (bf16[48,2048]{1,0:T(8,128)(2,1)S(1)}, bf16[48,2048]{1,0:T(8,128)(2,1)S(1)}, u32[]{:S(2)}, u32[]{:S(2)}) collective-permute-start(bf16[48,2048]{1,0:T(8,128)(2,1)S(1)} %get-tuple-element.125), channel_id=1, source_target_pairs={{0,16},{1,17},{2,18},{3,19},{4,20},{5,21},{6,22},{7,23},{8,24},{9,... | collective-permute-start | bytes 589832 | tf_op jit(solution)/shard_map/ppermute | solution.py:33
  (4 other events, 4.0 us)

commit v4 on v3

--- a/solution.py
+++ b/solution.py
@@ -228,16 +228,16 @@
             self.copy(i).start()
 
 
-def call(body, micros, me, near, loads, stores, scratch=(), after=()):
+def call(body, micros, me, near, loads, stores, scratch=(), after=(), raw=()):
     far = pl.BlockSpec(memory_space=pltpu.HBM)
-    counts = [len(near), len(loads), len(after), len(stores), len(loads), len(stores), len(scratch)]
+    counts = [len(near), len(loads), len(after), len(stores), len(raw), len(loads), len(stores), len(scratch)]
 
     def kernel(me_ref, *refs):
         groups, at = [], 0
         for count in counts:
             groups.append(refs[at : at + count])
             at += count
-        near_refs, sources, _unused, targets, in_buffers, out_buffers, rest = groups
+        near_refs, sources, _unused, targets, raw_refs, in_buffers, out_buffers, rest = groups
         in_sems, out_sems, near_sem = refs[at:]
         first, reads = 0, []
         for (_array, parts, box), source, buffer in zip(loads, sources, in_buffers):
@@ -247,7 +247,7 @@
         for (_shape, _type, parts), target, buffer in zip(stores, targets, out_buffers):
             writes.append(Store(target, buffer, out_sems, first, parts))
             first += parts
-        body(None if me is None else me_ref[0], (near_refs, near_sem), reads, writes, rest)
+        body(None if me is None else me_ref[0], (near_refs, near_sem, raw_refs), reads, writes, rest)
         for write in writes:
             for i in range(write.parts):
                 write.copy(i).wait()
@@ -256,16 +256,17 @@
     buffers += [(s, t) for s, t, _parts in stores]
     return pl.pallas_call(
         kernel,
-        out_shape=[jax.ShapeDtypeStruct(s, t) for s, t, _parts in stores],
+        out_shape=[jax.ShapeDtypeStruct(s, t) for s, t, _parts in stores]
+        + [jax.ShapeDtypeStruct(s, t) for s, t in raw],
         in_specs=[pl.BlockSpec(memory_space=pltpu.SMEM)]
         + [far] * (len(near) + len(loads))
         + [pl.BlockSpec(memory_space=pl.ANY)] * len(after),
-        out_specs=[far] * len(stores),
+        out_specs=[far] * (len(stores) + len(raw)),
         scratch_shapes=[pltpu.VMEM(s, t) for s, t in buffers + list(scratch)]
         + [
             pltpu.SemaphoreType.DMA((max(1, sum(parts for _array, parts, _box in loads)),)),
             pltpu.SemaphoreType.DMA((max(1, sum(parts for _shape, _type, parts in stores)),)),
-            pltpu.SemaphoreType.DMA((4,)),
+            pltpu.SemaphoreType.DMA((7,)),
         ],
         compiler_params=pltpu.CompilerParams(vmem_limit_bytes=VMEM_LIMIT),
         cost_estimate=pl.CostEstimate(flops=int(micros * 1.1e9), bytes_accessed=1000, transcendentals=0),
@@ -292,7 +293,7 @@
     marks, embeds = reads
     weights, vec, bias_up, base0, normed, normed0, query, keyval, probs, mixed = writes
     small, table, rows, tall, rows0, norm0 = scratch
-    pieces, sem = near
+    pieces, sem, _raw = near
     Place(me, pieces, weights.buffer, sem.at[0], lambda piece: piece).wait()
     small[...] = weights.buffer[:, 1536:].astype(F32).reshape(SHARDS, 16, 128)
     lane = iota((16, 128), 1)
@@ -313,29 +314,32 @@
     marks.whole()
     blocks = embeds.buffer.shape[0] // RB
 
-    def norm_pair(pair, _):
-        embeds.part(pair)
-        for half in range(2):
-            b = 2 * pair + half
-            rows[half] = dot(marks.buffer[block(b, RB), :], table[...].astype(LOW))
-            for c in range(RB // CH):
-                at = pl.ds(c * CH, CH)
-                here = pl.ds(pl.multiple_of(b * RB + c * CH, CH), CH)
-                base = embeds.buffer[here, :].astype(F32) + rows[half, at, :]
-                put_tall(tall.at[half], c * CH, base)
-                unit, _rate = norm_parts(base)
-                value = unit * gain + shift
-                put_tall(rows0.at[half], c * CH, value)
-                normed.buffer[here, :] = value.astype(LOW)
-            out = block(b, EB)
-            slots_first(tall.at[half], base0.buffer, out)
-            slots_first(rows0.at[half], norm0, out)
-            keyval.buffer[block(b, RB), :] = dot(normed.buffer[block(b, RB), :], weights.buffer[:, 512:1536]).astype(LOW)
-        normed.part(pair)
-        keyval.part(pair)
-        return 0
-
-    lax.fori_loop(0, blocks // 2, norm_pair, 0)
+    def project(b):
+        at = slice(b * RB, b * RB + RB)
+        keyval.buffer[at, :] = dot(normed.buffer[at, :], weights.buffer[:, 512:1536]).astype(LOW)
+        if b % 2 == 1:
+            normed.part(b // 2)
+            keyval.part(b // 2)
+
+    for b in range(blocks):
+        half = b % 2
+        if half == 0:
+            embeds.part(b // 2)
+        rows[half] = dot(marks.buffer[b * RB : b * RB + RB, :], table[...].astype(LOW))
+        if b > 0:
+            project(b - 1)
+        for c in range(RB // CH):
+            at, here = slice(c * CH, c * CH + CH), slice(b * RB + c * CH, b * RB + c * CH + CH)
+            base = embeds.buffer[here, :].astype(F32) + rows[half, at, :]
+            put_tall(tall.at[half], c * CH, base)
+            unit, _rate = norm_parts(base)
+            value = unit * gain + shift
+            put_tall(rows0.at[half], c * CH, value)
+            normed.buffer[here, :] = value.astype(LOW)
+        out = slice(b * EB, b * EB + EB)
+        slots_first(tall.at[half], base0.buffer, out)
+        slots_first(rows0.at[half], norm0, out)
+    project(blocks - 1)
     normed0.buffer[...] = norm0[...].astype(LOW)
     query.buffer[...] = dot(normed0.buffer[...], weights.buffer[:, :512]).astype(LOW)
     normed0.send()
@@ -345,42 +349,43 @@
     match = iota(shape, 0) // SLOTS == iota(shape, 1) % EB
     liver = jnp.where(iota((128, HEADS * EB), 0) == 8, 1.0, 0.0).astype(LOW)
 
-    def attend_pair(pair, _):
+    for pair in range(blocks // 2):
         for half in range(2):
             b = 2 * pair + half
-            at, out = block(b, RB), block(b, EB)
+            at, out = slice(b * RB, b * RB + RB), slice(b * EB, b * EB + EB)
             scores = dot_nt(keyval.buffer[at, :512], spread_heads(query.buffer[out, :])) * SCALE
             live = dot(marks.buffer[at, :], liver) > 0.5
             scores = jnp.where(live, scores, -1000000000.0).reshape(EB, SLOTS, HEADS * EB)
             top = jnp.max(scores, axis=1, keepdims=True)
             power = jnp.exp(scores - top)
-            part = (power / jnp.sum(power, axis=1, keepdims=True)).reshape(shape)
+            part = (power * (1.0 / jnp.sum(power, axis=1, keepdims=True))).reshape(shape)
             low = jnp.where(match, part, 0.0).astype(LOW)
             probs.buffer[at, :] = low
             mixed.buffer[out, :] = pick_heads(dot_tn(low, keyval.buffer[at, 512:])).astype(LOW)
         probs.part(pair)
-        return 0
-
-    lax.fori_loop(0, blocks // 2, attend_pair, 0)
+
     mixed.send()
 
 
 def ffn_kernel(me, near, reads, writes, scratch):
     cotangent, base0, mixed, vec, bias_up = reads
-    output, dfirst, dmixed, sum_up, sum_gain, sum_shift, sum_pool, own, *halves = writes
-    w_proj, w_up, w_down, w_out, first, norm_ffn, pre_low, dpool, hidden, slope, total = scratch
-    pieces, sem = near
+    output, dfirst, dmixed, sum_up, sum_gain, sum_shift, sum_pool = writes
+    w_proj, w_up, w_down, w_out, first, norm_ffn, pre_low, dpool, hidden, slope, low_proj, low_up, low_down = scratch
+    pieces, sem, halves = near
     out = Place(me, pieces[8:], w_out, sem.at[3], lambda piece: piece.at[pl.ds(64, 16)], turned=True)
     proj = Place(me, pieces[:8], w_proj, sem.at[0], lambda piece: piece.at[pl.ds(0, 16)])
     up = Place(me, pieces[:8], w_up, sem.at[1], lambda piece: piece.at[pl.ds(16, 16)])
     down = Place(me, pieces[8:], w_down, sem.at[2], lambda piece: piece.at[pl.ds(0, 64)], turned=True)
 
-    def share(row, steps, target, base=0):
+    copies = []
+
+    def share(grad, row, slot):
         for k in range(SHARDS):
-            half, place = (own, k) if k < 16 else (halves[k // 8 - 2], k % 8)
-            for step in range(steps):
-                at = pl.ds(pl.multiple_of(base + (shard_at(me, k) * steps + step) * 16, 16), 16)
-                half.buffer[place, row : row + 16, target(step)] = total[at, :].astype(LOW)
+            half, place = (halves[0], k) if k < 16 else (halves[k // 8 - 1], k % 8)
+            at = block(shard_at(me, k), 16)
+            copy = pltpu.make_async_copy(grad.at[at], half.at[place, pl.ds(row, 16)], sem.at[slot])
+            copy.start()
+            copies.append(copy)
 
     for read in (base0, mixed, vec):
         read.whole()
@@ -408,8 +413,12 @@
             below = 0.5 * (1.0 + lax.erf(value * (0.5**0.5)))
             hidden[at, lanes] = (value * below).astype(LOW)
             slope[at, lanes] = below + value * (jnp.exp(-0.5 * value * value) * 0.3989422804014327)
-        total[256 * k : 256 * k + 256, :] = dot_tn(hidden[:, lanes], low)
-    share(32, 4, lambda step: slice(512 * step, 512 * step + 512))
+        grad = dot_tn(hidden[:, lanes], low)
+        for r in range(4):
+            for j in range(4):
+                part = grad[64 * r + 16 * j : 64 * r + 16 * j + 16, :]
+                low_down[64 * k + 16 * r : 64 * k + 16 * r + 16, 512 * j : 512 * j + 512] = part.astype(LOW)
+    share(low_down, 32, 6)
     down.wait()
     for k in range(8):
         lanes = slice(256 * k, 256 * k + 256)
@@ -429,20 +438,23 @@
     sum_gain.buffer[...] = gains
     sum_shift.buffer[...] = shifts
     dmixed.buffer[...] = dot_nt(dfirst.buffer[...].astype(LOW), w_out[...]).astype(LOW)
+    for k in range(4):
+        lanes = slice(512 * k, 512 * k + 512)
+        low_up[:, lanes] = dot_tn(norm_ffn[...], pre_low[:, lanes]).astype(LOW)
+    share(low_up, 16, 4)
     for write in (dfirst, dmixed, sum_up, sum_gain, sum_shift, sum_pool):
         write.send()
     pooled = (first[...] + dot(hidden[...], w_down[...]) + vec.buffer[12:13, :]).astype(LOW)
     for k in range(4):
         lanes = slice(512 * k, 512 * k + 512)
-        total[:512, :] = dot_tn(pooled, cotangent.buffer[:, lanes])
-        share(0, 1, lambda _step: lanes)
-        total[512:1024, :] = dot_tn(norm_ffn[...], pre_low[:, lanes])
-        share(16, 1, lambda _step: lanes, 512)
+        low_proj[:, lanes] = dot_tn(pooled, cotangent.buffer[:, lanes]).astype(LOW)
+    share(low_proj, 0, 5)
+    for k in range(4):
+        lanes = slice(512 * k, 512 * k + 512)
         output.buffer[:, lanes] = dot(pooled, w_proj[:, lanes]).astype(LOW)
-    for half in halves:
-        half.send()
-    own.send()
     output.send()
+    for copy in copies:
+        copy.wait()
 
 
 def attend_back_kernel(me, _near, reads, writes, scratch):
@@ -451,12 +463,12 @@
     dmixed.whole()
     query.whole()
 
-    def attend_pair(pair, _):
+    for pair in range(keyval.buffer.shape[0] // RB // 2):
         probs.part(pair)
         keyval.part(pair)
         for half in range(2):
             b = 2 * pair + half
-            at, out = block(b, RB), block(b, EB)
+            at, out = slice(b * RB, b * RB + RB), slice(b * EB, b * EB + EB)
             low = probs.buffer[at, :]
             part = low.astype(F32)
             dmix = spread_heads(dmixed.buffer[out, :])
@@ -468,9 +480,7 @@
             dkeyval.buffer[at, :512] = (dot(dscores, spread_heads(query.buffer[out, :])) * SCALE).astype(LOW)
             dquery.buffer[out, :] = (pick_heads(dot_tn(dscores, keyval.buffer[at, :512])) * SCALE).astype(LOW)
         dkeyval.part(pair)
-        return 0
-
-    lax.fori_loop(0, keyval.buffer.shape[0] // RB // 2, attend_pair, 0)
+
     dquery.send()
     query_part.buffer[...] = dot_nt(dquery.buffer[...], weights.whole()[...])
     query_part.send()
@@ -489,36 +499,46 @@
     spread_first[...] = jnp.zeros_like(spread_first)
     gain = vec.buffer[8:9, :]
 
-    def norm_pair(pair, _):
-        dkeyval.part(pair)
-        embeds.part(pair)
-        for half in range(2):
-            b = 2 * pair + half
-            at, out = block(b, RB), block(b, EB)
-            put_first(spread_query.at[half], query_part.buffer[out, :])
-            put_first(spread_first.at[half], dfirst.buffer[out, :])
-            rows[half] = dot(marks.buffer[at, :], table[...])
-            work[half] = dot_nt(dkeyval.buffer[at, :], weights.buffer[...])
-            gains, shifts = jnp.zeros((8, 512), F32), jnp.zeros((8, 512), F32)
-            for c in range(RB // CH):
-                local = pl.ds(c * CH, CH)
-                here = pl.ds(pl.multiple_of(b * RB + c * CH, CH), CH)
-                grad = work[half, local, :] + get_tall(spread_query.at[half], c * CH, CH)
-                unit, rate = norm_parts(embeds.buffer[here, :].astype(F32) + rows[half, local, :])
-                gains += fold(grad * unit)
-                shifts += fold(grad)
-                value = norm_back(grad, unit, rate, gain) + get_tall(spread_first.at[half], c * CH, CH)
-                high = value.astype(LOW)
-                grad_embeds.buffer[here, :] = high
-                lower[half, local, :] = (value - high.astype(F32)).astype(LOW)
-            sums[half, 0:8, :] += gains
-            sums[half, 8:16, :] += shifts
-            mark = marks.buffer[at, :]
-            sums[half, 16:144, :] += dot_tn(mark, grad_embeds.buffer[at, :]) + dot_tn(mark, lower[half])
-        grad_embeds.part(pair)
-        return 0
-
-    lax.fori_loop(0, embeds.buffer.shape[0] // RB // 2, norm_pair, 0)
+    blocks = embeds.buffer.shape[0] // RB
+
+    def project(b):
+        at = slice(b * RB, b * RB + RB)
+        if b % 2 == 0:
+            dkeyval.part(b // 2)
+            embeds.part(b // 2)
+        rows[b % 2] = dot(marks.buffer[at, :], table[...])
+        work[b % 2] = dot_nt(dkeyval.buffer[at, :], weights.buffer[...])
+
+    def collect(b):
+        at = slice(b * RB, b * RB + RB)
+        mark = marks.buffer[at, :]
+        sums[b % 2, 16:144, :] += dot_tn(mark, grad_embeds.buffer[at, :]) + dot_tn(mark, lower[b % 2])
+        if b % 2 == 1:
+            grad_embeds.part(b // 2)
+
+    project(0)
+    for b in range(blocks):
+        half = b % 2
+        put_first(spread_query.at[half], query_part.buffer[b * EB : b * EB + EB, :])
+        put_first(spread_first.at[half], dfirst.buffer[b * EB : b * EB + EB, :])
+        if b + 1 < blocks:
+            project(b + 1)
+        if b > 0:
+            collect(b - 1)
+        gains, shifts = jnp.zeros((8, 512), F32), jnp.zeros((8, 512), F32)
+        for c in range(RB // CH):
+            local, here = slice(c * CH, c * CH + CH), slice(b * RB + c * CH, b * RB + c * CH + CH)
+            grad = work[half, local, :] + get_tall(spread_query.at[half], c * CH, CH)
+            unit, rate = norm_parts(embeds.buffer[here, :].astype(F32) + rows[half, local, :])
+            gains += fold(grad * unit)
+            shifts += fold(grad)
+            value = norm_back(grad, unit, rate, gain) + get_tall(spread_first.at[half], c * CH, CH)
+            high = value.astype(LOW)
+            grad_embeds.buffer[here, :] = high
+            lower[half, local, :] = (value - high.astype(F32)).astype(LOW)
+        sums[half, 0:8, :] += gains
+        sums[half, 8:16, :] += shifts
+    collect(blocks - 1)
     grad_out[...] = dot_tn(mixed.whole()[...], dfirst.buffer[...].astype(LOW))
     grad_qkv[:, :512] = dot_tn(normed0.whole()[...], dquery.whole()[...])
     normed.whole()
@@ -594,7 +614,9 @@
         lower, upper = spread(quad, LAYER[1], LAYER[2])
         upper = tie(upper, own2)
         pieces.append([quad, lower, upper, send(upper, LAYER[1])])
-        later = [tie(own2, upper)]
+        near2 = tie(pieces[1][1], upper)
+        early = [send(own2, CORE), send(near2, CORE)]
+        later = [tie(own2, near2)]
         group_ids, piece_counts = tie(group_ids, piece_counts, own, every=True)[:2]
     else:
         me = None
@@ -655,8 +677,8 @@
     )
     if tuned:
         mixed, *came = tie(mixed, *pieces[1], *pieces[2], every=True)
-        came += [send(part, CORE) for part in came]
-        pieces[1:] = [came[0:4] + came[8:12], came[4:8] + came[12:16]]
+        cores = [send(part, CORE) for part in came[2:]]
+        pieces[1:] = [came[0:4] + early + cores[:2], came[4:8] + cores[2:]]
     (
         output, dfirst, dmixed, sum_up, sum_gain, sum_shift, sum_pool, own_pair, *other_pair
     ) = call(
@@ -669,14 +691,14 @@
         ],
         [
             ((entries, 2048), low, 1), ((entries, 512), wide, 1), ((entries, 512), low, 1), ((8, 2048), wide, 1),
-            ((8, 512), wide, 1), ((8, 512), wide, 1), ((8, 512), wide, 1), ((16, 48, 2048), low, 1),
-            ((8, 48, 2048), low, 1), ((8, 48, 2048), low, 1),
+            ((8, 512), wide, 1), ((8, 512), wide, 1), ((8, 512), wide, 1),
         ],
         [
             ((512, 2048), low), ((512, 2048), low), ((2048, 512), low), ((512, 512), low), ((entries, 512), wide),
             ((entries, 512), low), ((entries, 2048), low), ((entries, 512), wide), ((entries, 2048), low),
-            ((entries, 2048), wide), ((2048, 512), wide),
+            ((entries, 2048), wide), ((512, 2048), low), ((512, 2048), low), ((512, 2048), low),
         ],
+        raw=[((16, 48, 2048), low), ((8, 48, 2048), low), ((8, 48, 2048), low)],
     )
     if tuned:
         pair = Sum(own_pair, *other_pair)

time: 167 us -> 163 us (0.976)
  starting transfers between devices: 40.8 us -> 47.9 us
  Pallas kernels: 52 us -> 45.9 us
  waiting for transfers between devices: 51.5 us -> 47 us
    ppermute x42, starting transfers between devices: 40.8 us -> 47.9 us  [send(): return lax.ppermute(value, 'dp', to)]
    pallas_call x4, Pallas kernels: 52 us -> 45.9 us  [call(): pl.pallas_call(kernel, out_shape=[jax.ShapeDtypeStruct(s, t) for s, t, _p...]
    ppermute x42, waiting for transfers between devices: 51.5 us -> 47 us  [send(): return lax.ppermute(value, 'dp', to)]
  transfers between devices with their start and end apart: 42 -> 42, of which waited for: 15 -> 16; matrix products, arithmetic and copies ran while one was open for 10% -> 10% of each run, Pallas kernels for 22% -> 21%
where the time goes in v4:
time: 163 us; the launch traced here: 162 us
  starting transfers between devices  47.9 us (29%)
  waiting for transfers between devices  47 us (29%)
  Pallas kernels  45.9 us (28%)
  other arithmetic  16.5 us (10%)
  local copies, waits for them, and re-layouts  3.93 us (2%)
    ppermute x42, starting transfers between devices, send(): return lax.ppermute(value, 'dp', to)  47.9 us
    ppermute x42, waiting for transfers between devices, send(): return lax.ppermute(value, 'dp', to)  47 us
    pallas_call x4, Pallas kernels, call(): pl.pallas_call(kernel, out_shape=[jax.ShapeDtypeStruct(s, t) for s, t, _p...  45.9 us
    convert_element_type x2, other arithmetic, first(): part = widen(self.own[8:], self.high).astype(LOW)  4.44 us
  transfers between devices with their start and end apart: 42, of which 16 were waited for; matrix products, arithmetic and copies ran while one was open for 10% of the time, Pallas kernels for 21%

profile of v4, /device:TPU:0, one launch (start us, length us, event | category | flops | bytes accessed | tf_op | source)
XLA Modules:
  0.0 162.4 jit_solution(18370628673355889079)
XLA Ops:
  0.7 0.9 pad_add_fusion.2
  1.6 5.1 %collective-permute-start.2 = (bf16[16,1664]{1,0:T(8,128)(2,1)S(1)}, bf16[16,1664]{1,0:T(8,128)(2,1)S(1)}, u32[]{:S(2)}, u32[]{:S(2)}) collective-permute-start(bf16[16,1664]{1,0:T(8,128)(2,1)S(1)} %pad_add_fusion.2), channel_id=1, source_target_pairs={{0,24},{1,25},{2,26},{3,27},{4,28},{5,29},{6,30},{7,31},{8,16},{9,... | collective-permute-start | bytes 159752 | tf_op jit(solution)/shard_map/ppermute | solution.py:33
  6.7 0.6 collective-permute-start.1
  7.3 0.9 pad_add_fusion.1
  8.2 1.6 %collective-permute-start.10 = (bf16[80,512]{1,0:T(8,128)(2,1)S(1)}, bf16[80,512]{1,0:T(8,128)(2,1)S(1)}, u32[]{:S(2)}, u32[]{:S(2)}) collective-permute-start(bf16[80,512]{1,0:T(8,128)(2,1)S(1)} %pad_add_fusion.1), channel_id=1, source_target_pairs={{0,2},{1,5},{2,0},{3,7},{4,6},{5,1},{6,4},{7,3},{8,10},{9,13},{10,... | collective-permute-start | bytes 245768 | tf_op jit(solution)/shard_map/ppermute | solution.py:33
  9.9 1.5 collective-permute-start.11
  11.4 0.9 fusion.5
  12.3 0.9 pad_add_fusion
  13.2 0.4 collective-permute-start.12
  13.6 2.3 %collective-permute-start.14 = (bf16[32,2048]{1,0:T(8,128)(2,1)S(1)}, bf16[32,2048]{1,0:T(8,128)(2,1)S(1)}, u32[]{:S(2)}, u32[]{:S(2)}) collective-permute-start(bf16[32,2048]{1,0:T(8,128)(2,1)S(1)} %pad_add_fusion), channel_id=1, source_target_pairs={{0,16},{1,17},{2,18},{3,19},{4,20},{5,21},{6,22},{7,23},{8,24},{9,... | collective-permute-start | bytes 393224 | tf_op jit(solution)/shard_map/ppermute | solution.py:33
  15.9 2.0 %collective-permute-start.13 = (bf16[32,2048]{1,0:T(8,128)(2,1)S(1)}, bf16[32,2048]{1,0:T(8,128)(2,1)S(1)}, u32[]{:S(2)}, u32[]{:S(2)}) collective-permute-start(bf16[32,2048]{1,0:T(8,128)(2,1)S(1)} %pad_add_fusion), channel_id=1, source_target_pairs={{0,8},{1,9},{2,10},{3,11},{4,12},{5,13},{6,14},{7,15},{8,0},{9,1},... | collective-permute-start | bytes 393224 | tf_op jit(solution)/shard_map/ppermute | solution.py:33
  18.0 3.3 %collective-permute-done.14 = bf16[32,2048]{1,0:T(8,128)(2,1)S(1)} collective-permute-done((bf16[32,2048]{1,0:T(8,128)(2,1)S(1)}, bf16[32,2048]{1,0:T(8,128)(2,1)S(1)}, u32[]{:S(2)}, u32[]{:S(2)}) %collective-permute-start.14) | collective-permute-done | bytes 131104 | tf_op jit(solution)/shard_map/ppermute | solution.py:33
  21.5 0.8 iota_compare_fusion
  22.3 1.6 collective-permute-start.3
  23.9 1.5 collective-permute-start.4
  25.4 0.5 collective-permute-start.5
  26.0 3.4 %collective-permute-start.17 = (bf16[4,80,512]{2,1,0:T(8,128)(2,1)S(1)}, bf16[4,80,512]{2,1,0:T(8,128)(2,1)S(1)}, u32[]{:S(2)}, u32[]{:S(2)}) collective-permute-start(bf16[4,80,512]{2,1,0:T(8,128)(2,1)S(1)} %pad_maximum_fusion.1.refs_8_), channel_id=1, source_target_pairs={{0,16},{1,17},{2,18},{3,19},{4,20},{5,21},{6,22},{7,23},{8,24},{9,... | collective-permute-start | bytes 983048 | tf_op jit(solution)/shard_map/ppermute | solution.py:33
  29.5 1.6 collective-permute-start.16
  31.4 3.2 %collective-permute-done.4.refs_2_ = bf16[4,16,1664]{2,1,0:T(8,128)(2,1)S(1)} collective-permute-done((bf16[4,16,1664]{2,1,0:T(8,128)(2,1)S(1)}, bf16[4,16,1664]{2,1,0:T(8,128)(2,1)S(1)}, u32[]{:S(2)}, u32[]{:S(2)}) %collective-permute-start.4) | collective-permute-done | bytes 213024 | tf_op jit(solution)/shard_map/ppermute | solution.py:33
  34.6 0.5 collective-permute-start.8
  35.1 5.7 %collective-permute-done.17.refs_10_ = bf16[4,80,512]{2,1,0:T(8,128)(2,1)S(1)} collective-permute-done((bf16[4,80,512]{2,1,0:T(8,128)(2,1)S(1)}, bf16[4,80,512]{2,1,0:T(8,128)(2,1)S(1)}, u32[]{:S(2)}, u32[]{:S(2)}) %collective-permute-start.17) | collective-permute-done | bytes 327712 | tf_op jit(solution)/shard_map/ppermute | solution.py:33
  40.7 1.1 fusion.refs_8_.refs_3_
  41.9 1.3 collective-permute-start.18
  43.2 1.4 collective-permute-start.19
  44.7 2.0 %collective-permute-start.21 = (bf16[4,80,512]{2,1,0:T(8,128)(2,1)S(1)}, bf16[4,80,512]{2,1,0:T(8,128)(2,1)S(1)}, u32[]{:S(2)}, u32[]{:S(2)}) collective-permute-start(bf16[4,80,512]{2,1,0:T(8,128)(2,1)S(1)} %collective-permute-done.17.refs_10_), channel_id=1, source_target_pairs={{0,8},{1,9},{2,10},{3,11},{4,12},{5,13},{6,14},{7,15},{8,0},{9,1},... | collective-permute-start | bytes 983048 | tf_op jit(solution)/shard_map/ppermute | solution.py:33
  46.7 11.3 %shard_map.263 = (bf16[512,1664]{1,0:T(8,128)(2,1)}, f32[16,512]{1,0:T(8,128)}, f32[8,2048]{1,0:T(8,128)}, f32[256,512]{1,0:T(8,128)}, bf16[2048,512]{1,0:T(8,12...) custom-call(s32[1]{0:T(128)} %bitcast.me_ref, ...), custom_call_target="tpu_custom_call" | custom-call | flops 16499999744 | bytes 1000 | tf_op jit(solution)/shard_map/pallas_call | solution.py:257
  58.1 0.9 collective-permute-done.21.refs_11_
  59.0 3.4 %collective-permute-start.26 = (bf16[4,80,512]{2,1,0:T(8,128)(2,1)S(1)}, bf16[4,80,512]{2,1,0:T(8,128)(2,1)S(1)}, u32[]{:S(2)}, u32[]{:S(2)}) collective-permute-start(bf16[4,80,512]{2,1,0:T(8,128)(2,1)S(1)} %pad_maximum_fusion.1.refs_8_), channel_id=1, source_target_pairs={{0,1},{1,0},{2,3},{3,2},{4,5},{5,4},{6,7},{7,6},{8,9},{9,8},{10,11... | collective-permute-start | bytes 983048 | tf_op jit(solution)/shard_map/ppermute | solution.py:33
  62.5 0.4 collective-permute-start.24
  63.0 0.5 collective-permute-start.23
  64.5 2.3 %collective-permute-done.28.refs_14_ = bf16[4,80,512]{2,1,0:T(8,128)(2,1)S(1)} collective-permute-done((bf16[4,80,512]{2,1,0:T(8,128)(2,1)S(1)}, bf16[4,80,512]{2,1,0:T(8,128)(2,1)S(1)}, u32[]{:S(2)}, u32[]{:S(2)}) %collective-permute-start.28) | collective-permute-done | bytes 327712 | tf_op jit(solution)/shard_map/ppermute | solution.py:33
  66.8 0.5 collective-permute-done.29.refs_15_
  67.6 0.5 copy-done.19
  68.6 12.2 %shard_map.264 = (bf16[256,2048]{1,0:T(8,128)(2,1)}, f32[256,512]{1,0:T(8,128)}, bf16[256,512]{1,0:T(8,128)(2,1)}, f32[8,2048]{1,0:T(8,128)}, f32[8,512]{1,0:T(8...) custom-call(s32[1]{0:T(128)} %bitcast.me_ref, ...), custom_call_target="tpu_custom_call" | custom-call | flops 13200000000 | bytes 1000 | tf_op jit(solution)/shard_map/pallas_call | solution.py:257
  80.8 0.4 collective-permute-start.30
  81.3 7.6 %shard_map.265 = (bf16[2048,1024]{1,0:T(8,128)(2,1)}, bf16[256,512]{1,0:T(8,128)(2,1)}, f32[256,512]{1,0:T(8,128)}) custom-call(s32[1]{0:T(128)} %bitcast.me_ref, bf16[256,512]{1,0:T(8,128)(2,1)} %get-tuple-element.92.refs_0_, bf16[256,512]{1,0:T(8,128)(2,1)} %get-tuple-element.93.refs_1_, bf16[2048,256]{1,0:T(8,128)(2,1)} %get-tuple-element.94.refs_2_, ...), custom_call_target="tpu_custom_call" | custom-call | flops 8800000000 | bytes 1000 | tf_op jit(solution)/shard_map/pallas_call | solution.py:257
  89.0 3.3 %add_convert_fusion.refs_15_ = bf16[8,48,2048]{2,1,0:T(8,128)(2,1)} fusion(bf16[8,48,2048]{2,1,0:T(8,128)(2,1)} %collective-permute-done.30, bf16[16,48,2048]{2,1,0:T(8,128)(2,1)S(1)} %copy-done), kind=kLoop, calls=%fused_computation | loop fusion | flops 3145728 | bytes 4718592 | tf_op jit(solution)/shard_map/convert_element_type | solution.py:72
  92.2 1.7 %collective-permute-start.35 = (bf16[8,48,2048]{2,1,0:T(8,128)(2,1)}, bf16[8,48,2048]{2,1,0:T(8,128)(2,1)}, u32[]{:S(2)}, u32[]{:S(2)}) collective-permute-start(bf16[8,48,2048]{2,1,0:T(8,128)(2,1)} %add_convert_fusion.refs_15_), channel_id=1, source_target_pairs={{0,4},{1,3},{2,6},{3,1},{4,0},{5,7},{6,2},{7,5},{8,12},{9,11},{10,... | collective-permute-start | bytes 4718600 | tf_op jit(solution)/shard_map/ppermute | solution.py:33
  93.9 14.8 %shard_map.266 = (bf16[2048,512]{1,0:T(8,128)(2,1)}, bf16[16,16,2176]{2,1,0:T(8,128)(2,1)}, bf16[8,16,2176]{2,1,0:T(8,128)(2,1)}, bf16[8,16,2176]{2,1,0:T(8,128)(2,1)}) custom-call(s32[1]{0:T(128)} %bitcast.me_ref, f32[16,512]{1,0:T(8,128)} %get-tuple-element.89.refs_19_.refs_0_, f32[256,512]{1,0:T(8,128)} %get-tuple-element.99.refs_1_, ...), custom_call_target="tpu_custom_call" | custom-call | flops 19800000512 | bytes 1000 | tf_op jit(solution)/shard_map/pallas_call | solution.py:257
  108.7 0.5 collective-permute-start.31
  109.2 1.7 %collective-permute-done.32 = bf16[8,16,2176]{2,1,0:T(8,128)(2,1)S(1)} collective-permute-done((bf16[8,16,2176]{2,1,0:T(8,128)(2,1)}, bf16[8,16,2176]{2,1,0:T(8,128)(2,1)S(1)}, u32[]{:S(2)}, u32[]{:S(2)}) %collective-permute-start.32) | collective-permute-done | bytes 557088 | tf_op jit(solution)/shard_map/ppermute | solution.py:33
  110.9 1.2 add_convert_fusion.2
  112.1 1.0 collective-permute-start.33
  113.1 1.5 add_convert_fusion.1
  114.7 1.4 collective-permute-start.37
  116.1 9.5 %collective-permute-done.33 = bf16[8,16,2176]{2,1,0:T(8,128)(2,1)S(1)} collective-permute-done((bf16[8,16,2176]{2,1,0:T(8,128)(2,1)S(1)}, bf16[8,16,2176]{2,1,0:T(8,128)(2,1)S(1)}, u32[]{:S(2)}, u32[]{:S(2)}) %collective-permute-start.33) | collective-permute-done | bytes 557088 | tf_op jit(solution)/shard_map/ppermute | solution.py:33
  125.7 2.6 %collective-permute-start.36 = (bf16[4,16,2176]{2,1,0:T(8,128)(2,1)S(1)}, bf16[4,16,2176]{2,1,0:T(8,128)(2,1)S(1)}, u32[]{:S(2)}, u32[]{:S(2)}) collective-permute-start(bf16[4,16,2176]{2,1,0:T(8,128)(2,1)S(1)} %add_convert_fusion.4), channel_id=1, source_target_pairs={{0,2},{1,5},{2,0},{3,7},{4,6},{5,1},{6,4},{7,3},{8,10},{9,13},{10,... | collective-permute-start | bytes 835592 | tf_op jit(solution)/shard_map/ppermute | solution.py:33
  128.3 1.0 collective-permute-done.37
  129.3 1.2 add_convert_fusion.3
  130.5 2.0 %collective-permute-start.39 = (bf16[2,48,2048]{2,1,0:T(8,128)(2,1)S(1)}, bf16[2,48,2048]{2,1,0:T(8,128)(2,1)S(1)}, u32[]{:S(2)}, u32[]{:S(2)}) collective-permute-start(bf16[2,48,2048]{2,1,0:T(8,128)(2,1)S(1)} %add_convert_fusion.3), channel_id=1, source_target_pairs={{0,8},{1,9},{2,10},{3,11},{4,12},{5,13},{6,14},{7,15},{8,0},{9,1},... | collective-permute-start | bytes 1179656 | tf_op jit(solution)/shard_map/ppermute | solution.py:33
  132.9 2.0 %collective-permute-start.38 = (bf16[2,16,2176]{2,1,0:T(8,128)(2,1)S(1)}, bf16[2,16,2176]{2,1,0:T(8,128)(2,1)S(1)}, u32[]{:S(2)}, u32[]{:S(2)}) collective-permute-start(bf16[2,16,2176]{2,1,0:T(8,128)(2,1)S(1)} %add_convert_fusion.6), channel_id=1, source_target_pairs={{0,8},{1,9},{2,10},{3,11},{4,12},{5,13},{6,14},{7,15},{8,0},{9,1},... | collective-permute-start | bytes 417800 | tf_op jit(solution)/shard_map/ppermute | solution.py:33
  134.9 7.5 %collective-permute-done.39 = bf16[2,48,2048]{2,1,0:T(8,128)(2,1)S(1)} collective-permute-done((bf16[2,48,2048]{2,1,0:T(8,128)(2,1)S(1)}, bf16[2,48,2048]{2,1,0:T(8,128)(2,1)S(1)}, u32[]{:S(2)}, u32[]{:S(2)}) %collective-permute-start.39) | collective-permute-done | bytes 393248 | tf_op jit(solution)/shard_map/ppermute | solution.py:33
  142.4 1.3 add_bitcast_fusion
  143.7 1.7 %collective-permute-done.38 = bf16[2,16,2176]{2,1,0:T(8,128)(2,1)S(1)} collective-permute-done((bf16[2,16,2176]{2,1,0:T(8,128)(2,1)S(1)}, bf16[2,16,2176]{2,1,0:T(8,128)(2,1)S(1)}, u32[]{:S(2)}, u32[]{:S(2)}) %collective-permute-start.38) | collective-permute-done | bytes 139296 | tf_op jit(solution)/shard_map/ppermute | solution.py:33
  145.5 3.1 %collective-permute-start.40 = (bf16[16,2176]{1,0:T(8,128)(2,1)S(1)}, bf16[16,2176]{1,0:T(8,128)(2,1)S(1)}, u32[]{:S(2)}, u32[]{:S(2)}) collective-permute-start(bf16[16,2176]{1,0:T(8,128)(2,1)S(1)} %get-tuple-element.128), channel_id=1, source_target_pairs={{0,16},{1,17},{2,18},{3,19},{4,20},{5,21},{6,22},{7,23},{8,24},{9,... | collective-permute-start | bytes 208904 | tf_op jit(solution)/shard_map/ppermute | solution.py:33
  148.7 8.2 %collective-permute-done.40 = bf16[16,2176]{1,0:T(8,128)(2,1)S(1)} collective-permute-done((bf16[16,2176]{1,0:T(8,128)(2,1)S(1)}, bf16[16,2176]{1,0:T(8,128)(2,1)S(1)}, u32[]{:S(2)}, u32[]{:S(2)}) %collective-permute-start.40) | collective-permute-done | bytes 69664 | tf_op jit(solution)/shard_map/ppermute | solution.py:33
  156.9 0.7 convert_add_fusion.1
  157.6 0.6 dynamic-slice_bitcast_fusion.5
  158.2 0.7 constant_dynamic-slice_fusion
  158.8 0.6 dynamic-slice_bitcast_fusion
  159.4 0.6 convert_add_fusion.2
  160.0 0.9 collective-permute-done.41
  161.0 0.7 fusion.3
  161.7 0.7 pad_maximum_fusion.3
  (108 shorter events, 3.6 us)
Async XLA Ops:
  0.6 30.4 %copy-start.5 = (s32[256]{0:T(256)S(1)}, s32[256]{0:T(256)}, u32[]{:S(2)}) copy-start(s32[256]{0:T(256)} %param.18) | copy-start | bytes 3076
  1.6 11.6 %collective-permute-start.2 = (bf16[16,1664]{1,0:T(8,128)(2,1)S(1)}, bf16[16,1664]{1,0:T(8,128)(2,1)S(1)}, u32[]{:S(2)}, u32[]{:S(2)}) collective-permute-start(bf16[16,1664]{1,0:T(8,128)(2,1)S(1)} %pad_add_fusion.2), channel_id=1, source_target_pairs={{0,24},{1,25},{2,26},{3,27},{4,28},{5,29},{6,30},{7,31},{8,16},{9,... | collective-permute-start | bytes 159752 | tf_op jit(solution)/shard_map/ppermute | solution.py:33
  6.7 6.9 %collective-permute-start = (bf16[16,1664]{1,0:T(8,128)(2,1)S(1)}, bf16[16,1664]{1,0:T(8,128)(2,1)S(1)}, u32[]{:S(2)}, u32[]{:S(2)}) collective-permute-start(bf16[16,1664]{1,0:T(8,128)(2,1)S(1)} %pad_add_fusion.2), channel_id=1, source_target_pairs={{0,8},{1,9},{2,10},{3,11},{4,12},{5,13},{6,14},{7,15},{8,0},{9,1},... | collective-permute-start | bytes 159752 | tf_op jit(solution)/shard_map/ppermute | solution.py:33
  6.7 9.2 %collective-permute-start.1 = (bf16[16,1664]{1,0:T(8,128)(2,1)S(1)}, bf16[16,1664]{1,0:T(8,128)(2,1)S(1)}, u32[]{:S(2)}, u32[]{:S(2)}) collective-permute-start(bf16[16,1664]{1,0:T(8,128)(2,1)S(1)} %pad_add_fusion.2), channel_id=1, source_target_pairs={{0,16},{1,17},{2,18},{3,19},{4,20},{5,21},{6,22},{7,23},{8,24},{9,... | collective-permute-start | bytes 159752 | tf_op jit(solution)/shard_map/ppermute | solution.py:33
  8.2 14.1 %collective-permute-start.10 = (bf16[80,512]{1,0:T(8,128)(2,1)S(1)}, bf16[80,512]{1,0:T(8,128)(2,1)S(1)}, u32[]{:S(2)}, u32[]{:S(2)}) collective-permute-start(bf16[80,512]{1,0:T(8,128)(2,1)S(1)} %pad_add_fusion.1), channel_id=1, source_target_pairs={{0,2},{1,5},{2,0},{3,7},{4,6},{5,1},{6,4},{7,3},{8,10},{9,13},{10,... | collective-permute-start | bytes 245768 | tf_op jit(solution)/shard_map/ppermute | solution.py:33
  9.9 14.0 %collective-permute-start.11 = (bf16[80,512]{1,0:T(8,128)(2,1)S(1)}, bf16[80,512]{1,0:T(8,128)(2,1)S(1)}, u32[]{:S(2)}, u32[]{:S(2)}) collective-permute-start(bf16[80,512]{1,0:T(8,128)(2,1)S(1)} %pad_add_fusion.1), channel_id=1, source_target_pairs={{0,4},{1,3},{2,6},{3,1},{4,0},{5,7},{6,2},{7,5},{8,12},{9,11},{10,... | collective-permute-start | bytes 245768 | tf_op jit(solution)/shard_map/ppermute | solution.py:33
  13.2 12.2 %collective-permute-start.12 = (bf16[80,512]{1,0:T(8,128)(2,1)S(1)}, bf16[80,512]{1,0:T(8,128)(2,1)S(1)}, u32[]{:S(2)}, u32[]{:S(2)}) collective-permute-start(bf16[80,512]{1,0:T(8,128)(2,1)S(1)} %pad_add_fusion.1), channel_id=1, source_target_pairs={{0,6},{1,7},{2,4},{3,5},{4,2},{5,3},{6,0},{7,1},{8,14},{9,15},{10,... | collective-permute-start | bytes 245768 | tf_op jit(solution)/shard_map/ppermute | solution.py:33
  13.6 7.7 %collective-permute-start.14 = (bf16[32,2048]{1,0:T(8,128)(2,1)S(1)}, bf16[32,2048]{1,0:T(8,128)(2,1)S(1)}, u32[]{:S(2)}, u32[]{:S(2)}) collective-permute-start(bf16[32,2048]{1,0:T(8,128)(2,1)S(1)} %pad_add_fusion), channel_id=1, source_target_pairs={{0,16},{1,17},{2,18},{3,19},{4,20},{5,21},{6,22},{7,23},{8,24},{9,... | collective-permute-start | bytes 393224 | tf_op jit(solution)/shard_map/ppermute | solution.py:33
  15.9 10.0 %collective-permute-start.13 = (bf16[32,2048]{1,0:T(8,128)(2,1)S(1)}, bf16[32,2048]{1,0:T(8,128)(2,1)S(1)}, u32[]{:S(2)}, u32[]{:S(2)}) collective-permute-start(bf16[32,2048]{1,0:T(8,128)(2,1)S(1)} %pad_add_fusion), channel_id=1, source_target_pairs={{0,8},{1,9},{2,10},{3,11},{4,12},{5,13},{6,14},{7,15},{8,0},{9,1},... | collective-permute-start | bytes 393224 | tf_op jit(solution)/shard_map/ppermute | solution.py:33
  18.0 28.7 %copy-start.4 = (bf16[4,16,1664]{2,1,0:T(8,128)(2,1)}, bf16[4,16,1664]{2,1,0:T(8,128)(2,1)S(1)}, u32[]{:S(2)}) copy-start(bf16[4,16,1664]{2,1,0:T(8,128)(2,1)S(1)} %pad_maximum_fusion.2.refs_0_) | copy-start | bytes 638980
  21.3 8.1 %collective-permute-start.15 = (bf16[32,2048]{1,0:T(8,128)(2,1)S(1)}, bf16[32,2048]{1,0:T(8,128)(2,1)S(1)}, u32[]{:S(2)}, u32[]{:S(2)}) collective-permute-start(bf16[32,2048]{1,0:T(8,128)(2,1)S(1)} %collective-permute-done.14), channel_id=1, source_target_pairs={{0,8},{1,9},{2,10},{3,11},{4,12},{5,13},{6,14},{7,15},{8,0},{9,1},... | collective-permute-start | bytes 393224 | tf_op jit(solution)/shard_map/ppermute | solution.py:33
  22.3 9.0 %collective-permute-start.3 = (bf16[4,16,1664]{2,1,0:T(8,128)(2,1)S(1)}, bf16[4,16,1664]{2,1,0:T(8,128)(2,1)S(1)}, u32[]{:S(2)}, u32[]{:S(2)}) collective-permute-start(bf16[4,16,1664]{2,1,0:T(8,128)(2,1)S(1)} %pad_maximum_fusion.2.refs_0_), channel_id=1, source_target_pairs={{0,2},{1,5},{2,0},{3,7},{4,6},{5,1},{6,4},{7,3},{8,10},{9,13},{10,... | collective-permute-start | bytes 638984 | tf_op jit(solution)/shard_map/ppermute | solution.py:33
  23.9 10.7 %collective-permute-start.4 = (bf16[4,16,1664]{2,1,0:T(8,128)(2,1)S(1)}, bf16[4,16,1664]{2,1,0:T(8,128)(2,1)S(1)}, u32[]{:S(2)}, u32[]{:S(2)}) collective-permute-start(bf16[4,16,1664]{2,1,0:T(8,128)(2,1)S(1)} %pad_maximum_fusion.2.refs_0_), channel_id=1, source_target_pairs={{0,4},{1,3},{2,6},{3,1},{4,0},{5,7},{6,2},{7,5},{8,12},{9,11},{10,... | collective-permute-start | bytes 638984 | tf_op jit(solution)/shard_map/ppermute | solution.py:33
  25.4 9.2 %collective-permute-start.5 = (bf16[4,16,1664]{2,1,0:T(8,128)(2,1)S(1)}, bf16[4,16,1664]{2,1,0:T(8,128)(2,1)S(1)}, u32[]{:S(2)}, u32[]{:S(2)}) collective-permute-start(bf16[4,16,1664]{2,1,0:T(8,128)(2,1)S(1)} %pad_maximum_fusion.2.refs_0_), channel_id=1, source_target_pairs={{0,6},{1,7},{2,4},{3,5},{4,2},{5,3},{6,0},{7,1},{8,14},{9,15},{10,... | collective-permute-start | bytes 638984 | tf_op jit(solution)/shard_map/ppermute | solution.py:33
  25.9 33.1 %copy-start.3 = (bf16[4,80,512]{2,1,0:T(8,128)(2,1)}, bf16[4,80,512]{2,1,0:T(8,128)(2,1)S(1)}, u32[]{:S(2)}) copy-start(bf16[4,80,512]{2,1,0:T(8,128)(2,1)S(1)} %pad_maximum_fusion.1.refs_8_) | copy-start | bytes 983044
  26.0 14.8 %collective-permute-start.17 = (bf16[4,80,512]{2,1,0:T(8,128)(2,1)S(1)}, bf16[4,80,512]{2,1,0:T(8,128)(2,1)S(1)}, u32[]{:S(2)}, u32[]{:S(2)}) collective-permute-start(bf16[4,80,512]{2,1,0:T(8,128)(2,1)S(1)} %pad_maximum_fusion.1.refs_8_), channel_id=1, source_target_pairs={{0,16},{1,17},{2,18},{3,19},{4,20},{5,21},{6,22},{7,23},{8,24},{9,... | collective-permute-start | bytes 983048 | tf_op jit(solution)/shard_map/ppermute | solution.py:33
  29.5 17.2 %copy-start.2 = (bf16[4,32,2048]{2,1,0:T(8,128)(2,1)}, bf16[4,32,2048]{2,1,0:T(8,128)(2,1)S(1)}, u32[]{:S(2)}) copy-start(bf16[4,32,2048]{2,1,0:T(8,128)(2,1)S(1)} %pad_maximum_fusion.refs_10_.refs_0_) | copy-start | bytes 1572868
  29.5 12.4 %collective-permute-start.16 = (bf16[4,32,2048]{2,1,0:T(8,128)(2,1)S(1)}, bf16[4,32,2048]{2,1,0:T(8,128)(2,1)S(1)}, u32[]{:S(2)}, u32[]{:S(2)}) collective-permute-start(bf16[4,32,2048]{2,1,0:T(8,128)(2,1)S(1)} %pad_maximum_fusion.refs_10_.refs_0_), channel_id=1, source_target_pairs={{0,2},{1,5},{2,0},{3,7},{4,6},{5,1},{6,4},{7,3},{8,10},{9,13},{10,... | collective-permute-start | bytes 1572872 | tf_op jit(solution)/shard_map/ppermute | solution.py:33
  31.3 15.4 %copy-start.20 = (bf16[4,16,1664]{2,1,0:T(8,128)(2,1)}, bf16[4,16,1664]{2,1,0:T(8,128)(2,1)S(1)}, u32[]{:S(2)}) copy-start(bf16[4,16,1664]{2,1,0:T(8,128)(2,1)S(1)} %collective-permute-done.3.refs_1_) | copy-start | bytes 638980
  31.3 10.6 %collective-permute-start.6 = (bf16[4,16,1664]{2,1,0:T(8,128)(2,1)S(1)}, bf16[4,16,1664]{2,1,0:T(8,128)(2,1)S(1)}, u32[]{:S(2)}, u32[]{:S(2)}) collective-permute-start(bf16[4,16,1664]{2,1,0:T(8,128)(2,1)S(1)} %pad_maximum_fusion.2.refs_0_), channel_id=1, source_target_pairs={{0,1},{1,0},{2,3},{3,2},{4,5},{5,4},{6,7},{7,6},{8,9},{9,8},{10,11... | collective-permute-start | bytes 638984 | tf_op jit(solution)/shard_map/ppermute | solution.py:33
  34.5 12.1 %copy-start.21 = (bf16[4,16,1664]{2,1,0:T(8,128)(2,1)}, bf16[4,16,1664]{2,1,0:T(8,128)(2,1)S(1)}, u32[]{:S(2)}) copy-start(bf16[4,16,1664]{2,1,0:T(8,128)(2,1)S(1)} %collective-permute-done.4.refs_2_) | copy-start | bytes 638980
  34.6 8.6 %collective-permute-start.7 = (bf16[4,16,1664]{2,1,0:T(8,128)(2,1)S(1)}, bf16[4,16,1664]{2,1,0:T(8,128)(2,1)S(1)}, u32[]{:S(2)}, u32[]{:S(2)}) collective-permute-start(bf16[4,16,1664]{2,1,0:T(8,128)(2,1)S(1)} %collective-permute-done.3.refs_1_), channel_id=1, source_target_pairs={{0,1},{1,0},{2,3},{3,2},{4,5},{5,4},{6,7},{7,6},{8,9},{9,8},{10,11... | collective-permute-start | bytes 638984 | tf_op jit(solution)/shard_map/ppermute | solution.py:33
  34.6 12.1 %copy-start.22 = (bf16[4,16,1664]{2,1,0:T(8,128)(2,1)}, bf16[4,16,1664]{2,1,0:T(8,128)(2,1)S(1)}, u32[]{:S(2)}) copy-start(bf16[4,16,1664]{2,1,0:T(8,128)(2,1)S(1)} %collective-permute-done.5.refs_3_) | copy-start | bytes 638980
  34.6 10.1 %collective-permute-start.8 = (bf16[4,16,1664]{2,1,0:T(8,128)(2,1)S(1)}, bf16[4,16,1664]{2,1,0:T(8,128)(2,1)S(1)}, u32[]{:S(2)}, u32[]{:S(2)}) collective-permute-start(bf16[4,16,1664]{2,1,0:T(8,128)(2,1)S(1)} %collective-permute-done.4.refs_2_), channel_id=1, source_target_pairs={{0,1},{1,0},{2,3},{3,2},{4,5},{5,4},{6,7},{7,6},{8,9},{9,8},{10,11... | collective-permute-start | bytes 638984 | tf_op jit(solution)/shard_map/ppermute | solution.py:33
  40.7 22.9 %copy-start.13 = (bf16[4,80,512]{2,1,0:T(8,128)(2,1)}, bf16[4,80,512]{2,1,0:T(8,128)(2,1)S(1)}, u32[]{:S(2)}) copy-start(bf16[4,80,512]{2,1,0:T(8,128)(2,1)S(1)} %collective-permute-done.17.refs_10_) | copy-start | bytes 983044
  40.7 3.9 %collective-permute-start.9 = (bf16[4,16,1664]{2,1,0:T(8,128)(2,1)S(1)}, bf16[4,16,1664]{2,1,0:T(8,128)(2,1)S(1)}, u32[]{:S(2)}, u32[]{:S(2)}) collective-permute-start(bf16[4,16,1664]{2,1,0:T(8,128)(2,1)S(1)} %collective-permute-done.5.refs_3_), channel_id=1, source_target_pairs={{0,1},{1,0},{2,3},{3,2},{4,5},{5,4},{6,7},{7,6},{8,9},{9,8},{10,11... | collective-permute-start | bytes 638984 | tf_op jit(solution)/shard_map/ppermute | solution.py:33
  41.9 21.1 %copy-start.6 = (bf16[4,32,2048]{2,1,0:T(8,128)(2,1)}, bf16[4,32,2048]{2,1,0:T(8,128)(2,1)S(1)}, u32[]{:S(2)}) copy-start(bf16[4,32,2048]{2,1,0:T(8,128)(2,1)S(1)} %collective-permute-done.16.refs_1_) | copy-start | bytes 1572868
  41.9 16.2 %collective-permute-start.20 = (bf16[4,80,512]{2,1,0:T(8,128)(2,1)S(1)}, bf16[4,80,512]{2,1,0:T(8,128)(2,1)S(1)}, u32[]{:S(2)}, u32[]{:S(2)}) collective-permute-start(bf16[4,80,512]{2,1,0:T(8,128)(2,1)S(1)} %pad_maximum_fusion.1.refs_8_), channel_id=1, source_target_pairs={{0,8},{1,9},{2,10},{3,11},{4,12},{5,13},{6,14},{7,15},{8,0},{9,1},... | collective-permute-start | bytes 983048 | tf_op jit(solution)/shard_map/ppermute | solution.py:33
  41.9 4.8 %copy-start.23 = (bf16[4,16,1664]{2,1,0:T(8,128)(2,1)}, bf16[4,16,1664]{2,1,0:T(8,128)(2,1)S(1)}, u32[]{:S(2)}) copy-start(bf16[4,16,1664]{2,1,0:T(8,128)(2,1)S(1)} %collective-permute-done.6.refs_4_) | copy-start | bytes 638980
  41.9 17.1 %collective-permute-start.18 = (bf16[4,32,2048]{2,1,0:T(8,128)(2,1)S(1)}, bf16[4,32,2048]{2,1,0:T(8,128)(2,1)S(1)}, u32[]{:S(2)}, u32[]{:S(2)}) collective-permute-start(bf16[4,32,2048]{2,1,0:T(8,128)(2,1)S(1)} %pad_maximum_fusion.refs_10_.refs_0_), channel_id=1, source_target_pairs={{0,4},{1,3},{2,6},{3,1},{4,0},{5,7},{6,2},{7,5},{8,12},{9,11},{10,... | collective-permute-start | bytes 1572872 | tf_op jit(solution)/shard_map/ppermute | solution.py:33
  43.2 3.5 %copy-start.24 = (bf16[4,16,1664]{2,1,0:T(8,128)(2,1)}, bf16[4,16,1664]{2,1,0:T(8,128)(2,1)S(1)}, u32[]{:S(2)}) copy-start(bf16[4,16,1664]{2,1,0:T(8,128)(2,1)S(1)} %collective-permute-done.7.refs_5_) | copy-start | bytes 638980
  43.2 15.8 %collective-permute-start.19 = (bf16[4,32,2048]{2,1,0:T(8,128)(2,1)S(1)}, bf16[4,32,2048]{2,1,0:T(8,128)(2,1)S(1)}, u32[]{:S(2)}, u32[]{:S(2)}) collective-permute-start(bf16[4,32,2048]{2,1,0:T(8,128)(2,1)S(1)} %pad_maximum_fusion.refs_10_.refs_0_), channel_id=1, source_target_pairs={{0,6},{1,7},{2,4},{3,5},{4,2},{5,3},{6,0},{7,1},{8,14},{9,15},{10,... | collective-permute-start | bytes 1572872 | tf_op jit(solution)/shard_map/ppermute | solution.py:33
  44.6 2.1 %copy-start.25 = (bf16[4,16,1664]{2,1,0:T(8,128)(2,1)}, bf16[4,16,1664]{2,1,0:T(8,128)(2,1)S(1)}, u32[]{:S(2)}) copy-start(bf16[4,16,1664]{2,1,0:T(8,128)(2,1)S(1)} %collective-permute-done.8.refs_6_) | copy-start | bytes 638980
  44.6 18.4 %collective-permute-start.22 = (bf16[4,32,2048]{2,1,0:T(8,128)(2,1)S(1)}, bf16[4,32,2048]{2,1,0:T(8,128)(2,1)S(1)}, u32[]{:S(2)}, u32[]{:S(2)}) collective-permute-start(bf16[4,32,2048]{2,1,0:T(8,128)(2,1)S(1)} %pad_maximum_fusion.refs_10_.refs_0_), channel_id=1, source_target_pairs={{0,1},{1,0},{2,3},{3,2},{4,5},{5,4},{6,7},{7,6},{8,9},{9,8},{10,11... | collective-permute-start | bytes 1572872 | tf_op jit(solution)/shard_map/ppermute | solution.py:33
  44.6 2.1 %copy-start.26 = (bf16[4,16,1664]{2,1,0:T(8,128)(2,1)}, bf16[4,16,1664]{2,1,0:T(8,128)(2,1)S(1)}, u32[]{:S(2)}) copy-start(bf16[4,16,1664]{2,1,0:T(8,128)(2,1)S(1)} %collective-permute-done.9.refs_7_) | copy-start | bytes 638980
  44.7 14.4 %collective-permute-start.21 = (bf16[4,80,512]{2,1,0:T(8,128)(2,1)S(1)}, bf16[4,80,512]{2,1,0:T(8,128)(2,1)S(1)}, u32[]{:S(2)}, u32[]{:S(2)}) collective-permute-start(bf16[4,80,512]{2,1,0:T(8,128)(2,1)S(1)} %collective-permute-done.17.refs_10_), channel_id=1, source_target_pairs={{0,8},{1,9},{2,10},{3,11},{4,12},{5,13},{6,14},{7,15},{8,0},{9,1},... | collective-permute-start | bytes 983048 | tf_op jit(solution)/shard_map/ppermute | solution.py:33
  58.1 9.3 %copy-start.14 = (bf16[4,80,512]{2,1,0:T(8,128)(2,1)}, bf16[4,80,512]{2,1,0:T(8,128)(2,1)S(1)}, u32[]{:S(2)}) copy-start(bf16[4,80,512]{2,1,0:T(8,128)(2,1)S(1)} %collective-permute-done.20.refs_9_) | copy-start | bytes 983044
  59.0 8.4 %copy-start.15 = (bf16[4,80,512]{2,1,0:T(8,128)(2,1)}, bf16[4,80,512]{2,1,0:T(8,128)(2,1)S(1)}, u32[]{:S(2)}) copy-start(bf16[4,80,512]{2,1,0:T(8,128)(2,1)S(1)} %collective-permute-done.21.refs_11_) | copy-start | bytes 983044
  59.0 8.4 %copy-start.7 = (bf16[4,32,2048]{2,1,0:T(8,128)(2,1)}, bf16[4,32,2048]{2,1,0:T(8,128)(2,1)S(1)}, u32[]{:S(2)}) copy-start(bf16[4,32,2048]{2,1,0:T(8,128)(2,1)S(1)} %collective-permute-done.18.refs_2_) | copy-start | bytes 1572868
  59.0 8.4 %copy-start.8 = (bf16[4,32,2048]{2,1,0:T(8,128)(2,1)}, bf16[4,32,2048]{2,1,0:T(8,128)(2,1)S(1)}, u32[]{:S(2)}) copy-start(bf16[4,32,2048]{2,1,0:T(8,128)(2,1)S(1)} %collective-permute-done.19.refs_3_) | copy-start | bytes 1572868
  59.0 4.6 %collective-permute-start.26 = (bf16[4,80,512]{2,1,0:T(8,128)(2,1)S(1)}, bf16[4,80,512]{2,1,0:T(8,128)(2,1)S(1)}, u32[]{:S(2)}, u32[]{:S(2)}) collective-permute-start(bf16[4,80,512]{2,1,0:T(8,128)(2,1)S(1)} %pad_maximum_fusion.1.refs_8_), channel_id=1, source_target_pairs={{0,1},{1,0},{2,3},{3,2},{4,5},{5,4},{6,7},{7,6},{8,9},{9,8},{10,11... | collective-permute-start | bytes 983048 | tf_op jit(solution)/shard_map/ppermute | solution.py:33
  62.4 1.7 %collective-permute-start.27 = (bf16[4,80,512]{2,1,0:T(8,128)(2,1)S(1)}, bf16[4,80,512]{2,1,0:T(8,128)(2,1)S(1)}, u32[]{:S(2)}, u32[]{:S(2)}) collective-permute-start(bf16[4,80,512]{2,1,0:T(8,128)(2,1)S(1)} %collective-permute-done.20.refs_9_), channel_id=1, source_target_pairs={{0,1},{1,0},{2,3},{3,2},{4,5},{5,4},{6,7},{7,6},{8,9},{9,8},{10,11... | collective-permute-start | bytes 983048 | tf_op jit(solution)/shard_map/ppermute | solution.py:33
  62.5 4.8 %collective-permute-start.24 = (bf16[4,32,2048]{2,1,0:T(8,128)(2,1)S(1)}, bf16[4,32,2048]{2,1,0:T(8,128)(2,1)S(1)}, u32[]{:S(2)}, u32[]{:S(2)}) collective-permute-start(bf16[4,32,2048]{2,1,0:T(8,128)(2,1)S(1)} %collective-permute-done.18.refs_2_), channel_id=1, source_target_pairs={{0,1},{1,0},{2,3},{3,2},{4,5},{5,4},{6,7},{7,6},{8,9},{9,8},{10,11... | collective-permute-start | bytes 1572872 | tf_op jit(solution)/shard_map/ppermute | solution.py:33
  62.9 4.4 %collective-permute-start.25 = (bf16[4,32,2048]{2,1,0:T(8,128)(2,1)S(1)}, bf16[4,32,2048]{2,1,0:T(8,128)(2,1)S(1)}, u32[]{:S(2)}, u32[]{:S(2)}) collective-permute-start(bf16[4,32,2048]{2,1,0:T(8,128)(2,1)S(1)} %collective-permute-done.19.refs_3_), channel_id=1, source_target_pairs={{0,1},{1,0},{2,3},{3,2},{4,5},{5,4},{6,7},{7,6},{8,9},{9,8},{10,11... | collective-permute-start | bytes 1572872 | tf_op jit(solution)/shard_map/ppermute | solution.py:33
  63.0 4.4 %copy-start.9 = (bf16[4,32,2048]{2,1,0:T(8,128)(2,1)}, bf16[4,32,2048]{2,1,0:T(8,128)(2,1)S(1)}, u32[]{:S(2)}) copy-start(bf16[4,32,2048]{2,1,0:T(8,128)(2,1)S(1)} %collective-permute-done.22.refs_4_) | copy-start | bytes 1572868
  63.0 4.3 %collective-permute-start.23 = (bf16[4,32,2048]{2,1,0:T(8,128)(2,1)S(1)}, bf16[4,32,2048]{2,1,0:T(8,128)(2,1)S(1)}, u32[]{:S(2)}, u32[]{:S(2)}) collective-permute-start(bf16[4,32,2048]{2,1,0:T(8,128)(2,1)S(1)} %collective-permute-done.16.refs_1_), channel_id=1, source_target_pairs={{0,1},{1,0},{2,3},{3,2},{4,5},{5,4},{6,7},{7,6},{8,9},{9,8},{10,11... | collective-permute-start | bytes 1572872 | tf_op jit(solution)/shard_map/ppermute | solution.py:33
  63.7 3.7 %copy-start.16 = (bf16[4,80,512]{2,1,0:T(8,128)(2,1)}, bf16[4,80,512]{2,1,0:T(8,128)(2,1)S(1)}, u32[]{:S(2)}) copy-start(bf16[4,80,512]{2,1,0:T(8,128)(2,1)S(1)} %collective-permute-done.26.refs_12_) | copy-start | bytes 983044
  63.7 3.2 %collective-permute-start.28 = (bf16[4,80,512]{2,1,0:T(8,128)(2,1)S(1)}, bf16[4,80,512]{2,1,0:T(8,128)(2,1)S(1)}, u32[]{:S(2)}, u32[]{:S(2)}) collective-permute-start(bf16[4,80,512]{2,1,0:T(8,128)(2,1)S(1)} %collective-permute-done.17.refs_10_), channel_id=1, source_target_pairs={{0,1},{1,0},{2,3},{3,2},{4,5},{5,4},{6,7},{7,6},{8,9},{9,8},{10,11... | collective-permute-start | bytes 983048 | tf_op jit(solution)/shard_map/ppermute | solution.py:33
  64.1 3.3 %copy-start.17 = (bf16[4,80,512]{2,1,0:T(8,128)(2,1)}, bf16[4,80,512]{2,1,0:T(8,128)(2,1)S(1)}, u32[]{:S(2)}) copy-start(bf16[4,80,512]{2,1,0:T(8,128)(2,1)S(1)} %collective-permute-done.27.refs_13_) | copy-start | bytes 983044
  64.1 3.2 %collective-permute-start.29 = (bf16[4,80,512]{2,1,0:T(8,128)(2,1)S(1)}, bf16[4,80,512]{2,1,0:T(8,128)(2,1)S(1)}, u32[]{:S(2)}, u32[]{:S(2)}) collective-permute-start(bf16[4,80,512]{2,1,0:T(8,128)(2,1)S(1)} %collective-permute-done.21.refs_11_), channel_id=1, source_target_pairs={{0,1},{1,0},{2,3},{3,2},{4,5},{5,4},{6,7},{7,6},{8,9},{9,8},{10,11... | collective-permute-start | bytes 983048 | tf_op jit(solution)/shard_map/ppermute | solution.py:33
  80.8 8.2 %collective-permute-start.30 = (bf16[8,48,2048]{2,1,0:T(8,128)(2,1)}, bf16[8,48,2048]{2,1,0:T(8,128)(2,1)}, u32[]{:S(2)}, u32[]{:S(2)}) collective-permute-start(bf16[8,48,2048]{2,1,0:T(8,128)(2,1)} %get-tuple-element.98), channel_id=1, source_target_pairs={{0,1},{1,0},{2,3},{3,2},{4,5},{5,4},{6,7},{7,6},{8,9},{9,8},{10,11... | collective-permute-start | bytes 4718600 | tf_op jit(solution)/shard_map/ppermute | solution.py:33
  81.2 31.9 %collective-permute-start.34 = (bf16[8,48,2048]{2,1,0:T(8,128)(2,1)}, bf16[8,48,2048]{2,1,0:T(8,128)(2,1)S(1)}, u32[]{:S(2)}, u32[]{:S(2)}) collective-permute-start(bf16[8,48,2048]{2,1,0:T(8,128)(2,1)} %get-tuple-element.115), channel_id=1, source_target_pairs={{0,1},{1,0},{2,3},{3,2},{4,5},{5,4},{6,7},{7,6},{8,9},{9,8},{10,11... | collective-permute-start | bytes 4718600 | tf_op jit(solution)/shard_map/ppermute | solution.py:33
  81.3 7.6 %copy-start = (bf16[16,48,2048]{2,1,0:T(8,128)(2,1)S(1)}, bf16[16,48,2048]{2,1,0:T(8,128)(2,1)}, u32[]{:S(2)}) copy-start(bf16[16,48,2048]{2,1,0:T(8,128)(2,1)} %get-tuple-element.109) | copy-start | bytes 9437188
  92.2 20.9 %collective-permute-start.35 = (bf16[8,48,2048]{2,1,0:T(8,128)(2,1)}, bf16[8,48,2048]{2,1,0:T(8,128)(2,1)}, u32[]{:S(2)}, u32[]{:S(2)}) collective-permute-start(bf16[8,48,2048]{2,1,0:T(8,128)(2,1)} %add_convert_fusion.refs_15_), channel_id=1, source_target_pairs={{0,4},{1,3},{2,6},{3,1},{4,0},{5,7},{6,2},{7,5},{8,12},{9,11},{10,... | collective-permute-start | bytes 4718600 | tf_op jit(solution)/shard_map/ppermute | solution.py:33
  108.6 2.2 %collective-permute-start.32 = (bf16[8,16,2176]{2,1,0:T(8,128)(2,1)}, bf16[8,16,2176]{2,1,0:T(8,128)(2,1)S(1)}, u32[]{:S(2)}, u32[]{:S(2)}) collective-permute-start(bf16[8,16,2176]{2,1,0:T(8,128)(2,1)} %get-tuple-element.114), channel_id=1, source_target_pairs={{0,1},{1,0},{2,3},{3,2},{4,5},{5,4},{6,7},{7,6},{8,9},{9,8},{10,11... | collective-permute-start | bytes 1671176 | tf_op jit(solution)/shard_map/ppermute | solution.py:33
  108.7 16.9 %collective-permute-start.31 = (bf16[8,16,2176]{2,1,0:T(8,128)(2,1)}, bf16[8,16,2176]{2,1,0:T(8,128)(2,1)S(1)}, u32[]{:S(2)}, u32[]{:S(2)}) collective-permute-start(bf16[8,16,2176]{2,1,0:T(8,128)(2,1)} %get-tuple-element.113), channel_id=1, source_target_pairs={{0,1},{1,0},{2,3},{3,2},{4,5},{5,4},{6,7},{7,6},{8,9},{9,8},{10,11... | collective-permute-start | bytes 1671176 | tf_op jit(solution)/shard_map/ppermute | solution.py:33
  112.1 13.5 %copy-start.1 = (bf16[16,16,2176]{2,1,0:T(8,128)(2,1)S(1)}, bf16[16,16,2176]{2,1,0:T(8,128)(2,1)}, u32[]{:S(2)}) copy-start(bf16[16,16,2176]{2,1,0:T(8,128)(2,1)} %get-tuple-element.112) | copy-start | bytes 3342340
  112.1 13.5 %collective-permute-start.33 = (bf16[8,16,2176]{2,1,0:T(8,128)(2,1)S(1)}, bf16[8,16,2176]{2,1,0:T(8,128)(2,1)S(1)}, u32[]{:S(2)}, u32[]{:S(2)}) collective-permute-start(bf16[8,16,2176]{2,1,0:T(8,128)(2,1)S(1)} %add_convert_fusion.2), channel_id=1, source_target_pairs={{0,4},{1,3},{2,6},{3,1},{4,0},{5,7},{6,2},{7,5},{8,12},{9,11},{10,... | collective-permute-start | bytes 1671176 | tf_op jit(solution)/shard_map/ppermute | solution.py:33
  114.7 14.6 %collective-permute-start.37 = (bf16[4,48,2048]{2,1,0:T(8,128)(2,1)S(1)}, bf16[4,48,2048]{2,1,0:T(8,128)(2,1)S(1)}, u32[]{:S(2)}, u32[]{:S(2)}) collective-permute-start(bf16[4,48,2048]{2,1,0:T(8,128)(2,1)S(1)} %add_convert_fusion.1), channel_id=1, source_target_pairs={{0,2},{1,5},{2,0},{3,7},{4,6},{5,1},{6,4},{7,3},{8,10},{9,13},{10,... | collective-permute-start | bytes 2359304 | tf_op jit(solution)/shard_map/ppermute | solution.py:33
  125.7 7.1 %collective-permute-start.36 = (bf16[4,16,2176]{2,1,0:T(8,128)(2,1)S(1)}, bf16[4,16,2176]{2,1,0:T(8,128)(2,1)S(1)}, u32[]{:S(2)}, u32[]{:S(2)}) collective-permute-start(bf16[4,16,2176]{2,1,0:T(8,128)(2,1)S(1)} %add_convert_fusion.4), channel_id=1, source_target_pairs={{0,2},{1,5},{2,0},{3,7},{4,6},{5,1},{6,4},{7,3},{8,10},{9,13},{10,... | collective-permute-start | bytes 835592 | tf_op jit(solution)/shard_map/ppermute | solution.py:33
  130.5 11.9 %collective-permute-start.39 = (bf16[2,48,2048]{2,1,0:T(8,128)(2,1)S(1)}, bf16[2,48,2048]{2,1,0:T(8,128)(2,1)S(1)}, u32[]{:S(2)}, u32[]{:S(2)}) collective-permute-start(bf16[2,48,2048]{2,1,0:T(8,128)(2,1)S(1)} %add_convert_fusion.3), channel_id=1, source_target_pairs={{0,8},{1,9},{2,10},{3,11},{4,12},{5,13},{6,14},{7,15},{8,0},{9,1},... | collective-permute-start | bytes 1179656 | tf_op jit(solution)/shard_map/ppermute | solution.py:33
  132.9 12.5 %collective-permute-start.38 = (bf16[2,16,2176]{2,1,0:T(8,128)(2,1)S(1)}, bf16[2,16,2176]{2,1,0:T(8,128)(2,1)S(1)}, u32[]{:S(2)}, u32[]{:S(2)}) collective-permute-start(bf16[2,16,2176]{2,1,0:T(8,128)(2,1)S(1)} %add_convert_fusion.6), channel_id=1, source_target_pairs={{0,8},{1,9},{2,10},{3,11},{4,12},{5,13},{6,14},{7,15},{8,0},{9,1},... | collective-permute-start | bytes 417800 | tf_op jit(solution)/shard_map/ppermute | solution.py:33
  145.5 11.5 %collective-permute-start.40 = (bf16[16,2176]{1,0:T(8,128)(2,1)S(1)}, bf16[16,2176]{1,0:T(8,128)(2,1)S(1)}, u32[]{:S(2)}, u32[]{:S(2)}) collective-permute-start(bf16[16,2176]{1,0:T(8,128)(2,1)S(1)} %get-tuple-element.128), channel_id=1, source_target_pairs={{0,16},{1,17},{2,18},{3,19},{4,20},{5,21},{6,22},{7,23},{8,24},{9,... | collective-permute-start | bytes 208904 | tf_op jit(solution)/shard_map/ppermute | solution.py:33
  148.6 12.4 %collective-permute-start.41 = (bf16[48,2048]{1,0:T(8,128)(2,1)S(1)}, bf16[48,2048]{1,0:T(8,128)(2,1)S(1)}, u32[]{:S(2)}, u32[]{:S(2)}) collective-permute-start(bf16[48,2048]{1,0:T(8,128)(2,1)S(1)} %get-tuple-element.127), channel_id=1, source_target_pairs={{0,16},{1,17},{2,18},{3,19},{4,20},{5,21},{6,22},{7,23},{8,24},{9,... | collective-permute-start | bytes 589832 | tf_op jit(solution)/shard_map/ppermute | solution.py:33
  (5 other events, 4.7 us)

commit v5 on v4

--- a/solution.py
+++ b/solution.py
@@ -63,13 +63,15 @@
 
 
 class Sum:
-    def __init__(self, own, low, high):
+    def __init__(self, own, low, *high):
         self.own = own
-        self.high = send(high, CORE)
+        self.high = [send(part, CORE) for part in high]
         self.low = send(low, CORE)
 
     def first(self):
-        part = widen(self.own[8:], self.high).astype(LOW)
+        size = 8 // len(self.high)
+        parts = [widen(self.own[8 + size * i : 8 + size * i + size], part) for i, part in enumerate(self.high)]
+        part = jnp.concatenate(parts).astype(LOW)
         self.far = send(part, FAR)
         return part
 
@@ -94,6 +96,40 @@
 
     def done(self):
         return widen(self.rest, self.beyond)
+
+
+class LayersFirst:
+    def __init__(self, own, other):
+        self.own = own
+        self.core = send(other, CORE)
+
+    def first(self):
+        part = widen(self.own[1::2], self.core[1::2]).astype(LOW)
+        self.beside = send(part, LAYER[1])
+        return part
+
+    def second(self):
+        part = widen(self.own[2::4], self.core[2::4], self.beside[1::2]).astype(LOW)
+        self.beyond = send(part, LAYER[2])
+        return part
+
+    def total(self, quad):
+        at = slice(4 * quad, 4 * quad + 1)
+        half = slice(2 * quad, 2 * quad + 1)
+        return widen(self.own[at], self.core[at], self.beside[half], self.beyond[quad : quad + 1])
+
+    def third(self):
+        part = widen(self.own[8::4], self.core[8::4], self.beside[4::2], self.beyond[2:]).astype(LOW)
+        self.far = send(part, FAR)
+        return part
+
+    def fourth(self):
+        part = widen(self.total(1), self.far[1:]).astype(LOW)
+        self.near = send(part, NEAR)
+        return part
+
+    def done(self):
+        return widen(self.total(0), self.far[:1], self.near)[0]
 
 
 def shard_at(me, k, turned=False):
@@ -381,9 +417,13 @@
 
     def share(grad, row, slot):
         for k in range(SHARDS):
-            half, place = (halves[0], k) if k < 16 else (halves[k // 8 - 1], k % 8)
+            if row is None:
+                half, place, row_at = halves[3 + k // 16], k % 16, 0
+            else:
+                half, place = (halves[0], k) if k < 16 else (halves[k // 8 - 1], k % 8)
+                row_at = row
             at = block(shard_at(me, k), 16)
-            copy = pltpu.make_async_copy(grad.at[at], half.at[place, pl.ds(row, 16)], sem.at[slot])
+            copy = pltpu.make_async_copy(grad.at[at], half.at[place, pl.ds(row_at, 16)], sem.at[slot])
             copy.start()
             copies.append(copy)
 
@@ -418,7 +458,7 @@
             for j in range(4):
                 part = grad[64 * r + 16 * j : 64 * r + 16 * j + 16, :]
                 low_down[64 * k + 16 * r : 64 * k + 16 * r + 16, 512 * j : 512 * j + 512] = part.astype(LOW)
-    share(low_down, 32, 6)
+    share(low_down, None, 6)
     down.wait()
     for k in range(8):
         lanes = slice(256 * k, 256 * k + 256)
@@ -559,7 +599,7 @@
         rows[0, 8 * r : 8 * r + 8, 0:128] = tile[0:8]
         rows[0, 8 * r : 8 * r + 8, 128:256] = tile[8:16]
     for k in range(SHARDS):
-        half, place = (own, k) if k < 16 else (halves[k // 8 - 2], k % 8)
+        half, place = (own, k) if k < 16 else (halves[0], k % 8) if k < 24 else (halves[k // 4 - 5], k % 4)
         at, near = block(shard_at(me, k), 16), block(shard_at(me, k), 8)
         half.buffer[place, :, :1536] = grad_qkv[at, :].astype(LOW)
         half.buffer[place, :, 1536:2048] = grad_out[at, :].astype(LOW)
@@ -680,7 +720,7 @@
         cores = [send(part, CORE) for part in came[2:]]
         pieces[1:] = [came[0:4] + early + cores[:2], came[4:8] + cores[2:]]
     (
-        output, dfirst, dmixed, sum_up, sum_gain, sum_shift, sum_pool, own_pair, *other_pair
+        output, dfirst, dmixed, sum_up, sum_gain, sum_shift, sum_pool, own_pair, low_pair, high_pair, *both_down
     ) = call(
         ffn_kernel,
         12,
@@ -698,10 +738,11 @@
             ((entries, 512), low), ((entries, 2048), low), ((entries, 512), wide), ((entries, 2048), low),
             ((entries, 2048), wide), ((512, 2048), low), ((512, 2048), low), ((512, 2048), low),
         ],
-        raw=[((16, 48, 2048), low), ((8, 48, 2048), low), ((8, 48, 2048), low)],
+        raw=[((16, 32, 2048), low), *[((8, 32, 2048), low)] * 2, *[((16, 16, 2048), low)] * 2],
     )
     if tuned:
-        pair = Sum(own_pair, *other_pair)
+        pair = Sum(own_pair, low_pair, high_pair)
+        down = LayersFirst(*both_down)
     (dkeyval, dquery, query_part) = call(
         attend_back_kernel, 8,
         me,
@@ -714,8 +755,10 @@
     )
     part = own_pair
     if tuned:
-        query_part, pair.high = tie(query_part, pair.high, every=True)
+        query_part, pair.high[0], down.core = tie(query_part, pair.high[0], down.core, every=True)
         part = pair.first()
+        down.core = tie(down.core, part)
+        part = down.first()
     (grad_embeds, own_last, *other_last) = call(
         input_back_kernel,
         18,
@@ -726,7 +769,7 @@
             (dkeyval, steps, None), (flat, steps, None), (sum_gain, 1, None), (sum_shift, 1, None), (sum_pool, 1, None),
             (sum_up, 1, None), (mixed, 1, None), (normed0, 1, None), (dquery, 1, None), (normed, 1, None),
         ],
-        [((rows, 512), low, steps), ((16, 16, 2176), low, 1), ((8, 16, 2176), low, 1), ((8, 16, 2176), low, 1)],
+        [((rows, 512), low, steps), ((16, 16, 2176), low, 1), ((8, 16, 2176), low, 1), *[((4, 16, 2176), low, 1)] * 2],
         [
             ((512, 1536), wide), ((512, 512), wide), ((128, 512), low), ((2, RB, 512), wide), ((2, RB, 512), wide),
             ((2, RB, 512), low), ((2, 4 * RB, 128), wide), ((2, 4 * RB, 128), wide), ((16, 512), wide),
@@ -736,28 +779,37 @@
     )
     if tuned:
         last = Sum(own_last, *other_last)
+        pair.far, down.beside, *last.high = tie(pair.far, down.beside, *last.high, every=True)
         part = last.first()
-        pair.far = tie(pair.far, part)
+        pair.far, down.beside = tie(pair.far, down.beside, part, every=True)[:2]
         part = pair.second()
+        down.beside = tie(down.beside, part)
+        part = down.second()
         last.far = tie(last.far, part)
         part = last.second()
         pair.near = tie(pair.near, part)
         part = pair.third()
+        down.beyond = tie(down.beyond, part)
+        part = down.third()
         last.near = tie(last.near, part)
         part = last.third()
-        pair.beside = tie(pair.beside, part)
+        pair.beside, down.far = tie(pair.beside, down.far, part, every=True)[:2]
         part = pair.fourth()
+        down.far = tie(down.far, part)
+        part = down.fourth()
         last.beside = tie(last.beside, part)
         part = last.fourth()
-        last.beyond = tie(last.beyond, part)
+        down.near = tie(down.near, part)
+        sum_down = down.done()
+        pair.beyond = tie(pair.beyond, sum_down)
+        pair = pair.done()
+        last.beyond = tie(last.beyond, pair)
         sum_qkv, sum_out, last_small = [
             widen(last.rest[:, at], last.beyond[:, at])
             for at in (slice(0, 1536), slice(1536, 2048), slice(2048, 2176))
         ]
-        pair.beyond = tie(pair.beyond, sum_qkv)
-        pair = pair.done()
-        sum_proj, sum_up = pair[:16], pair[16:32]
-        sum_down = jnp.concatenate([pair[32:, 512 * j : 512 * j + 512] for j in range(4)])
+        sum_proj, sum_up = pair[:16], pair[16:]
+        sum_down = jnp.concatenate([sum_down[:, 512 * j : 512 * j + 512] for j in range(4)])
         me = lax.axis_index("dp")
         sums = lax.dynamic_slice(last_small, (0, 16 * (me % 8)), (13, 16))
         sum_upbias = lax.dynamic_slice(last_small, (13, 64 * (me % 2)), (1, 64))[0]
@@ -766,11 +818,12 @@
         def share(full):
             return lax.psum_scatter(full.reshape(-1, full.shape[-1]), "dp", scatter_dimension=0, tiled=True)
 
-        pair_all = jnp.concatenate([own_pair, *other_pair]).astype(F32)
+        pair_all = jnp.concatenate([own_pair, low_pair, high_pair]).astype(F32)
+        down_all = jnp.concatenate(both_down).astype(F32)
         last_all = jnp.concatenate([own_last, *other_last]).astype(F32)
         sum_proj = share(pair_all[:, :16])
-        sum_up = share(pair_all[:, 16:32])
-        sum_down = share(pair_all[:, 32:].reshape(SHARDS, 16, 4, 512).transpose(0, 2, 1, 3))
+        sum_up = share(pair_all[:, 16:])
+        sum_down = share(down_all.reshape(SHARDS, 16, 4, 512).transpose(0, 2, 1, 3))
         sum_qkv = share(last_all[:, :, :1536])
         sum_out = share(last_all[:, :, 1536:2048])
         small = last_all[:, :, 2048:]

time: 163 us -> 155 us (0.951)
  waiting for transfers between devices: 47 us -> 34.1 us
  starting transfers between devices: 47.9 us -> 49.6 us
    ppermute x42 -> x48, waiting for transfers between devices: 47 us -> 34.1 us  [send(): return lax.ppermute(value, 'dp', to)]
    ppermute x42 -> x48, starting transfers between devices: 47.9 us -> 49.6 us  [send(): return lax.ppermute(value, 'dp', to)]
    convert_element_type x2 -> x5, other arithmetic: 4.44 us -> 4.24 us  [the longest x1 1.05 us: second(): part = widen(self.own[2::4], self.core[2::4], self.beside[1::2]).astype(LOW)]
  transfers between devices with their start and end apart: 42 -> 48, of which waited for: 16 -> 17; matrix products, arithmetic and copies ran while one was open for 10% -> 11% of each run, Pallas kernels for 21% -> 22%
where the time goes in v5:
time: 155 us; the launch traced here: 154 us
  starting transfers between devices  49.6 us (32%)
  Pallas kernels  45.9 us (30%)
  waiting for transfers between devices  34.1 us (22%)
  other arithmetic  18.1 us (12%)
  local copies, waits for them, and re-layouts  5.28 us (3%)
    ppermute x48, starting transfers between devices, send(): return lax.ppermute(value, 'dp', to)  49.6 us
    pallas_call x4, Pallas kernels, call(): pl.pallas_call(kernel, out_shape=[jax.ShapeDtypeStruct(s, t) for s, t, _p...  45.9 us
    ppermute x48, waiting for transfers between devices, send(): return lax.ppermute(value, 'dp', to)  34.1 us
  transfers between devices with their start and end apart: 48, of which 17 were waited for; matrix products, arithmetic and copies ran while one was open for 11% of the time, Pallas kernels for 22%

profile of v5, /device:TPU:0, one launch (start us, length us, event | category | flops | bytes accessed | tf_op | source)
XLA Modules:
  0.0 154.0 jit_solution(12407451768462141211)
XLA Ops:
  0.7 0.9 pad_add_fusion.2
  1.6 5.1 %collective-permute-start.2 = (bf16[16,1664]{1,0:T(8,128)(2,1)S(1)}, bf16[16,1664]{1,0:T(8,128)(2,1)S(1)}, u32[]{:S(2)}, u32[]{:S(2)}) collective-permute-start(bf16[16,1664]{1,0:T(8,128)(2,1)S(1)} %pad_add_fusion.2), channel_id=1, source_target_pairs={{0,24},{1,25},{2,26},{3,27},{4,28},{5,29},{6,30},{7,31},{8,16},{9,... | collective-permute-start | bytes 159752 | tf_op jit(solution)/shard_map/ppermute | solution.py:33
  6.7 0.6 collective-permute-start.1
  7.3 0.9 pad_add_fusion.1
  8.2 1.6 %collective-permute-start.10 = (bf16[80,512]{1,0:T(8,128)(2,1)S(1)}, bf16[80,512]{1,0:T(8,128)(2,1)S(1)}, u32[]{:S(2)}, u32[]{:S(2)}) collective-permute-start(bf16[80,512]{1,0:T(8,128)(2,1)S(1)} %pad_add_fusion.1), channel_id=1, source_target_pairs={{0,2},{1,5},{2,0},{3,7},{4,6},{5,1},{6,4},{7,3},{8,10},{9,13},{10,... | collective-permute-start | bytes 245768 | tf_op jit(solution)/shard_map/ppermute | solution.py:33
  9.9 1.5 collective-permute-start.11
  11.4 0.9 fusion.5
  12.3 0.9 pad_add_fusion
  13.6 2.3 %collective-permute-start.14 = (bf16[32,2048]{1,0:T(8,128)(2,1)S(1)}, bf16[32,2048]{1,0:T(8,128)(2,1)S(1)}, u32[]{:S(2)}, u32[]{:S(2)}) collective-permute-start(bf16[32,2048]{1,0:T(8,128)(2,1)S(1)} %pad_add_fusion), channel_id=1, source_target_pairs={{0,16},{1,17},{2,18},{3,19},{4,20},{5,21},{6,22},{7,23},{8,24},{9,... | collective-permute-start | bytes 393224 | tf_op jit(solution)/shard_map/ppermute | solution.py:33
  15.9 2.0 %collective-permute-start.13 = (bf16[32,2048]{1,0:T(8,128)(2,1)S(1)}, bf16[32,2048]{1,0:T(8,128)(2,1)S(1)}, u32[]{:S(2)}, u32[]{:S(2)}) collective-permute-start(bf16[32,2048]{1,0:T(8,128)(2,1)S(1)} %pad_add_fusion), channel_id=1, source_target_pairs={{0,8},{1,9},{2,10},{3,11},{4,12},{5,13},{6,14},{7,15},{8,0},{9,1},... | collective-permute-start | bytes 393224 | tf_op jit(solution)/shard_map/ppermute | solution.py:33
  18.0 3.3 %collective-permute-done.14 = bf16[32,2048]{1,0:T(8,128)(2,1)S(1)} collective-permute-done((bf16[32,2048]{1,0:T(8,128)(2,1)S(1)}, bf16[32,2048]{1,0:T(8,128)(2,1)S(1)}, u32[]{:S(2)}, u32[]{:S(2)}) %collective-permute-start.14) | collective-permute-done | bytes 131104 | tf_op jit(solution)/shard_map/ppermute | solution.py:33
  21.5 0.8 iota_compare_fusion
  22.3 1.6 %collective-permute-start.3 = (bf16[4,16,1664]{2,1,0:T(8,128)(2,1)S(1)}, bf16[4,16,1664]{2,1,0:T(8,128)(2,1)S(1)}, u32[]{:S(2)}, u32[]{:S(2)}) collective-permute-start(bf16[4,16,1664]{2,1,0:T(8,128)(2,1)S(1)} %pad_maximum_fusion.3.refs_0_), channel_id=1, source_target_pairs={{0,2},{1,5},{2,0},{3,7},{4,6},{5,1},{6,4},{7,3},{8,10},{9,13},{10,... | collective-permute-start | bytes 638984 | tf_op jit(solution)/shard_map/ppermute | solution.py:33
  23.9 1.5 collective-permute-start.4
  26.0 3.4 %collective-permute-start.17 = (bf16[4,80,512]{2,1,0:T(8,128)(2,1)S(1)}, bf16[4,80,512]{2,1,0:T(8,128)(2,1)S(1)}, u32[]{:S(2)}, u32[]{:S(2)}) collective-permute-start(bf16[4,80,512]{2,1,0:T(8,128)(2,1)S(1)} %pad_maximum_fusion.2.refs_8_), channel_id=1, source_target_pairs={{0,16},{1,17},{2,18},{3,19},{4,20},{5,21},{6,22},{7,23},{8,24},{9,... | collective-permute-start | bytes 983048 | tf_op jit(solution)/shard_map/ppermute | solution.py:33
  29.5 1.6 %collective-permute-start.16 = (bf16[4,32,2048]{2,1,0:T(8,128)(2,1)S(1)}, bf16[4,32,2048]{2,1,0:T(8,128)(2,1)S(1)}, u32[]{:S(2)}, u32[]{:S(2)}) collective-permute-start(bf16[4,32,2048]{2,1,0:T(8,128)(2,1)S(1)} %pad_maximum_fusion.1.refs_10_.refs_0_), channel_id=1, source_target_pairs={{0,2},{1,5},{2,0},{3,7},{4,6},{5,1},{6,4},{7,3},{8,10},{9,13},{10,... | collective-permute-start | bytes 1572872 | tf_op jit(solution)/shard_map/ppermute | solution.py:33
  31.4 3.2 %collective-permute-done.4.refs_2_ = bf16[4,16,1664]{2,1,0:T(8,128)(2,1)S(1)} collective-permute-done((bf16[4,16,1664]{2,1,0:T(8,128)(2,1)S(1)}, bf16[4,16,1664]{2,1,0:T(8,128)(2,1)S(1)}, u32[]{:S(2)}, u32[]{:S(2)}) %collective-permute-start.4) | collective-permute-done | bytes 213024 | tf_op jit(solution)/shard_map/ppermute | solution.py:33
  35.1 5.7 %collective-permute-done.17.refs_10_ = bf16[4,80,512]{2,1,0:T(8,128)(2,1)S(1)} collective-permute-done((bf16[4,80,512]{2,1,0:T(8,128)(2,1)S(1)}, bf16[4,80,512]{2,1,0:T(8,128)(2,1)S(1)}, u32[]{:S(2)}, u32[]{:S(2)}) %collective-permute-start.17) | collective-permute-done | bytes 327712 | tf_op jit(solution)/shard_map/ppermute | solution.py:33
  40.7 1.1 fusion.refs_8_.refs_3_
  41.9 1.3 collective-permute-start.18
  43.2 1.4 collective-permute-start.19
  44.7 2.0 %collective-permute-start.21 = (bf16[4,80,512]{2,1,0:T(8,128)(2,1)S(1)}, bf16[4,80,512]{2,1,0:T(8,128)(2,1)S(1)}, u32[]{:S(2)}, u32[]{:S(2)}) collective-permute-start(bf16[4,80,512]{2,1,0:T(8,128)(2,1)S(1)} %collective-permute-done.17.refs_10_), channel_id=1, source_target_pairs={{0,8},{1,9},{2,10},{3,11},{4,12},{5,13},{6,14},{7,15},{8,0},{9,1},... | collective-permute-start | bytes 983048 | tf_op jit(solution)/shard_map/ppermute | solution.py:33
  46.7 11.3 %shard_map.263 = (bf16[512,1664]{1,0:T(8,128)(2,1)}, f32[16,512]{1,0:T(8,128)}, f32[8,2048]{1,0:T(8,128)}, f32[256,512]{1,0:T(8,128)}, bf16[2048,512]{1,0:T(8,12...) custom-call(s32[1]{0:T(128)} %bitcast.me_ref, ...), custom_call_target="tpu_custom_call" | custom-call | flops 16499999744 | bytes 1000 | tf_op jit(solution)/shard_map/pallas_call | solution.py:293
  58.1 0.9 collective-permute-done.21.refs_11_
  59.1 3.4 %collective-permute-start.26 = (bf16[4,80,512]{2,1,0:T(8,128)(2,1)S(1)}, bf16[4,80,512]{2,1,0:T(8,128)(2,1)S(1)}, u32[]{:S(2)}, u32[]{:S(2)}) collective-permute-start(bf16[4,80,512]{2,1,0:T(8,128)(2,1)S(1)} %pad_maximum_fusion.2.refs_8_), channel_id=1, source_target_pairs={{0,1},{1,0},{2,3},{3,2},{4,5},{5,4},{6,7},{7,6},{8,9},{9,8},{10,11... | collective-permute-start | bytes 983048 | tf_op jit(solution)/shard_map/ppermute | solution.py:33
  63.0 0.5 collective-permute-start.23
  64.5 2.3 %collective-permute-done.28.refs_14_ = bf16[4,80,512]{2,1,0:T(8,128)(2,1)S(1)} collective-permute-done((bf16[4,80,512]{2,1,0:T(8,128)(2,1)S(1)}, bf16[4,80,512]{2,1,0:T(8,128)(2,1)S(1)}, u32[]{:S(2)}, u32[]{:S(2)}) %collective-permute-start.28) | collective-permute-done | bytes 327712 | tf_op jit(solution)/shard_map/ppermute | solution.py:33
  67.4 0.7 copy-done.24
  68.9 12.2 %shard_map.264 = (bf16[256,2048]{1,0:T(8,128)(2,1)}, f32[256,512]{1,0:T(8,128)}, bf16[256,512]{1,0:T(8,128)(2,1)}, f32[8,2048]{1,0:T(8,128)}, f32[8,512]{1,0:T(8...) custom-call(s32[1]{0:T(128)} %bitcast.me_ref, ...), custom_call_target="tpu_custom_call" | custom-call | flops 13200000000 | bytes 1000 | tf_op jit(solution)/shard_map/pallas_call | solution.py:293
  81.7 7.6 %shard_map.265 = (bf16[2048,1024]{1,0:T(8,128)(2,1)}, bf16[256,512]{1,0:T(8,128)(2,1)}, f32[256,512]{1,0:T(8,128)}) custom-call(s32[1]{0:T(128)} %bitcast.me_ref, bf16[256,512]{1,0:T(8,128)(2,1)} %get-tuple-element.107.refs_0_, bf16[256,512]{1,0:T(8,128)(2,1)} %get-tuple-element.108.refs_1_, bf16[2048,256]{1,0:T(8,128)(2,1)} %get-tuple-element.109.refs_2_, ...), custom_call_target="tpu_custom_call" | custom-call | flops 8800000000 | bytes 1000 | tf_op jit(solution)/shard_map/pallas_call | solution.py:293
  89.3 1.0 copy-done.4
  90.7 1.7 %collective-permute-start.33 = (bf16[8,32,2048]{2,1,0:T(8,128)(2,1)S(1)}, bf16[8,32,2048]{2,1,0:T(8,128)(2,1)}, u32[]{:S(2)}, u32[]{:S(2)}) collective-permute-start(bf16[8,32,2048]{2,1,0:T(8,128)(2,1)S(1)} %add_convert_fusion), channel_id=1, source_target_pairs={{0,4},{1,3},{2,6},{3,1},{4,0},{5,7},{6,2},{7,5},{8,12},{9,11},{10,... | collective-permute-start | bytes 3145736 | tf_op jit(solution)/shard_map/ppermute | solution.py:33
  92.4 0.9 add_convert_fusion.2.refs_15_
  93.4 1.9 %collective-permute-start.34 = (bf16[8,16,2048]{2,1,0:T(8,128)(2,1)}, bf16[8,16,2048]{2,1,0:T(8,128)(2,1)}, u32[]{:S(2)}, u32[]{:S(2)}) collective-permute-start(bf16[8,16,2048]{2,1,0:T(8,128)(2,1)} %add_convert_fusion.2.refs_15_), channel_id=1, source_target_pairs={{0,8},{1,9},{2,10},{3,11},{4,12},{5,13},{6,14},{7,15},{8,0},{9,1},... | collective-permute-start | bytes 1572872 | tf_op jit(solution)/shard_map/ppermute | solution.py:33
  95.3 14.8 %shard_map.266 = (bf16[2048,512]{1,0:T(8,128)(2,1)}, bf16[16,16,2176]{2,1,0:T(8,128)(2,1)}, bf16[8,16,2176]{2,1,0:T(8,128)(2,1)}, bf16[4,16,2176]{2,1,0:T(8,128)(2,1)}, bf16[4,16,2176]{2,1,0:T(8,128)(2,1)}) custom-call(s32[1]{0:T(128)} %bitcast.me_ref, f32[16,512]{1,0:T(8,128)} %get-tuple-element.104.refs_19_.refs_0_, ...), custom_call_target="tpu_custom_call" | custom-call | flops 19800000512 | bytes 1000 | tf_op jit(solution)/shard_map/pallas_call | solution.py:293
  110.8 1.2 collective-permute-done.35
  112.5 1.4 add_convert_fusion.5
  114.0 0.9 collective-permute-start.37
  114.9 1.3 add_convert_fusion.1
  116.2 1.6 %collective-permute-start.41 = (bf16[4,32,2048]{2,1,0:T(8,128)(2,1)S(1)}, bf16[4,32,2048]{2,1,0:T(8,128)(2,1)S(1)}, u32[]{:S(2)}, u32[]{:S(2)}) collective-permute-start(bf16[4,32,2048]{2,1,0:T(8,128)(2,1)S(1)} %add_convert_fusion.1), channel_id=1, source_target_pairs={{0,2},{1,5},{2,0},{3,7},{4,6},{5,1},{6,4},{7,3},{8,10},{9,13},{10,... | collective-permute-start | bytes 1572872 | tf_op jit(solution)/shard_map/ppermute | solution.py:33
  117.7 1.0 add_convert_fusion.7
  118.8 1.1 collective-permute-start.40
  119.9 7.9 %collective-permute-done.37 = bf16[8,16,2176]{2,1,0:T(8,128)(2,1)S(1)} collective-permute-done((bf16[8,16,2176]{2,1,0:T(8,128)(2,1)S(1)}, bf16[8,16,2176]{2,1,0:T(8,128)(2,1)S(1)}, u32[]{:S(2)}, u32[]{:S(2)}) %collective-permute-start.37) | collective-permute-done | bytes 557088 | tf_op jit(solution)/shard_map/ppermute | solution.py:33
  127.9 2.6 %collective-permute-start.39 = (bf16[4,16,2176]{2,1,0:T(8,128)(2,1)S(1)}, bf16[4,16,2176]{2,1,0:T(8,128)(2,1)S(1)}, u32[]{:S(2)}, u32[]{:S(2)}) collective-permute-start(bf16[4,16,2176]{2,1,0:T(8,128)(2,1)S(1)} %add_convert_fusion.3), channel_id=1, source_target_pairs={{0,2},{1,5},{2,0},{3,7},{4,6},{5,1},{6,4},{7,3},{8,10},{9,13},{10,... | collective-permute-start | bytes 835592 | tf_op jit(solution)/shard_map/ppermute | solution.py:33
  130.5 1.1 add_convert_fusion.6
  131.7 1.2 collective-permute-done.40
  132.9 1.0 add_convert_fusion.10
  133.9 1.3 collective-permute-start.44
  135.6 3.3 %collective-permute-done.44 = bf16[2,16,2048]{2,1,0:T(8,128)(2,1)S(1)} collective-permute-done((bf16[2,16,2048]{2,1,0:T(8,128)(2,1)S(1)}, bf16[2,16,2048]{2,1,0:T(8,128)(2,1)S(1)}, u32[]{:S(2)}, u32[]{:S(2)}) %collective-permute-start.44) | collective-permute-done | bytes 131104 | tf_op jit(solution)/shard_map/ppermute | solution.py:33
  138.9 1.2 collective-permute-done.43
  140.2 1.1 add_bitcast_fusion
  141.3 1.3 collective-permute-start.46
  142.6 0.9 add_convert_fusion.12
  144.0 2.0 %collective-permute-start.45 = (bf16[16,2176]{1,0:T(8,128)(2,1)S(1)}, bf16[16,2176]{1,0:T(8,128)(2,1)S(1)}, u32[]{:S(2)}, u32[]{:S(2)}) collective-permute-start(bf16[16,2176]{1,0:T(8,128)(2,1)S(1)} %get-tuple-element.158), channel_id=1, source_target_pairs={{0,16},{1,17},{2,18},{3,19},{4,20},{5,21},{6,22},{7,23},{8,24},{9,... | collective-permute-start | bytes 208904 | tf_op jit(solution)/shard_map/ppermute | solution.py:33
  146.0 1.8 %collective-permute-done.47 = bf16[1,16,2048]{2,1,0:T(8,128)(2,1)S(1)} collective-permute-done((bf16[1,16,2048]{2,1,0:T(8,128)(2,1)S(1)}, bf16[1,16,2048]{2,1,0:T(8,128)(2,1)S(1)}, u32[]{:S(2)}, u32[]{:S(2)}) %collective-permute-start.47) | collective-permute-done | bytes 65568 | tf_op jit(solution)/shard_map/ppermute | solution.py:33
  147.8 0.9 add_bitcast_fusion.2
  148.7 0.7 collective-permute-done.46
  149.4 0.7 fusion.3
  150.2 0.7 pad_maximum_fusion.4
  150.9 0.6 convert_add_fusion.2
  151.5 0.7 convert_add_fusion.1
  152.2 0.6 dynamic-slice_bitcast_fusion.5
  152.8 0.7 constant_dynamic-slice_fusion
  153.4 0.6 dynamic-slice_bitcast_fusion
  (136 shorter events, 8.6 us)
Async XLA Ops:
  0.6 30.4 %copy-start.10 = (s32[256]{0:T(256)S(1)}, s32[256]{0:T(256)}, u32[]{:S(2)}) copy-start(s32[256]{0:T(256)} %param.18) | copy-start | bytes 3076
  1.6 11.6 %collective-permute-start.2 = (bf16[16,1664]{1,0:T(8,128)(2,1)S(1)}, bf16[16,1664]{1,0:T(8,128)(2,1)S(1)}, u32[]{:S(2)}, u32[]{:S(2)}) collective-permute-start(bf16[16,1664]{1,0:T(8,128)(2,1)S(1)} %pad_add_fusion.2), channel_id=1, source_target_pairs={{0,24},{1,25},{2,26},{3,27},{4,28},{5,29},{6,30},{7,31},{8,16},{9,... | collective-permute-start | bytes 159752 | tf_op jit(solution)/shard_map/ppermute | solution.py:33
  6.7 6.9 %collective-permute-start = (bf16[16,1664]{1,0:T(8,128)(2,1)S(1)}, bf16[16,1664]{1,0:T(8,128)(2,1)S(1)}, u32[]{:S(2)}, u32[]{:S(2)}) collective-permute-start(bf16[16,1664]{1,0:T(8,128)(2,1)S(1)} %pad_add_fusion.2), channel_id=1, source_target_pairs={{0,8},{1,9},{2,10},{3,11},{4,12},{5,13},{6,14},{7,15},{8,0},{9,1},... | collective-permute-start | bytes 159752 | tf_op jit(solution)/shard_map/ppermute | solution.py:33
  6.7 9.2 %collective-permute-start.1 = (bf16[16,1664]{1,0:T(8,128)(2,1)S(1)}, bf16[16,1664]{1,0:T(8,128)(2,1)S(1)}, u32[]{:S(2)}, u32[]{:S(2)}) collective-permute-start(bf16[16,1664]{1,0:T(8,128)(2,1)S(1)} %pad_add_fusion.2), channel_id=1, source_target_pairs={{0,16},{1,17},{2,18},{3,19},{4,20},{5,21},{6,22},{7,23},{8,24},{9,... | collective-permute-start | bytes 159752 | tf_op jit(solution)/shard_map/ppermute | solution.py:33
  8.2 14.1 %collective-permute-start.10 = (bf16[80,512]{1,0:T(8,128)(2,1)S(1)}, bf16[80,512]{1,0:T(8,128)(2,1)S(1)}, u32[]{:S(2)}, u32[]{:S(2)}) collective-permute-start(bf16[80,512]{1,0:T(8,128)(2,1)S(1)} %pad_add_fusion.1), channel_id=1, source_target_pairs={{0,2},{1,5},{2,0},{3,7},{4,6},{5,1},{6,4},{7,3},{8,10},{9,13},{10,... | collective-permute-start | bytes 245768 | tf_op jit(solution)/shard_map/ppermute | solution.py:33
  9.9 14.0 %collective-permute-start.11 = (bf16[80,512]{1,0:T(8,128)(2,1)S(1)}, bf16[80,512]{1,0:T(8,128)(2,1)S(1)}, u32[]{:S(2)}, u32[]{:S(2)}) collective-permute-start(bf16[80,512]{1,0:T(8,128)(2,1)S(1)} %pad_add_fusion.1), channel_id=1, source_target_pairs={{0,4},{1,3},{2,6},{3,1},{4,0},{5,7},{6,2},{7,5},{8,12},{9,11},{10,... | collective-permute-start | bytes 245768 | tf_op jit(solution)/shard_map/ppermute | solution.py:33
  13.2 12.2 %collective-permute-start.12 = (bf16[80,512]{1,0:T(8,128)(2,1)S(1)}, bf16[80,512]{1,0:T(8,128)(2,1)S(1)}, u32[]{:S(2)}, u32[]{:S(2)}) collective-permute-start(bf16[80,512]{1,0:T(8,128)(2,1)S(1)} %pad_add_fusion.1), channel_id=1, source_target_pairs={{0,6},{1,7},{2,4},{3,5},{4,2},{5,3},{6,0},{7,1},{8,14},{9,15},{10,... | collective-permute-start | bytes 245768 | tf_op jit(solution)/shard_map/ppermute | solution.py:33
  13.6 7.7 %collective-permute-start.14 = (bf16[32,2048]{1,0:T(8,128)(2,1)S(1)}, bf16[32,2048]{1,0:T(8,128)(2,1)S(1)}, u32[]{:S(2)}, u32[]{:S(2)}) collective-permute-start(bf16[32,2048]{1,0:T(8,128)(2,1)S(1)} %pad_add_fusion), channel_id=1, source_target_pairs={{0,16},{1,17},{2,18},{3,19},{4,20},{5,21},{6,22},{7,23},{8,24},{9,... | collective-permute-start | bytes 393224 | tf_op jit(solution)/shard_map/ppermute | solution.py:33
  15.9 10.0 %collective-permute-start.13 = (bf16[32,2048]{1,0:T(8,128)(2,1)S(1)}, bf16[32,2048]{1,0:T(8,128)(2,1)S(1)}, u32[]{:S(2)}, u32[]{:S(2)}) collective-permute-start(bf16[32,2048]{1,0:T(8,128)(2,1)S(1)} %pad_add_fusion), channel_id=1, source_target_pairs={{0,8},{1,9},{2,10},{3,11},{4,12},{5,13},{6,14},{7,15},{8,0},{9,1},... | collective-permute-start | bytes 393224 | tf_op jit(solution)/shard_map/ppermute | solution.py:33
  18.0 28.7 %copy-start.9 = (bf16[4,16,1664]{2,1,0:T(8,128)(2,1)}, bf16[4,16,1664]{2,1,0:T(8,128)(2,1)S(1)}, u32[]{:S(2)}) copy-start(bf16[4,16,1664]{2,1,0:T(8,128)(2,1)S(1)} %pad_maximum_fusion.3.refs_0_) | copy-start | bytes 638980
  21.3 8.1 %collective-permute-start.15 = (bf16[32,2048]{1,0:T(8,128)(2,1)S(1)}, bf16[32,2048]{1,0:T(8,128)(2,1)S(1)}, u32[]{:S(2)}, u32[]{:S(2)}) collective-permute-start(bf16[32,2048]{1,0:T(8,128)(2,1)S(1)} %collective-permute-done.14), channel_id=1, source_target_pairs={{0,8},{1,9},{2,10},{3,11},{4,12},{5,13},{6,14},{7,15},{8,0},{9,1},... | collective-permute-start | bytes 393224 | tf_op jit(solution)/shard_map/ppermute | solution.py:33
  22.3 9.0 %collective-permute-start.3 = (bf16[4,16,1664]{2,1,0:T(8,128)(2,1)S(1)}, bf16[4,16,1664]{2,1,0:T(8,128)(2,1)S(1)}, u32[]{:S(2)}, u32[]{:S(2)}) collective-permute-start(bf16[4,16,1664]{2,1,0:T(8,128)(2,1)S(1)} %pad_maximum_fusion.3.refs_0_), channel_id=1, source_target_pairs={{0,2},{1,5},{2,0},{3,7},{4,6},{5,1},{6,4},{7,3},{8,10},{9,13},{10,... | collective-permute-start | bytes 638984 | tf_op jit(solution)/shard_map/ppermute | solution.py:33
  23.9 10.7 %collective-permute-start.4 = (bf16[4,16,1664]{2,1,0:T(8,128)(2,1)S(1)}, bf16[4,16,1664]{2,1,0:T(8,128)(2,1)S(1)}, u32[]{:S(2)}, u32[]{:S(2)}) collective-permute-start(bf16[4,16,1664]{2,1,0:T(8,128)(2,1)S(1)} %pad_maximum_fusion.3.refs_0_), channel_id=1, source_target_pairs={{0,4},{1,3},{2,6},{3,1},{4,0},{5,7},{6,2},{7,5},{8,12},{9,11},{10,... | collective-permute-start | bytes 638984 | tf_op jit(solution)/shard_map/ppermute | solution.py:33
  25.4 9.2 %collective-permute-start.5 = (bf16[4,16,1664]{2,1,0:T(8,128)(2,1)S(1)}, bf16[4,16,1664]{2,1,0:T(8,128)(2,1)S(1)}, u32[]{:S(2)}, u32[]{:S(2)}) collective-permute-start(bf16[4,16,1664]{2,1,0:T(8,128)(2,1)S(1)} %pad_maximum_fusion.3.refs_0_), channel_id=1, source_target_pairs={{0,6},{1,7},{2,4},{3,5},{4,2},{5,3},{6,0},{7,1},{8,14},{9,15},{10,... | collective-permute-start | bytes 638984 | tf_op jit(solution)/shard_map/ppermute | solution.py:33
  25.9 33.1 %copy-start.8 = (bf16[4,80,512]{2,1,0:T(8,128)(2,1)}, bf16[4,80,512]{2,1,0:T(8,128)(2,1)S(1)}, u32[]{:S(2)}) copy-start(bf16[4,80,512]{2,1,0:T(8,128)(2,1)S(1)} %pad_maximum_fusion.2.refs_8_) | copy-start | bytes 983044
  26.0 14.8 %collective-permute-start.17 = (bf16[4,80,512]{2,1,0:T(8,128)(2,1)S(1)}, bf16[4,80,512]{2,1,0:T(8,128)(2,1)S(1)}, u32[]{:S(2)}, u32[]{:S(2)}) collective-permute-start(bf16[4,80,512]{2,1,0:T(8,128)(2,1)S(1)} %pad_maximum_fusion.2.refs_8_), channel_id=1, source_target_pairs={{0,16},{1,17},{2,18},{3,19},{4,20},{5,21},{6,22},{7,23},{8,24},{9,... | collective-permute-start | bytes 983048 | tf_op jit(solution)/shard_map/ppermute | solution.py:33
  29.5 17.2 %copy-start.7 = (bf16[4,32,2048]{2,1,0:T(8,128)(2,1)}, bf16[4,32,2048]{2,1,0:T(8,128)(2,1)S(1)}, u32[]{:S(2)}) copy-start(bf16[4,32,2048]{2,1,0:T(8,128)(2,1)S(1)} %pad_maximum_fusion.1.refs_10_.refs_0_) | copy-start | bytes 1572868
  29.5 12.4 %collective-permute-start.16 = (bf16[4,32,2048]{2,1,0:T(8,128)(2,1)S(1)}, bf16[4,32,2048]{2,1,0:T(8,128)(2,1)S(1)}, u32[]{:S(2)}, u32[]{:S(2)}) collective-permute-start(bf16[4,32,2048]{2,1,0:T(8,128)(2,1)S(1)} %pad_maximum_fusion.1.refs_10_.refs_0_), channel_id=1, source_target_pairs={{0,2},{1,5},{2,0},{3,7},{4,6},{5,1},{6,4},{7,3},{8,10},{9,13},{10,... | collective-permute-start | bytes 1572872 | tf_op jit(solution)/shard_map/ppermute | solution.py:33
  31.3 15.4 %copy-start.25 = (bf16[4,16,1664]{2,1,0:T(8,128)(2,1)}, bf16[4,16,1664]{2,1,0:T(8,128)(2,1)S(1)}, u32[]{:S(2)}) copy-start(bf16[4,16,1664]{2,1,0:T(8,128)(2,1)S(1)} %collective-permute-done.3.refs_1_) | copy-start | bytes 638980
  31.3 10.6 %collective-permute-start.6 = (bf16[4,16,1664]{2,1,0:T(8,128)(2,1)S(1)}, bf16[4,16,1664]{2,1,0:T(8,128)(2,1)S(1)}, u32[]{:S(2)}, u32[]{:S(2)}) collective-permute-start(bf16[4,16,1664]{2,1,0:T(8,128)(2,1)S(1)} %pad_maximum_fusion.3.refs_0_), channel_id=1, source_target_pairs={{0,1},{1,0},{2,3},{3,2},{4,5},{5,4},{6,7},{7,6},{8,9},{9,8},{10,11... | collective-permute-start | bytes 638984 | tf_op jit(solution)/shard_map/ppermute | solution.py:33
  34.5 12.1 %copy-start.26 = (bf16[4,16,1664]{2,1,0:T(8,128)(2,1)}, bf16[4,16,1664]{2,1,0:T(8,128)(2,1)S(1)}, u32[]{:S(2)}) copy-start(bf16[4,16,1664]{2,1,0:T(8,128)(2,1)S(1)} %collective-permute-done.4.refs_2_) | copy-start | bytes 638980
  34.6 8.6 %collective-permute-start.7 = (bf16[4,16,1664]{2,1,0:T(8,128)(2,1)S(1)}, bf16[4,16,1664]{2,1,0:T(8,128)(2,1)S(1)}, u32[]{:S(2)}, u32[]{:S(2)}) collective-permute-start(bf16[4,16,1664]{2,1,0:T(8,128)(2,1)S(1)} %collective-permute-done.3.refs_1_), channel_id=1, source_target_pairs={{0,1},{1,0},{2,3},{3,2},{4,5},{5,4},{6,7},{7,6},{8,9},{9,8},{10,11... | collective-permute-start | bytes 638984 | tf_op jit(solution)/shard_map/ppermute | solution.py:33
  34.6 12.1 %copy-start.27 = (bf16[4,16,1664]{2,1,0:T(8,128)(2,1)}, bf16[4,16,1664]{2,1,0:T(8,128)(2,1)S(1)}, u32[]{:S(2)}) copy-start(bf16[4,16,1664]{2,1,0:T(8,128)(2,1)S(1)} %collective-permute-done.5.refs_3_) | copy-start | bytes 638980
  34.6 10.1 %collective-permute-start.8 = (bf16[4,16,1664]{2,1,0:T(8,128)(2,1)S(1)}, bf16[4,16,1664]{2,1,0:T(8,128)(2,1)S(1)}, u32[]{:S(2)}, u32[]{:S(2)}) collective-permute-start(bf16[4,16,1664]{2,1,0:T(8,128)(2,1)S(1)} %collective-permute-done.4.refs_2_), channel_id=1, source_target_pairs={{0,1},{1,0},{2,3},{3,2},{4,5},{5,4},{6,7},{7,6},{8,9},{9,8},{10,11... | collective-permute-start | bytes 638984 | tf_op jit(solution)/shard_map/ppermute | solution.py:33
  40.7 22.9 %copy-start.18 = (bf16[4,80,512]{2,1,0:T(8,128)(2,1)}, bf16[4,80,512]{2,1,0:T(8,128)(2,1)S(1)}, u32[]{:S(2)}) copy-start(bf16[4,80,512]{2,1,0:T(8,128)(2,1)S(1)} %collective-permute-done.17.refs_10_) | copy-start | bytes 983044
  40.7 3.9 %collective-permute-start.9 = (bf16[4,16,1664]{2,1,0:T(8,128)(2,1)S(1)}, bf16[4,16,1664]{2,1,0:T(8,128)(2,1)S(1)}, u32[]{:S(2)}, u32[]{:S(2)}) collective-permute-start(bf16[4,16,1664]{2,1,0:T(8,128)(2,1)S(1)} %collective-permute-done.5.refs_3_), channel_id=1, source_target_pairs={{0,1},{1,0},{2,3},{3,2},{4,5},{5,4},{6,7},{7,6},{8,9},{9,8},{10,11... | collective-permute-start | bytes 638984 | tf_op jit(solution)/shard_map/ppermute | solution.py:33
  41.9 21.1 %copy-start.11 = (bf16[4,32,2048]{2,1,0:T(8,128)(2,1)}, bf16[4,32,2048]{2,1,0:T(8,128)(2,1)S(1)}, u32[]{:S(2)}) copy-start(bf16[4,32,2048]{2,1,0:T(8,128)(2,1)S(1)} %collective-permute-done.16.refs_1_) | copy-start | bytes 1572868
  41.9 16.2 %collective-permute-start.20 = (bf16[4,80,512]{2,1,0:T(8,128)(2,1)S(1)}, bf16[4,80,512]{2,1,0:T(8,128)(2,1)S(1)}, u32[]{:S(2)}, u32[]{:S(2)}) collective-permute-start(bf16[4,80,512]{2,1,0:T(8,128)(2,1)S(1)} %pad_maximum_fusion.2.refs_8_), channel_id=1, source_target_pairs={{0,8},{1,9},{2,10},{3,11},{4,12},{5,13},{6,14},{7,15},{8,0},{9,1},... | collective-permute-start | bytes 983048 | tf_op jit(solution)/shard_map/ppermute | solution.py:33
  41.9 17.1 %collective-permute-start.18 = (bf16[4,32,2048]{2,1,0:T(8,128)(2,1)S(1)}, bf16[4,32,2048]{2,1,0:T(8,128)(2,1)S(1)}, u32[]{:S(2)}, u32[]{:S(2)}) collective-permute-start(bf16[4,32,2048]{2,1,0:T(8,128)(2,1)S(1)} %pad_maximum_fusion.1.refs_10_.refs_0_), channel_id=1, source_target_pairs={{0,4},{1,3},{2,6},{3,1},{4,0},{5,7},{6,2},{7,5},{8,12},{9,11},{10,... | collective-permute-start | bytes 1572872 | tf_op jit(solution)/shard_map/ppermute | solution.py:33
  43.2 15.8 %collective-permute-start.19 = (bf16[4,32,2048]{2,1,0:T(8,128)(2,1)S(1)}, bf16[4,32,2048]{2,1,0:T(8,128)(2,1)S(1)}, u32[]{:S(2)}, u32[]{:S(2)}) collective-permute-start(bf16[4,32,2048]{2,1,0:T(8,128)(2,1)S(1)} %pad_maximum_fusion.1.refs_10_.refs_0_), channel_id=1, source_target_pairs={{0,6},{1,7},{2,4},{3,5},{4,2},{5,3},{6,0},{7,1},{8,14},{9,15},{10,... | collective-permute-start | bytes 1572872 | tf_op jit(solution)/shard_map/ppermute | solution.py:33
  44.6 18.4 %collective-permute-start.22 = (bf16[4,32,2048]{2,1,0:T(8,128)(2,1)S(1)}, bf16[4,32,2048]{2,1,0:T(8,128)(2,1)S(1)}, u32[]{:S(2)}, u32[]{:S(2)}) collective-permute-start(bf16[4,32,2048]{2,1,0:T(8,128)(2,1)S(1)} %pad_maximum_fusion.1.refs_10_.refs_0_), channel_id=1, source_target_pairs={{0,1},{1,0},{2,3},{3,2},{4,5},{5,4},{6,7},{7,6},{8,9},{9,8},{10,11... | collective-permute-start | bytes 1572872 | tf_op jit(solution)/shard_map/ppermute | solution.py:33
  44.7 14.4 %collective-permute-start.21 = (bf16[4,80,512]{2,1,0:T(8,128)(2,1)S(1)}, bf16[4,80,512]{2,1,0:T(8,128)(2,1)S(1)}, u32[]{:S(2)}, u32[]{:S(2)}) collective-permute-start(bf16[4,80,512]{2,1,0:T(8,128)(2,1)S(1)} %collective-permute-done.17.refs_10_), channel_id=1, source_target_pairs={{0,8},{1,9},{2,10},{3,11},{4,12},{5,13},{6,14},{7,15},{8,0},{9,1},... | collective-permute-start | bytes 983048 | tf_op jit(solution)/shard_map/ppermute | solution.py:33
  58.1 10.0 %copy-start.19 = (bf16[4,80,512]{2,1,0:T(8,128)(2,1)}, bf16[4,80,512]{2,1,0:T(8,128)(2,1)S(1)}, u32[]{:S(2)}) copy-start(bf16[4,80,512]{2,1,0:T(8,128)(2,1)S(1)} %collective-permute-done.20.refs_9_) | copy-start | bytes 983044
  59.0 9.0 %copy-start.20 = (bf16[4,80,512]{2,1,0:T(8,128)(2,1)}, bf16[4,80,512]{2,1,0:T(8,128)(2,1)S(1)}, u32[]{:S(2)}) copy-start(bf16[4,80,512]{2,1,0:T(8,128)(2,1)S(1)} %collective-permute-done.21.refs_11_) | copy-start | bytes 983044
  59.0 9.0 %copy-start.12 = (bf16[4,32,2048]{2,1,0:T(8,128)(2,1)}, bf16[4,32,2048]{2,1,0:T(8,128)(2,1)S(1)}, u32[]{:S(2)}) copy-start(bf16[4,32,2048]{2,1,0:T(8,128)(2,1)S(1)} %collective-permute-done.18.refs_2_) | copy-start | bytes 1572868
  59.0 9.0 %copy-start.13 = (bf16[4,32,2048]{2,1,0:T(8,128)(2,1)}, bf16[4,32,2048]{2,1,0:T(8,128)(2,1)S(1)}, u32[]{:S(2)}) copy-start(bf16[4,32,2048]{2,1,0:T(8,128)(2,1)S(1)} %collective-permute-done.19.refs_3_) | copy-start | bytes 1572868
  59.1 4.6 %collective-permute-start.26 = (bf16[4,80,512]{2,1,0:T(8,128)(2,1)S(1)}, bf16[4,80,512]{2,1,0:T(8,128)(2,1)S(1)}, u32[]{:S(2)}, u32[]{:S(2)}) collective-permute-start(bf16[4,80,512]{2,1,0:T(8,128)(2,1)S(1)} %pad_maximum_fusion.2.refs_8_), channel_id=1, source_target_pairs={{0,1},{1,0},{2,3},{3,2},{4,5},{5,4},{6,7},{7,6},{8,9},{9,8},{10,11... | collective-permute-start | bytes 983048 | tf_op jit(solution)/shard_map/ppermute | solution.py:33
  62.4 1.7 %collective-permute-start.27 = (bf16[4,80,512]{2,1,0:T(8,128)(2,1)S(1)}, bf16[4,80,512]{2,1,0:T(8,128)(2,1)S(1)}, u32[]{:S(2)}, u32[]{:S(2)}) collective-permute-start(bf16[4,80,512]{2,1,0:T(8,128)(2,1)S(1)} %collective-permute-done.20.refs_9_), channel_id=1, source_target_pairs={{0,1},{1,0},{2,3},{3,2},{4,5},{5,4},{6,7},{7,6},{8,9},{9,8},{10,11... | collective-permute-start | bytes 983048 | tf_op jit(solution)/shard_map/ppermute | solution.py:33
  62.5 4.8 %collective-permute-start.24 = (bf16[4,32,2048]{2,1,0:T(8,128)(2,1)S(1)}, bf16[4,32,2048]{2,1,0:T(8,128)(2,1)S(1)}, u32[]{:S(2)}, u32[]{:S(2)}) collective-permute-start(bf16[4,32,2048]{2,1,0:T(8,128)(2,1)S(1)} %collective-permute-done.18.refs_2_), channel_id=1, source_target_pairs={{0,1},{1,0},{2,3},{3,2},{4,5},{5,4},{6,7},{7,6},{8,9},{9,8},{10,11... | collective-permute-start | bytes 1572872 | tf_op jit(solution)/shard_map/ppermute | solution.py:33
  62.9 4.4 %collective-permute-start.25 = (bf16[4,32,2048]{2,1,0:T(8,128)(2,1)S(1)}, bf16[4,32,2048]{2,1,0:T(8,128)(2,1)S(1)}, u32[]{:S(2)}, u32[]{:S(2)}) collective-permute-start(bf16[4,32,2048]{2,1,0:T(8,128)(2,1)S(1)} %collective-permute-done.19.refs_3_), channel_id=1, source_target_pairs={{0,1},{1,0},{2,3},{3,2},{4,5},{5,4},{6,7},{7,6},{8,9},{9,8},{10,11... | collective-permute-start | bytes 1572872 | tf_op jit(solution)/shard_map/ppermute | solution.py:33
  63.0 4.3 %collective-permute-start.23 = (bf16[4,32,2048]{2,1,0:T(8,128)(2,1)S(1)}, bf16[4,32,2048]{2,1,0:T(8,128)(2,1)S(1)}, u32[]{:S(2)}, u32[]{:S(2)}) collective-permute-start(bf16[4,32,2048]{2,1,0:T(8,128)(2,1)S(1)} %collective-permute-done.16.refs_1_), channel_id=1, source_target_pairs={{0,1},{1,0},{2,3},{3,2},{4,5},{5,4},{6,7},{7,6},{8,9},{9,8},{10,11... | collective-permute-start | bytes 1572872 | tf_op jit(solution)/shard_map/ppermute | solution.py:33
  63.7 3.2 %collective-permute-start.28 = (bf16[4,80,512]{2,1,0:T(8,128)(2,1)S(1)}, bf16[4,80,512]{2,1,0:T(8,128)(2,1)S(1)}, u32[]{:S(2)}, u32[]{:S(2)}) collective-permute-start(bf16[4,80,512]{2,1,0:T(8,128)(2,1)S(1)} %collective-permute-done.17.refs_10_), channel_id=1, source_target_pairs={{0,1},{1,0},{2,3},{3,2},{4,5},{5,4},{6,7},{7,6},{8,9},{9,8},{10,11... | collective-permute-start | bytes 983048 | tf_op jit(solution)/shard_map/ppermute | solution.py:33
  64.1 3.2 %collective-permute-start.29 = (bf16[4,80,512]{2,1,0:T(8,128)(2,1)S(1)}, bf16[4,80,512]{2,1,0:T(8,128)(2,1)S(1)}, u32[]{:S(2)}, u32[]{:S(2)}) collective-permute-start(bf16[4,80,512]{2,1,0:T(8,128)(2,1)S(1)} %collective-permute-done.21.refs_11_), channel_id=1, source_target_pairs={{0,1},{1,0},{2,3},{3,2},{4,5},{5,4},{6,7},{7,6},{8,9},{9,8},{10,11... | collective-permute-start | bytes 983048 | tf_op jit(solution)/shard_map/ppermute | solution.py:33
  81.1 8.2 %collective-permute-start.30 = (bf16[8,32,2048]{2,1,0:T(8,128)(2,1)}, bf16[8,32,2048]{2,1,0:T(8,128)(2,1)S(1)}, u32[]{:S(2)}, u32[]{:S(2)}) collective-permute-start(bf16[8,32,2048]{2,1,0:T(8,128)(2,1)} %get-tuple-element.113), channel_id=1, source_target_pairs={{0,1},{1,0},{2,3},{3,2},{4,5},{5,4},{6,7},{7,6},{8,9},{9,8},{10,11... | collective-permute-start | bytes 3145736 | tf_op jit(solution)/shard_map/ppermute | solution.py:33
  81.5 7.8 %collective-permute-start.31 = (bf16[16,16,2048]{2,1,0:T(8,128)(2,1)}, bf16[16,16,2048]{2,1,0:T(8,128)(2,1)S(1)}, u32[]{:S(2)}, u32[]{:S(2)}) collective-permute-start(bf16[16,16,2048]{2,1,0:T(8,128)(2,1)} %get-tuple-element.114), channel_id=1, source_target_pairs={{0,1},{1,0},{2,3},{3,2},{4,5},{5,4},{6,7},{7,6},{8,9},{9,8},{10,11... | collective-permute-start | bytes 3145736 | tf_op jit(solution)/shard_map/ppermute | solution.py:33
  81.7 8.6 %copy-start = (bf16[16,32,2048]{2,1,0:T(8,128)(2,1)S(1)}, bf16[16,32,2048]{2,1,0:T(8,128)(2,1)}, u32[]{:S(2)}) copy-start(bf16[16,32,2048]{2,1,0:T(8,128)(2,1)} %get-tuple-element.127) | copy-start | bytes 6291460
  90.7 21.8 %collective-permute-start.33 = (bf16[8,32,2048]{2,1,0:T(8,128)(2,1)S(1)}, bf16[8,32,2048]{2,1,0:T(8,128)(2,1)}, u32[]{:S(2)}, u32[]{:S(2)}) collective-permute-start(bf16[8,32,2048]{2,1,0:T(8,128)(2,1)S(1)} %add_convert_fusion), channel_id=1, source_target_pairs={{0,4},{1,3},{2,6},{3,1},{4,0},{5,7},{6,2},{7,5},{8,12},{9,11},{10,... | collective-permute-start | bytes 3145736 | tf_op jit(solution)/shard_map/ppermute | solution.py:33
  93.4 19.1 %collective-permute-start.34 = (bf16[8,16,2048]{2,1,0:T(8,128)(2,1)}, bf16[8,16,2048]{2,1,0:T(8,128)(2,1)}, u32[]{:S(2)}, u32[]{:S(2)}) collective-permute-start(bf16[8,16,2048]{2,1,0:T(8,128)(2,1)} %add_convert_fusion.2.refs_15_), channel_id=1, source_target_pairs={{0,8},{1,9},{2,10},{3,11},{4,12},{5,13},{6,14},{7,15},{8,0},{9,1},... | collective-permute-start | bytes 1572872 | tf_op jit(solution)/shard_map/ppermute | solution.py:33
  110.1 1.8 %collective-permute-start.35 = (bf16[4,16,2176]{2,1,0:T(8,128)(2,1)}, bf16[4,16,2176]{2,1,0:T(8,128)(2,1)S(1)}, u32[]{:S(2)}, u32[]{:S(2)}) collective-permute-start(bf16[4,16,2176]{2,1,0:T(8,128)(2,1)} %get-tuple-element.133), channel_id=1, source_target_pairs={{0,1},{1,0},{2,3},{3,2},{4,5},{5,4},{6,7},{7,6},{8,9},{9,8},{10,11... | collective-permute-start | bytes 835592 | tf_op jit(solution)/shard_map/ppermute | solution.py:33
  110.2 2.3 %collective-permute-start.36 = (bf16[4,16,2176]{2,1,0:T(8,128)(2,1)}, bf16[4,16,2176]{2,1,0:T(8,128)(2,1)}, u32[]{:S(2)}, u32[]{:S(2)}) collective-permute-start(bf16[4,16,2176]{2,1,0:T(8,128)(2,1)} %get-tuple-element.134), channel_id=1, source_target_pairs={{0,1},{1,0},{2,3},{3,2},{4,5},{5,4},{6,7},{7,6},{8,9},{9,8},{10,11... | collective-permute-start | bytes 835592 | tf_op jit(solution)/shard_map/ppermute | solution.py:33
  110.7 4.2 %collective-permute-start.38 = (bf16[8,32,2048]{2,1,0:T(8,128)(2,1)}, bf16[8,32,2048]{2,1,0:T(8,128)(2,1)S(1)}, u32[]{:S(2)}, u32[]{:S(2)}) collective-permute-start(bf16[8,32,2048]{2,1,0:T(8,128)(2,1)} %get-tuple-element.140), channel_id=1, source_target_pairs={{0,1},{1,0},{2,3},{3,2},{4,5},{5,4},{6,7},{7,6},{8,9},{9,8},{10,11... | collective-permute-start | bytes 3145736 | tf_op jit(solution)/shard_map/ppermute | solution.py:33
  111.9 15.8 %collective-permute-start.32 = (bf16[8,16,2176]{2,1,0:T(8,128)(2,1)}, bf16[8,16,2176]{2,1,0:T(8,128)(2,1)S(1)}, u32[]{:S(2)}, u32[]{:S(2)}) collective-permute-start(bf16[8,16,2176]{2,1,0:T(8,128)(2,1)} %get-tuple-element.132), channel_id=1, source_target_pairs={{0,1},{1,0},{2,3},{3,2},{4,5},{5,4},{6,7},{7,6},{8,9},{9,8},{10,11... | collective-permute-start | bytes 1671176 | tf_op jit(solution)/shard_map/ppermute | solution.py:33
  112.5 5.2 %copy-start.3 = (bf16[16,16,2048]{2,1,0:T(8,128)(2,1)S(1)}, bf16[16,16,2048]{2,1,0:T(8,128)(2,1)}, u32[]{:S(2)}) copy-start(bf16[16,16,2048]{2,1,0:T(8,128)(2,1)} %get-tuple-element.125) | copy-start | bytes 3145732
  113.9 13.9 %copy-start.1 = (bf16[16,16,2176]{2,1,0:T(8,128)(2,1)S(1)}, bf16[16,16,2176]{2,1,0:T(8,128)(2,1)}, u32[]{:S(2)}) copy-start(bf16[16,16,2176]{2,1,0:T(8,128)(2,1)} %get-tuple-element.131) | copy-start | bytes 3342340
  114.0 13.8 %collective-permute-start.37 = (bf16[8,16,2176]{2,1,0:T(8,128)(2,1)S(1)}, bf16[8,16,2176]{2,1,0:T(8,128)(2,1)S(1)}, u32[]{:S(2)}, u32[]{:S(2)}) collective-permute-start(bf16[8,16,2176]{2,1,0:T(8,128)(2,1)S(1)} %pad_maximum_fusion), channel_id=1, source_target_pairs={{0,4},{1,3},{2,6},{3,1},{4,0},{5,7},{6,2},{7,5},{8,12},{9,11},{10,... | collective-permute-start | bytes 1671176 | tf_op jit(solution)/shard_map/ppermute | solution.py:33
  116.2 14.3 %collective-permute-start.41 = (bf16[4,32,2048]{2,1,0:T(8,128)(2,1)S(1)}, bf16[4,32,2048]{2,1,0:T(8,128)(2,1)S(1)}, u32[]{:S(2)}, u32[]{:S(2)}) collective-permute-start(bf16[4,32,2048]{2,1,0:T(8,128)(2,1)S(1)} %add_convert_fusion.1), channel_id=1, source_target_pairs={{0,2},{1,5},{2,0},{3,7},{4,6},{5,1},{6,4},{7,3},{8,10},{9,13},{10,... | collective-permute-start | bytes 1572872 | tf_op jit(solution)/shard_map/ppermute | solution.py:33
  118.8 14.1 %collective-permute-start.40 = (bf16[4,16,2048]{2,1,0:T(8,128)(2,1)S(1)}, bf16[4,16,2048]{2,1,0:T(8,128)(2,1)S(1)}, u32[]{:S(2)}, u32[]{:S(2)}) collective-permute-start(bf16[4,16,2048]{2,1,0:T(8,128)(2,1)S(1)} %add_convert_fusion.7), channel_id=1, source_target_pairs={{0,16},{1,17},{2,18},{3,19},{4,20},{5,21},{6,22},{7,23},{8,24},{9,... | collective-permute-start | bytes 786440 | tf_op jit(solution)/shard_map/ppermute | solution.py:33
  127.9 7.3 %collective-permute-start.39 = (bf16[4,16,2176]{2,1,0:T(8,128)(2,1)S(1)}, bf16[4,16,2176]{2,1,0:T(8,128)(2,1)S(1)}, u32[]{:S(2)}, u32[]{:S(2)}) collective-permute-start(bf16[4,16,2176]{2,1,0:T(8,128)(2,1)S(1)} %add_convert_fusion.3), channel_id=1, source_target_pairs={{0,2},{1,5},{2,0},{3,7},{4,6},{5,1},{6,4},{7,3},{8,10},{9,13},{10,... | collective-permute-start | bytes 835592 | tf_op jit(solution)/shard_map/ppermute | solution.py:33
  131.6 8.6 %collective-permute-start.43 = (bf16[2,32,2048]{2,1,0:T(8,128)(2,1)S(1)}, bf16[2,32,2048]{2,1,0:T(8,128)(2,1)S(1)}, u32[]{:S(2)}, u32[]{:S(2)}) collective-permute-start(bf16[2,32,2048]{2,1,0:T(8,128)(2,1)S(1)} %add_convert_fusion.6), channel_id=1, source_target_pairs={{0,8},{1,9},{2,10},{3,11},{4,12},{5,13},{6,14},{7,15},{8,0},{9,1},... | collective-permute-start | bytes 786440 | tf_op jit(solution)/shard_map/ppermute | solution.py:33
  133.9 5.0 %collective-permute-start.44 = (bf16[2,16,2048]{2,1,0:T(8,128)(2,1)S(1)}, bf16[2,16,2048]{2,1,0:T(8,128)(2,1)S(1)}, u32[]{:S(2)}, u32[]{:S(2)}) collective-permute-start(bf16[2,16,2048]{2,1,0:T(8,128)(2,1)S(1)} %add_convert_fusion.10), channel_id=1, source_target_pairs={{0,4},{1,3},{2,6},{3,1},{4,0},{5,7},{6,2},{7,5},{8,12},{9,11},{10,... | collective-permute-start | bytes 393224 | tf_op jit(solution)/shard_map/ppermute | solution.py:33
  135.2 8.7 %collective-permute-start.42 = (bf16[2,16,2176]{2,1,0:T(8,128)(2,1)S(1)}, bf16[2,16,2176]{2,1,0:T(8,128)(2,1)S(1)}, u32[]{:S(2)}, u32[]{:S(2)}) collective-permute-start(bf16[2,16,2176]{2,1,0:T(8,128)(2,1)S(1)} %add_convert_fusion.8), channel_id=1, source_target_pairs={{0,8},{1,9},{2,10},{3,11},{4,12},{5,13},{6,14},{7,15},{8,0},{9,1},... | collective-permute-start | bytes 417800 | tf_op jit(solution)/shard_map/ppermute | solution.py:33
  141.3 8.1 %collective-permute-start.46 = (bf16[32,2048]{1,0:T(8,128)(2,1)S(1)}, bf16[32,2048]{1,0:T(8,128)(2,1)S(1)}, u32[]{:S(2)}, u32[]{:S(2)}) collective-permute-start(bf16[32,2048]{1,0:T(8,128)(2,1)S(1)} %get-tuple-element.157), channel_id=1, source_target_pairs={{0,16},{1,17},{2,18},{3,19},{4,20},{5,21},{6,22},{7,23},{8,24},{9,... | collective-permute-start | bytes 393224 | tf_op jit(solution)/shard_map/ppermute | solution.py:33
  143.5 4.3 %collective-permute-start.47 = (bf16[1,16,2048]{2,1,0:T(8,128)(2,1)S(1)}, bf16[1,16,2048]{2,1,0:T(8,128)(2,1)S(1)}, u32[]{:S(2)}, u32[]{:S(2)}) collective-permute-start(bf16[1,16,2048]{2,1,0:T(8,128)(2,1)S(1)} %add_convert_fusion.12), channel_id=1, source_target_pairs={{0,2},{1,5},{2,0},{3,7},{4,6},{5,1},{6,4},{7,3},{8,10},{9,13},{10,... | collective-permute-start | bytes 196616 | tf_op jit(solution)/shard_map/ppermute | solution.py:33
  144.0 6.9 %collective-permute-start.45 = (bf16[16,2176]{1,0:T(8,128)(2,1)S(1)}, bf16[16,2176]{1,0:T(8,128)(2,1)S(1)}, u32[]{:S(2)}, u32[]{:S(2)}) collective-permute-start(bf16[16,2176]{1,0:T(8,128)(2,1)S(1)} %get-tuple-element.158), channel_id=1, source_target_pairs={{0,16},{1,17},{2,18},{3,19},{4,20},{5,21},{6,22},{7,23},{8,24},{9,... | collective-permute-start | bytes 208904 | tf_op jit(solution)/shard_map/ppermute | solution.py:33
  (16 other events, 42.2 us)

commit v6 on v5

--- a/solution.py
+++ b/solution.py
@@ -12,7 +12,7 @@
 EB = 32
 RB = EB * SLOTS
 CH = 64
-VMEM_LIMIT = 58 * 2**20
+VMEM_LIMIT = 50 * 2**20
 SCALE = HEAD_DIM ** (-0.5)
 F32 = jnp.float32
 LOW = jnp.bfloat16
@@ -650,12 +650,12 @@
         upper, lower = spread(shard, LAYER[2], LAYER[1])
         quad = jnp.stack([tie(third, own), *quad[1:]])
         own2 = jnp.stack([tie(shard, quad), lower, upper, send(tie(upper, own), LAYER[1])])
-        pieces.append([own2, *spread(own2, NEAR, FAR, ACROSS)])
+        pieces.append([own2, *spread(own2, NEAR, FAR)])
         lower, upper = spread(quad, LAYER[1], LAYER[2])
         upper = tie(upper, own2)
         pieces.append([quad, lower, upper, send(upper, LAYER[1])])
         near2 = tie(pieces[1][1], upper)
-        early = [send(own2, CORE), send(near2, CORE)]
+        pieces[1].append(send(near2, FAR))
         later = [tie(own2, near2)]
         group_ids, piece_counts = tie(group_ids, piece_counts, own, every=True)[:2]
     else:
@@ -717,8 +717,8 @@
     )
     if tuned:
         mixed, *came = tie(mixed, *pieces[1], *pieces[2], every=True)
-        cores = [send(part, CORE) for part in came[2:]]
-        pieces[1:] = [came[0:4] + early + cores[:2], came[4:8] + cores[2:]]
+        cores = [send(part, CORE) for part in came]
+        pieces[1:] = [came[0:4] + cores[:4], came[4:8] + cores[4:]]
     (
         output, dfirst, dmixed, sum_up, sum_gain, sum_shift, sum_pool, own_pair, low_pair, high_pair, *both_down
     ) = call(

time: 155 us -> 149 us (0.961)
  waiting for transfers between devices: 34.1 us -> 30.7 us
  starting transfers between devices: 49.6 us -> 48 us
    ppermute x48, waiting for transfers between devices: 34.1 us -> 30.7 us  [send(): return lax.ppermute(value, 'dp', to)]
    ppermute x48, starting transfers between devices: 49.6 us -> 48 us  [send(): return lax.ppermute(value, 'dp', to)]
  transfers between devices with their start and end apart: 48 -> 48, of which waited for: 17 -> 15; matrix products, arithmetic and copies ran while one was open for 11% -> 10% of each run, Pallas kernels for 22% -> 22%
where the time goes in v6:
time: 149 us; the launch traced here: 148 us
  starting transfers between devices  48 us (32%)
  Pallas kernels  46 us (31%)
  waiting for transfers between devices  30.7 us (21%)
  other arithmetic  17.5 us (12%)
  local copies, waits for them, and re-layouts  4.85 us (3%)
    ppermute x48, starting transfers between devices, send(): return lax.ppermute(value, 'dp', to)  48 us
    pallas_call x4, Pallas kernels, call(): pl.pallas_call(kernel, out_shape=[jax.ShapeDtypeStruct(s, t) for s, t, _p...  46 us
    ppermute x48, waiting for transfers between devices, send(): return lax.ppermute(value, 'dp', to)  30.7 us
  transfers between devices with their start and end apart: 48, of which 15 were waited for; matrix products, arithmetic and copies ran while one was open for 10% of the time, Pallas kernels for 22%

profile of v6, /device:TPU:0, one launch (start us, length us, event | category | flops | bytes accessed | tf_op | source)
XLA Modules:
  0.0 148.1 jit_solution(5717582970578847657)
XLA Ops:
  0.7 0.9 pad_add_fusion.2
  1.6 5.1 %collective-permute-start.2 = (bf16[16,1664]{1,0:T(8,128)(2,1)S(1)}, bf16[16,1664]{1,0:T(8,128)(2,1)S(1)}, u32[]{:S(2)}, u32[]{:S(2)}) collective-permute-start(bf16[16,1664]{1,0:T(8,128)(2,1)S(1)} %pad_add_fusion.2), channel_id=1, source_target_pairs={{0,24},{1,25},{2,26},{3,27},{4,28},{5,29},{6,30},{7,31},{8,16},{9,... | collective-permute-start | bytes 159752 | tf_op jit(solution)/shard_map/ppermute | solution.py:33
  6.7 0.6 collective-permute-start.1
  7.3 0.9 pad_add_fusion.1
  8.2 1.6 %collective-permute-start.10 = (bf16[80,512]{1,0:T(8,128)(2,1)S(1)}, bf16[80,512]{1,0:T(8,128)(2,1)S(1)}, u32[]{:S(2)}, u32[]{:S(2)}) collective-permute-start(bf16[80,512]{1,0:T(8,128)(2,1)S(1)} %pad_add_fusion.1), channel_id=1, source_target_pairs={{0,2},{1,5},{2,0},{3,7},{4,6},{5,1},{6,4},{7,3},{8,10},{9,13},{10,... | collective-permute-start | bytes 245768 | tf_op jit(solution)/shard_map/ppermute | solution.py:33
  9.9 1.5 %collective-permute-start.11 = (bf16[80,512]{1,0:T(8,128)(2,1)S(1)}, bf16[80,512]{1,0:T(8,128)(2,1)S(1)}, u32[]{:S(2)}, u32[]{:S(2)}) collective-permute-start(bf16[80,512]{1,0:T(8,128)(2,1)S(1)} %pad_add_fusion.1), channel_id=1, source_target_pairs={{0,4},{1,3},{2,6},{3,1},{4,0},{5,7},{6,2},{7,5},{8,12},{9,11},{10,... | collective-permute-start | bytes 245768 | tf_op jit(solution)/shard_map/ppermute | solution.py:33
  11.4 0.9 fusion.5
  12.3 0.9 pad_add_fusion
  13.6 2.3 %collective-permute-start.14 = (bf16[32,2048]{1,0:T(8,128)(2,1)S(1)}, bf16[32,2048]{1,0:T(8,128)(2,1)S(1)}, u32[]{:S(2)}, u32[]{:S(2)}) collective-permute-start(bf16[32,2048]{1,0:T(8,128)(2,1)S(1)} %pad_add_fusion), channel_id=1, source_target_pairs={{0,16},{1,17},{2,18},{3,19},{4,20},{5,21},{6,22},{7,23},{8,24},{9,... | collective-permute-start | bytes 393224 | tf_op jit(solution)/shard_map/ppermute | solution.py:33
  15.9 2.0 %collective-permute-start.13 = (bf16[32,2048]{1,0:T(8,128)(2,1)S(1)}, bf16[32,2048]{1,0:T(8,128)(2,1)S(1)}, u32[]{:S(2)}, u32[]{:S(2)}) collective-permute-start(bf16[32,2048]{1,0:T(8,128)(2,1)S(1)} %pad_add_fusion), channel_id=1, source_target_pairs={{0,8},{1,9},{2,10},{3,11},{4,12},{5,13},{6,14},{7,15},{8,0},{9,1},... | collective-permute-start | bytes 393224 | tf_op jit(solution)/shard_map/ppermute | solution.py:33
  18.0 3.3 %collective-permute-done.14 = bf16[32,2048]{1,0:T(8,128)(2,1)S(1)} collective-permute-done((bf16[32,2048]{1,0:T(8,128)(2,1)S(1)}, bf16[32,2048]{1,0:T(8,128)(2,1)S(1)}, u32[]{:S(2)}, u32[]{:S(2)}) %collective-permute-start.14) | collective-permute-done | bytes 131104 | tf_op jit(solution)/shard_map/ppermute | solution.py:33
  21.5 0.8 iota_compare_fusion
  22.3 1.6 %collective-permute-start.3 = (bf16[4,16,1664]{2,1,0:T(8,128)(2,1)S(1)}, bf16[4,16,1664]{2,1,0:T(8,128)(2,1)S(1)}, u32[]{:S(2)}, u32[]{:S(2)}) collective-permute-start(bf16[4,16,1664]{2,1,0:T(8,128)(2,1)S(1)} %pad_maximum_fusion.3.refs_0_), channel_id=1, source_target_pairs={{0,2},{1,5},{2,0},{3,7},{4,6},{5,1},{6,4},{7,3},{8,10},{9,13},{10,... | collective-permute-start | bytes 638984 | tf_op jit(solution)/shard_map/ppermute | solution.py:33
  23.9 1.5 %collective-permute-start.4 = (bf16[4,16,1664]{2,1,0:T(8,128)(2,1)S(1)}, bf16[4,16,1664]{2,1,0:T(8,128)(2,1)S(1)}, u32[]{:S(2)}, u32[]{:S(2)}) collective-permute-start(bf16[4,16,1664]{2,1,0:T(8,128)(2,1)S(1)} %pad_maximum_fusion.3.refs_0_), channel_id=1, source_target_pairs={{0,4},{1,3},{2,6},{3,1},{4,0},{5,7},{6,2},{7,5},{8,12},{9,11},{10,... | collective-permute-start | bytes 638984 | tf_op jit(solution)/shard_map/ppermute | solution.py:33
  25.9 3.4 %collective-permute-start.17 = (bf16[4,80,512]{2,1,0:T(8,128)(2,1)S(1)}, bf16[4,80,512]{2,1,0:T(8,128)(2,1)S(1)}, u32[]{:S(2)}, u32[]{:S(2)}) collective-permute-start(bf16[4,80,512]{2,1,0:T(8,128)(2,1)S(1)} %pad_maximum_fusion.2.refs_8_), channel_id=1, source_target_pairs={{0,16},{1,17},{2,18},{3,19},{4,20},{5,21},{6,22},{7,23},{8,24},{9,... | collective-permute-start | bytes 983048 | tf_op jit(solution)/shard_map/ppermute | solution.py:33
  29.5 1.6 %collective-permute-start.16 = (bf16[4,32,2048]{2,1,0:T(8,128)(2,1)S(1)}, bf16[4,32,2048]{2,1,0:T(8,128)(2,1)S(1)}, u32[]{:S(2)}, u32[]{:S(2)}) collective-permute-start(bf16[4,32,2048]{2,1,0:T(8,128)(2,1)S(1)} %pad_maximum_fusion.1.refs_10_.refs_0_), channel_id=1, source_target_pairs={{0,2},{1,5},{2,0},{3,7},{4,6},{5,1},{6,4},{7,3},{8,10},{9,13},{10,... | collective-permute-start | bytes 1572872 | tf_op jit(solution)/shard_map/ppermute | solution.py:33
  31.4 3.2 %collective-permute-done.4.refs_2_ = bf16[4,16,1664]{2,1,0:T(8,128)(2,1)S(1)} collective-permute-done((bf16[4,16,1664]{2,1,0:T(8,128)(2,1)S(1)}, bf16[4,16,1664]{2,1,0:T(8,128)(2,1)S(1)}, u32[]{:S(2)}, u32[]{:S(2)}) %collective-permute-start.4) | collective-permute-done | bytes 213024 | tf_op jit(solution)/shard_map/ppermute | solution.py:33
  34.6 0.5 collective-permute-start.8
  35.1 5.7 %collective-permute-done.17.refs_10_ = bf16[4,80,512]{2,1,0:T(8,128)(2,1)S(1)} collective-permute-done((bf16[4,80,512]{2,1,0:T(8,128)(2,1)S(1)}, bf16[4,80,512]{2,1,0:T(8,128)(2,1)S(1)}, u32[]{:S(2)}, u32[]{:S(2)}) %collective-permute-start.17) | collective-permute-done | bytes 327712 | tf_op jit(solution)/shard_map/ppermute | solution.py:33
  41.2 1.3 collective-permute-start.18
  42.5 1.9 %collective-permute-start.21 = (bf16[4,80,512]{2,1,0:T(8,128)(2,1)S(1)}, bf16[4,80,512]{2,1,0:T(8,128)(2,1)S(1)}, u32[]{:S(2)}, u32[]{:S(2)}) collective-permute-start(bf16[4,80,512]{2,1,0:T(8,128)(2,1)S(1)} %collective-permute-done.17.refs_10_), channel_id=1, source_target_pairs={{0,8},{1,9},{2,10},{3,11},{4,12},{5,13},{6,14},{7,15},{8,0},{9,1},... | collective-permute-start | bytes 983048 | tf_op jit(solution)/shard_map/ppermute | solution.py:33
  44.4 0.8 collective-permute-start.19
  45.2 11.8 %shard_map.263 = (bf16[512,1664]{1,0:T(8,128)(2,1)}, f32[16,512]{1,0:T(8,128)S(1)}, f32[8,2048]{1,0:T(8,128)S(1)}, f32[256,512]{1,0:T(8,128)S(1)}, bf16[2048,512...) custom-call(s32[1]{0:T(128)} %bitcast.me_ref, ...), custom_call_target="tpu_custom_call" | custom-call | flops 16499999744 | bytes 1000 | tf_op jit(solution)/shard_map/pallas_call | solution.py:293
  57.0 0.8 copy-done.2
  58.4 0.5 collective-permute-start.27
  59.5 0.5 collective-permute-done.26.refs_12_
  60.6 0.8 collective-permute-done.28.refs_14_
  61.6 2.9 %collective-permute-done.29.refs_15_ = bf16[4,80,512]{2,1,0:T(8,128)(2,1)S(1)} collective-permute-done((bf16[4,80,512]{2,1,0:T(8,128)(2,1)S(1)}, bf16[4,80,512]{2,1,0:T(8,128)(2,1)S(1)}, u32[]{:S(2)}, u32[]{:S(2)}) %collective-permute-start.29) | collective-permute-done | bytes 327712 | tf_op jit(solution)/shard_map/ppermute | solution.py:33
  64.5 0.7 copy-done.14
  65.8 13.3 %shard_map.264 = (bf16[256,2048]{1,0:T(8,128)(2,1)}, f32[256,512]{1,0:T(8,128)S(1)}, bf16[256,512]{1,0:T(8,128)(2,1)S(1)}, f32[8,2048]{1,0:T(8,128)S(1)}, f32[8,...) custom-call(s32[1]{0:T(128)} %bitcast.me_ref, ...), custom_call_target="tpu_custom_call" | custom-call | flops 13200000000 | bytes 1000 | tf_op jit(solution)/shard_map/pallas_call | solution.py:293
  79.7 6.9 %shard_map.265 = (bf16[2048,1024]{1,0:T(8,128)(2,1)}, bf16[256,512]{1,0:T(8,128)(2,1)S(1)}, f32[256,512]{1,0:T(8,128)S(1)}) custom-call(s32[1]{0:T(128)} %bitcast.me_ref, bf16[256,512]{1,0:T(8,128)(2,1)S(1)} %get-tuple-element.107.refs_0_, bf16[256,512]{1,0:T(8,128)(2,1)S(1)} %get-tuple-element.108.refs_1_, bf16[2048,256]{1,0:T(8,128)(2,1)S(1)} %copy-done.1, ...), custom_call_target="tpu_custom_call" | custom-call | flops 8800000000 | bytes 1000 | tf_op jit(solution)/shard_map/pallas_call | solution.py:293
  86.7 1.4 add_convert_fusion
  88.1 1.2 collective-permute-start.33
  89.8 14.0 %shard_map.266 = (bf16[2048,512]{1,0:T(8,128)(2,1)}, bf16[16,16,2176]{2,1,0:T(8,128)(2,1)}, bf16[8,16,2176]{2,1,0:T(8,128)(2,1)}, bf16[4,16,2176]{2,1,0:T(8,128)(2,1)S(1)}, bf16[4,16,2176]{2,1,0:T(8,128)(2,1)S(1)}) custom-call(s32[1]{0:T(128)} %bitcast.me_ref, f32[16,512]{1,0:T(8,128)S(1)} %get-tuple-element.104.refs_19_.refs_0_, ...), custom_call_target="tpu_custom_call" | custom-call | flops 19800000512 | bytes 1000 | tf_op jit(solution)/shard_map/pallas_call | solution.py:293
  103.9 0.5 collective-permute-start.36
  104.5 1.0 collective-permute-done.35
  106.0 1.4 add_convert_fusion.5
  107.5 0.9 collective-permute-start.37
  108.4 1.3 add_convert_fusion.1
  109.7 1.3 collective-permute-start.41
  110.9 1.0 add_convert_fusion.7
  112.0 2.7 %collective-permute-start.40 = (bf16[4,16,2048]{2,1,0:T(8,128)(2,1)S(1)}, bf16[4,16,2048]{2,1,0:T(8,128)(2,1)S(1)}, u32[]{:S(2)}, u32[]{:S(2)}) collective-permute-start(bf16[4,16,2048]{2,1,0:T(8,128)(2,1)S(1)} %add_convert_fusion.7), channel_id=1, source_target_pairs={{0,16},{1,17},{2,18},{3,19},{4,20},{5,21},{6,22},{7,23},{8,24},{9,... | collective-permute-start | bytes 786440 | tf_op jit(solution)/shard_map/ppermute | solution.py:33
  114.7 6.5 %collective-permute-done.37 = bf16[8,16,2176]{2,1,0:T(8,128)(2,1)S(1)} collective-permute-done((bf16[8,16,2176]{2,1,0:T(8,128)(2,1)S(1)}, bf16[8,16,2176]{2,1,0:T(8,128)(2,1)S(1)}, u32[]{:S(2)}, u32[]{:S(2)}) %collective-permute-start.37) | collective-permute-done | bytes 557088 | tf_op jit(solution)/shard_map/ppermute | solution.py:33
  121.4 2.6 %collective-permute-start.39 = (bf16[4,16,2176]{2,1,0:T(8,128)(2,1)S(1)}, bf16[4,16,2176]{2,1,0:T(8,128)(2,1)S(1)}, u32[]{:S(2)}, u32[]{:S(2)}) collective-permute-start(bf16[4,16,2176]{2,1,0:T(8,128)(2,1)S(1)} %add_convert_fusion.3), channel_id=1, source_target_pairs={{0,2},{1,5},{2,0},{3,7},{4,6},{5,1},{6,4},{7,3},{8,10},{9,13},{10,... | collective-permute-start | bytes 835592 | tf_op jit(solution)/shard_map/ppermute | solution.py:33
  124.0 1.1 add_convert_fusion.6
  125.1 1.8 %collective-permute-start.43 = (bf16[2,32,2048]{2,1,0:T(8,128)(2,1)S(1)}, bf16[2,32,2048]{2,1,0:T(8,128)(2,1)S(1)}, u32[]{:S(2)}, u32[]{:S(2)}) collective-permute-start(bf16[2,32,2048]{2,1,0:T(8,128)(2,1)S(1)} %add_convert_fusion.6), channel_id=1, source_target_pairs={{0,8},{1,9},{2,10},{3,11},{4,12},{5,13},{6,14},{7,15},{8,0},{9,1},... | collective-permute-start | bytes 786440 | tf_op jit(solution)/shard_map/ppermute | solution.py:33
  126.9 1.0 add_convert_fusion.10
  127.9 1.2 collective-permute-start.44
  129.1 2.2 %collective-permute-start.42 = (bf16[2,16,2176]{2,1,0:T(8,128)(2,1)S(1)}, bf16[2,16,2176]{2,1,0:T(8,128)(2,1)S(1)}, u32[]{:S(2)}, u32[]{:S(2)}) collective-permute-start(bf16[2,16,2176]{2,1,0:T(8,128)(2,1)S(1)} %add_convert_fusion.8), channel_id=1, source_target_pairs={{0,8},{1,9},{2,10},{3,11},{4,12},{5,13},{6,14},{7,15},{8,0},{9,1},... | collective-permute-start | bytes 417800 | tf_op jit(solution)/shard_map/ppermute | solution.py:33
  131.3 1.6 %collective-permute-done.44 = bf16[2,16,2048]{2,1,0:T(8,128)(2,1)S(1)} collective-permute-done((bf16[2,16,2048]{2,1,0:T(8,128)(2,1)S(1)}, bf16[2,16,2048]{2,1,0:T(8,128)(2,1)S(1)}, u32[]{:S(2)}, u32[]{:S(2)}) %collective-permute-start.44) | collective-permute-done | bytes 131104 | tf_op jit(solution)/shard_map/ppermute | solution.py:33
  132.9 0.8 collective-permute-done.43
  133.7 1.1 add_bitcast_fusion
  134.8 2.5 %collective-permute-start.46 = (bf16[32,2048]{1,0:T(8,128)(2,1)S(1)}, bf16[32,2048]{1,0:T(8,128)(2,1)S(1)}, u32[]{:S(2)}, u32[]{:S(2)}) collective-permute-start(bf16[32,2048]{1,0:T(8,128)(2,1)S(1)} %get-tuple-element.157), channel_id=1, source_target_pairs={{0,16},{1,17},{2,18},{3,19},{4,20},{5,21},{6,22},{7,23},{8,24},{9,... | collective-permute-start | bytes 393224 | tf_op jit(solution)/shard_map/ppermute | solution.py:33
  137.3 0.9 add_convert_fusion.12
  138.2 1.0 collective-permute-start.47
  139.5 2.9 %collective-permute-done.47 = bf16[1,16,2048]{2,1,0:T(8,128)(2,1)S(1)} collective-permute-done((bf16[1,16,2048]{2,1,0:T(8,128)(2,1)S(1)}, bf16[1,16,2048]{2,1,0:T(8,128)(2,1)S(1)}, u32[]{:S(2)}, u32[]{:S(2)}) %collective-permute-start.47) | collective-permute-done | bytes 65568 | tf_op jit(solution)/shard_map/ppermute | solution.py:33
  142.5 0.9 add_bitcast_fusion.2
  143.4 0.7 fusion.3
  144.2 0.7 pad_maximum_fusion.4
  145.0 0.6 convert_add_fusion.2
  145.6 0.7 convert_add_fusion.1
  146.3 0.6 dynamic-slice_bitcast_fusion.5
  146.8 0.7 constant_dynamic-slice_fusion
  147.5 0.6 dynamic-slice_bitcast_fusion
  (108 shorter events, 7.1 us)
Async XLA Ops:
  0.6 30.4 %copy-start.10 = (s32[256]{0:T(256)S(1)}, s32[256]{0:T(256)}, u32[]{:S(2)}) copy-start(s32[256]{0:T(256)} %param.18) | copy-start | bytes 3076
  1.6 11.6 %collective-permute-start.2 = (bf16[16,1664]{1,0:T(8,128)(2,1)S(1)}, bf16[16,1664]{1,0:T(8,128)(2,1)S(1)}, u32[]{:S(2)}, u32[]{:S(2)}) collective-permute-start(bf16[16,1664]{1,0:T(8,128)(2,1)S(1)} %pad_add_fusion.2), channel_id=1, source_target_pairs={{0,24},{1,25},{2,26},{3,27},{4,28},{5,29},{6,30},{7,31},{8,16},{9,... | collective-permute-start | bytes 159752 | tf_op jit(solution)/shard_map/ppermute | solution.py:33
  6.7 6.9 %collective-permute-start = (bf16[16,1664]{1,0:T(8,128)(2,1)S(1)}, bf16[16,1664]{1,0:T(8,128)(2,1)S(1)}, u32[]{:S(2)}, u32[]{:S(2)}) collective-permute-start(bf16[16,1664]{1,0:T(8,128)(2,1)S(1)} %pad_add_fusion.2), channel_id=1, source_target_pairs={{0,8},{1,9},{2,10},{3,11},{4,12},{5,13},{6,14},{7,15},{8,0},{9,1},... | collective-permute-start | bytes 159752 | tf_op jit(solution)/shard_map/ppermute | solution.py:33
  6.7 9.2 %collective-permute-start.1 = (bf16[16,1664]{1,0:T(8,128)(2,1)S(1)}, bf16[16,1664]{1,0:T(8,128)(2,1)S(1)}, u32[]{:S(2)}, u32[]{:S(2)}) collective-permute-start(bf16[16,1664]{1,0:T(8,128)(2,1)S(1)} %pad_add_fusion.2), channel_id=1, source_target_pairs={{0,16},{1,17},{2,18},{3,19},{4,20},{5,21},{6,22},{7,23},{8,24},{9,... | collective-permute-start | bytes 159752 | tf_op jit(solution)/shard_map/ppermute | solution.py:33
  8.2 14.1 %collective-permute-start.10 = (bf16[80,512]{1,0:T(8,128)(2,1)S(1)}, bf16[80,512]{1,0:T(8,128)(2,1)S(1)}, u32[]{:S(2)}, u32[]{:S(2)}) collective-permute-start(bf16[80,512]{1,0:T(8,128)(2,1)S(1)} %pad_add_fusion.1), channel_id=1, source_target_pairs={{0,2},{1,5},{2,0},{3,7},{4,6},{5,1},{6,4},{7,3},{8,10},{9,13},{10,... | collective-permute-start | bytes 245768 | tf_op jit(solution)/shard_map/ppermute | solution.py:33
  9.9 14.0 %collective-permute-start.11 = (bf16[80,512]{1,0:T(8,128)(2,1)S(1)}, bf16[80,512]{1,0:T(8,128)(2,1)S(1)}, u32[]{:S(2)}, u32[]{:S(2)}) collective-permute-start(bf16[80,512]{1,0:T(8,128)(2,1)S(1)} %pad_add_fusion.1), channel_id=1, source_target_pairs={{0,4},{1,3},{2,6},{3,1},{4,0},{5,7},{6,2},{7,5},{8,12},{9,11},{10,... | collective-permute-start | bytes 245768 | tf_op jit(solution)/shard_map/ppermute | solution.py:33
  13.2 12.2 %collective-permute-start.12 = (bf16[80,512]{1,0:T(8,128)(2,1)S(1)}, bf16[80,512]{1,0:T(8,128)(2,1)S(1)}, u32[]{:S(2)}, u32[]{:S(2)}) collective-permute-start(bf16[80,512]{1,0:T(8,128)(2,1)S(1)} %pad_add_fusion.1), channel_id=1, source_target_pairs={{0,6},{1,7},{2,4},{3,5},{4,2},{5,3},{6,0},{7,1},{8,14},{9,15},{10,... | collective-permute-start | bytes 245768 | tf_op jit(solution)/shard_map/ppermute | solution.py:33
  13.6 7.7 %collective-permute-start.14 = (bf16[32,2048]{1,0:T(8,128)(2,1)S(1)}, bf16[32,2048]{1,0:T(8,128)(2,1)S(1)}, u32[]{:S(2)}, u32[]{:S(2)}) collective-permute-start(bf16[32,2048]{1,0:T(8,128)(2,1)S(1)} %pad_add_fusion), channel_id=1, source_target_pairs={{0,16},{1,17},{2,18},{3,19},{4,20},{5,21},{6,22},{7,23},{8,24},{9,... | collective-permute-start | bytes 393224 | tf_op jit(solution)/shard_map/ppermute | solution.py:33
  15.9 10.0 %collective-permute-start.13 = (bf16[32,2048]{1,0:T(8,128)(2,1)S(1)}, bf16[32,2048]{1,0:T(8,128)(2,1)S(1)}, u32[]{:S(2)}, u32[]{:S(2)}) collective-permute-start(bf16[32,2048]{1,0:T(8,128)(2,1)S(1)} %pad_add_fusion), channel_id=1, source_target_pairs={{0,8},{1,9},{2,10},{3,11},{4,12},{5,13},{6,14},{7,15},{8,0},{9,1},... | collective-permute-start | bytes 393224 | tf_op jit(solution)/shard_map/ppermute | solution.py:33
  21.3 8.1 %collective-permute-start.15 = (bf16[32,2048]{1,0:T(8,128)(2,1)S(1)}, bf16[32,2048]{1,0:T(8,128)(2,1)S(1)}, u32[]{:S(2)}, u32[]{:S(2)}) collective-permute-start(bf16[32,2048]{1,0:T(8,128)(2,1)S(1)} %collective-permute-done.14), channel_id=1, source_target_pairs={{0,8},{1,9},{2,10},{3,11},{4,12},{5,13},{6,14},{7,15},{8,0},{9,1},... | collective-permute-start | bytes 393224 | tf_op jit(solution)/shard_map/ppermute | solution.py:33
  22.3 9.0 %collective-permute-start.3 = (bf16[4,16,1664]{2,1,0:T(8,128)(2,1)S(1)}, bf16[4,16,1664]{2,1,0:T(8,128)(2,1)S(1)}, u32[]{:S(2)}, u32[]{:S(2)}) collective-permute-start(bf16[4,16,1664]{2,1,0:T(8,128)(2,1)S(1)} %pad_maximum_fusion.3.refs_0_), channel_id=1, source_target_pairs={{0,2},{1,5},{2,0},{3,7},{4,6},{5,1},{6,4},{7,3},{8,10},{9,13},{10,... | collective-permute-start | bytes 638984 | tf_op jit(solution)/shard_map/ppermute | solution.py:33
  23.9 10.7 %collective-permute-start.4 = (bf16[4,16,1664]{2,1,0:T(8,128)(2,1)S(1)}, bf16[4,16,1664]{2,1,0:T(8,128)(2,1)S(1)}, u32[]{:S(2)}, u32[]{:S(2)}) collective-permute-start(bf16[4,16,1664]{2,1,0:T(8,128)(2,1)S(1)} %pad_maximum_fusion.3.refs_0_), channel_id=1, source_target_pairs={{0,4},{1,3},{2,6},{3,1},{4,0},{5,7},{6,2},{7,5},{8,12},{9,11},{10,... | collective-permute-start | bytes 638984 | tf_op jit(solution)/shard_map/ppermute | solution.py:33
  25.4 9.2 %collective-permute-start.5 = (bf16[4,16,1664]{2,1,0:T(8,128)(2,1)S(1)}, bf16[4,16,1664]{2,1,0:T(8,128)(2,1)S(1)}, u32[]{:S(2)}, u32[]{:S(2)}) collective-permute-start(bf16[4,16,1664]{2,1,0:T(8,128)(2,1)S(1)} %pad_maximum_fusion.3.refs_0_), channel_id=1, source_target_pairs={{0,6},{1,7},{2,4},{3,5},{4,2},{5,3},{6,0},{7,1},{8,14},{9,15},{10,... | collective-permute-start | bytes 638984 | tf_op jit(solution)/shard_map/ppermute | solution.py:33
  25.9 14.8 %collective-permute-start.17 = (bf16[4,80,512]{2,1,0:T(8,128)(2,1)S(1)}, bf16[4,80,512]{2,1,0:T(8,128)(2,1)S(1)}, u32[]{:S(2)}, u32[]{:S(2)}) collective-permute-start(bf16[4,80,512]{2,1,0:T(8,128)(2,1)S(1)} %pad_maximum_fusion.2.refs_8_), channel_id=1, source_target_pairs={{0,16},{1,17},{2,18},{3,19},{4,20},{5,21},{6,22},{7,23},{8,24},{9,... | collective-permute-start | bytes 983048 | tf_op jit(solution)/shard_map/ppermute | solution.py:33
  29.5 15.8 %copy-start.9 = (bf16[4,32,2048]{2,1,0:T(8,128)(2,1)}, bf16[4,32,2048]{2,1,0:T(8,128)(2,1)S(1)}, u32[]{:S(2)}) copy-start(bf16[4,32,2048]{2,1,0:T(8,128)(2,1)S(1)} %pad_maximum_fusion.1.refs_10_.refs_0_) | copy-start | bytes 1572868
  29.5 11.6 %collective-permute-start.16 = (bf16[4,32,2048]{2,1,0:T(8,128)(2,1)S(1)}, bf16[4,32,2048]{2,1,0:T(8,128)(2,1)S(1)}, u32[]{:S(2)}, u32[]{:S(2)}) collective-permute-start(bf16[4,32,2048]{2,1,0:T(8,128)(2,1)S(1)} %pad_maximum_fusion.1.refs_10_.refs_0_), channel_id=1, source_target_pairs={{0,2},{1,5},{2,0},{3,7},{4,6},{5,1},{6,4},{7,3},{8,10},{9,13},{10,... | collective-permute-start | bytes 1572872 | tf_op jit(solution)/shard_map/ppermute | solution.py:33
  31.3 9.9 %collective-permute-start.6 = (bf16[4,16,1664]{2,1,0:T(8,128)(2,1)S(1)}, bf16[4,16,1664]{2,1,0:T(8,128)(2,1)S(1)}, u32[]{:S(2)}, u32[]{:S(2)}) collective-permute-start(bf16[4,16,1664]{2,1,0:T(8,128)(2,1)S(1)} %pad_maximum_fusion.3.refs_0_), channel_id=1, source_target_pairs={{0,1},{1,0},{2,3},{3,2},{4,5},{5,4},{6,7},{7,6},{8,9},{9,8},{10,11... | collective-permute-start | bytes 638984 | tf_op jit(solution)/shard_map/ppermute | solution.py:33
  34.6 7.9 %collective-permute-start.7 = (bf16[4,16,1664]{2,1,0:T(8,128)(2,1)S(1)}, bf16[4,16,1664]{2,1,0:T(8,128)(2,1)S(1)}, u32[]{:S(2)}, u32[]{:S(2)}) collective-permute-start(bf16[4,16,1664]{2,1,0:T(8,128)(2,1)S(1)} %collective-permute-done.3.refs_1_), channel_id=1, source_target_pairs={{0,1},{1,0},{2,3},{3,2},{4,5},{5,4},{6,7},{7,6},{8,9},{9,8},{10,11... | collective-permute-start | bytes 638984 | tf_op jit(solution)/shard_map/ppermute | solution.py:33
  34.6 9.9 %collective-permute-start.8 = (bf16[4,16,1664]{2,1,0:T(8,128)(2,1)S(1)}, bf16[4,16,1664]{2,1,0:T(8,128)(2,1)S(1)}, u32[]{:S(2)}, u32[]{:S(2)}) collective-permute-start(bf16[4,16,1664]{2,1,0:T(8,128)(2,1)S(1)} %collective-permute-done.4.refs_2_), channel_id=1, source_target_pairs={{0,1},{1,0},{2,3},{3,2},{4,5},{5,4},{6,7},{7,6},{8,9},{9,8},{10,11... | collective-permute-start | bytes 638984 | tf_op jit(solution)/shard_map/ppermute | solution.py:33
  40.7 4.5 %collective-permute-start.9 = (bf16[4,16,1664]{2,1,0:T(8,128)(2,1)S(1)}, bf16[4,16,1664]{2,1,0:T(8,128)(2,1)S(1)}, u32[]{:S(2)}, u32[]{:S(2)}) collective-permute-start(bf16[4,16,1664]{2,1,0:T(8,128)(2,1)S(1)} %collective-permute-done.5.refs_3_), channel_id=1, source_target_pairs={{0,1},{1,0},{2,3},{3,2},{4,5},{5,4},{6,7},{7,6},{8,9},{9,8},{10,11... | collective-permute-start | bytes 638984 | tf_op jit(solution)/shard_map/ppermute | solution.py:33
  41.1 18.3 %copy-start.11 = (bf16[4,32,2048]{2,1,0:T(8,128)(2,1)}, bf16[4,32,2048]{2,1,0:T(8,128)(2,1)S(1)}, u32[]{:S(2)}) copy-start(bf16[4,32,2048]{2,1,0:T(8,128)(2,1)S(1)} %collective-permute-done.16.refs_1_) | copy-start | bytes 1572868
  41.1 16.7 %collective-permute-start.20 = (bf16[4,80,512]{2,1,0:T(8,128)(2,1)S(1)}, bf16[4,80,512]{2,1,0:T(8,128)(2,1)S(1)}, u32[]{:S(2)}, u32[]{:S(2)}) collective-permute-start(bf16[4,80,512]{2,1,0:T(8,128)(2,1)S(1)} %pad_maximum_fusion.2.refs_8_), channel_id=1, source_target_pairs={{0,8},{1,9},{2,10},{3,11},{4,12},{5,13},{6,14},{7,15},{8,0},{9,1},... | collective-permute-start | bytes 983048 | tf_op jit(solution)/shard_map/ppermute | solution.py:33
  41.2 17.1 %collective-permute-start.18 = (bf16[4,32,2048]{2,1,0:T(8,128)(2,1)S(1)}, bf16[4,32,2048]{2,1,0:T(8,128)(2,1)S(1)}, u32[]{:S(2)}, u32[]{:S(2)}) collective-permute-start(bf16[4,32,2048]{2,1,0:T(8,128)(2,1)S(1)} %pad_maximum_fusion.1.refs_10_.refs_0_), channel_id=1, source_target_pairs={{0,4},{1,3},{2,6},{3,1},{4,0},{5,7},{6,2},{7,5},{8,12},{9,11},{10,... | collective-permute-start | bytes 1572872 | tf_op jit(solution)/shard_map/ppermute | solution.py:33
  42.5 15.8 %collective-permute-start.21 = (bf16[4,80,512]{2,1,0:T(8,128)(2,1)S(1)}, bf16[4,80,512]{2,1,0:T(8,128)(2,1)S(1)}, u32[]{:S(2)}, u32[]{:S(2)}) collective-permute-start(bf16[4,80,512]{2,1,0:T(8,128)(2,1)S(1)} %collective-permute-done.17.refs_10_), channel_id=1, source_target_pairs={{0,8},{1,9},{2,10},{3,11},{4,12},{5,13},{6,14},{7,15},{8,0},{9,1},... | collective-permute-start | bytes 983048 | tf_op jit(solution)/shard_map/ppermute | solution.py:33
  44.4 13.9 %collective-permute-start.19 = (bf16[4,32,2048]{2,1,0:T(8,128)(2,1)S(1)}, bf16[4,32,2048]{2,1,0:T(8,128)(2,1)S(1)}, u32[]{:S(2)}, u32[]{:S(2)}) collective-permute-start(bf16[4,32,2048]{2,1,0:T(8,128)(2,1)S(1)} %collective-permute-done.16.refs_1_), channel_id=1, source_target_pairs={{0,4},{1,3},{2,6},{3,1},{4,0},{5,7},{6,2},{7,5},{8,12},{9,11},{10,... | collective-permute-start | bytes 1572872 | tf_op jit(solution)/shard_map/ppermute | solution.py:33
  58.3 6.2 %copy-start.12 = (bf16[4,32,2048]{2,1,0:T(8,128)(2,1)}, bf16[4,32,2048]{2,1,0:T(8,128)(2,1)S(1)}, u32[]{:S(2)}) copy-start(bf16[4,32,2048]{2,1,0:T(8,128)(2,1)S(1)} %collective-permute-done.18.refs_2_) | copy-start | bytes 1572868
  58.3 6.2 %copy-start.13 = (bf16[4,32,2048]{2,1,0:T(8,128)(2,1)}, bf16[4,32,2048]{2,1,0:T(8,128)(2,1)S(1)}, u32[]{:S(2)}) copy-start(bf16[4,32,2048]{2,1,0:T(8,128)(2,1)S(1)} %collective-permute-done.19.refs_3_) | copy-start | bytes 1572868
  58.3 1.7 %collective-permute-start.26 = (bf16[4,80,512]{2,1,0:T(8,128)(2,1)S(1)}, bf16[4,80,512]{2,1,0:T(8,128)(2,1)S(1)}, u32[]{:S(2)}, u32[]{:S(2)}) collective-permute-start(bf16[4,80,512]{2,1,0:T(8,128)(2,1)S(1)} %pad_maximum_fusion.2.refs_8_), channel_id=1, source_target_pairs={{0,1},{1,0},{2,3},{3,2},{4,5},{5,4},{6,7},{7,6},{8,9},{9,8},{10,11... | collective-permute-start | bytes 983048 | tf_op jit(solution)/shard_map/ppermute | solution.py:33
  58.4 2.1 %collective-permute-start.27 = (bf16[4,80,512]{2,1,0:T(8,128)(2,1)S(1)}, bf16[4,80,512]{2,1,0:T(8,128)(2,1)S(1)}, u32[]{:S(2)}, u32[]{:S(2)}) collective-permute-start(bf16[4,80,512]{2,1,0:T(8,128)(2,1)S(1)} %collective-permute-done.20.refs_9_), channel_id=1, source_target_pairs={{0,1},{1,0},{2,3},{3,2},{4,5},{5,4},{6,7},{7,6},{8,9},{9,8},{10,11... | collective-permute-start | bytes 983048 | tf_op jit(solution)/shard_map/ppermute | solution.py:33
  58.9 2.5 %collective-permute-start.28 = (bf16[4,80,512]{2,1,0:T(8,128)(2,1)S(1)}, bf16[4,80,512]{2,1,0:T(8,128)(2,1)S(1)}, u32[]{:S(2)}, u32[]{:S(2)}) collective-permute-start(bf16[4,80,512]{2,1,0:T(8,128)(2,1)S(1)} %collective-permute-done.17.refs_10_), channel_id=1, source_target_pairs={{0,1},{1,0},{2,3},{3,2},{4,5},{5,4},{6,7},{7,6},{8,9},{9,8},{10,11... | collective-permute-start | bytes 983048 | tf_op jit(solution)/shard_map/ppermute | solution.py:33
  59.0 5.4 %collective-permute-start.22 = (bf16[4,32,2048]{2,1,0:T(8,128)(2,1)}, bf16[4,32,2048]{2,1,0:T(8,128)(2,1)S(1)}, u32[]{:S(2)}, u32[]{:S(2)}) collective-permute-start(bf16[4,32,2048]{2,1,0:T(8,128)(2,1)} %copy-done.9), channel_id=1, source_target_pairs={{0,1},{1,0},{2,3},{3,2},{4,5},{5,4},{6,7},{7,6},{8,9},{9,8},{10,11... | collective-permute-start | bytes 1572872 | tf_op jit(solution)/shard_map/ppermute | solution.py:33
  59.4 5.0 %collective-permute-start.23 = (bf16[4,32,2048]{2,1,0:T(8,128)(2,1)S(1)}, bf16[4,32,2048]{2,1,0:T(8,128)(2,1)S(1)}, u32[]{:S(2)}, u32[]{:S(2)}) collective-permute-start(bf16[4,32,2048]{2,1,0:T(8,128)(2,1)S(1)} %collective-permute-done.16.refs_1_), channel_id=1, source_target_pairs={{0,1},{1,0},{2,3},{3,2},{4,5},{5,4},{6,7},{7,6},{8,9},{9,8},{10,11... | collective-permute-start | bytes 1572872 | tf_op jit(solution)/shard_map/ppermute | solution.py:33
  60.0 4.4 %collective-permute-start.24 = (bf16[4,32,2048]{2,1,0:T(8,128)(2,1)S(1)}, bf16[4,32,2048]{2,1,0:T(8,128)(2,1)S(1)}, u32[]{:S(2)}, u32[]{:S(2)}) collective-permute-start(bf16[4,32,2048]{2,1,0:T(8,128)(2,1)S(1)} %collective-permute-done.18.refs_2_), channel_id=1, source_target_pairs={{0,1},{1,0},{2,3},{3,2},{4,5},{5,4},{6,7},{7,6},{8,9},{9,8},{10,11... | collective-permute-start | bytes 1572872 | tf_op jit(solution)/shard_map/ppermute | solution.py:33
  60.5 4.0 %collective-permute-start.25 = (bf16[4,32,2048]{2,1,0:T(8,128)(2,1)S(1)}, bf16[4,32,2048]{2,1,0:T(8,128)(2,1)S(1)}, u32[]{:S(2)}, u32[]{:S(2)}) collective-permute-start(bf16[4,32,2048]{2,1,0:T(8,128)(2,1)S(1)} %collective-permute-done.19.refs_3_), channel_id=1, source_target_pairs={{0,1},{1,0},{2,3},{3,2},{4,5},{5,4},{6,7},{7,6},{8,9},{9,8},{10,11... | collective-permute-start | bytes 1572872 | tf_op jit(solution)/shard_map/ppermute | solution.py:33
  61.4 3.0 %collective-permute-start.29 = (bf16[4,80,512]{2,1,0:T(8,128)(2,1)S(1)}, bf16[4,80,512]{2,1,0:T(8,128)(2,1)S(1)}, u32[]{:S(2)}, u32[]{:S(2)}) collective-permute-start(bf16[4,80,512]{2,1,0:T(8,128)(2,1)S(1)} %collective-permute-done.21.refs_11_), channel_id=1, source_target_pairs={{0,1},{1,0},{2,3},{3,2},{4,5},{5,4},{6,7},{7,6},{8,9},{9,8},{10,11... | collective-permute-start | bytes 983048 | tf_op jit(solution)/shard_map/ppermute | solution.py:33
  64.4 1.1 copy-start.15
  64.5 1.1 copy-start.16
  64.5 1.3 copy-start.17
  65.8 13.9 %copy-start = (bf16[512,1664]{1,0:T(8,128)(2,1)S(1)}, bf16[512,1664]{1,0:T(8,128)(2,1)}, u32[]{:S(2)}) copy-start(bf16[512,1664]{1,0:T(8,128)(2,1)} %get-tuple-element.111.refs_4_) | copy-start | bytes 5111812
  65.8 13.9 %copy-start.1 = (bf16[2048,256]{1,0:T(8,128)(2,1)S(1)}, bf16[2048,256]{1,0:T(8,128)(2,1)}, u32[]{:S(2)}) copy-start(bf16[2048,256]{1,0:T(8,128)(2,1)} %get-tuple-element.109.refs_2_) | copy-start | bytes 3145732
  79.2 7.5 %collective-permute-start.30 = (bf16[8,32,2048]{2,1,0:T(8,128)(2,1)}, bf16[8,32,2048]{2,1,0:T(8,128)(2,1)S(1)}, u32[]{:S(2)}, u32[]{:S(2)}) collective-permute-start(bf16[8,32,2048]{2,1,0:T(8,128)(2,1)} %get-tuple-element.113), channel_id=1, source_target_pairs={{0,1},{1,0},{2,3},{3,2},{4,5},{5,4},{6,7},{7,6},{8,9},{9,8},{10,11... | collective-permute-start | bytes 3145736 | tf_op jit(solution)/shard_map/ppermute | solution.py:33
  79.4 7.3 %collective-permute-start.31 = (bf16[16,16,2048]{2,1,0:T(8,128)(2,1)}, bf16[16,16,2048]{2,1,0:T(8,128)(2,1)S(1)}, u32[]{:S(2)}, u32[]{:S(2)}) collective-permute-start(bf16[16,16,2048]{2,1,0:T(8,128)(2,1)} %get-tuple-element.114), channel_id=1, source_target_pairs={{0,1},{1,0},{2,3},{3,2},{4,5},{5,4},{6,7},{7,6},{8,9},{9,8},{10,11... | collective-permute-start | bytes 3145736 | tf_op jit(solution)/shard_map/ppermute | solution.py:33
  79.7 7.0 %copy-start.3 = (bf16[16,32,2048]{2,1,0:T(8,128)(2,1)S(1)}, bf16[16,32,2048]{2,1,0:T(8,128)(2,1)}, u32[]{:S(2)}) copy-start(bf16[16,32,2048]{2,1,0:T(8,128)(2,1)} %get-tuple-element.127) | copy-start | bytes 6291460
  86.7 2.7 %copy-start.5 = (bf16[16,16,2048]{2,1,0:T(8,128)(2,1)S(1)}, bf16[16,16,2048]{2,1,0:T(8,128)(2,1)}, u32[]{:S(2)}) copy-start(bf16[16,16,2048]{2,1,0:T(8,128)(2,1)} %get-tuple-element.125) | copy-start | bytes 3145732
  86.7 2.8 %copy-start.7 = (bf16[16,16,2048]{2,1,0:T(8,128)(2,1)}, bf16[16,16,2048]{2,1,0:T(8,128)(2,1)S(1)}, u32[]{:S(2)}) copy-start(bf16[16,16,2048]{2,1,0:T(8,128)(2,1)S(1)} %collective-permute-done.31) | copy-start | bytes 3145732
  88.1 17.9 %collective-permute-start.33 = (bf16[8,32,2048]{2,1,0:T(8,128)(2,1)}, bf16[8,32,2048]{2,1,0:T(8,128)(2,1)}, u32[]{:S(2)}, u32[]{:S(2)}) collective-permute-start(bf16[8,32,2048]{2,1,0:T(8,128)(2,1)} %add_convert_fusion), channel_id=1, source_target_pairs={{0,4},{1,3},{2,6},{3,1},{4,0},{5,7},{6,2},{7,5},{8,12},{9,11},{10,... | collective-permute-start | bytes 3145736 | tf_op jit(solution)/shard_map/ppermute | solution.py:33
  89.5 16.5 %collective-permute-start.34 = (bf16[8,16,2048]{2,1,0:T(8,128)(2,1)S(1)}, bf16[8,16,2048]{2,1,0:T(8,128)(2,1)}, u32[]{:S(2)}, u32[]{:S(2)}) collective-permute-start(bf16[8,16,2048]{2,1,0:T(8,128)(2,1)S(1)} %add_convert_fusion.2.refs_15_), channel_id=1, source_target_pairs={{0,8},{1,9},{2,10},{3,11},{4,12},{5,13},{6,14},{7,15},{8,0},{9,1},... | collective-permute-start | bytes 1572872 | tf_op jit(solution)/shard_map/ppermute | solution.py:33
  103.8 1.6 %collective-permute-start.35 = (bf16[4,16,2176]{2,1,0:T(8,128)(2,1)S(1)}, bf16[4,16,2176]{2,1,0:T(8,128)(2,1)S(1)}, u32[]{:S(2)}, u32[]{:S(2)}) collective-permute-start(bf16[4,16,2176]{2,1,0:T(8,128)(2,1)S(1)} %get-tuple-element.133), channel_id=1, source_target_pairs={{0,1},{1,0},{2,3},{3,2},{4,5},{5,4},{6,7},{7,6},{8,9},{9,8},{10,11... | collective-permute-start | bytes 835592 | tf_op jit(solution)/shard_map/ppermute | solution.py:33
  103.9 2.1 %collective-permute-start.36 = (bf16[4,16,2176]{2,1,0:T(8,128)(2,1)S(1)}, bf16[4,16,2176]{2,1,0:T(8,128)(2,1)}, u32[]{:S(2)}, u32[]{:S(2)}) collective-permute-start(bf16[4,16,2176]{2,1,0:T(8,128)(2,1)S(1)} %get-tuple-element.134), channel_id=1, source_target_pairs={{0,1},{1,0},{2,3},{3,2},{4,5},{5,4},{6,7},{7,6},{8,9},{9,8},{10,11... | collective-permute-start | bytes 835592 | tf_op jit(solution)/shard_map/ppermute | solution.py:33
  104.4 4.0 %collective-permute-start.38 = (bf16[8,32,2048]{2,1,0:T(8,128)(2,1)}, bf16[8,32,2048]{2,1,0:T(8,128)(2,1)S(1)}, u32[]{:S(2)}, u32[]{:S(2)}) collective-permute-start(bf16[8,32,2048]{2,1,0:T(8,128)(2,1)} %get-tuple-element.140), channel_id=1, source_target_pairs={{0,1},{1,0},{2,3},{3,2},{4,5},{5,4},{6,7},{7,6},{8,9},{9,8},{10,11... | collective-permute-start | bytes 3145736 | tf_op jit(solution)/shard_map/ppermute | solution.py:33
  105.5 15.8 %collective-permute-start.32 = (bf16[8,16,2176]{2,1,0:T(8,128)(2,1)}, bf16[8,16,2176]{2,1,0:T(8,128)(2,1)S(1)}, u32[]{:S(2)}, u32[]{:S(2)}) collective-permute-start(bf16[8,16,2176]{2,1,0:T(8,128)(2,1)} %get-tuple-element.132), channel_id=1, source_target_pairs={{0,1},{1,0},{2,3},{3,2},{4,5},{5,4},{6,7},{7,6},{8,9},{9,8},{10,11... | collective-permute-start | bytes 1671176 | tf_op jit(solution)/shard_map/ppermute | solution.py:33
  106.0 4.9 %copy-start.6 = (bf16[16,16,2048]{2,1,0:T(8,128)(2,1)S(1)}, bf16[16,16,2048]{2,1,0:T(8,128)(2,1)}, u32[]{:S(2)}) copy-start(bf16[16,16,2048]{2,1,0:T(8,128)(2,1)} %get-tuple-element.125) | copy-start | bytes 3145732
  106.0 4.9 %copy-start.8 = (bf16[16,16,2048]{2,1,0:T(8,128)(2,1)S(1)}, bf16[16,16,2048]{2,1,0:T(8,128)(2,1)}, u32[]{:S(2)}) copy-start(bf16[16,16,2048]{2,1,0:T(8,128)(2,1)} %copy-done.7) | copy-start | bytes 3145732
  107.4 13.9 %copy-start.4 = (bf16[16,16,2176]{2,1,0:T(8,128)(2,1)S(1)}, bf16[16,16,2176]{2,1,0:T(8,128)(2,1)}, u32[]{:S(2)}) copy-start(bf16[16,16,2176]{2,1,0:T(8,128)(2,1)} %get-tuple-element.131) | copy-start | bytes 3342340
  107.5 13.8 %collective-permute-start.37 = (bf16[8,16,2176]{2,1,0:T(8,128)(2,1)S(1)}, bf16[8,16,2176]{2,1,0:T(8,128)(2,1)S(1)}, u32[]{:S(2)}, u32[]{:S(2)}) collective-permute-start(bf16[8,16,2176]{2,1,0:T(8,128)(2,1)S(1)} %pad_maximum_fusion), channel_id=1, source_target_pairs={{0,4},{1,3},{2,6},{3,1},{4,0},{5,7},{6,2},{7,5},{8,12},{9,11},{10,... | collective-permute-start | bytes 1671176 | tf_op jit(solution)/shard_map/ppermute | solution.py:33
  109.7 14.3 %collective-permute-start.41 = (bf16[4,32,2048]{2,1,0:T(8,128)(2,1)S(1)}, bf16[4,32,2048]{2,1,0:T(8,128)(2,1)S(1)}, u32[]{:S(2)}, u32[]{:S(2)}) collective-permute-start(bf16[4,32,2048]{2,1,0:T(8,128)(2,1)S(1)} %add_convert_fusion.1), channel_id=1, source_target_pairs={{0,2},{1,5},{2,0},{3,7},{4,6},{5,1},{6,4},{7,3},{8,10},{9,13},{10,... | collective-permute-start | bytes 1572872 | tf_op jit(solution)/shard_map/ppermute | solution.py:33
  112.0 14.9 %collective-permute-start.40 = (bf16[4,16,2048]{2,1,0:T(8,128)(2,1)S(1)}, bf16[4,16,2048]{2,1,0:T(8,128)(2,1)S(1)}, u32[]{:S(2)}, u32[]{:S(2)}) collective-permute-start(bf16[4,16,2048]{2,1,0:T(8,128)(2,1)S(1)} %add_convert_fusion.7), channel_id=1, source_target_pairs={{0,16},{1,17},{2,18},{3,19},{4,20},{5,21},{6,22},{7,23},{8,24},{9,... | collective-permute-start | bytes 786440 | tf_op jit(solution)/shard_map/ppermute | solution.py:33
  121.4 7.7 %collective-permute-start.39 = (bf16[4,16,2176]{2,1,0:T(8,128)(2,1)S(1)}, bf16[4,16,2176]{2,1,0:T(8,128)(2,1)S(1)}, u32[]{:S(2)}, u32[]{:S(2)}) collective-permute-start(bf16[4,16,2176]{2,1,0:T(8,128)(2,1)S(1)} %add_convert_fusion.3), channel_id=1, source_target_pairs={{0,2},{1,5},{2,0},{3,7},{4,6},{5,1},{6,4},{7,3},{8,10},{9,13},{10,... | collective-permute-start | bytes 835592 | tf_op jit(solution)/shard_map/ppermute | solution.py:33
  125.1 8.6 %collective-permute-start.43 = (bf16[2,32,2048]{2,1,0:T(8,128)(2,1)S(1)}, bf16[2,32,2048]{2,1,0:T(8,128)(2,1)S(1)}, u32[]{:S(2)}, u32[]{:S(2)}) collective-permute-start(bf16[2,32,2048]{2,1,0:T(8,128)(2,1)S(1)} %add_convert_fusion.6), channel_id=1, source_target_pairs={{0,8},{1,9},{2,10},{3,11},{4,12},{5,13},{6,14},{7,15},{8,0},{9,1},... | collective-permute-start | bytes 786440 | tf_op jit(solution)/shard_map/ppermute | solution.py:33
  127.9 5.0 %collective-permute-start.44 = (bf16[2,16,2048]{2,1,0:T(8,128)(2,1)S(1)}, bf16[2,16,2048]{2,1,0:T(8,128)(2,1)S(1)}, u32[]{:S(2)}, u32[]{:S(2)}) collective-permute-start(bf16[2,16,2048]{2,1,0:T(8,128)(2,1)S(1)} %add_convert_fusion.10), channel_id=1, source_target_pairs={{0,4},{1,3},{2,6},{3,1},{4,0},{5,7},{6,2},{7,5},{8,12},{9,11},{10,... | collective-permute-start | bytes 393224 | tf_op jit(solution)/shard_map/ppermute | solution.py:33
  129.1 10.1 %collective-permute-start.42 = (bf16[2,16,2176]{2,1,0:T(8,128)(2,1)S(1)}, bf16[2,16,2176]{2,1,0:T(8,128)(2,1)S(1)}, u32[]{:S(2)}, u32[]{:S(2)}) collective-permute-start(bf16[2,16,2176]{2,1,0:T(8,128)(2,1)S(1)} %add_convert_fusion.8), channel_id=1, source_target_pairs={{0,8},{1,9},{2,10},{3,11},{4,12},{5,13},{6,14},{7,15},{8,0},{9,1},... | collective-permute-start | bytes 417800 | tf_op jit(solution)/shard_map/ppermute | solution.py:33
  134.8 8.6 %collective-permute-start.46 = (bf16[32,2048]{1,0:T(8,128)(2,1)S(1)}, bf16[32,2048]{1,0:T(8,128)(2,1)S(1)}, u32[]{:S(2)}, u32[]{:S(2)}) collective-permute-start(bf16[32,2048]{1,0:T(8,128)(2,1)S(1)} %get-tuple-element.157), channel_id=1, source_target_pairs={{0,16},{1,17},{2,18},{3,19},{4,20},{5,21},{6,22},{7,23},{8,24},{9,... | collective-permute-start | bytes 393224 | tf_op jit(solution)/shard_map/ppermute | solution.py:33
  138.2 4.3 %collective-permute-start.47 = (bf16[1,16,2048]{2,1,0:T(8,128)(2,1)S(1)}, bf16[1,16,2048]{2,1,0:T(8,128)(2,1)S(1)}, u32[]{:S(2)}, u32[]{:S(2)}) collective-permute-start(bf16[1,16,2048]{2,1,0:T(8,128)(2,1)S(1)} %add_convert_fusion.12), channel_id=1, source_target_pairs={{0,2},{1,5},{2,0},{3,7},{4,6},{5,1},{6,4},{7,3},{8,10},{9,13},{10,... | collective-permute-start | bytes 196616 | tf_op jit(solution)/shard_map/ppermute | solution.py:33
  139.3 5.7 %collective-permute-start.45 = (bf16[16,2176]{1,0:T(8,128)(2,1)S(1)}, bf16[16,2176]{1,0:T(8,128)(2,1)S(1)}, u32[]{:S(2)}, u32[]{:S(2)}) collective-permute-start(bf16[16,2176]{1,0:T(8,128)(2,1)S(1)} %get-tuple-element.158), channel_id=1, source_target_pairs={{0,16},{1,17},{2,18},{3,19},{4,20},{5,21},{6,22},{7,23},{8,24},{9,... | collective-permute-start | bytes 208904 | tf_op jit(solution)/shard_map/ppermute | solution.py:33
  (2 other events, 1.6 us)
